TPU v7x, 128 devices: a whole 4x4x4 slice. The times are simulated.
128 devices in a mesh: blk: 8 (over x, z_lo), cuts: 16 (over y, z_hi, core).
Axes of the slice: x: 4, y: 4, z: 4 (z_hi: 2, z_lo: 2; z = z_hi * 2 + z_lo), core: 2. Of those that a mesh axis runs over, the one named last changes fastest.
Arguments:
- summaries: bfloat16 [16384, 5120], P('blk', 'cuts')
- head: bfloat16 [5120, 1024], P('cuts'), may hold values from -0.078125 to 0.078125
- partner: int32 [16384], P('blk'), may hold values from 0 to 16383, as said below
Outputs:
- loss: float32 [], replicated
- grad_summaries: bfloat16 [16384, 5120], P('blk', 'cuts')
- grad_head: float32 [5120, 1024], P('cuts')
Inputs may be any that keep to these rules, and one draw needn't show every extreme that they name: partner pairs the rows: partner[partner[i]] = i and partner[i] != i for every row i.
All inputs are finite; a program needn't handle non-finite values.
Results may differ from a plain program's by a relative error of at most 0.017.
Values may be sent and summed in bfloat16 or wider, within the bound.
No kernel may reach another device: no remote copies, remote signals or barrier semaphores. Data moves between devices by JAX's collectives and lax.ppermute only.
A program may use at most 64 MiB of HBM per device.

v0:
```python
import jax
import jax.numpy as jnp
from jax import lax
from jax.sharding import PartitionSpec as P


def shards(summaries, head, partner):
    group = summaries.shape[0]
    count_cuts = lax.axis_size("cuts")
    count_blk = lax.axis_size("blk")
    rows = group // count_cuts
    blk_index = lax.axis_index("blk")
    cut_index = lax.axis_index("cuts")
    total_rows = group * count_blk
    piece = summaries
    z = lax.psum_scatter(
        jnp.dot(piece, head, preferred_element_type=jnp.float32),
        "cuts",
        scatter_dimension=0,
        tiled=True,
    )
    inv = lax.rsqrt(jnp.sum(z * z, axis=1, keepdims=True) + 1e-06)
    unit = z * inv
    emb = unit.astype(jnp.bfloat16)
    queries = lax.all_gather(emb, "cuts", axis=0, tiled=True)
    keys = lax.all_gather(emb, "blk", axis=0, tiled=True)
    key_local = jnp.arange(keys.shape[0], dtype=jnp.int32)
    kglob = key_local // rows * group + cut_index * rows + key_local % rows
    qglob = blk_index * group + jnp.arange(group, dtype=jnp.int32)
    scores = 20.0 * lax.dot_general(
        queries, keys, (((1,), (1,)), ((), ())), preferred_element_type=jnp.float32
    )
    live = qglob[:, None] != kglob[None, :]
    weights = jnp.where(live, jnp.exp(scores), jnp.float32(0.0))
    hit = (partner[:, None] == kglob[None, :]).astype(jnp.float32)
    den_part = jnp.sum(weights, axis=1)
    pos_part = jnp.sum(scores * hit, axis=1)
    den, pos = lax.psum((den_part, pos_part), "cuts")
    losses = jnp.log(den) - pos
    grad_scores = (20.0 * (weights / den[:, None] - hit)).astype(jnp.bfloat16)
    piece = grad_scores
    query_grad = lax.psum_scatter(
        jnp.dot(piece, keys, preferred_element_type=jnp.float32),
        "cuts",
        scatter_dimension=0,
        tiled=True,
    )
    piece = grad_scores
    key_grad = lax.psum_scatter(
        lax.dot_general(
            piece, queries, (((0,), (0,)), ((), ())), preferred_element_type=jnp.float32
        ),
        "blk",
        scatter_dimension=0,
        tiled=True,
    )
    grad_emb = query_grad + key_grad
    grad_z = (inv * (grad_emb - unit * jnp.sum(unit * grad_emb, axis=1, keepdims=True))).astype(
        jnp.bfloat16
    )
    grad_group = lax.all_gather(grad_z, "cuts", axis=0, tiled=True)
    grad_summaries = lax.dot_general(
        grad_group, head, (((1,), (1,)), ((), ())), preferred_element_type=jnp.float32
    ).astype(jnp.bfloat16)
    head_part = lax.dot_general(
        summaries, grad_group, (((0,), (0,)), ((), ())), preferred_element_type=jnp.float32
    )
    grad_head = lax.psum(head_part.astype(jnp.bfloat16), "blk").astype(jnp.float32)
    own_losses = lax.dynamic_slice_in_dim(losses, cut_index * rows, rows, 0)
    loss = lax.psum(jnp.sum(own_losses), ("blk", "cuts")) / total_rows
    return (loss, grad_summaries, grad_head)


def solution(mesh):
    in_specs = (P("blk", "cuts"), P("cuts", None), P("blk"))
    out_specs = (P(), P("blk", "cuts"), P("cuts", None))
    return jax.shard_map(shards, mesh=mesh, in_specs=in_specs, out_specs=out_specs, check_vma=False)
```

profile of v0, /device:TPU:0, one launch (start us, length us, event | category | flops | bytes accessed | tf_op | source)
XLA Modules:
  0.0 665.8 jit_solution(7561169033253658944)
XLA Ops:
  7.2 0.0 copy-start
  7.2 0.0 reduce-scatter.4.cloned.1.call-start
  7.2 1.3 copy-done
  8.5 6.7 %fusion.17 = f32[2048,1024]{1,0:T(8,128)} fusion(bf16[2048,320]{0,1:T(8,128)(2,1)S(1)} %copy-done, bf16[320,1024]{1,0:T(8,128)(2,1)} %param.4), kind=kOutput, calls=%fused_computation.34 | convolution fusion | flops 1342177280 | bytes 10354688 | tf_op jit(solution)/shard_map/dot_general | solution.py:17
  15.2 0.0 copy-start.4
  15.2 0.0 reduce-scatter.4.cloned.1.call-update
  15.2 0.0 all-gather.6.cloned.1.call-start
  15.2 105.2 %reduce-scatter.4.cloned.1.call-done = f32[128,1024]{1,0:T(8,128)} async-done(((f32[2048,1024]{1,0:T(8,128)}), f32[128,1024]{1,0:T(8,128)}) %reduce-scatter.4.cloned.1.call-update) | async-done | bytes 524304 | tf_op jit(solution)/shard_map/reduce_scatter | solution.py:16
  120.5 1.2 multiply_reduce_fusion.1
  121.6 1.8 multiply_convert_fusion.1
  123.5 0.0 all-gather.6.cloned.1.call-update
  123.5 0.0 all-gather.4.cloned.1.call-start
  123.5 0.7 all-gather.4.cloned.1.call-update
  124.2 0.0 reduce-scatter.8.cloned.1.call-start
  124.3 49.2 %all-gather.6.cloned.1.call-done = bf16[1024,1024]{1,0:T(8,128)(2,1)} async-done(((bf16[128,1024]{1,0:T(8,128)(2,1)}), bf16[1024,1024]{1,0:T(8,128)(2,1)}) %all-gather.6.cloned.1.call-update) | async-done | bytes 2097168 | tf_op jit(solution)/shard_map/all_gather | solution.py:26
  173.5 59.3 %all-gather.4.cloned.1.call-done = bf16[2048,1024]{1,0:T(8,128)(2,1)} async-done(((bf16[128,1024]{1,0:T(8,128)(2,1)}), bf16[2048,1024]{1,0:T(8,128)(2,1)}) %all-gather.4.cloned.1.call-update) | async-done | bytes 4194320 | tf_op jit(solution)/shard_map/all_gather | solution.py:25
  232.8 0.0 copy-done.4
  232.8 10.7 %fusion.4 = (f32[2048]{0:T(1024)S(1)}, f32[2048]{0:T(1024)S(1)}, f32[2048,1024]{0,1:T(8,128)}) fusion(s32[2048]{0:T(1024)S(1)} %iota_add_fusion, s32[1024]{0:T(1024)S(1)} %fusion.14, s32[2048]{0:T(1024)S(1)} %copy-done.4, bf16[2048,1024]{1,0:T(8,128)(2,1)} %all-gather.4.cloned.1.call-done, bf16[1024,1024]{1,0:T(8,128)(2,1)} %all-gather.6.cloned.1.call-done), kind=kOutput, calls=%fused_computation.7 | convolution fusion | flops 4309643264 | bytes 14716928 | tf_op jit(solution)/shard_map/dot_general | solution.py:30
  243.5 66.9 %all-reduce = (f32[2048]{0:T(1024)S(1)}, f32[2048]{0:T(1024)S(1)}) all-reduce(f32[2048]{0:T(1024)S(1)} %get-tuple-element.4, f32[2048]{0:T(1024)S(1)} %get-tuple-element.3), channel_id=1, replica_groups=mesh['blk'=8,'cuts'=16] {'cuts'}, use_global_device_ids=true, to_apply=%region_5.6 | all-reduce | flops 4096 | bytes 32768 | tf_op jit(solution)/shard_map/psum | solution.py:38
  310.4 0.0 copy-start.5
  310.4 5.5 fusion.3
  315.9 0.0 copy-start.2
  315.9 2.0 copy-done.2
  317.8 0.0 copy-done.5
  317.8 6.0 fusion.19
  323.9 0.0 reduce-scatter.8.cloned.1.call-update
  323.9 0.2 reduce-scatter.6.cloned.1.call-start
  324.1 10.7 %fusion.18 = f32[2048,1024]{1,0:T(8,128)} fusion(bf16[2048,1024]{0,1:T(8,128)(2,1)} %copy-done.2, bf16[1024,1024]{1,0:T(8,128)(2,1)} %all-gather.6.cloned.1.call-done), kind=kOutput, calls=%fused_computation.35 | convolution fusion | flops 4294967296 | bytes 14680064 | tf_op jit(solution)/shard_map/dot_general | solution.py:43
  334.8 0.0 copy-start.1
  334.8 0.0 reduce-scatter.6.cloned.1.call-update
  334.8 0.0 all-gather.8.cloned.1.call-start
  334.9 76.7 %reduce-scatter.8.cloned.1.call-done = f32[128,1024]{1,0:T(8,128)} async-done(((f32[1024,1024]{1,0:T(8,128)}), f32[128,1024]{1,0:T(8,128)}) %reduce-scatter.8.cloned.1.call-update) | async-done | bytes 524304 | tf_op jit(solution)/shard_map/reduce_scatter | solution.py:49
  411.6 107.8 %reduce-scatter.6.cloned.1.call-done = f32[128,1024]{1,0:T(8,128)} async-done(((f32[2048,1024]{1,0:T(8,128)}), f32[128,1024]{1,0:T(8,128)}) %reduce-scatter.6.cloned.1.call-update) | async-done | bytes 524304 | tf_op jit(solution)/shard_map/reduce_scatter | solution.py:42
  519.4 0.0 copy-done.1
  519.4 1.4 multiply_reduce_fusion
  520.8 0.9 multiply_convert_fusion
  521.6 0.0 all-gather.8.cloned.1.call-update
  521.7 0.0 copy-start.3
  521.7 0.0 all-reduce.3.cloned.1.call-start
  521.7 55.2 %all-gather.8.cloned.1.call-done = bf16[2048,1024]{1,0:T(8,128)(2,1)} async-done(((bf16[128,1024]{1,0:T(8,128)(2,1)}), bf16[2048,1024]{1,0:T(8,128)(2,1)}) %all-gather.8.cloned.1.call-update) | async-done | bytes 4194320 | tf_op jit(solution)/shard_map/all_gather | solution.py:61
  576.9 4.5 fusion.5
  581.5 0.0 all-reduce.3.cloned.1.call-update
  581.5 0.7 fusion.16
  582.2 65.4 %psum.30 = f32[]{:T(128)} all-reduce(f32[]{:T(128)} %fusion.16), channel_id=1, replica_groups=mesh['blk'=8,'cuts'=16] {'blk','cuts'}, use_global_device_ids=true, to_apply=%region_7.8 | all-reduce | flops 1 | bytes 8 | tf_op jit(solution)/shard_map/psum | solution.py:70
  648.2 0.0 copy-done.3
  648.2 4.8 convolution_convert_fusion
  653.1 2.5 all-reduce.3.cloned.1.call-done
  655.5 2.3 convert_element_type.31
  (3 shorter events, 0.0 us)
Async XLA Ops:
  7.2 1.3 copy-start
  7.2 113.3 %reduce-scatter.4.cloned.1.call-start = ((), (), s32[]{:S(2)}) async-start(), calls=%async_computation.3 | async-start | bytes 8912896 | tf_op jit(solution)/shard_map/reduce_scatter | solution.py:16
  15.2 217.6 %copy-start.4 = (s32[2048]{0:T(1024)S(1)}, s32[2048]{0:T(1024)}, u32[]{:S(2)}) copy-start(s32[2048]{0:T(1024)} %param.5) | copy-start | bytes 24580
  15.2 158.3 %all-gather.6.cloned.1.call-start = ((), (), s32[]{:S(2)}) async-start(), calls=%async_computation.5 | async-start | bytes 2359296 | tf_op jit(solution)/shard_map/all_gather | solution.py:26
  123.5 109.3 %all-gather.4.cloned.1.call-start = ((), (), s32[]{:S(2)}) async-start(), calls=%async_computation.4 | async-start | bytes 4456448 | tf_op jit(solution)/shard_map/all_gather | solution.py:25
  124.2 287.3 %reduce-scatter.8.cloned.1.call-start = ((), (), s32[]{:S(2)}) async-start(), calls=%async_computation.7 | async-start | bytes 4718592 | tf_op jit(solution)/shard_map/reduce_scatter | solution.py:49
  310.4 7.5 %copy-start.5 = (bf16[2048,1024]{1,0:T(8,128)(2,1)S(1)}, bf16[2048,1024]{1,0:T(8,128)(2,1)}, u32[]{:S(2)}) copy-start(bf16[2048,1024]{1,0:T(8,128)(2,1)} %all-gather.4.cloned.1.call-done) | copy-start | bytes 12582916
  315.9 2.0 copy-start.2
  323.9 195.5 %reduce-scatter.6.cloned.1.call-start = ((), (), s32[]{:S(2)}) async-start(), calls=%async_computation.6 | async-start | bytes 8912896 | tf_op jit(solution)/shard_map/reduce_scatter | solution.py:42
  334.8 184.6 %copy-start.1 = (f32[128,1024]{1,0:T(8,128)S(1)}, f32[128,1024]{1,0:T(8,128)}, u32[]{:S(2)}) copy-start(f32[128,1024]{1,0:T(8,128)} %reduce-scatter.4.cloned.1.call-done) | copy-start | bytes 1572868
  334.8 242.1 %all-gather.8.cloned.1.call-start = ((), (), s32[]{:S(2)}) async-start(), calls=%async_computation.8 | async-start | bytes 4456448 | tf_op jit(solution)/shard_map/all_gather | solution.py:61
  521.7 126.6 %copy-start.3 = (bf16[320,1024]{1,0:T(8,128)(2,1)S(1)}, bf16[320,1024]{1,0:T(8,128)(2,1)}, u32[]{:S(2)}) copy-start(bf16[320,1024]{1,0:T(8,128)(2,1)} %param.4) | copy-start | bytes 1966084
  521.7 133.8 %all-reduce.3.cloned.1.call-start = ((), (), s32[]{:S(2)}) async-start(), calls=%async_computation.9 | async-start | bytes 1310720 | tf_op jit(solution)/shard_map/psum | solution.py:68
Sparse Core Ops, SparseCore 0:
  15.3 105.0 reduce-scatter.3
  123.6 49.8 all-gather.5
  176.5 56.2 all-gather.3
  324.0 87.4 reduce-scatter.7
  415.7 103.6 reduce-scatter.5
  522.2 54.6 all-gather.7
  581.6 73.8 all-reduce.2
where the time goes:
time: 666 us
  waiting for transfers between devices  457 us (69%)
  blocking collectives  132 us (20%)
  matrix products  43.4 us (7%)
  between operations  16 us (2%)
  other arithmetic  13.8 us (2%)
    reduce_scatter x1, waiting for transfers between devices, shards(): lax.psum_scatter(jnp.dot(piece, keys, preferred_element_type=jnp.float32)...  108 us
    reduce_scatter x1, waiting for transfers between devices, shards(): lax.psum_scatter(jnp.dot(piece, head, preferred_element_type=jnp.float32)...  105 us
    reduce_scatter x1, waiting for transfers between devices, shards(): lax.psum_scatter(lax.dot_general(piece, queries, (((0,), (0,)), ((), ()))...  76.7 us
    psum x1, blocking collectives, shards(): den, pos = lax.psum((den_part, pos_part), 'cuts')  66.9 us
    psum x1, blocking collectives, shards(): loss = lax.psum(jnp.sum(own_losses), ('blk', 'cuts')) / total_rows  65.4 us
    all_gather x1, waiting for transfers between devices, shards(): queries = lax.all_gather(emb, 'cuts', axis=0, tiled=True)  59.3 us
    all_gather x1, waiting for transfers between devices, shards(): grad_group = lax.all_gather(grad_z, 'cuts', axis=0, tiled=True)  55.2 us
    all_gather x1, waiting for transfers between devices, shards(): keys = lax.all_gather(emb, 'blk', axis=0, tiled=True)  49.2 us
  transfers between devices with their start and end apart: 7, of which 7 were waited for; matrix products, arithmetic and copies ran while one was open for 2% of the time, Pallas kernels for 0%

commit v1 on v0

v1 whole, which is shorter than its diff:
```python
import jax
import jax.numpy as jnp
from jax import lax
from jax.sharding import Mesh
from jax.sharding import PartitionSpec as P

F32 = jnp.float32
BF16 = jnp.bfloat16
SWAP = [(0, 1), (1, 0)]
RING = {s: [(i, (i + s) % 4) for i in range(4)] for s in (1, 2, 3)}


def core_swap(value):
    return lax.ppermute(value, "c", SWAP)


def gather_ring(own, long_axis, short_axis):
    rows = own.shape[0]
    other = lax.ppermute(own, short_axis, SWAP)
    first = lax.axis_index(short_axis) == 0
    pair = jnp.concatenate([jnp.where(first, own, other), jnp.where(first, other, own)], 0)
    after = lax.ppermute(pair, long_axis, RING[3])
    before = lax.ppermute(pair, long_axis, RING[1])
    far_top = lax.ppermute(after[:rows], long_axis, RING[3])
    far_low = lax.ppermute(before[rows:], long_axis, RING[1])
    at = lax.axis_index(long_axis)
    out = jnp.zeros((8 * rows, own.shape[1]), own.dtype)
    for shift, part, skip in (
        (0, pair, 0),
        (1, after, 0),
        (3, before, 0),
        (2, far_top, 0),
        (2, far_low, rows),
    ):
        start = lax.rem(at + shift, 4) * (2 * rows) + skip
        out = lax.dynamic_update_slice_in_dim(out, part, start, 0)
    return out


def sum_exchange(parts, axes):
    got = lax.all_to_all(parts, axes, 0, 0)
    return jnp.sum(got.astype(F32), axis=0)


def sum_everywhere(vector, axes):
    vector = vector.reshape(-1, 128)
    got = lax.all_to_all(jnp.broadcast_to(vector[None], (8,) + vector.shape), axes, 0, 0)
    return jnp.sum(got, axis=0).reshape(-1)


def shards(summaries, head, partner):
    yz, xz = ("y", "zh"), ("x", "zl")
    core = lax.axis_index("c")
    group_at = lax.axis_index("x") * 2 + lax.axis_index("zl")
    chunk_at = lax.axis_index("y") * 2 + lax.axis_index("zh")
    half = summaries.shape[0] // 2
    rows = half // 8
    width = head.shape[1]

    mine = lax.dynamic_slice_in_dim(summaries, core * half, half, 0)
    theirs = core_swap(lax.dynamic_slice_in_dim(summaries, (1 - core) * half, half, 0))
    other_head = core_swap(head)
    z_part = jnp.dot(mine, head, preferred_element_type=F32) + jnp.dot(
        theirs, other_head, preferred_element_type=F32
    )
    z = sum_exchange(z_part.astype(BF16).reshape(8, rows, width), yz)
    inv = lax.rsqrt(jnp.sum(z * z, axis=1, keepdims=True) + 1e-06)
    unit = z * inv
    emb = unit.astype(BF16)

    queries = gather_ring(emb, "y", "zh")
    keys_mine = gather_ring(emb, "x", "zl")
    keys = jnp.concatenate([keys_mine, core_swap(keys_mine)], 0)

    qglob = group_at * (2 * half) + core * half + jnp.arange(half, dtype=jnp.int32)
    local = jnp.arange(2 * half, dtype=jnp.int32)
    key_core = jnp.where(local < half, core, 1 - core)
    kglob = (local % half) // rows * (2 * half) + key_core * half + chunk_at * rows + local % rows
    mates = lax.dynamic_slice_in_dim(partner, core * half, half, 0)

    scores = 20.0 * lax.dot_general(
        queries, keys, (((1,), (1,)), ((), ())), preferred_element_type=F32
    )
    weights = jnp.where(qglob[:, None] != kglob[None, :], jnp.exp(scores), F32(0.0))
    hit = mates[:, None] == kglob[None, :]
    pos_part = jnp.sum(jnp.where(hit, scores, 0.0))
    row_part = jnp.sum(weights, axis=1)
    column_part = jnp.sum(weights, axis=0)
    swapped = core_swap(column_part.reshape(-1, 128)).reshape(-1)
    column_part = column_part + jnp.concatenate([swapped[half:], swapped[:half]])
    pos_row = jnp.zeros((1024,), F32).at[0].set(pos_part)
    row_sums = sum_everywhere(jnp.concatenate([row_part, pos_row]), yz)
    den_q, pos = row_sums[:half], row_sums[half]
    den_k = sum_everywhere(column_part, xz)

    grad_scores = (
        weights * ((20.0 / den_q)[:, None] + (20.0 / den_k)[None, :]) - jnp.where(hit, 40.0, 0.0)
    ).astype(BF16)
    grad_part = jnp.dot(grad_scores, keys, preferred_element_type=F32).astype(BF16)
    grad_emb = sum_exchange(grad_part.reshape(8, rows, width), yz)

    loss = jnp.full((8, 128), jnp.sum(jnp.log(den_q)) - pos, F32)
    loss = loss + core_swap(loss)
    loss = loss + lax.ppermute(loss, "zl", SWAP)
    loss = loss + lax.ppermute(loss, "x", RING[2])
    loss = loss + lax.ppermute(loss, "x", RING[1])
    loss = loss[0, 0] / (16 * half)

    grad_z = (inv * (grad_emb - unit * jnp.sum(unit * grad_emb, axis=1, keepdims=True))).astype(BF16)
    grad_half = gather_ring(grad_z, "y", "zh")

    contract_first = (((0,), (0,)), ((), ()))
    head_theirs = lax.dot_general(
        theirs, grad_half, contract_first, preferred_element_type=F32
    ).astype(BF16)
    head_mine = lax.dot_general(mine, grad_half, contract_first, preferred_element_type=F32)
    head_part = (head_mine + core_swap(head_theirs).astype(F32)).astype(BF16)
    features = head.shape[0]
    pieces = head_part.reshape(features, 8, width // 8).transpose(1, 0, 2)
    head_sum = sum_exchange(pieces, xz).astype(BF16)
    spread = lax.all_to_all(jnp.broadcast_to(head_sum[None], (8,) + head_sum.shape), xz, 0, 0)
    grad_head = spread.transpose(1, 0, 2).reshape(features, width).astype(F32)

    contract_last = (((1,), (1,)), ((), ()))
    out_theirs = lax.dot_general(
        other_head, grad_half, contract_last, preferred_element_type=F32
    ).astype(BF16)
    out_mine = lax.dot_general(head, grad_half, contract_last, preferred_element_type=F32).astype(BF16)
    got = core_swap(out_theirs)
    first = core == 0
    out = jnp.concatenate([jnp.where(first, out_mine, got), jnp.where(first, got, out_mine)], 1)
    return loss, out.T, grad_head


def solution(mesh):
    fine = Mesh(mesh.devices.reshape(4, 2, 4, 2, 2), ("x", "zl", "y", "zh", "c"))
    blk, cuts = ("x", "zl"), ("y", "zh", "c")
    return jax.shard_map(
        shards,
        mesh=fine,
        in_specs=(P(blk, cuts), P(cuts, None), P(blk)),
        out_specs=(P(), P(blk, cuts), P(cuts, None)),
        check_vma=False,
    )
```

time: 666 us -> 269 us (0.40)
  waiting for transfers between devices: 457 us -> 93.6 us
  blocking collectives: 132 us -> 65.4 us
  starting transfers between devices: 0.47 us -> 44.9 us
  local copies, waits for them, and re-layouts: 3.25 us -> 17.8 us
  between operations: 16 us -> 4.09 us
  matrix products: 43.4 us -> 35.3 us
  other arithmetic: 13.8 us -> 6.95 us
    reduce_scatter x3 -> x0, waiting for transfers between devices: 290 us -> none  [the longest x1 108 us: shards(): lax.psum_scatter(jnp.dot(piece, keys, preferred_element_type=jnp.float32)...]
    all_gather x3 -> x0, waiting for transfers between devices: 164 us -> none  [the longest x1 59.3 us: shards(): queries = lax.all_gather(emb, 'cuts', axis=0, tiled=True)]
    psum x2 -> x0, blocking collectives: 132 us -> none  [the longest x1 66.9 us: shards(): den, pos = lax.psum((den_part, pos_part), 'cuts')]
    ppermute x0 -> x25, waiting for transfers between devices: none -> 74.8 us  [the longest x3 32.2 us: gather_ring(): after = lax.ppermute(pair, long_axis, RING[3])]
    all_to_all x0 -> x2, blocking collectives: none -> 65.4 us  [sum_exchange(): got = lax.all_to_all(parts, axes, 0, 0)]
    ppermute x0 -> x25, starting transfers between devices: none -> 31 us  [the longest x3 7.47 us: gather_ring(): far_top = lax.ppermute(after[:rows], long_axis, RING[3])]
    all_to_all x0 -> x4, waiting for transfers between devices: none -> 18.8 us  [the longest x2 13.2 us: sum_everywhere(): lax.all_to_all(jnp.broadcast_to(vector[None], (8,) + vector.shape), axes,...]
    all_to_all x0 -> x4, starting transfers between devices: none -> 13.9 us  [the longest x2 6.7 us: sum_everywhere(): lax.all_to_all(jnp.broadcast_to(vector[None], (8,) + vector.shape), axes,...]
  transfers between devices with their start and end apart: 7 -> 29, of which waited for: 7 -> 20; matrix products, arithmetic and copies ran while one was open for 2% -> 9% of each run, Pallas kernels for 0% -> 0%
where the time goes in v1:
time: 269 us; the launch traced here: 268 us
  waiting for transfers between devices  93.6 us (35%)
  blocking collectives  65.4 us (24%)
  starting transfers between devices  44.9 us (17%)
  matrix products  35.3 us (13%)
  local copies, waits for them, and re-layouts  17.8 us (7%)
  other arithmetic  6.95 us (3%)
  between operations  4.09 us (2%)
    all_to_all x2, blocking collectives, sum_exchange(): got = lax.all_to_all(parts, axes, 0, 0)  65.4 us
    ppermute x3, waiting for transfers between devices, gather_ring(): after = lax.ppermute(pair, long_axis, RING[3])  32.2 us
    ppermute x3, waiting for transfers between devices, gather_ring(): other = lax.ppermute(own, short_axis, SWAP)  17.2 us
    all_to_all x2, waiting for transfers between devices, sum_everywhere(): lax.all_to_all(jnp.broadcast_to(vector[None], (8,) + vector.shape), axes,...  13.2 us
    dot_general x1, matrix products, shards(): lax.dot_general(queries, keys, (((1,), (1,)), ((), ())), preferred_elemen...  12.5 us
    ppermute x3, waiting for transfers between devices, gather_ring(): far_top = lax.ppermute(after[:rows], long_axis, RING[3])  10.2 us
    dot_general x1, matrix products, shards(): jnp.dot(grad_scores, keys, preferred_element_type=F32).astype(BF16)  9.94 us
    ppermute x3, starting transfers between devices, gather_ring(): far_top = lax.ppermute(after[:rows], long_axis, RING[3])  7.47 us
  transfers between devices with their start and end apart: 29, of which 20 were waited for; matrix products, arithmetic and copies ran while one was open for 9% of the time, Pallas kernels for 0%

profile of v1, /device:TPU:0, one launch (start us, length us, event | category | flops | bytes accessed | tf_op | source)
XLA Modules:
  0.0 267.9 jit_solution(12132247368311983507)
XLA Ops:
  0.7 1.3 copy-done
  2.6 2.4 fusion.16
  5.3 2.7 %add_convert_fusion = bf16[1024,1024]{1,0:T(8,128)(2,1)S(1)} fusion(f32[1024,1024]{1,0:T(8,128)S(1)} %fusion.16, bf16[1024,320]{0,1:T(8,128)(2,1)} %collective-permute-done, bf16[320,1024]{1,0:T(8,128)(2,1)S(1)} %collective-permute-done.1), kind=kOutput, calls=%fused_computation.11 | convolution fusion | flops 673185792 | bytes 7602176 | tf_op jit(solution)/shard_map/dot_general | solution.py:63
  8.1 36.1 %all_to_all.30 = bf16[8,128,1024]{2,1,0:T(8,128)(2,1)S(1)} all-to-all(bf16[8,128,1024]{2,1,0:T(8,128)(2,1)S(1)} %bitcast.46), channel_id=1, replica_groups=mesh['x'=4,'zl'=2,'y'=4,'zh'=2,'c'=2] {'y','zh'}, dimensions={0} | all-to-all | bytes 4194304 | tf_op jit(solution)/shard_map/all_to_all | solution.py:41
  45.8 1.8 collective-permute-start.2
  47.6 6.4 %collective-permute-done.7 = bf16[128,1024]{1,0:T(8,128)(2,1)S(1)} collective-permute-done((bf16[128,1024]{1,0:T(8,128)(2,1)S(1)}, bf16[128,1024]{1,0:T(8,128)(2,1)S(1)}, u32[]{:S(2)}, u32[]{:S(2)}) %collective-permute-start.7) | collective-permute-done | bytes 262176 | tf_op jit(solution)/shard_map/ppermute | solution.py:19
  54.0 4.4 %collective-permute-done.2 = bf16[128,1024]{1,0:T(8,128)(2,1)S(1)} collective-permute-done((bf16[128,1024]{1,0:T(8,128)(2,1)S(1)}, bf16[128,1024]{1,0:T(8,128)(2,1)S(1)}, u32[]{:S(2)}, u32[]{:S(2)}) %collective-permute-start.2) | collective-permute-done | bytes 262176 | tf_op jit(solution)/shard_map/ppermute | solution.py:19
  58.6 1.6 broadcast.149.clone.1
  61.3 2.7 %collective-permute-start.8 = (bf16[256,1024]{1,0:T(8,128)(2,1)}, bf16[256,1024]{1,0:T(8,128)(2,1)S(1)}, u32[]{:S(2)}, u32[]{:S(2)}) collective-permute-start(bf16[256,1024]{1,0:T(8,128)(2,1)} %get-tuple-element.24), channel_id=1, source_target_pairs={{0,96},{32,0},{64,32},{96,64},{1,97},{33,1},{65,33},{97,65},{2,98}... | collective-permute-start | bytes 1572872 | tf_op jit(solution)/shard_map/ppermute | solution.py:22
  64.0 9.7 %collective-permute-done.8 = bf16[256,1024]{1,0:T(8,128)(2,1)S(1)} collective-permute-done((bf16[256,1024]{1,0:T(8,128)(2,1)}, bf16[256,1024]{1,0:T(8,128)(2,1)S(1)}, u32[]{:S(2)}, u32[]{:S(2)}) %collective-permute-start.8) | collective-permute-done | bytes 524320 | tf_op jit(solution)/shard_map/ppermute | solution.py:22
  74.5 3.6 %collective-permute-start.10 = (bf16[128,1024]{1,0:T(8,128)(2,1)}, bf16[128,1024]{1,0:T(8,128)(2,1)}, u32[]{:S(2)}, u32[]{:S(2)}) collective-permute-start(bf16[128,1024]{1,0:T(8,128)(2,1)} %slice.58), channel_id=1, source_target_pairs={{0,96},{32,0},{64,32},{96,64},{1,97},{33,1},{65,33},{97,65},{2,98}... | collective-permute-start | bytes 786440 | tf_op jit(solution)/shard_map/ppermute | solution.py:24
  79.9 2.4 collective-permute-done.10
  82.3 1.7 constant_dynamic-update-slice_fusion.6
  84.0 1.8 collective-permute-done.11
  86.5 1.6 broadcast.149.clone
  89.2 1.2 collective-permute-start.3
  91.2 12.5 %collective-permute-done.3 = bf16[256,1024]{1,0:T(8,128)(2,1)S(1)} collective-permute-done((bf16[256,1024]{1,0:T(8,128)(2,1)}, bf16[256,1024]{1,0:T(8,128)(2,1)S(1)}, u32[]{:S(2)}, u32[]{:S(2)}) %collective-permute-start.3) | collective-permute-done | bytes 524320 | tf_op jit(solution)/shard_map/ppermute | solution.py:22
  103.7 2.4 collective-permute-start.5
  108.2 3.6 %collective-permute-done.5 = bf16[128,1024]{1,0:T(8,128)(2,1)S(1)} collective-permute-done((bf16[128,1024]{1,0:T(8,128)(2,1)S(1)}, bf16[128,1024]{1,0:T(8,128)(2,1)S(1)}, u32[]{:S(2)}, u32[]{:S(2)}) %collective-permute-start.5) | collective-permute-done | bytes 262176 | tf_op jit(solution)/shard_map/ppermute | solution.py:24
  112.5 2.9 %collective-permute-done.6 = bf16[128,1024]{1,0:T(8,128)(2,1)S(1)} collective-permute-done((bf16[128,1024]{1,0:T(8,128)(2,1)S(1)}, bf16[128,1024]{1,0:T(8,128)(2,1)S(1)}, u32[]{:S(2)}, u32[]{:S(2)}) %collective-permute-start.6) | collective-permute-done | bytes 262176 | tf_op jit(solution)/shard_map/ppermute | solution.py:25
  116.1 12.5 %fusion.3 = (f32[2048]{0:T(1024)S(1)}, f32[1024]{0:T(1024)S(1)}, f32[]{:T(128)}, f32[1024,2048]{1,0:T(8,128)}) fusion(s32[2048]{0:T(1024)S(1)} %fusion.22, s32[1024]{0:T(1024)S(1)} %iota_add_fusion, s32[1024]{0:T(1024)S(1)} %dynamic_slice.11, bf16[1024,1024]{1,0:T(8,128)(2,1)} %constant_dynamic-update-slice_fusion.10, ...), kind=kOutput, calls=%fused_computation.6 | convolution fusion | flops 4320130048 | bytes 14708740 | tf_op jit(solution)/shard_map/dot_general | solution.py:81
  130.0 3.4 %all-to-all-start.1 = ((f32[8,16,128]{2,1,0:T(8,128)}), f32[8,16,128]{2,1,0:T(8,128)S(1)}, u32[]{:S(2)}, u32[]{:S(2)}) async-start(f32[8,16,128]{2,1,0:T(8,128)} %broadcast_in_dim.31), calls=%async_computation.1 | async-start | bytes 131072 | tf_op jit(solution)/shard_map/all_to_all | solution.py:47
  133.4 7.7 %all-to-all-done.1 = f32[8,16,128]{2,1,0:T(8,128)S(1)} async-done(((f32[8,16,128]{2,1,0:T(8,128)}), f32[8,16,128]{2,1,0:T(8,128)S(1)}, u32[]{:S(2)}, u32[]{:S(2)}) %all-to-all-start.1) | async-done | bytes 65568 | tf_op jit(solution)/shard_map/all_to_all | solution.py:47
  141.7 3.4 %all-to-all-start.2 = ((f32[8,16,128]{2,1,0:T(8,128)}), f32[8,16,128]{2,1,0:T(8,128)S(1)}, u32[]{:S(2)}, u32[]{:S(2)}) async-start(f32[8,16,128]{2,1,0:T(8,128)} %broadcast_in_dim.53), calls=%async_computation.2 | async-start | bytes 131072 | tf_op jit(solution)/shard_map/all_to_all | solution.py:47
  145.7 5.6 %all-to-all-done.2 = f32[8,16,128]{2,1,0:T(8,128)S(1)} async-done(((f32[8,16,128]{2,1,0:T(8,128)}), f32[8,16,128]{2,1,0:T(8,128)S(1)}, u32[]{:S(2)}, u32[]{:S(2)}) %all-to-all-start.2) | async-done | bytes 65568 | tf_op jit(solution)/shard_map/all_to_all | solution.py:47
  151.2 9.9 %fusion.8 = bf16[1024,1024]{1,0:T(8,128)(2,1)S(1)} fusion(bf16[1024,1024]{1,0:T(8,128)(2,1)} %collective-permute-done.12, bf16[1024,1024]{1,0:T(8,128)(2,1)} %constant_dynamic-update-slice_fusion.5, f32[1024,2048]{1,0:T(8,128)} %get-tuple-element.38, f32[2048]{0:T(1024)S(1)} %divide_bitcast_fusion, f32[1024]{0:T(1024)S(1)} %get-tuple-element.34, ...), kind=kOutput, calls=%fused_computation.14 | convolution fusion | flops 4323278848 | bytes 14708736 | tf_op jit(solution)/shard_map/dot_general | solution.py:99
  161.2 29.3 %all_to_all.31 = bf16[8,128,1024]{2,1,0:T(8,128)(2,1)S(1)} all-to-all(bf16[8,128,1024]{2,1,0:T(8,128)(2,1)S(1)} %bitcast.47), channel_id=1, replica_groups=mesh['x'=4,'zl'=2,'y'=4,'zh'=2,'c'=2] {'y','zh'}, dimensions={0} | all-to-all | bytes 4194304 | tf_op jit(solution)/shard_map/all_to_all | solution.py:41
  191.2 1.6 collective-permute-start.18
  192.8 6.4 %collective-permute-done.18 = bf16[128,1024]{1,0:T(8,128)(2,1)S(1)} collective-permute-done((bf16[128,1024]{1,0:T(8,128)(2,1)S(1)}, bf16[128,1024]{1,0:T(8,128)(2,1)S(1)}, u32[]{:S(2)}, u32[]{:S(2)}) %collective-permute-start.18) | collective-permute-done | bytes 262176 | tf_op jit(solution)/shard_map/ppermute | solution.py:19
  199.6 1.4 collective-permute-start.19
  201.7 10.0 %collective-permute-done.19 = bf16[256,1024]{1,0:T(8,128)(2,1)S(1)} collective-permute-done((bf16[256,1024]{1,0:T(8,128)(2,1)S(1)}, bf16[256,1024]{1,0:T(8,128)(2,1)S(1)}, u32[]{:S(2)}, u32[]{:S(2)}) %collective-permute-start.19) | collective-permute-done | bytes 524320 | tf_op jit(solution)/shard_map/ppermute | solution.py:22
  211.7 1.4 collective-permute-start.21
  214.0 4.2 %collective-permute-done.21 = bf16[128,1024]{1,0:T(8,128)(2,1)S(1)} collective-permute-done((bf16[128,1024]{1,0:T(8,128)(2,1)S(1)}, bf16[128,1024]{1,0:T(8,128)(2,1)S(1)}, u32[]{:S(2)}, u32[]{:S(2)}) %collective-permute-start.21) | collective-permute-done | bytes 262176 | tf_op jit(solution)/shard_map/ppermute | solution.py:24
  218.2 2.7 collective-permute-done.22
  220.9 2.5 convolution_convert_fusion
  223.5 1.8 fusion.14
  227.5 3.7 %all-to-all-start.4 = ((bf16[8,320,128]{2,1,0:T(8,128)(2,1)}), bf16[8,320,128]{2,1,0:T(8,128)(2,1)S(1)}, u32[]{:S(2)}, u32[]{:S(2)}) async-start(bf16[8,320,128]{2,1,0:T(8,128)(2,1)} %bitcast.45), calls=%async_computation.4 | async-start | bytes 1310720 | tf_op jit(solution)/shard_map/all_to_all | solution.py:41
  234.3 1.9 collective-permute-start.14
  236.2 2.0 collective-permute-done.14
  238.3 5.7 %collective-permute-start.15 = (f32[8,128]{1,0:T(8,128)S(1)}, f32[8,128]{1,0:T(8,128)S(1)}, u32[]{:S(2)}, u32[]{:S(2)}) collective-permute-start(f32[8,128]{1,0:T(8,128)S(1)} %fusion.50), channel_id=1, source_target_pairs={{0,64},{32,96},{64,0},{96,32},{1,65},{33,97},{65,1},{97,33},{2,66}... | collective-permute-start | bytes 12296 | tf_op jit(solution)/shard_map/ppermute | solution.py:105
  244.0 1.6 collective-permute-done.15
  245.6 2.1 collective-permute-start.16
  247.7 2.8 %collective-permute-done.16 = f32[8,128]{1,0:T(8,128)S(1)} collective-permute-done((f32[8,128]{1,0:T(8,128)S(1)}, f32[8,128]{1,0:T(8,128)S(1)}, u32[]{:S(2)}, u32[]{:S(2)}) %collective-permute-start.16) | collective-permute-done | bytes 4128 | tf_op jit(solution)/shard_map/ppermute | solution.py:106
  252.7 3.6 %all-to-all-start.5 = ((bf16[8,320,128]{2,1,0:T(8,128)(2,1)}), bf16[8,320,128]{2,1,0:T(8,128)(2,1)S(1)}, u32[]{:S(2)}, u32[]{:S(2)}) async-start(bf16[8,320,128]{2,1,0:T(8,128)(2,1)} %broadcast_in_dim.55), calls=%async_computation.5 | async-start | bytes 1310720 | tf_op jit(solution)/shard_map/all_to_all | solution.py:121
  256.2 2.6 broadcast_select_fusion.1
  258.9 1.2 maximum_bitcast_fusion
  260.0 5.6 %all-to-all-done.5 = bf16[8,320,128]{2,1,0:T(8,128)(2,1)S(1)} async-done(((bf16[8,320,128]{2,1,0:T(8,128)(2,1)}), bf16[8,320,128]{2,1,0:T(8,128)(2,1)S(1)}, u32[]{:S(2)}, u32[]{:S(2)}) %all-to-all-start.5) | async-done | bytes 655392 | tf_op jit(solution)/shard_map/all_to_all | solution.py:121
  265.6 1.2 copy_bitcast_fusion
  (91 shorter events, 23.6 us)
Async XLA Ops:
  0.6 1.3 copy-start
  2.0 3.0 %collective-permute-start = (bf16[1024,320]{0,1:T(8,128)(2,1)S(1)}, bf16[1024,320]{0,1:T(8,128)(2,1)}, u32[]{:S(2)}, u32[]{:S(2)}) collective-permute-start(bf16[1024,320]{0,1:T(8,128)(2,1)S(1)} %constant_dynamic-slice_fusion), channel_id=1, source_target_pairs={{0,1},{1,0},{2,3},{3,2},{4,5},{5,4},{6,7},{7,6},{8,9},{9,8},{10,11... | collective-permute-start | bytes 1966088 | tf_op jit(solution)/shard_map/ppermute | solution.py:14
  2.1 3.2 %collective-permute-start.1 = (bf16[320,1024]{1,0:T(8,128)(2,1)}, bf16[320,1024]{1,0:T(8,128)(2,1)S(1)}, u32[]{:S(2)}, u32[]{:S(2)}) collective-permute-start(bf16[320,1024]{1,0:T(8,128)(2,1)} %param.6), channel_id=1, source_target_pairs={{0,1},{1,0},{2,3},{3,2},{4,5},{5,4},{6,7},{7,6},{8,9},{9,8},{10,11... | collective-permute-start | bytes 1966088 | tf_op jit(solution)/shard_map/ppermute | solution.py:14
  5.3 2.7 %copy-start.3 = (bf16[320,1024]{1,0:T(8,128)(2,1)}, bf16[320,1024]{1,0:T(8,128)(2,1)S(1)}, u32[]{:S(2)}) copy-start(bf16[320,1024]{1,0:T(8,128)(2,1)S(1)} %collective-permute-done.1) | copy-start | bytes 1966084
  44.7 9.3 %collective-permute-start.7 = (bf16[128,1024]{1,0:T(8,128)(2,1)S(1)}, bf16[128,1024]{1,0:T(8,128)(2,1)S(1)}, u32[]{:S(2)}, u32[]{:S(2)}) collective-permute-start(bf16[128,1024]{1,0:T(8,128)(2,1)S(1)} %multiply_convert_fusion.1), channel_id=1, source_target_pairs={{0,16},{16,0},{1,17},{17,1},{2,18},{18,2},{3,19},{19,3},{4,20},{20... | collective-permute-start | bytes 786440 | tf_op jit(solution)/shard_map/ppermute | solution.py:19
  45.8 12.6 %collective-permute-start.2 = (bf16[128,1024]{1,0:T(8,128)(2,1)S(1)}, bf16[128,1024]{1,0:T(8,128)(2,1)S(1)}, u32[]{:S(2)}, u32[]{:S(2)}) collective-permute-start(bf16[128,1024]{1,0:T(8,128)(2,1)S(1)} %multiply_convert_fusion.1), channel_id=1, source_target_pairs={{0,2},{2,0},{1,3},{3,1},{4,6},{6,4},{5,7},{7,5},{8,10},{10,8},{9,1... | collective-permute-start | bytes 786440 | tf_op jit(solution)/shard_map/ppermute | solution.py:19
  61.3 12.5 %collective-permute-start.8 = (bf16[256,1024]{1,0:T(8,128)(2,1)}, bf16[256,1024]{1,0:T(8,128)(2,1)S(1)}, u32[]{:S(2)}, u32[]{:S(2)}) collective-permute-start(bf16[256,1024]{1,0:T(8,128)(2,1)} %get-tuple-element.24), channel_id=1, source_target_pairs={{0,96},{32,0},{64,32},{96,64},{1,97},{33,1},{65,33},{97,65},{2,98}... | collective-permute-start | bytes 1572872 | tf_op jit(solution)/shard_map/ppermute | solution.py:22
  64.0 14.1 %collective-permute-start.9 = (bf16[256,1024]{1,0:T(8,128)(2,1)}, bf16[256,1024]{1,0:T(8,128)(2,1)S(1)}, u32[]{:S(2)}, u32[]{:S(2)}) collective-permute-start(bf16[256,1024]{1,0:T(8,128)(2,1)} %get-tuple-element.24), channel_id=1, source_target_pairs={{0,32},{32,64},{64,96},{96,0},{1,33},{33,65},{65,97},{97,1},{2,34}... | collective-permute-start | bytes 1572872 | tf_op jit(solution)/shard_map/ppermute | solution.py:23
  74.5 7.8 %collective-permute-start.10 = (bf16[128,1024]{1,0:T(8,128)(2,1)}, bf16[128,1024]{1,0:T(8,128)(2,1)}, u32[]{:S(2)}, u32[]{:S(2)}) collective-permute-start(bf16[128,1024]{1,0:T(8,128)(2,1)} %slice.58), channel_id=1, source_target_pairs={{0,96},{32,0},{64,32},{96,64},{1,97},{33,1},{65,33},{97,65},{2,98}... | collective-permute-start | bytes 786440 | tf_op jit(solution)/shard_map/ppermute | solution.py:24
  78.1 7.7 %collective-permute-start.11 = (bf16[128,1024]{1,0:T(8,128)(2,1)S(1)}, bf16[128,1024]{1,0:T(8,128)(2,1)S(1)}, u32[]{:S(2)}, u32[]{:S(2)}) collective-permute-start(bf16[128,1024]{1,0:T(8,128)(2,1)S(1)} %slice.59), channel_id=1, source_target_pairs={{0,32},{32,64},{64,96},{96,0},{1,33},{33,65},{65,97},{97,1},{2,34}... | collective-permute-start | bytes 786440 | tf_op jit(solution)/shard_map/ppermute | solution.py:25
  86.5 29.6 %collective-permute-start.12 = (bf16[1024,1024]{1,0:T(8,128)(2,1)}, bf16[1024,1024]{1,0:T(8,128)(2,1)}, u32[]{:S(2)}, u32[]{:S(2)}) collective-permute-start(bf16[1024,1024]{1,0:T(8,128)(2,1)} %constant_dynamic-update-slice_fusion.5), channel_id=1, source_target_pairs={{0,1},{1,0},{2,3},{3,2},{4,5},{5,4},{6,7},{7,6},{8,9},{9,8},{10,11... | collective-permute-start | bytes 6291464 | tf_op jit(solution)/shard_map/ppermute | solution.py:14
  86.5 19.7 %copy-start.5 = (s32[2048]{0:T(1024)S(1)}, s32[2048]{0:T(1024)}, u32[]{:S(2)}) copy-start(s32[2048]{0:T(1024)} %param.7) | copy-start | bytes 24580
  89.2 14.5 %collective-permute-start.3 = (bf16[256,1024]{1,0:T(8,128)(2,1)}, bf16[256,1024]{1,0:T(8,128)(2,1)S(1)}, u32[]{:S(2)}, u32[]{:S(2)}) collective-permute-start(bf16[256,1024]{1,0:T(8,128)(2,1)} %get-tuple-element.28), channel_id=1, source_target_pairs={{0,12},{4,0},{8,4},{12,8},{1,13},{5,1},{9,5},{13,9},{2,14},{6,2},{... | collective-permute-start | bytes 1572872 | tf_op jit(solution)/shard_map/ppermute | solution.py:22
  90.3 15.9 %collective-permute-start.4 = (bf16[256,1024]{1,0:T(8,128)(2,1)}, bf16[256,1024]{1,0:T(8,128)(2,1)S(1)}, u32[]{:S(2)}, u32[]{:S(2)}) collective-permute-start(bf16[256,1024]{1,0:T(8,128)(2,1)} %get-tuple-element.28), channel_id=1, source_target_pairs={{0,4},{4,8},{8,12},{12,0},{1,5},{5,9},{9,13},{13,1},{2,6},{6,10},{... | collective-permute-start | bytes 1572872 | tf_op jit(solution)/shard_map/ppermute | solution.py:23
  103.7 8.0 %collective-permute-start.5 = (bf16[128,1024]{1,0:T(8,128)(2,1)S(1)}, bf16[128,1024]{1,0:T(8,128)(2,1)S(1)}, u32[]{:S(2)}, u32[]{:S(2)}) collective-permute-start(bf16[128,1024]{1,0:T(8,128)(2,1)S(1)} %slice.56), channel_id=1, source_target_pairs={{0,12},{4,0},{8,4},{12,8},{1,13},{5,1},{9,5},{13,9},{2,14},{6,2},{... | collective-permute-start | bytes 786440 | tf_op jit(solution)/shard_map/ppermute | solution.py:24
  106.2 9.1 %collective-permute-start.6 = (bf16[128,1024]{1,0:T(8,128)(2,1)S(1)}, bf16[128,1024]{1,0:T(8,128)(2,1)S(1)}, u32[]{:S(2)}, u32[]{:S(2)}) collective-permute-start(bf16[128,1024]{1,0:T(8,128)(2,1)S(1)} %slice.57), channel_id=1, source_target_pairs={{0,4},{4,8},{8,12},{12,0},{1,5},{5,9},{9,13},{13,1},{2,6},{6,10},{... | collective-permute-start | bytes 786440 | tf_op jit(solution)/shard_map/ppermute | solution.py:25
  129.3 4.1 %collective-permute-start.17 = (f32[16,128]{1,0:T(8,128)S(1)}, f32[16,128]{1,0:T(8,128)S(1)}, u32[]{:S(2)}, u32[]{:S(2)}) collective-permute-start(f32[16,128]{1,0:T(8,128)S(1)} %bitcast.49), channel_id=1, source_target_pairs={{0,1},{1,0},{2,3},{3,2},{4,5},{5,4},{6,7},{7,6},{8,9},{9,8},{10,11... | collective-permute-start | bytes 24584 | tf_op jit(solution)/shard_map/ppermute | solution.py:14
  130.0 11.0 %all-to-all-start.1 = ((f32[8,16,128]{2,1,0:T(8,128)}), f32[8,16,128]{2,1,0:T(8,128)S(1)}, u32[]{:S(2)}, u32[]{:S(2)}) async-start(f32[8,16,128]{2,1,0:T(8,128)} %broadcast_in_dim.31), calls=%async_computation.1 | async-start | bytes 131072 | tf_op jit(solution)/shard_map/all_to_all | solution.py:47
  141.7 9.5 %all-to-all-start.2 = ((f32[8,16,128]{2,1,0:T(8,128)}), f32[8,16,128]{2,1,0:T(8,128)S(1)}, u32[]{:S(2)}, u32[]{:S(2)}) async-start(f32[8,16,128]{2,1,0:T(8,128)} %broadcast_in_dim.53), calls=%async_computation.2 | async-start | bytes 131072 | tf_op jit(solution)/shard_map/all_to_all | solution.py:47
  191.2 8.0 %collective-permute-start.18 = (bf16[128,1024]{1,0:T(8,128)(2,1)S(1)}, bf16[128,1024]{1,0:T(8,128)(2,1)S(1)}, u32[]{:S(2)}, u32[]{:S(2)}) collective-permute-start(bf16[128,1024]{1,0:T(8,128)(2,1)S(1)} %multiply_convert_fusion), channel_id=1, source_target_pairs={{0,2},{2,0},{1,3},{3,1},{4,6},{6,4},{5,7},{7,5},{8,10},{10,8},{9,1... | collective-permute-start | bytes 786440 | tf_op jit(solution)/shard_map/ppermute | solution.py:19
  199.6 12.1 %collective-permute-start.19 = (bf16[256,1024]{1,0:T(8,128)(2,1)S(1)}, bf16[256,1024]{1,0:T(8,128)(2,1)S(1)}, u32[]{:S(2)}, u32[]{:S(2)}) collective-permute-start(bf16[256,1024]{1,0:T(8,128)(2,1)S(1)} %get-tuple-element.20), channel_id=1, source_target_pairs={{0,12},{4,0},{8,4},{12,8},{1,13},{5,1},{9,5},{13,9},{2,14},{6,2},{... | collective-permute-start | bytes 1572872 | tf_op jit(solution)/shard_map/ppermute | solution.py:22
  201.0 12.1 %collective-permute-start.20 = (bf16[256,1024]{1,0:T(8,128)(2,1)S(1)}, bf16[256,1024]{1,0:T(8,128)(2,1)S(1)}, u32[]{:S(2)}, u32[]{:S(2)}) collective-permute-start(bf16[256,1024]{1,0:T(8,128)(2,1)S(1)} %get-tuple-element.20), channel_id=1, source_target_pairs={{0,4},{4,8},{8,12},{12,0},{1,5},{5,9},{9,13},{13,1},{2,6},{6,10},{... | collective-permute-start | bytes 1572872 | tf_op jit(solution)/shard_map/ppermute | solution.py:23
  211.7 6.4 %collective-permute-start.21 = (bf16[128,1024]{1,0:T(8,128)(2,1)S(1)}, bf16[128,1024]{1,0:T(8,128)(2,1)S(1)}, u32[]{:S(2)}, u32[]{:S(2)}) collective-permute-start(bf16[128,1024]{1,0:T(8,128)(2,1)S(1)} %slice.64), channel_id=1, source_target_pairs={{0,12},{4,0},{8,4},{12,8},{1,13},{5,1},{9,5},{13,9},{2,14},{6,2},{... | collective-permute-start | bytes 786440 | tf_op jit(solution)/shard_map/ppermute | solution.py:24
  213.2 7.7 %collective-permute-start.22 = (bf16[128,1024]{1,0:T(8,128)(2,1)S(1)}, bf16[128,1024]{1,0:T(8,128)(2,1)S(1)}, u32[]{:S(2)}, u32[]{:S(2)}) collective-permute-start(bf16[128,1024]{1,0:T(8,128)(2,1)S(1)} %slice.65), channel_id=1, source_target_pairs={{0,4},{4,8},{8,12},{12,0},{1,5},{5,9},{9,13},{13,1},{2,6},{6,10},{... | collective-permute-start | bytes 786440 | tf_op jit(solution)/shard_map/ppermute | solution.py:25
  220.8 4.9 %copy-start.1 = (bf16[1024,1024]{1,0:T(8,128)(2,1)}, bf16[1024,1024]{1,0:T(8,128)(2,1)S(1)}, u32[]{:S(2)}) copy-start(bf16[1024,1024]{1,0:T(8,128)(2,1)S(1)} %constant_dynamic-update-slice_fusion) | copy-start | bytes 6291460
  220.8 2.6 copy-start.4
  223.4 2.4 collective-permute-start.24
  225.2 31.0 %collective-permute-start.23 = (bf16[320,1024]{1,0:T(8,128)(2,1)}, bf16[320,1024]{1,0:T(8,128)(2,1)}, u32[]{:S(2)}, u32[]{:S(2)}) collective-permute-start(bf16[320,1024]{1,0:T(8,128)(2,1)} %fusion.14), channel_id=1, source_target_pairs={{0,1},{1,0},{2,3},{3,2},{4,5},{5,4},{6,7},{7,6},{8,9},{9,8},{10,11... | collective-permute-start | bytes 1966088 | tf_op jit(solution)/shard_map/ppermute | solution.py:14
  227.5 28.7 %copy-start.2 = (bf16[320,1024]{1,0:T(8,128)(2,1)S(1)}, bf16[320,1024]{1,0:T(8,128)(2,1)}, u32[]{:S(2)}) copy-start(bf16[320,1024]{1,0:T(8,128)(2,1)} %param.6) | copy-start | bytes 1966084
  227.5 24.1 %all-to-all-start.4 = ((bf16[8,320,128]{2,1,0:T(8,128)(2,1)}), bf16[8,320,128]{2,1,0:T(8,128)(2,1)S(1)}, u32[]{:S(2)}, u32[]{:S(2)}) async-start(bf16[8,320,128]{2,1,0:T(8,128)(2,1)} %bitcast.45), calls=%async_computation.4 | async-start | bytes 1310720 | tf_op jit(solution)/shard_map/all_to_all | solution.py:41
  233.1 1.2 collective-permute-start.13
  234.3 3.9 %collective-permute-start.14 = (f32[8,128]{1,0:T(8,128)S(1)}, f32[8,128]{1,0:T(8,128)S(1)}, u32[]{:S(2)}, u32[]{:S(2)}) collective-permute-start(f32[8,128]{1,0:T(8,128)S(1)} %broadcast_add_fusion), channel_id=1, source_target_pairs={{0,16},{16,0},{1,17},{17,1},{2,18},{18,2},{3,19},{19,3},{4,20},{20... | collective-permute-start | bytes 12296 | tf_op jit(solution)/shard_map/ppermute | solution.py:104
  238.3 7.3 %collective-permute-start.15 = (f32[8,128]{1,0:T(8,128)S(1)}, f32[8,128]{1,0:T(8,128)S(1)}, u32[]{:S(2)}, u32[]{:S(2)}) collective-permute-start(f32[8,128]{1,0:T(8,128)S(1)} %fusion.50), channel_id=1, source_target_pairs={{0,64},{32,96},{64,0},{96,32},{1,65},{33,97},{65,1},{97,33},{2,66}... | collective-permute-start | bytes 12296 | tf_op jit(solution)/shard_map/ppermute | solution.py:105
  245.6 4.9 %collective-permute-start.16 = (f32[8,128]{1,0:T(8,128)S(1)}, f32[8,128]{1,0:T(8,128)S(1)}, u32[]{:S(2)}, u32[]{:S(2)}) collective-permute-start(f32[8,128]{1,0:T(8,128)S(1)} %add.232), channel_id=1, source_target_pairs={{0,32},{32,64},{64,96},{96,0},{1,33},{33,65},{65,97},{97,1},{2,34}... | collective-permute-start | bytes 12296 | tf_op jit(solution)/shard_map/ppermute | solution.py:106
  252.7 12.9 %all-to-all-start.5 = ((bf16[8,320,128]{2,1,0:T(8,128)(2,1)}), bf16[8,320,128]{2,1,0:T(8,128)(2,1)S(1)}, u32[]{:S(2)}, u32[]{:S(2)}) async-start(bf16[8,320,128]{2,1,0:T(8,128)(2,1)} %broadcast_in_dim.55), calls=%async_computation.5 | async-start | bytes 1310720 | tf_op jit(solution)/shard_map/all_to_all | solution.py:121

commit v2 on v0

v2 whole, which is shorter than its diff:
```python
import jax
import jax.numpy as jnp
from jax import lax
from jax.experimental import pallas as pl
from jax.experimental.pallas import tpu as pltpu
from jax.sharding import Mesh
from jax.sharding import PartitionSpec as P

F32 = jnp.float32
BF16 = jnp.bfloat16
I32 = jnp.int32
SWAP = [(0, 1), (1, 0)]
ROWS = 128
HALF = 1024
GROUP = 2048
TOTAL = 16384
WIDTH = 1024
PART = 512
VMEM_LIMIT = 40 * 1024 * 1024
YZ, XZ, CUTS = ("y", "zh"), ("x", "zl"), ("y", "zh", "c")


def core_swap(value):
    return lax.ppermute(value, "c", SWAP)


def spread(value, axes, count):
    return lax.all_to_all(jnp.broadcast_to(value[None], (count,) + value.shape), axes, 0, 0)


def sum_exchange(parts, axes):
    return jnp.sum(lax.all_to_all(parts, axes, 0, 0).astype(F32), axis=0)


def key_ids(place, tile):
    zl = jnp.where(tile < 4, place[1], 1 - place[1])
    base = (lax.rem(tile, 4) * 2 + zl) * GROUP + place[4] * HALF + (place[2] * 2 + place[3]) * ROWS
    return base + lax.broadcasted_iota(I32, (ROWS, 1), 0)


def query_block(place, n):
    core = place[4] if n < 2 else 1 - place[4]
    zh = place[3] if n % 2 == 0 else 1 - place[3]
    return core, zh, core * 2 + zh


def query_ids(place, n):
    core, zh, _ = query_block(place, n)
    base = (place[0] * 2 + place[1]) * GROUP + core * HALF + zh * ROWS
    at = lax.broadcasted_iota(I32, (1, PART), 1)
    return base + (at // ROWS) * (2 * ROWS) + at % ROWS


def score_kernel(place, ka, kb, q0, q1, q2, q3, mates, w_ref, row_ref, col_ref):
    tile = pl.program_id(0)
    kid = key_ids(place, tile)

    @pl.when(tile == 0)
    def _():
        col_ref[...] = jnp.zeros_like(col_ref)

    def run(source, first):
        keys = source[pl.ds((tile - first) * ROWS, ROWS), :]
        row = jnp.zeros((ROWS, 1), F32)
        for n, q in enumerate((q0, q1, q2, q3)):
            block = query_block(place, n)[2]
            scores = 20.0 * lax.dot_general(
                keys, q[...], (((1,), (1,)), ((), ())), preferred_element_type=F32
            )
            weights = jnp.where(kid != query_ids(place, n), jnp.exp(scores), 0.0)
            w_ref[:, n * PART : (n + 1) * PART] = weights
            row = row + jnp.sum(weights, axis=1, keepdims=True)
            hits = jnp.where(kid == mates[block], scores, 0.0)
            col_ref[block, 0:8, :] += jnp.sum(weights.reshape(ROWS // 8, 8, PART), axis=0)
            col_ref[block, 8:16, :] += jnp.sum(hits.reshape(ROWS // 8, 8, PART), axis=0)
        row_ref[0] = row

    @pl.when(tile < 4)
    def _():
        run(ka, 0)

    @pl.when(tile >= 4)
    def _():
        run(kb, 4)


def grad_kernel(place, w_ref, rk_ref, rq_ref, mates, q0, q1, q2, q3, out_ref):
    tile = pl.program_id(0)
    kid = key_ids(place, tile)
    total = jnp.zeros((ROWS, WIDTH), F32)
    for n, q in enumerate((q0, q1, q2, q3)):
        block = query_block(place, n)[2]
        weights = w_ref[:, n * PART : (n + 1) * PART]
        grads = weights * (rk_ref[0] + rq_ref[block]) - jnp.where(kid == mates[block], 40.0, 0.0)
        total = total + jnp.dot(grads.astype(BF16), q[...], preferred_element_type=F32)
    out_ref[0] = total.astype(BF16)


def whole(shape):
    return pl.BlockSpec(shape, lambda t, place: (0,) * len(shape))


def piece(t, place):
    return lax.rem(t, 4) * 2 + jnp.where(t < 4, place[1], 1 - place[1])


def score_call(place, ka, kb, queries, mates):
    half = whole((PART, WIDTH))
    return pl.pallas_call(
        score_kernel,
        grid_spec=pltpu.PrefetchScalarGridSpec(
            num_scalar_prefetch=1,
            grid=(8,),
            in_specs=[half] * 6 + [whole((4, 1, PART))],
            out_specs=[
                pl.BlockSpec((ROWS, GROUP), lambda t, place: (t, 0)),
                pl.BlockSpec((1, ROWS, 1), lambda t, place: (piece(t, place), 0, 0)),
                whole((4, 16, PART)),
            ],
        ),
        out_shape=[
            jax.ShapeDtypeStruct((HALF, GROUP), F32),
            jax.ShapeDtypeStruct((8, ROWS, 1), F32),
            jax.ShapeDtypeStruct((4, 16, PART), F32),
        ],
        compiler_params=pltpu.CompilerParams(vmem_limit_bytes=VMEM_LIMIT),
        cost_estimate=pl.CostEstimate(
            flops=2 * HALF * GROUP * WIDTH, bytes_accessed=14 << 20, transcendentals=HALF * GROUP
        ),
        name="scores",
    )(place, ka, kb, *queries, mates)


def grad_call(place, weights, rk, rq, mates, queries):
    half = whole((PART, WIDTH))
    return pl.pallas_call(
        grad_kernel,
        grid_spec=pltpu.PrefetchScalarGridSpec(
            num_scalar_prefetch=1,
            grid=(8,),
            in_specs=[
                pl.BlockSpec((ROWS, GROUP), lambda t, place: (t, 0)),
                pl.BlockSpec((1, ROWS, 1), lambda t, place: (piece(t, place), 0, 0)),
                whole((4, 1, PART)),
                whole((4, 1, PART)),
            ]
            + [half] * 4,
            out_specs=pl.BlockSpec(
                (1, ROWS, WIDTH), lambda t, place: (piece(t, place), 0, 0)
            ),
        ),
        out_shape=jax.ShapeDtypeStruct((8, ROWS, WIDTH), BF16),
        compiler_params=pltpu.CompilerParams(vmem_limit_bytes=VMEM_LIMIT),
        cost_estimate=pl.CostEstimate(
            flops=2 * HALF * GROUP * WIDTH, bytes_accessed=14 << 20, transcendentals=0
        ),
        name="grads",
    )(place, weights, rk, rq, mates, *queries)


def shards(summaries, head, partner):
    core, zh = lax.axis_index("c"), lax.axis_index("zh")
    place = jnp.stack([lax.axis_index(a) for a in ("x", "zl", "y", "zh", "c")]).astype(I32)
    mates = partner.reshape(2, 4, 2, ROWS).transpose(0, 2, 1, 3).reshape(4, 1, PART)

    mine = lax.dynamic_slice_in_dim(summaries, core * HALF, HALF, 0)
    theirs = core_swap(lax.dynamic_slice_in_dim(summaries, (1 - core) * HALF, HALF, 0))
    other_head = core_swap(head)
    z_part = jnp.dot(mine, head, preferred_element_type=F32) + jnp.dot(
        theirs, other_head, preferred_element_type=F32
    )
    z = sum_exchange(z_part.astype(BF16).reshape(8, ROWS, WIDTH), YZ)
    inv = lax.rsqrt(jnp.sum(z * z, axis=1, keepdims=True) + 1e-06)
    unit = z * inv
    emb = unit.astype(BF16)

    q_other = lax.ppermute(emb, "zh", SWAP)
    k_other = lax.ppermute(emb, "zl", SWAP)
    q_near, k_near = spread(emb, "y", 4), spread(emb, "x", 4)
    q_far, k_far = spread(q_other, "y", 4), spread(k_other, "x", 4)
    queries = [a.reshape(PART, WIDTH) for a in (q_near, q_far)]
    queries += [core_swap(a) for a in queries]
    weights, row_part, col_part = score_call(
        place, k_near.reshape(PART, WIDTH), k_far.reshape(PART, WIDTH), queries, mates
    )

    pos_part = jnp.sum(col_part[:, 8:])
    col_part = jnp.sum(col_part[:, :8], axis=1).reshape(16, 128)
    col_part = jnp.concatenate([col_part, jnp.full((8, 128), pos_part, F32)], 0)
    row_part = row_part.reshape(8, ROWS)
    col_part, row_part = lax.optimization_barrier((col_part, row_part))
    cols = jnp.sum(spread(col_part, CUTS, 16), axis=0)
    rows = jnp.sum(spread(row_part, XZ, 8), axis=0)
    den_q, pos = cols[:16], cols[16, 0]
    rk = (20.0 / rows).reshape(8, ROWS, 1)
    rq = (20.0 / den_q).reshape(4, 1, PART)
    grad_part = grad_call(place, weights, rk, rq, mates, queries)

    loss = jnp.full((8, 128), jnp.sum(jnp.log(den_q)) - pos, F32)
    loss = jnp.sum(spread(loss, XZ, 8), axis=0)[0, 0] / TOTAL

    grad_emb = sum_exchange(grad_part, XZ)
    grad_emb, loss = lax.optimization_barrier((grad_emb, loss))
    grad_z = (inv * (grad_emb - unit * jnp.sum(unit * grad_emb, axis=1, keepdims=True))).astype(BF16)

    g_other = lax.ppermute(grad_z, "zh", SWAP)
    g_near = spread(grad_z, "y", 4).reshape(PART, WIDTH)
    g_far = spread(g_other, "y", 4).reshape(PART, WIDTH)

    def by_zh(rows_of, at):
        return lax.dynamic_index_in_dim(rows_of.reshape(4, 2, ROWS, -1), at, 1, False).reshape(
            PART, -1
        )

    def head_sum(rows_of):
        contract = (((0,), (0,)), ((), ()))
        return lax.dot_general(
            by_zh(rows_of, zh), g_near, contract, preferred_element_type=F32
        ) + lax.dot_general(by_zh(rows_of, 1 - zh), g_far, contract, preferred_element_type=F32)

    features = head.shape[0]
    got = core_swap(head_sum(theirs).astype(BF16)).astype(F32)
    head_part = (head_sum(mine) + got).astype(BF16)
    pieces = head_part.reshape(features, 8, WIDTH // 8).transpose(1, 0, 2)
    head_own = sum_exchange(pieces, XZ).astype(BF16)
    grad_head = spread(head_own, XZ, 8).transpose(1, 0, 2).reshape(features, WIDTH).astype(F32)

    def back(weight):
        contract = (((1,), (1,)), ((), ()))
        near = lax.dot_general(weight, g_near, contract, preferred_element_type=F32).astype(BF16)
        far = lax.dot_general(weight, g_far, contract, preferred_element_type=F32).astype(BF16)
        near, far = near.reshape(features, 4, 1, ROWS), far.reshape(features, 4, 1, ROWS)
        low, high = jnp.where(zh == 0, near, far), jnp.where(zh == 0, far, near)
        return jnp.concatenate([low, high], 2).reshape(features, HALF)

    got = core_swap(back(other_head))
    own = back(head)
    out = jnp.concatenate([jnp.where(core == 0, own, got), jnp.where(core == 0, got, own)], 1)
    return loss, out.T, grad_head


def solution(mesh):
    fine = Mesh(mesh.devices.reshape(4, 2, 4, 2, 2), ("x", "zl", "y", "zh", "c"))
    return jax.shard_map(
        shards,
        mesh=fine,
        in_specs=(P(XZ, CUTS), P(CUTS, None), P(XZ)),
        out_specs=(P(), P(XZ, CUTS), P(CUTS, None)),
        check_vma=False,
    )
```

time: 666 us -> 295 us (0.44)
  waiting for transfers between devices: 457 us -> 102 us
  blocking collectives: 132 us -> 61.3 us
  starting transfers between devices: 0.47 us -> 44.9 us
  matrix products: 43.4 us -> 12.8 us
  Pallas kernels: 0 us -> 28.8 us
  local copies, waits for them, and re-layouts: 3.25 us -> 31.3 us
  between operations: 16 us -> 4.21 us
    reduce_scatter x3 -> x0, waiting for transfers between devices: 290 us -> none  [the longest x1 108 us: shards(): lax.psum_scatter(jnp.dot(piece, keys, preferred_element_type=jnp.float32)...]
    all_gather x3 -> x0, waiting for transfers between devices: 164 us -> none  [the longest x1 59.3 us: shards(): queries = lax.all_gather(emb, 'cuts', axis=0, tiled=True)]
    psum x2 -> x0, blocking collectives: 132 us -> none  [the longest x1 66.9 us: shards(): den, pos = lax.psum((den_part, pos_part), 'cuts')]
    all_to_all x0 -> x10, waiting for transfers between devices: none -> 89.6 us  [the longest x8 51 us: spread(): lax.all_to_all(jnp.broadcast_to(value[None], (count,) + value.shape), axe...]
    all_to_all x0 -> x3, blocking collectives: none -> 61.3 us  [the longest x1 36.3 us: sum_exchange(): return jnp.sum(lax.all_to_all(parts, axes, 0, 0).astype(F32), axis=0)]
    all_to_all x0 -> x10, starting transfers between devices: none -> 40.1 us  [the longest x8 30.9 us: spread(): lax.all_to_all(jnp.broadcast_to(value[None], (count,) + value.shape), axe...]
    dot_general x6 -> x10, matrix products: 43.4 us -> 12.8 us  [the longest x2 4.08 us: head_sum(): lax.dot_general(by_zh(rows_of, 1 - zh), g_far, contract, preferred_elemen...]
    pallas_call x0 -> x2, Pallas kernels: none -> 28.8 us  [the longest x1 17.5 us: score_call(): pl.pallas_call(score_kernel, grid_spec=pltpu.PrefetchScalarGridSpec(num_s...]
  transfers between devices with their start and end apart: 7 -> 19, of which waited for: 7 -> 12; matrix products, arithmetic and copies ran while one was open for 2% -> 11% of each run, Pallas kernels for 0% -> 4%
where the time goes in v2:
time: 295 us; the launch traced here: 293 us
  waiting for transfers between devices  102 us (35%)
  blocking collectives  61.3 us (21%)
  starting transfers between devices  44.9 us (15%)
  local copies, waits for them, and re-layouts  31.3 us (11%)
  Pallas kernels  28.8 us (10%)
  matrix products  12.8 us (4%)
  other arithmetic  7.31 us (2%)
  between operations  4.21 us (1%)
    all_to_all x8, waiting for transfers between devices, spread(): lax.all_to_all(jnp.broadcast_to(value[None], (count,) + value.shape), axe...  51 us
    all_to_all x2, waiting for transfers between devices, sum_exchange(): return jnp.sum(lax.all_to_all(parts, axes, 0, 0).astype(F32), axis=0)  38.6 us
    all_to_all x1, blocking collectives, sum_exchange(): return jnp.sum(lax.all_to_all(parts, axes, 0, 0).astype(F32), axis=0)  36.3 us
    all_to_all x8, starting transfers between devices, spread(): lax.all_to_all(jnp.broadcast_to(value[None], (count,) + value.shape), axe...  30.9 us
    all_to_all x2, blocking collectives, spread(): lax.all_to_all(jnp.broadcast_to(value[None], (count,) + value.shape), axe...  25 us
    pallas_call x1, Pallas kernels, score_call(): pl.pallas_call(score_kernel, grid_spec=pltpu.PrefetchScalarGridSpec(num_s...  17.5 us
    pallas_call x1, Pallas kernels, grad_call(): pl.pallas_call(grad_kernel, grid_spec=pltpu.PrefetchScalarGridSpec(num_sc...  11.3 us
    all_to_all x2, starting transfers between devices, sum_exchange(): return jnp.sum(lax.all_to_all(parts, axes, 0, 0).astype(F32), axis=0)  9.16 us
  transfers between devices with their start and end apart: 19, of which 12 were waited for; matrix products, arithmetic and copies ran while one was open for 11% of the time, Pallas kernels for 4%

profile of v2, /device:TPU:0, one launch (start us, length us, event | category | flops | bytes accessed | tf_op | source)
XLA Modules:
  0.0 293.0 jit_solution(13376734154162769360)
XLA Ops:
  0.7 1.4 constant_dynamic-slice_fusion
  2.8 1.3 fusion.14
  4.5 1.3 add_convert_fusion
  5.9 36.3 %all_to_all.65 = bf16[8,128,1024]{2,1,0:T(8,128)(2,1)S(1)} all-to-all(bf16[8,128,1024]{2,1,0:T(8,128)(2,1)S(1)} %bitcast.107), channel_id=1, replica_groups=mesh['x'=4,'zl'=2,'y'=4,'zh'=2,'c'=2] {'y','zh'}, dimensions={0} | all-to-all | bytes 4194304 | tf_op jit(solution)/shard_map/all_to_all | solution.py:32
  43.4 1.1 broadcast_in_dim.16
  44.5 3.5 %all-to-all-start.3 = ((bf16[4,128,1024]{2,1,0:T(8,128)(2,1)}), bf16[4,128,1024]{2,1,0:T(8,128)(2,1)S(1)}, u32[]{:S(2)}, u32[]{:S(2)}) async-start(bf16[4,128,1024]{2,1,0:T(8,128)(2,1)} %broadcast_in_dim.16), calls=%async_computation.3 | async-start | bytes 2097152 | tf_op jit(solution)/shard_map/all_to_all | solution.py:28
  48.0 1.3 collective-permute-start.3
  49.3 7.5 %collective-permute-done.3 = bf16[128,1024]{1,0:T(8,128)(2,1)S(1)} collective-permute-done((bf16[128,1024]{1,0:T(8,128)(2,1)S(1)}, bf16[128,1024]{1,0:T(8,128)(2,1)S(1)}, u32[]{:S(2)}, u32[]{:S(2)}) %collective-permute-start.3) | collective-permute-done | bytes 262176 | tf_op jit(solution)/shard_map/ppermute | solution.py:177
  56.8 5.7 %all-to-all-done.3 = bf16[4,128,1024]{2,1,0:T(8,128)(2,1)S(1)} async-done(((bf16[4,128,1024]{2,1,0:T(8,128)(2,1)}), bf16[4,128,1024]{2,1,0:T(8,128)(2,1)S(1)}, u32[]{:S(2)}, u32[]{:S(2)}) %all-to-all-start.3) | async-done | bytes 1048608 | tf_op jit(solution)/shard_map/all_to_all | solution.py:28
  62.6 16.0 %all_to_all.66 = bf16[4,128,1024]{2,1,0:T(8,128)(2,1)S(1)} all-to-all(bf16[4,128,1024]{2,1,0:T(8,128)(2,1)S(1)} %broadcast_in_dim.18), channel_id=1, replica_groups=mesh['x'=4,'zl'=2,'y'=4,'zh'=2,'c'=2] {'y'}, dimensions={0} | all-to-all | bytes 2097152 | tf_op jit(solution)/shard_map/all_to_all | solution.py:28
  78.6 4.3 %all-to-all-start.1 = ((bf16[4,128,1024]{2,1,0:T(8,128)(2,1)}), bf16[4,128,1024]{2,1,0:T(8,128)(2,1)S(1)}, u32[]{:S(2)}, u32[]{:S(2)}) async-start(bf16[4,128,1024]{2,1,0:T(8,128)(2,1)} %broadcast_in_dim.16), calls=%async_computation.1 | async-start | bytes 2097152 | tf_op jit(solution)/shard_map/all_to_all | solution.py:28
  82.9 1.1 collective-permute-start.2
  84.5 4.9 %collective-permute-done.2 = bf16[128,1024]{1,0:T(8,128)(2,1)} collective-permute-done((bf16[128,1024]{1,0:T(8,128)(2,1)S(1)}, bf16[128,1024]{1,0:T(8,128)(2,1)}, u32[]{:S(2)}, u32[]{:S(2)}) %collective-permute-start.2) | collective-permute-done | bytes 262176 | tf_op jit(solution)/shard_map/ppermute | solution.py:178
  89.4 5.9 %all-to-all-done.1 = bf16[4,128,1024]{2,1,0:T(8,128)(2,1)S(1)} async-done(((bf16[4,128,1024]{2,1,0:T(8,128)(2,1)}), bf16[4,128,1024]{2,1,0:T(8,128)(2,1)S(1)}, u32[]{:S(2)}, u32[]{:S(2)}) %all-to-all-start.1) | async-done | bytes 1048608 | tf_op jit(solution)/shard_map/all_to_all | solution.py:28
  95.2 2.0 broadcast_in_dim.17
  97.3 4.4 %all-to-all-start.2 = ((bf16[4,128,1024]{2,1,0:T(8,128)(2,1)}), bf16[4,128,1024]{2,1,0:T(8,128)(2,1)}, u32[]{:S(2)}, u32[]{:S(2)}) async-start(bf16[4,128,1024]{2,1,0:T(8,128)(2,1)} %broadcast_in_dim.17), calls=%async_computation.2 | async-start | bytes 2097152 | tf_op jit(solution)/shard_map/all_to_all | solution.py:28
  101.8 11.1 %all-to-all-done.2 = bf16[4,128,1024]{2,1,0:T(8,128)(2,1)} async-done(((bf16[4,128,1024]{2,1,0:T(8,128)(2,1)}), bf16[4,128,1024]{2,1,0:T(8,128)(2,1)}, u32[]{:S(2)}, u32[]{:S(2)}) %all-to-all-start.2) | async-done | bytes 1048608 | tf_op jit(solution)/shard_map/all_to_all | solution.py:28
  112.9 17.5 %scores.1 = (f32[1024,2048]{1,0:T(8,128)}, f32[8,128,1]{2,1,0:T(8,128)S(1)}, f32[4,16,512]{2,1,0:T(8,128)S(1)}) custom-call(s32[5]{0:T(128)S(1)} %stack.23.place, bf16[512,1024]{1,0:T(8,128)(2,1)S(1)} %bitcast.95, bf16[512,1024]{1,0:T(8,128)(2,1)} %bitcast.7.kb, bf16[512,1024]{1,0:T(8,128)(2,1)S(1)} %bitcast.90, bf16[512,1024]{1,0:T(8,128)(2,1)S(1)} %bitcast.93, ...), custom_call_target="tpu_custom_call" | custom-call | flops 4294967296 | bytes 14680064 | tf_op jit(solution)/shard_map/scores/pallas_call | solution.py:109
  131.8 1.2 reduce.1
  133.8 9.0 %all_to_all.67 = f32[8,8,128]{2,1,0:T(8,128)S(1)} all-to-all(f32[8,8,128]{2,1,0:T(8,128)S(1)} %broadcast_in_dim.19), channel_id=1, replica_groups=mesh['x'=4,'zl'=2,'y'=4,'zh'=2,'c'=2] {'x','zl'}, dimensions={0} | all-to-all | bytes 65536 | tf_op jit(solution)/shard_map/all_to_all | solution.py:28
  143.4 4.6 %all-to-all-start.6 = ((f32[16,24,128]{2,1,0:T(8,128)}), f32[16,24,128]{2,1,0:T(8,128)S(1)}, u32[]{:S(2)}, u32[]{:S(2)}) async-start(f32[16,24,128]{2,1,0:T(8,128)} %broadcast_in_dim.20), calls=%async_computation.6 | async-start | bytes 393216 | tf_op jit(solution)/shard_map/all_to_all | solution.py:28
  148.2 8.3 %all-to-all-done.6 = f32[16,24,128]{2,1,0:T(8,128)S(1)} async-done(((f32[16,24,128]{2,1,0:T(8,128)}), f32[16,24,128]{2,1,0:T(8,128)S(1)}, u32[]{:S(2)}, u32[]{:S(2)}) %all-to-all-start.6) | async-done | bytes 196640 | tf_op jit(solution)/shard_map/all_to_all | solution.py:28
  159.6 3.3 %all-to-all-start.8 = ((f32[8,8,128]{2,1,0:T(8,128)}), f32[8,8,128]{2,1,0:T(8,128)S(1)}, u32[]{:S(2)}, u32[]{:S(2)}) async-start(f32[8,8,128]{2,1,0:T(8,128)} %broadcast_in_dim_broadcast_in_dim_broadcast_in_dim.3), calls=%async_computation.8 | async-start | bytes 65536 | tf_op jit(solution)/shard_map/all_to_all | solution.py:28
  163.0 11.3 %grads.1 = bf16[8,128,1024]{2,1,0:T(8,128)(2,1)} custom-call(s32[5]{0:T(128)S(1)} %stack.23.place, f32[1024,2048]{1,0:T(8,128)} %get-tuple-element.10.w_ref, f32[8,128,1]{2,1,0:T(8,128)S(1)} %copy.36.rk_ref, f32[4,1,512]{2,1,0:T(1,128)S(1)} %bitcast.98, s32[4,1,512]{2,1,0:T(1,128)S(1)} %bitcast.97, bf16[512,1024]{1,0:T(8,128)(2,1)S(1)} %bitcast.91, ...), custom_call_target="tpu_custom_call" | custom-call | flops 4294967296 | bytes 14680064 | tf_op jit(solution)/shard_map/grads/pallas_call | solution.py:136
  174.3 5.6 %all-to-all-start.7 = ((bf16[8,128,1024]{2,1,0:T(8,128)(2,1)}), bf16[8,128,1024]{2,1,0:T(8,128)(2,1)S(1)}, u32[]{:S(2)}, u32[]{:S(2)}) async-start(bf16[8,128,1024]{2,1,0:T(8,128)(2,1)} %grads.1), calls=%async_computation.7 | async-start | bytes 4194304 | tf_op jit(solution)/shard_map/all_to_all | solution.py:32
  181.1 29.9 %all-to-all-done.7 = bf16[8,128,1024]{2,1,0:T(8,128)(2,1)S(1)} async-done(((bf16[8,128,1024]{2,1,0:T(8,128)(2,1)}), bf16[8,128,1024]{2,1,0:T(8,128)(2,1)S(1)}, u32[]{:S(2)}, u32[]{:S(2)}) %all-to-all-start.7) | async-done | bytes 2097184 | tf_op jit(solution)/shard_map/all_to_all | solution.py:32
  211.8 1.1 broadcast_in_dim.21
  212.9 3.6 %all-to-all-start.9 = ((bf16[4,128,1024]{2,1,0:T(8,128)(2,1)}), bf16[4,128,1024]{2,1,0:T(8,128)(2,1)S(1)}, u32[]{:S(2)}, u32[]{:S(2)}) async-start(bf16[4,128,1024]{2,1,0:T(8,128)(2,1)} %broadcast_in_dim.21), calls=%async_computation.9 | async-start | bytes 2097152 | tf_op jit(solution)/shard_map/all_to_all | solution.py:28
  216.6 1.2 collective-permute-start.6
  218.8 8.9 %dynamic-slice_reduce_fusion = (bf16[4,128,320]{1,0,2:T(4,128)(2,1)}, bf16[4,128,320]{1,0,2:T(4,128)(2,1)}, bf16[4,128,320]{1,0,2:T(4,128)(2,1)}, bf16[4,128,320]{1,0,2:T(4,128)(2,1)}) fusion(bf16[4,2,128,320]{2,1,0,3:T(2,128)(2,1)S(1)} %reshape.229, s32[]{:T(128)S(6)} %select_n.122, s32[]{:T(128)S(6)} %select_n.121, bf16[4,2,128,320]{2,1,0,3:T(2,128)(2,1)S(1)} %reshape.226), kind=kLoop, calls=%fused_computation.19 | loop fusion | bytes 2621448 | tf_op jit(solution)/shard_map/jit(dynamic_index_in_dim)/dynamic_slice | solution.py:211
  227.7 3.2 %all-to-all-done.9 = bf16[4,128,1024]{2,1,0:T(8,128)(2,1)S(1)} async-done(((bf16[4,128,1024]{2,1,0:T(8,128)(2,1)}), bf16[4,128,1024]{2,1,0:T(8,128)(2,1)S(1)}, u32[]{:S(2)}, u32[]{:S(2)}) %all-to-all-start.9) | async-done | bytes 1048608 | tf_op jit(solution)/shard_map/all_to_all | solution.py:28
  231.0 1.1 broadcast_in_dim.22
  232.1 3.6 %all-to-all-start.10 = ((bf16[4,128,1024]{2,1,0:T(8,128)(2,1)}), bf16[4,128,1024]{2,1,0:T(8,128)(2,1)S(1)}, u32[]{:S(2)}, u32[]{:S(2)}) async-start(bf16[4,128,1024]{2,1,0:T(8,128)(2,1)} %broadcast_in_dim.22), calls=%async_computation.10 | async-start | bytes 2097152 | tf_op jit(solution)/shard_map/all_to_all | solution.py:28
  235.7 1.3 convolution_convert_fusion.3
  238.0 1.6 fusion.11
  239.6 9.6 %all-to-all-done.10 = bf16[4,128,1024]{2,1,0:T(8,128)(2,1)S(1)} async-done(((bf16[4,128,1024]{2,1,0:T(8,128)(2,1)}), bf16[4,128,1024]{2,1,0:T(8,128)(2,1)S(1)}, u32[]{:S(2)}, u32[]{:S(2)}) %all-to-all-start.10) | async-done | bytes 1048608 | tf_op jit(solution)/shard_map/all_to_all | solution.py:28
  249.2 2.4 fusion.2
  253.6 1.6 select_bitcast_fusion.1
  255.2 1.2 select_n.115
  256.4 1.8 select_n.118
  258.2 1.7 fusion.3
  260.9 3.5 %all-to-all-start.11 = ((bf16[8,320,128]{2,1,0:T(8,128)(2,1)}), bf16[8,320,128]{2,1,0:T(8,128)(2,1)S(1)}, u32[]{:S(2)}, u32[]{:S(2)}) async-start(bf16[8,320,128]{2,1,0:T(8,128)(2,1)} %bitcast.88), calls=%async_computation.11 | async-start | bytes 1310720 | tf_op jit(solution)/shard_map/all_to_all | solution.py:32
  264.9 1.0 copy.38
  267.0 8.7 %all-to-all-done.11 = bf16[8,320,128]{2,1,0:T(8,128)(2,1)S(1)} async-done(((bf16[8,320,128]{2,1,0:T(8,128)(2,1)}), bf16[8,320,128]{2,1,0:T(8,128)(2,1)S(1)}, u32[]{:S(2)}, u32[]{:S(2)}) %all-to-all-start.11) | async-done | bytes 655392 | tf_op jit(solution)/shard_map/all_to_all | solution.py:32
  276.7 3.5 %all-to-all-start.12 = ((bf16[8,320,128]{2,1,0:T(8,128)(2,1)}), bf16[8,320,128]{2,1,0:T(8,128)(2,1)S(1)}, u32[]{:S(2)}, u32[]{:S(2)}) async-start(bf16[8,320,128]{2,1,0:T(8,128)(2,1)} %broadcast_in_dim.23), calls=%async_computation.12 | async-start | bytes 1310720 | tf_op jit(solution)/shard_map/all_to_all | solution.py:28
  282.3 1.2 maximum_bitcast_fusion
  283.5 7.1 %all-to-all-done.12 = bf16[8,320,128]{2,1,0:T(8,128)(2,1)S(1)} async-done(((bf16[8,320,128]{2,1,0:T(8,128)(2,1)}), bf16[8,320,128]{2,1,0:T(8,128)(2,1)S(1)}, u32[]{:S(2)}, u32[]{:S(2)}) %all-to-all-start.12) | async-done | bytes 655392 | tf_op jit(solution)/shard_map/all_to_all | solution.py:28
  290.6 1.2 copy_bitcast_fusion
  (94 shorter events, 18.5 us)
Async XLA Ops:
  0.6 3.4 %collective-permute-start.1 = (bf16[320,1024]{1,0:T(8,128)(2,1)}, bf16[320,1024]{1,0:T(8,128)(2,1)S(1)}, u32[]{:S(2)}, u32[]{:S(2)}) collective-permute-start(bf16[320,1024]{1,0:T(8,128)(2,1)} %param.4), channel_id=1, source_target_pairs={{0,1},{1,0},{2,3},{3,2},{4,5},{5,4},{6,7},{7,6},{8,9},{9,8},{10,11... | collective-permute-start | bytes 1966088 | tf_op jit(solution)/shard_map/ppermute | solution.py:24
  0.7 2.0 copy-start.11
  2.2 1.9 copy-start.3
  2.2 2.3 collective-permute-start
  4.1 1.8 copy-start.14
  4.5 1.4 copy-start.6
  42.5 0.8 copy-start.1
  44.5 18.0 %all-to-all-start.3 = ((bf16[4,128,1024]{2,1,0:T(8,128)(2,1)}), bf16[4,128,1024]{2,1,0:T(8,128)(2,1)S(1)}, u32[]{:S(2)}, u32[]{:S(2)}) async-start(bf16[4,128,1024]{2,1,0:T(8,128)(2,1)} %broadcast_in_dim.16), calls=%async_computation.3 | async-start | bytes 2097152 | tf_op jit(solution)/shard_map/all_to_all | solution.py:28
  48.0 8.8 %collective-permute-start.3 = (bf16[128,1024]{1,0:T(8,128)(2,1)S(1)}, bf16[128,1024]{1,0:T(8,128)(2,1)S(1)}, u32[]{:S(2)}, u32[]{:S(2)}) collective-permute-start(bf16[128,1024]{1,0:T(8,128)(2,1)S(1)} %multiply_convert_fusion.1), channel_id=1, source_target_pairs={{0,2},{2,0},{1,3},{3,1},{4,6},{6,4},{5,7},{7,5},{8,10},{10,8},{9,1... | collective-permute-start | bytes 786440 | tf_op jit(solution)/shard_map/ppermute | solution.py:177
  78.6 16.6 %all-to-all-start.1 = ((bf16[4,128,1024]{2,1,0:T(8,128)(2,1)}), bf16[4,128,1024]{2,1,0:T(8,128)(2,1)S(1)}, u32[]{:S(2)}, u32[]{:S(2)}) async-start(bf16[4,128,1024]{2,1,0:T(8,128)(2,1)} %broadcast_in_dim.16), calls=%async_computation.1 | async-start | bytes 2097152 | tf_op jit(solution)/shard_map/all_to_all | solution.py:28
  82.9 6.5 %collective-permute-start.2 = (bf16[128,1024]{1,0:T(8,128)(2,1)S(1)}, bf16[128,1024]{1,0:T(8,128)(2,1)}, u32[]{:S(2)}, u32[]{:S(2)}) collective-permute-start(bf16[128,1024]{1,0:T(8,128)(2,1)S(1)} %multiply_convert_fusion.1), channel_id=1, source_target_pairs={{0,16},{16,0},{1,17},{17,1},{2,18},{18,2},{3,19},{19,3},{4,20},{20... | collective-permute-start | bytes 786440 | tf_op jit(solution)/shard_map/ppermute | solution.py:178
  83.9 29.0 %collective-permute-start.4 = (bf16[512,1024]{1,0:T(8,128)(2,1)S(1)}, bf16[512,1024]{1,0:T(8,128)(2,1)}, u32[]{:S(2)}, u32[]{:S(2)}) collective-permute-start(bf16[512,1024]{1,0:T(8,128)(2,1)S(1)} %bitcast.89), channel_id=1, source_target_pairs={{0,1},{1,0},{2,3},{3,2},{4,5},{5,4},{6,7},{7,6},{8,9},{9,8},{10,11... | collective-permute-start | bytes 3145736 | tf_op jit(solution)/shard_map/ppermute | solution.py:24
  83.9 29.0 %collective-permute-start.5 = (bf16[512,1024]{1,0:T(8,128)(2,1)S(1)}, bf16[512,1024]{1,0:T(8,128)(2,1)}, u32[]{:S(2)}, u32[]{:S(2)}) collective-permute-start(bf16[512,1024]{1,0:T(8,128)(2,1)S(1)} %bitcast.92), channel_id=1, source_target_pairs={{0,1},{1,0},{2,3},{3,2},{4,5},{5,4},{6,7},{7,6},{8,9},{9,8},{10,11... | collective-permute-start | bytes 3145736 | tf_op jit(solution)/shard_map/ppermute | solution.py:24
  97.3 4.4 %copy-start.18 = (s32[2048]{0:T(1024)S(1)}, s32[2048]{0:T(1024)}, u32[]{:S(2)}) copy-start(s32[2048]{0:T(1024)} %param.5) | copy-start | bytes 24580
  97.3 15.6 %all-to-all-start.2 = ((bf16[4,128,1024]{2,1,0:T(8,128)(2,1)}), bf16[4,128,1024]{2,1,0:T(8,128)(2,1)}, u32[]{:S(2)}, u32[]{:S(2)}) async-start(bf16[4,128,1024]{2,1,0:T(8,128)(2,1)} %broadcast_in_dim.17), calls=%async_computation.2 | async-start | bytes 2097152 | tf_op jit(solution)/shard_map/all_to_all | solution.py:28
  130.4 0.8 copy-start
  143.4 13.2 %all-to-all-start.6 = ((f32[16,24,128]{2,1,0:T(8,128)}), f32[16,24,128]{2,1,0:T(8,128)S(1)}, u32[]{:S(2)}, u32[]{:S(2)}) async-start(f32[16,24,128]{2,1,0:T(8,128)} %broadcast_in_dim.20), calls=%async_computation.6 | async-start | bytes 393216 | tf_op jit(solution)/shard_map/all_to_all | solution.py:28
  159.6 14.7 %all-to-all-start.8 = ((f32[8,8,128]{2,1,0:T(8,128)}), f32[8,8,128]{2,1,0:T(8,128)S(1)}, u32[]{:S(2)}, u32[]{:S(2)}) async-start(f32[8,8,128]{2,1,0:T(8,128)} %broadcast_in_dim_broadcast_in_dim_broadcast_in_dim.3), calls=%async_computation.8 | async-start | bytes 65536 | tf_op jit(solution)/shard_map/all_to_all | solution.py:28
  174.3 36.8 %all-to-all-start.7 = ((bf16[8,128,1024]{2,1,0:T(8,128)(2,1)}), bf16[8,128,1024]{2,1,0:T(8,128)(2,1)S(1)}, u32[]{:S(2)}, u32[]{:S(2)}) async-start(bf16[8,128,1024]{2,1,0:T(8,128)(2,1)} %grads.1), calls=%async_computation.7 | async-start | bytes 4194304 | tf_op jit(solution)/shard_map/all_to_all | solution.py:32
  181.1 30.3 %copy-start.2 = (f32[128,1024]{1,0:T(8,128)S(1)}, f32[128,1024]{1,0:T(8,128)}, u32[]{:S(2)}) copy-start(f32[128,1024]{1,0:T(8,128)} %copy-done.1) | copy-start | bytes 1572868
  212.9 4.9 %copy-start.4 = (bf16[1024,320]{0,1:T(8,128)(2,1)S(1)}, bf16[1024,320]{0,1:T(8,128)(2,1)}, u32[]{:S(2)}) copy-start(bf16[1024,320]{0,1:T(8,128)(2,1)} %copy-done.3) | copy-start | bytes 1966084
  212.9 5.4 %copy-start.7 = (bf16[1024,320]{0,1:T(8,128)(2,1)S(1)}, bf16[1024,320]{0,1:T(8,128)(2,1)}, u32[]{:S(2)}) copy-start(bf16[1024,320]{0,1:T(8,128)(2,1)} %copy-done.6) | copy-start | bytes 1966084
  212.9 18.0 %all-to-all-start.9 = ((bf16[4,128,1024]{2,1,0:T(8,128)(2,1)}), bf16[4,128,1024]{2,1,0:T(8,128)(2,1)S(1)}, u32[]{:S(2)}, u32[]{:S(2)}) async-start(bf16[4,128,1024]{2,1,0:T(8,128)(2,1)} %broadcast_in_dim.21), calls=%async_computation.9 | async-start | bytes 2097152 | tf_op jit(solution)/shard_map/all_to_all | solution.py:28
  216.6 11.1 %collective-permute-start.6 = (bf16[128,1024]{1,0:T(8,128)(2,1)S(1)}, bf16[128,1024]{1,0:T(8,128)(2,1)S(1)}, u32[]{:S(2)}, u32[]{:S(2)}) collective-permute-start(bf16[128,1024]{1,0:T(8,128)(2,1)S(1)} %multiply_convert_fusion), channel_id=1, source_target_pairs={{0,2},{2,0},{1,3},{3,1},{4,6},{6,4},{5,7},{7,5},{8,10},{10,8},{9,1... | collective-permute-start | bytes 786440 | tf_op jit(solution)/shard_map/ppermute | solution.py:206
  232.1 3.7 %copy-start.12 = (bf16[320,1024]{1,0:T(8,128)(2,1)S(1)}, bf16[320,1024]{1,0:T(8,128)(2,1)}, u32[]{:S(2)}) copy-start(bf16[320,1024]{1,0:T(8,128)(2,1)} %param.4) | copy-start | bytes 1966084
  232.1 17.1 %all-to-all-start.10 = ((bf16[4,128,1024]{2,1,0:T(8,128)(2,1)}), bf16[4,128,1024]{2,1,0:T(8,128)(2,1)S(1)}, u32[]{:S(2)}, u32[]{:S(2)}) async-start(bf16[4,128,1024]{2,1,0:T(8,128)(2,1)} %broadcast_in_dim.22), calls=%async_computation.10 | async-start | bytes 2097152 | tf_op jit(solution)/shard_map/all_to_all | solution.py:28
  235.7 1.3 copy-start.9
  237.0 1.0 copy-start.8
  249.2 2.4 copy-start.13
  251.6 1.1 copy-start.15
  251.6 6.7 %collective-permute-start.8 = (bf16[320,1024]{1,0:T(8,128)(2,1)}, bf16[320,1024]{1,0:T(8,128)(2,1)}, u32[]{:S(2)}, u32[]{:S(2)}) collective-permute-start(bf16[320,1024]{1,0:T(8,128)(2,1)} %fusion.2), channel_id=1, source_target_pairs={{0,1},{1,0},{2,3},{3,2},{4,5},{5,4},{6,7},{7,6},{8,9},{9,8},{10,11... | collective-permute-start | bytes 1966088 | tf_op jit(solution)/shard_map/ppermute | solution.py:24
  252.7 1.0 copy-start.19
  255.2 3.0 %copy-start.5 = (f32[320,1024]{1,0:T(8,128)S(1)}, f32[320,1024]{1,0:T(8,128)}, u32[]{:S(2)}) copy-start(f32[320,1024]{1,0:T(8,128)} %fusion.11) | copy-start | bytes 3932164
  259.9 4.5 %copy-start.10 = (bf16[320,4,1,128]{3,1,0,2:T(4,128)(2,1)S(1)}, bf16[320,4,1,128]{3,1,0,2:T(4,128)(2,1)}, u32[]{:S(2)}) copy-start(bf16[320,4,1,128]{3,1,0,2:T(4,128)(2,1)} %select_n.118) | copy-start | bytes 983044
  260.9 14.8 %all-to-all-start.11 = ((bf16[8,320,128]{2,1,0:T(8,128)(2,1)}), bf16[8,320,128]{2,1,0:T(8,128)(2,1)S(1)}, u32[]{:S(2)}, u32[]{:S(2)}) async-start(bf16[8,320,128]{2,1,0:T(8,128)(2,1)} %bitcast.88), calls=%async_computation.11 | async-start | bytes 1310720 | tf_op jit(solution)/shard_map/all_to_all | solution.py:32
  264.9 1.6 copy-start.17
  266.0 1.0 copy-start.16
  266.4 15.8 %collective-permute-start.7 = (bf16[320,1024]{1,0:T(8,128)(2,1)S(1)}, bf16[320,1024]{1,0:T(8,128)(2,1)S(1)}, u32[]{:S(2)}, u32[]{:S(2)}) collective-permute-start(bf16[320,1024]{1,0:T(8,128)(2,1)S(1)} %reshape.225), channel_id=1, source_target_pairs={{0,1},{1,0},{2,3},{3,2},{4,5},{5,4},{6,7},{7,6},{8,9},{9,8},{10,11... | collective-permute-start | bytes 1966088 | tf_op jit(solution)/shard_map/ppermute | solution.py:24
  276.7 13.9 %all-to-all-start.12 = ((bf16[8,320,128]{2,1,0:T(8,128)(2,1)}), bf16[8,320,128]{2,1,0:T(8,128)(2,1)S(1)}, u32[]{:S(2)}, u32[]{:S(2)}) async-start(bf16[8,320,128]{2,1,0:T(8,128)(2,1)} %broadcast_in_dim.23), calls=%async_computation.12 | async-start | bytes 1310720 | tf_op jit(solution)/shard_map/all_to_all | solution.py:28

commit v3 on v1

v3 whole, which is shorter than its diff:
```python
import jax
import jax.numpy as jnp
from jax import lax
from jax.experimental import pallas as pl
from jax.experimental.pallas import tpu as pltpu
from jax.sharding import Mesh
from jax.sharding import PartitionSpec as P

F32 = jnp.float32
BF16 = jnp.bfloat16
I32 = jnp.int32
SWAP = [(0, 1), (1, 0)]
RING = {s: [(i, (i + s) % 4) for i in range(4)] for s in (1, 2, 3)}
ROWS = 128
PAIR = 256
HALF = 1024
GROUP = 2048
TOTAL = 16384
WIDTH = 1024
VMEM_LIMIT = 40 * 1024 * 1024
YZ, XZ, CUTS = ("y", "zh"), ("x", "zl"), ("y", "zh", "c")
OFFSET = (0, 1, 3, 2)
EXP2_SCALE = 28.853900817779268


def core_swap(value):
    return lax.ppermute(value, "c", SWAP)


def spread(value, axes, count):
    return lax.all_to_all(jnp.broadcast_to(value[None], (count,) + value.shape), axes, 0, 0)


def sum_exchange(parts, axes):
    return jnp.sum(lax.all_to_all(parts, axes, 0, 0).astype(F32), axis=0)


def gather_ring(own, long_axis, short_axis):
    rows = own.shape[0]
    other = lax.ppermute(own, short_axis, SWAP)
    first = lax.axis_index(short_axis) == 0
    pair = jnp.concatenate([jnp.where(first, own, other), jnp.where(first, other, own)], 0)
    after = lax.ppermute(pair, long_axis, RING[3])
    before = lax.ppermute(pair, long_axis, RING[1])
    far_top = lax.ppermute(after[:rows], long_axis, RING[3])
    far_low = lax.ppermute(before[rows:], long_axis, RING[1])
    at = lax.axis_index(long_axis)
    out = jnp.zeros((8 * rows, own.shape[1]), own.dtype)
    for shift, part, skip in (
        (0, pair, 0),
        (1, after, 0),
        (3, before, 0),
        (2, far_top, 0),
        (2, far_low, rows),
    ):
        start = lax.rem(at + shift, 4) * (2 * rows) + skip
        out = lax.dynamic_update_slice_in_dim(out, part, start, 0)
    return out


def chunk_of(start, p, which, own_low):
    return lax.rem(start + OFFSET[p], 4) * 2 + (own_low if which == 0 else 1 - own_low)


def key_column(place, p):
    inner = place[4] * HALF + (place[2] * 2 + place[3]) * ROWS
    near, far = (chunk_of(place[0], p, which, place[1]) * GROUP + inner for which in (0, 1))
    at = lax.broadcasted_iota(I32, (PAIR, 1), 0)
    return at % ROWS + jnp.where(at < ROWS, near, far)


def query_core(place, n):
    return place[4] if n < 4 else 1 - place[4]


def query_chunks(place, n):
    return [
        query_core(place, n) * 8 + chunk_of(place[2], n % 4, which, place[3]) for which in (0, 1)
    ]


def score_kernel(place, *refs):
    key_refs, query_refs = refs[:4], refs[4:12]
    mates, w_ref, row_ref, col_ref, keys, queries, lanes, key_sem, query_sem = refs[12:]
    step = pl.program_id(0)

    def key_copy(p):
        return pltpu.make_async_copy(
            key_refs[p], keys.at[pl.ds(p * PAIR, PAIR), :], key_sem.at[p]
        )

    def query_copy(n):
        return pltpu.make_async_copy(query_refs[n], queries.at[n], query_sem.at[n])

    @pl.when(step == 0)
    def _():
        query_copy(0).start()
        for p in range(4):
            key_copy(p).start()
        for n in range(1, 8):
            query_copy(n).start()
        lanes[...] = jnp.zeros_like(lanes)
        for p in range(4):
            key_copy(p).wait()

    def run(n, masked):
        query_copy(n).wait()
        near, far = query_chunks(place, n)
        mate = jnp.concatenate([mates[near], mates[far]], axis=1)
        col = jnp.zeros((8, PAIR), F32)
        pos = jnp.zeros((8, PAIR), F32)
        for p in range(4):
            at = pl.ds(p * PAIR, PAIR)
            scores = lax.dot_general(
                keys[at, :], queries[n], (((1,), (1,)), ((), ())), preferred_element_type=F32
            )
            kid = key_column(place, p)
            weights = jnp.exp2(scores * EXP2_SCALE)
            if masked and p == 0:
                group = (place[0] * 2 + place[1]) * GROUP
                lane = lax.broadcasted_iota(I32, (1, PAIR), 1)
                qid = group + lane % ROWS + jnp.where(lane < ROWS, near, far) * ROWS
                weights = jnp.where(kid != qid, weights, 0.0)
            w_ref[at, :] = weights
            lanes[at, :] += weights[:, :ROWS] + weights[:, ROWS:]
            hits = jnp.where(kid == mate, scores, 0.0)
            col = col + jnp.sum(weights.reshape(PAIR // 8, 8, PAIR), axis=0)
            pos = pos + jnp.sum(hits.reshape(PAIR // 8, 8, PAIR), axis=0)
        col_ref[near, 0:8, :] = col[:, :ROWS]
        col_ref[far, 0:8, :] = col[:, ROWS:]
        col_ref[near, 8:16, :] = pos[:, :ROWS]
        col_ref[far, 8:16, :] = pos[:, ROWS:]

    for n in range(8):

        @pl.when(step == n)
        def _(n=n):
            run(n, n == 0)

    @pl.when(step == 7)
    def _():
        for p in range(4):
            for which in (0, 1):
                at = pl.ds(p * PAIR + which * ROWS, ROWS)
                row_ref[chunk_of(place[0], p, which, place[1])] = jnp.sum(
                    lanes[at, :], axis=1, keepdims=True
                )


def grad_kernel(place, w_ref, rk_ref, rq_ref, mates, *refs):
    query_refs, (out_ref, queries, query_sem) = refs[:8], refs[8:]
    step = pl.program_id(0)

    def query_copy(n):
        return pltpu.make_async_copy(
            query_refs[n], queries.at[pl.ds(n * PAIR, PAIR), :], query_sem.at[n]
        )

    @pl.when(step == 0)
    def _():
        for n in range(8):
            query_copy(n).start()
        for n in range(8):
            query_copy(n).wait()

    def run(p):
        kid = key_column(place, p)
        near, far = (chunk_of(place[0], p, which, place[1]) for which in (0, 1))
        rk = jnp.concatenate([rk_ref[near], rk_ref[far]], axis=0)
        parts = []
        for n in range(8):
            low, high = query_chunks(place, n)
            rq = jnp.concatenate([rq_ref[low], rq_ref[high]], axis=1)
            mate = jnp.concatenate([mates[low], mates[high]], axis=1)
            grads = w_ref[:, n * PAIR : (n + 1) * PAIR] * (rk + rq)
            parts.append(jnp.where(kid == mate, grads - 40.0, grads).astype(BF16))
        total = jnp.dot(
            jnp.concatenate(parts, axis=1), queries[...], preferred_element_type=F32
        ).astype(BF16)
        out_ref[0, place[1]] = total[:ROWS]
        out_ref[0, 1 - place[1]] = total[ROWS:]

    for p in range(4):

        @pl.when(step == p)
        def _(p=p):
            run(p)


def whole(shape):
    return pl.BlockSpec(shape, lambda t, place: (0,) * len(shape))


def score_call(place, keys, queries, mates):
    return pl.pallas_call(
        score_kernel,
        grid_spec=pltpu.PrefetchScalarGridSpec(
            num_scalar_prefetch=1,
            grid=(8,),
            in_specs=[pl.BlockSpec(memory_space=pl.ANY)] * 12 + [whole((16, 1, ROWS))],
            out_specs=[
                pl.BlockSpec((HALF, PAIR), lambda t, place: (0, t)),
                whole((8, ROWS, 1)),
                whole((16, 16, ROWS)),
            ],
            scratch_shapes=[
                pltpu.VMEM((HALF, WIDTH), BF16),
                pltpu.VMEM((8, PAIR, WIDTH), BF16),
                pltpu.VMEM((HALF, ROWS), F32),
                pltpu.SemaphoreType.DMA((4,)),
                pltpu.SemaphoreType.DMA((8,)),
            ],
        ),
        out_shape=[
            jax.ShapeDtypeStruct((HALF, GROUP), F32),
            jax.ShapeDtypeStruct((8, ROWS, 1), F32),
            jax.ShapeDtypeStruct((16, 16, ROWS), F32),
        ],
        compiler_params=pltpu.CompilerParams(vmem_limit_bytes=VMEM_LIMIT),
        cost_estimate=pl.CostEstimate(
            flops=2 * HALF * GROUP * WIDTH, bytes_accessed=14 << 20, transcendentals=HALF * GROUP
        ),
        name="scores",
    )(place, *keys, *queries, mates)


def grad_call(place, weights, rk, rq, mates, queries):
    return pl.pallas_call(
        grad_kernel,
        grid_spec=pltpu.PrefetchScalarGridSpec(
            num_scalar_prefetch=1,
            grid=(4,),
            in_specs=[
                pl.BlockSpec((PAIR, GROUP), lambda t, place: (t, 0)),
                whole((8, ROWS, 1)),
                whole((16, 1, ROWS)),
                whole((16, 1, ROWS)),
            ]
            + [pl.BlockSpec(memory_space=pl.ANY)] * 8,
            out_specs=pl.BlockSpec(
                (1, 2, ROWS, WIDTH),
                lambda t, place: (
                    lax.rem(place[0] + t + jnp.where(t == 2, 1, 0) - jnp.where(t == 3, 1, 0), 4),
                    0,
                    0,
                    0,
                ),
            ),
            scratch_shapes=[pltpu.VMEM((GROUP, WIDTH), BF16), pltpu.SemaphoreType.DMA((8,))],
        ),
        out_shape=jax.ShapeDtypeStruct((4, 2, ROWS, WIDTH), BF16),
        compiler_params=pltpu.CompilerParams(vmem_limit_bytes=VMEM_LIMIT),
        cost_estimate=pl.CostEstimate(
            flops=2 * HALF * GROUP * WIDTH, bytes_accessed=14 << 20, transcendentals=0
        ),
        name="grads",
    )(place, weights, rk, rq, mates, *queries)


def shards(summaries, head, partner):
    core = lax.axis_index("c")
    place = jnp.stack([lax.axis_index(a) for a in ("x", "zl", "y", "zh", "c")]).astype(I32)
    mates = partner.reshape(16, 1, ROWS)

    mine = lax.dynamic_slice_in_dim(summaries, core * HALF, HALF, 0)
    theirs = core_swap(lax.dynamic_slice_in_dim(summaries, (1 - core) * HALF, HALF, 0))
    other_head = core_swap(head)
    z_part = jnp.dot(mine, head, preferred_element_type=F32) + jnp.dot(
        theirs, other_head, preferred_element_type=F32
    )
    z = sum_exchange(z_part.astype(BF16).reshape(8, ROWS, WIDTH), YZ)
    inv = lax.rsqrt(jnp.sum(z * z, axis=1, keepdims=True) + 1e-06)
    unit = z * inv
    emb = unit.astype(BF16)

    q_pair = jnp.concatenate([emb, lax.ppermute(emb, "zh", SWAP)], 0)
    k_pair = jnp.concatenate([emb, lax.ppermute(emb, "zl", SWAP)], 0)
    queries = [q_pair] + [lax.ppermute(q_pair, "y", RING[4 - s]) for s in OFFSET[1:]]
    keys = [k_pair] + [lax.ppermute(k_pair, "x", RING[4 - s]) for s in OFFSET[1:]]
    queries += [core_swap(a) for a in queries]
    weights, row_part, col_part = score_call(place, keys, queries, mates)

    pos_part = 20.0 * jnp.sum(col_part[:, 8:])
    col_part = jnp.sum(col_part[:, :8], axis=1)
    col_part = jnp.concatenate([col_part, jnp.full((8, ROWS), pos_part, F32)], 0)
    cols = jnp.sum(spread(col_part, CUTS, 16), axis=0)
    rows = jnp.sum(spread(row_part.reshape(8, ROWS), XZ, 8), axis=0)
    den_q, pos = cols[:16], cols[16, 0]
    rk = (20.0 / rows).reshape(8, ROWS, 1)
    rq = (20.0 / den_q).reshape(16, 1, ROWS)
    grad_part = grad_call(place, weights, rk, rq, mates, queries)

    loss = jnp.full((8, 128), jnp.sum(jnp.log(den_q)) - pos, F32)
    loss = jnp.sum(spread(loss, XZ, 8), axis=0)[0, 0] / TOTAL

    grad_emb = sum_exchange(grad_part.reshape(8, ROWS, WIDTH), XZ)
    grad_emb, loss = lax.optimization_barrier((grad_emb, loss))
    grad_z = (inv * (grad_emb - unit * jnp.sum(unit * grad_emb, axis=1, keepdims=True))).astype(BF16)
    grad_half = gather_ring(grad_z, "y", "zh")

    contract_first = (((0,), (0,)), ((), ()))
    head_theirs = lax.dot_general(
        theirs, grad_half, contract_first, preferred_element_type=F32
    ).astype(BF16)
    head_mine = lax.dot_general(mine, grad_half, contract_first, preferred_element_type=F32)
    head_part = (head_mine + core_swap(head_theirs).astype(F32)).astype(BF16)
    features = head.shape[0]
    pieces = head_part.reshape(features, 8, WIDTH // 8).transpose(1, 0, 2)
    head_sum = sum_exchange(pieces, XZ).astype(BF16)
    grad_head = spread(head_sum, XZ, 8).transpose(1, 0, 2).reshape(features, WIDTH).astype(F32)

    contract_last = (((1,), (1,)), ((), ()))
    out_theirs = lax.dot_general(
        other_head, grad_half, contract_last, preferred_element_type=F32
    ).astype(BF16)
    out_mine = lax.dot_general(head, grad_half, contract_last, preferred_element_type=F32).astype(BF16)
    got = core_swap(out_theirs)
    first = core == 0
    out = jnp.concatenate([jnp.where(first, out_mine, got), jnp.where(first, got, out_mine)], 1)
    return loss, out.T, grad_head


def solution(mesh):
    fine = Mesh(mesh.devices.reshape(4, 2, 4, 2, 2), ("x", "zl", "y", "zh", "c"))
    return jax.shard_map(
        shards,
        mesh=fine,
        in_specs=(P(XZ, CUTS), P(CUTS, None), P(XZ)),
        out_specs=(P(), P(XZ, CUTS), P(CUTS, None)),
        check_vma=False,
    )
```

time: 269 us -> 265 us (0.985)
  blocking collectives: 65.4 us -> 36 us
  matrix products: 35.3 us -> 9.74 us
  waiting for transfers between devices: 93.6 us -> 119 us
  Pallas kernels: 0 us -> 21.6 us
  local copies, waits for them, and re-layouts: 17.8 us -> 20.8 us
    all_to_all x4 -> x6, waiting for transfers between devices: 18.8 us -> 62.6 us  [the longest x2 42.3 us: sum_exchange(): return jnp.sum(lax.all_to_all(parts, axes, 0, 0).astype(F32), axis=0)]
    all_to_all x2 -> x1, blocking collectives: 65.4 us -> 36 us  [sum_exchange(): return jnp.sum(lax.all_to_all(parts, axes, 0, 0).astype(F32), axis=0)]
    ppermute x3 -> x8, waiting for transfers between devices: 6.36 us -> 33.6 us  [the longest x3 15 us: shards(): lax.ppermute(q_pair, 'y', RING[4 - s])]
    dot_general x2 -> x0, matrix products: 22.5 us -> none  [the longest x1 12.5 us: shards(): lax.dot_general(queries, keys, (((1,), (1,)), ((), ())), preferred_elemen...]
    ppermute x3 -> x1, waiting for transfers between devices: 32.2 us -> 9.98 us  [gather_ring(): after = lax.ppermute(pair, long_axis, RING[3])]
    pallas_call x0 -> x2, Pallas kernels: none -> 21.6 us  [the longest x1 10.9 us: score_call(): pl.pallas_call(score_kernel, grid_spec=pltpu.PrefetchScalarGridSpec(num_s...]
    all_to_all x4 -> x6, starting transfers between devices: 13.9 us -> 24.5 us  [the longest x4 15.1 us: spread(): lax.all_to_all(jnp.broadcast_to(value[None], (count,) + value.shape), axe...]
    ppermute x3 -> x1, waiting for transfers between devices: 17.2 us -> 7.61 us  [gather_ring(): other = lax.ppermute(own, short_axis, SWAP)]
  transfers between devices with their start and end apart: 29 -> 27, of which waited for: 20 -> 17; matrix products, arithmetic and copies ran while one was open for 9% -> 6% of each run, Pallas kernels for 0% -> 4%
where the time goes in v3:
time: 265 us; the launch traced here: 264 us
  waiting for transfers between devices  119 us (45%)
  starting transfers between devices  44.4 us (17%)
  blocking collectives  36 us (14%)
  Pallas kernels  21.6 us (8%)
  local copies, waits for them, and re-layouts  20.8 us (8%)
  matrix products  9.74 us (4%)
  other arithmetic  8.02 us (3%)
  between operations  4.82 us (2%)
    all_to_all x2, waiting for transfers between devices, sum_exchange(): return jnp.sum(lax.all_to_all(parts, axes, 0, 0).astype(F32), axis=0)  42.3 us
    all_to_all x1, blocking collectives, sum_exchange(): return jnp.sum(lax.all_to_all(parts, axes, 0, 0).astype(F32), axis=0)  36 us
    all_to_all x4, waiting for transfers between devices, spread(): lax.all_to_all(jnp.broadcast_to(value[None], (count,) + value.shape), axe...  20.4 us
    all_to_all x4, starting transfers between devices, spread(): lax.all_to_all(jnp.broadcast_to(value[None], (count,) + value.shape), axe...  15.1 us
    ppermute x3, waiting for transfers between devices, shards(): lax.ppermute(q_pair, 'y', RING[4 - s])  15 us
    pallas_call x1, Pallas kernels, score_call(): pl.pallas_call(score_kernel, grid_spec=pltpu.PrefetchScalarGridSpec(num_s...  10.9 us
    pallas_call x1, Pallas kernels, grad_call(): pl.pallas_call(grad_kernel, grid_spec=pltpu.PrefetchScalarGridSpec(num_sc...  10.7 us
    unnamed x38, local copies, waits for them, and re-layouts  10.4 us
  transfers between devices with their start and end apart: 27, of which 17 were waited for; matrix products, arithmetic and copies ran while one was open for 6% of the time, Pallas kernels for 4%

profile of v3, /device:TPU:0, one launch (start us, length us, event | category | flops | bytes accessed | tf_op | source)
XLA Modules:
  0.0 264.1 jit_solution(4542032060550530697)
XLA Ops:
  0.7 1.3 copy-done
  2.6 2.4 fusion.5
  5.3 1.3 add_convert_fusion
  6.7 36.0 %all_to_all.35 = bf16[8,128,1024]{2,1,0:T(8,128)(2,1)S(1)} all-to-all(bf16[8,128,1024]{2,1,0:T(8,128)(2,1)S(1)} %bitcast.46), channel_id=1, replica_groups=mesh['x'=4,'zl'=2,'y'=4,'zh'=2,'c'=2] {'y','zh'}, dimensions={0} | all-to-all | bytes 4194304 | tf_op jit(solution)/shard_map/all_to_all | solution.py:35
  43.4 1.1 collective-permute-start.2
  44.5 1.8 collective-permute-start.6
  46.3 6.4 %collective-permute-done.2 = bf16[128,1024]{1,0:T(8,128)(2,1)S(1)} collective-permute-done((bf16[128,1024]{1,0:T(8,128)(2,1)S(1)}, bf16[128,1024]{1,0:T(8,128)(2,1)S(1)}, u32[]{:S(2)}, u32[]{:S(2)}) %collective-permute-start.2) | collective-permute-done | bytes 262176 | tf_op jit(solution)/shard_map/ppermute | solution.py:277
  52.7 4.4 %collective-permute-done.6 = bf16[128,1024]{1,0:T(8,128)(2,1)S(1)} collective-permute-done((bf16[128,1024]{1,0:T(8,128)(2,1)S(1)}, bf16[128,1024]{1,0:T(8,128)(2,1)S(1)}, u32[]{:S(2)}, u32[]{:S(2)}) %collective-permute-start.6) | collective-permute-done | bytes 262176 | tf_op jit(solution)/shard_map/ppermute | solution.py:276
  57.2 1.2 collective-permute-start.7
  59.3 1.5 collective-permute-start.9
  60.8 2.8 %collective-permute-start.3 = (bf16[256,1024]{1,0:T(8,128)(2,1)S(1)}, bf16[256,1024]{1,0:T(8,128)(2,1)S(1)}, u32[]{:S(2)}, u32[]{:S(2)}) collective-permute-start(bf16[256,1024]{1,0:T(8,128)(2,1)S(1)} %get-tuple-element.22.refs_0_), channel_id=1, source_target_pairs={{0,96},{32,0},{64,32},{96,64},{1,97},{33,1},{65,33},{97,65},{2,98}... | collective-permute-start | bytes 1572872 | tf_op jit(solution)/shard_map/ppermute | solution.py:279
  63.6 8.6 %collective-permute-done.7.refs_5_.refs_1_ = bf16[256,1024]{1,0:T(8,128)(2,1)S(1)} collective-permute-done((bf16[256,1024]{1,0:T(8,128)(2,1)S(1)}, bf16[256,1024]{1,0:T(8,128)(2,1)S(1)}, u32[]{:S(2)}, u32[]{:S(2)}) %collective-permute-start.7) | collective-permute-done | bytes 524320 | tf_op jit(solution)/shard_map/ppermute | solution.py:278
  72.1 1.5 collective-permute-start.4
  73.6 2.7 %collective-permute-start.5 = (bf16[256,1024]{1,0:T(8,128)(2,1)S(1)}, bf16[256,1024]{1,0:T(8,128)(2,1)}, u32[]{:S(2)}, u32[]{:S(2)}) collective-permute-start(bf16[256,1024]{1,0:T(8,128)(2,1)S(1)} %get-tuple-element.22.refs_0_), channel_id=1, source_target_pairs={{0,64},{32,96},{64,0},{96,32},{1,65},{33,97},{65,1},{97,33},{2,66}... | collective-permute-start | bytes 1572872 | tf_op jit(solution)/shard_map/ppermute | solution.py:279
  76.4 6.4 %collective-permute-done.9.refs_7_.refs_3_ = bf16[256,1024]{1,0:T(8,128)(2,1)} collective-permute-done((bf16[256,1024]{1,0:T(8,128)(2,1)S(1)}, bf16[256,1024]{1,0:T(8,128)(2,1)}, u32[]{:S(2)}, u32[]{:S(2)}) %collective-permute-start.9) | collective-permute-done | bytes 524320 | tf_op jit(solution)/shard_map/ppermute | solution.py:278
  84.9 1.8 collective-permute-done.3.refs_1_
  88.1 5.6 %collective-permute-done.5.refs_3_ = bf16[256,1024]{1,0:T(8,128)(2,1)} collective-permute-done((bf16[256,1024]{1,0:T(8,128)(2,1)S(1)}, bf16[256,1024]{1,0:T(8,128)(2,1)}, u32[]{:S(2)}, u32[]{:S(2)}) %collective-permute-start.5) | collective-permute-done | bytes 524320 | tf_op jit(solution)/shard_map/ppermute | solution.py:279
  94.8 1.0 copy-done.5
  95.8 1.0 copy-done.8
  96.8 10.9 %scores.1 = (f32[1024,2048]{1,0:T(8,128)}, f32[8,128,1]{2,1,0:T(8,128)S(1)}, f32[16,16,128]{2,1,0:T(8,128)S(1)}) custom-call(s32[5]{0:T(128)S(1)} %stack.23.place, bf16[256,1024]{1,0:T(8,128)(2,1)S(1)} %get-tuple-element.22.refs_0_, bf16[256,1024]{1,0:T(8,128)(2,1)S(1)} %copy-done.8, bf16[256,1024]{1,0:T(8,128)(2,1)} %collective-permute-done.4.refs_2_, ...), custom_call_target="tpu_custom_call" | custom-call | flops 4294967296 | bytes 14680064 | tf_op jit(solution)/shard_map/scores/pallas_call | solution.py:195
  108.6 3.3 %all-to-all-start.1 = ((f32[8,8,128]{2,1,0:T(8,128)}), f32[8,8,128]{2,1,0:T(8,128)S(1)}, u32[]{:S(2)}, u32[]{:S(2)}) async-start(f32[8,8,128]{2,1,0:T(8,128)} %broadcast_in_dim.11), calls=%async_computation.1 | async-start | bytes 65536 | tf_op jit(solution)/shard_map/all_to_all | solution.py:31
  113.2 4.9 %all-to-all-done.1 = f32[8,8,128]{2,1,0:T(8,128)S(1)} async-done(((f32[8,8,128]{2,1,0:T(8,128)}), f32[8,8,128]{2,1,0:T(8,128)S(1)}, u32[]{:S(2)}, u32[]{:S(2)}) %all-to-all-start.1) | async-done | bytes 32800 | tf_op jit(solution)/shard_map/all_to_all | solution.py:31
  118.8 4.9 %all-to-all-start.2 = ((f32[16,24,128]{2,1,0:T(8,128)}), f32[16,24,128]{2,1,0:T(8,128)S(1)}, u32[]{:S(2)}, u32[]{:S(2)}) async-start(f32[16,24,128]{2,1,0:T(8,128)} %broadcast_in_dim.12), calls=%async_computation.2 | async-start | bytes 393216 | tf_op jit(solution)/shard_map/all_to_all | solution.py:31
  123.9 8.3 %all-to-all-done.2 = f32[16,24,128]{2,1,0:T(8,128)S(1)} async-done(((f32[16,24,128]{2,1,0:T(8,128)}), f32[16,24,128]{2,1,0:T(8,128)S(1)}, u32[]{:S(2)}, u32[]{:S(2)}) %all-to-all-start.2) | async-done | bytes 196640 | tf_op jit(solution)/shard_map/all_to_all | solution.py:31
  135.4 3.3 %all-to-all-start.4 = ((f32[8,8,128]{2,1,0:T(8,128)}), f32[8,8,128]{2,1,0:T(8,128)S(1)}, u32[]{:S(2)}, u32[]{:S(2)}) async-start(f32[8,8,128]{2,1,0:T(8,128)} %broadcast_in_dim_broadcast_in_dim_broadcast_in_dim.3), calls=%async_computation.4 | async-start | bytes 65536 | tf_op jit(solution)/shard_map/all_to_all | solution.py:31
  139.8 1.0 copy-done.6
  140.8 10.7 %grads.1 = bf16[4,2,128,1024]{3,2,1,0:T(8,128)(2,1)} custom-call(s32[5]{0:T(128)S(1)} %stack.23.place, f32[1024,2048]{1,0:T(8,128)} %get-tuple-element.8.w_ref, f32[8,128,1]{2,1,0:T(8,128)S(1)} %copy.12.rk_ref, f32[16,1,128]{2,1,0:T(1,128)S(1)} %bitcast.43, s32[16,1,128]{2,1,0:T(1,128)S(1)} %bitcast.45, ...), custom_call_target="tpu_custom_call" | custom-call | flops 4294967296 | bytes 14680064 | tf_op jit(solution)/shard_map/grads/pallas_call | solution.py:228
  151.6 5.7 %all-to-all-start.3 = ((bf16[8,128,1024]{2,1,0:T(8,128)(2,1)}), bf16[8,128,1024]{2,1,0:T(8,128)(2,1)}, u32[]{:S(2)}, u32[]{:S(2)}) async-start(bf16[8,128,1024]{2,1,0:T(8,128)(2,1)} %bitcast.9), calls=%async_computation.3 | async-start | bytes 4194304 | tf_op jit(solution)/shard_map/all_to_all | solution.py:35
  158.5 30.1 %all-to-all-done.3 = bf16[8,128,1024]{2,1,0:T(8,128)(2,1)} async-done(((bf16[8,128,1024]{2,1,0:T(8,128)(2,1)}), bf16[8,128,1024]{2,1,0:T(8,128)(2,1)}, u32[]{:S(2)}, u32[]{:S(2)}) %all-to-all-start.3) | async-done | bytes 2097184 | tf_op jit(solution)/shard_map/all_to_all | solution.py:35
  188.5 2.0 convert_reduce_fusion
  191.0 1.1 collective-permute-start.14
  192.0 7.6 %collective-permute-done.14 = bf16[128,1024]{1,0:T(8,128)(2,1)S(1)} collective-permute-done((bf16[128,1024]{1,0:T(8,128)(2,1)S(1)}, bf16[128,1024]{1,0:T(8,128)(2,1)S(1)}, u32[]{:S(2)}, u32[]{:S(2)}) %collective-permute-start.14) | collective-permute-done | bytes 262176 | tf_op jit(solution)/shard_map/ppermute | solution.py:40
  201.8 1.1 collective-permute-start.16
  202.9 10.0 %collective-permute-done.15 = bf16[256,1024]{1,0:T(8,128)(2,1)S(1)} collective-permute-done((bf16[256,1024]{1,0:T(8,128)(2,1)}, bf16[256,1024]{1,0:T(8,128)(2,1)S(1)}, u32[]{:S(2)}, u32[]{:S(2)}) %collective-permute-start.15) | collective-permute-done | bytes 524320 | tf_op jit(solution)/shard_map/ppermute | solution.py:43
  214.4 2.1 collective-permute-start.17
  216.5 1.0 slice.31
  217.6 1.1 constant_dynamic-update-slice_fusion.3
  218.7 1.1 constant_dynamic-update-slice_fusion.2
  219.8 1.3 collective-permute-done.17
  222.1 3.1 %collective-permute-done.18 = bf16[128,1024]{1,0:T(8,128)(2,1)S(1)} collective-permute-done((bf16[128,1024]{1,0:T(8,128)(2,1)S(1)}, bf16[128,1024]{1,0:T(8,128)(2,1)S(1)}, u32[]{:S(2)}, u32[]{:S(2)}) %collective-permute-start.18) | collective-permute-done | bytes 262176 | tf_op jit(solution)/shard_map/ppermute | solution.py:46
  226.8 1.7 fusion.3
  230.4 3.7 %all-to-all-start.5 = ((bf16[8,320,128]{2,1,0:T(8,128)(2,1)}), bf16[8,320,128]{2,1,0:T(8,128)(2,1)S(1)}, u32[]{:S(2)}, u32[]{:S(2)}) async-start(bf16[8,320,128]{2,1,0:T(8,128)(2,1)} %bitcast.42), calls=%async_computation.5 | async-start | bytes 1310720 | tf_op jit(solution)/shard_map/all_to_all | solution.py:35
  234.1 12.2 %all-to-all-done.5 = bf16[8,320,128]{2,1,0:T(8,128)(2,1)S(1)} async-done(((bf16[8,320,128]{2,1,0:T(8,128)(2,1)}), bf16[8,320,128]{2,1,0:T(8,128)(2,1)S(1)}, u32[]{:S(2)}, u32[]{:S(2)}) %all-to-all-start.5) | async-done | bytes 655392 | tf_op jit(solution)/shard_map/all_to_all | solution.py:35
  247.3 3.5 %all-to-all-start.6 = ((bf16[8,320,128]{2,1,0:T(8,128)(2,1)}), bf16[8,320,128]{2,1,0:T(8,128)(2,1)S(1)}, u32[]{:S(2)}, u32[]{:S(2)}) async-start(bf16[8,320,128]{2,1,0:T(8,128)(2,1)} %broadcast_in_dim.14), calls=%async_computation.6 | async-start | bytes 1310720 | tf_op jit(solution)/shard_map/all_to_all | solution.py:31
  250.8 2.6 broadcast_select_fusion.1
  253.4 1.2 maximum_bitcast_fusion
  254.6 7.2 %all-to-all-done.6 = bf16[8,320,128]{2,1,0:T(8,128)(2,1)S(1)} async-done(((bf16[8,320,128]{2,1,0:T(8,128)(2,1)}), bf16[8,320,128]{2,1,0:T(8,128)(2,1)S(1)}, u32[]{:S(2)}, u32[]{:S(2)}) %all-to-all-start.6) | async-done | bytes 655392 | tf_op jit(solution)/shard_map/all_to_all | solution.py:31
  261.8 1.2 copy_bitcast_fusion
  (91 shorter events, 22.4 us)
Async XLA Ops:
  0.6 1.3 copy-start
  2.0 3.0 %collective-permute-start = (bf16[1024,320]{0,1:T(8,128)(2,1)S(1)}, bf16[1024,320]{0,1:T(8,128)(2,1)S(1)}, u32[]{:S(2)}, u32[]{:S(2)}) collective-permute-start(bf16[1024,320]{0,1:T(8,128)(2,1)S(1)} %constant_dynamic-slice_fusion), channel_id=1, source_target_pairs={{0,1},{1,0},{2,3},{3,2},{4,5},{5,4},{6,7},{7,6},{8,9},{9,8},{10,11... | collective-permute-start | bytes 1966088 | tf_op jit(solution)/shard_map/ppermute | solution.py:27
  2.1 3.2 %collective-permute-start.1 = (bf16[320,1024]{1,0:T(8,128)(2,1)}, bf16[320,1024]{1,0:T(8,128)(2,1)S(1)}, u32[]{:S(2)}, u32[]{:S(2)}) collective-permute-start(bf16[320,1024]{1,0:T(8,128)(2,1)} %param.4), channel_id=1, source_target_pairs={{0,1},{1,0},{2,3},{3,2},{4,5},{5,4},{6,7},{7,6},{8,9},{9,8},{10,11... | collective-permute-start | bytes 1966088 | tf_op jit(solution)/shard_map/ppermute | solution.py:27
  5.0 1.7 copy-start.17
  5.3 1.4 copy-start.15
  43.1 9.6 %copy-start.10 = (f32[128,1024]{1,0:T(8,128)}, f32[128,1024]{1,0:T(8,128)S(1)}, u32[]{:S(2)}) copy-start(f32[128,1024]{1,0:T(8,128)S(1)} %convert_reduce_fusion.1) | copy-start | bytes 1572868
  43.1 50.6 %copy-start.9 = (s32[2048]{0:T(1024)S(1)}, s32[2048]{0:T(1024)}, u32[]{:S(2)}) copy-start(s32[2048]{0:T(1024)} %param.5) | copy-start | bytes 24580
  43.4 9.3 %collective-permute-start.2 = (bf16[128,1024]{1,0:T(8,128)(2,1)S(1)}, bf16[128,1024]{1,0:T(8,128)(2,1)S(1)}, u32[]{:S(2)}, u32[]{:S(2)}) collective-permute-start(bf16[128,1024]{1,0:T(8,128)(2,1)S(1)} %multiply_convert_fusion.1), channel_id=1, source_target_pairs={{0,16},{16,0},{1,17},{17,1},{2,18},{18,2},{3,19},{19,3},{4,20},{20... | collective-permute-start | bytes 786440 | tf_op jit(solution)/shard_map/ppermute | solution.py:277
  44.5 12.6 %collective-permute-start.6 = (bf16[128,1024]{1,0:T(8,128)(2,1)S(1)}, bf16[128,1024]{1,0:T(8,128)(2,1)S(1)}, u32[]{:S(2)}, u32[]{:S(2)}) collective-permute-start(bf16[128,1024]{1,0:T(8,128)(2,1)S(1)} %multiply_convert_fusion.1), channel_id=1, source_target_pairs={{0,2},{2,0},{1,3},{3,1},{4,6},{6,4},{5,7},{7,5},{8,10},{10,8},{9,1... | collective-permute-start | bytes 786440 | tf_op jit(solution)/shard_map/ppermute | solution.py:276
  57.2 14.9 %collective-permute-start.7 = (bf16[256,1024]{1,0:T(8,128)(2,1)S(1)}, bf16[256,1024]{1,0:T(8,128)(2,1)S(1)}, u32[]{:S(2)}, u32[]{:S(2)}) collective-permute-start(bf16[256,1024]{1,0:T(8,128)(2,1)S(1)} %get-tuple-element.21.refs_4_.refs_0_), channel_id=1, source_target_pairs={{0,12},{4,0},{8,4},{12,8},{1,13},{5,1},{9,5},{13,9},{2,14},{6,2},{... | collective-permute-start | bytes 1572872 | tf_op jit(solution)/shard_map/ppermute | solution.py:278
  58.4 15.2 %collective-permute-start.8 = (bf16[256,1024]{1,0:T(8,128)(2,1)S(1)}, bf16[256,1024]{1,0:T(8,128)(2,1)S(1)}, u32[]{:S(2)}, u32[]{:S(2)}) collective-permute-start(bf16[256,1024]{1,0:T(8,128)(2,1)S(1)} %get-tuple-element.21.refs_4_.refs_0_), channel_id=1, source_target_pairs={{0,4},{4,8},{8,12},{12,0},{1,5},{5,9},{9,13},{13,1},{2,6},{6,10},{... | collective-permute-start | bytes 1572872 | tf_op jit(solution)/shard_map/ppermute | solution.py:278
  59.3 23.5 %collective-permute-start.9 = (bf16[256,1024]{1,0:T(8,128)(2,1)S(1)}, bf16[256,1024]{1,0:T(8,128)(2,1)}, u32[]{:S(2)}, u32[]{:S(2)}) collective-permute-start(bf16[256,1024]{1,0:T(8,128)(2,1)S(1)} %get-tuple-element.21.refs_4_.refs_0_), channel_id=1, source_target_pairs={{0,8},{4,12},{8,0},{12,4},{1,9},{5,13},{9,1},{13,5},{2,10},{6,14},... | collective-permute-start | bytes 1572872 | tf_op jit(solution)/shard_map/ppermute | solution.py:278
  60.8 22.0 %collective-permute-start.10 = (bf16[256,1024]{1,0:T(8,128)(2,1)S(1)}, bf16[256,1024]{1,0:T(8,128)(2,1)S(1)}, u32[]{:S(2)}, u32[]{:S(2)}) collective-permute-start(bf16[256,1024]{1,0:T(8,128)(2,1)S(1)} %get-tuple-element.21.refs_4_.refs_0_), channel_id=1, source_target_pairs={{0,1},{1,0},{2,3},{3,2},{4,5},{5,4},{6,7},{7,6},{8,9},{9,8},{10,11... | collective-permute-start | bytes 1572872 | tf_op jit(solution)/shard_map/ppermute | solution.py:27
  60.8 25.9 %collective-permute-start.3 = (bf16[256,1024]{1,0:T(8,128)(2,1)S(1)}, bf16[256,1024]{1,0:T(8,128)(2,1)S(1)}, u32[]{:S(2)}, u32[]{:S(2)}) collective-permute-start(bf16[256,1024]{1,0:T(8,128)(2,1)S(1)} %get-tuple-element.22.refs_0_), channel_id=1, source_target_pairs={{0,96},{32,0},{64,32},{96,64},{1,97},{33,1},{65,33},{97,65},{2,98}... | collective-permute-start | bytes 1572872 | tf_op jit(solution)/shard_map/ppermute | solution.py:279
  72.1 15.9 %collective-permute-start.4 = (bf16[256,1024]{1,0:T(8,128)(2,1)S(1)}, bf16[256,1024]{1,0:T(8,128)(2,1)}, u32[]{:S(2)}, u32[]{:S(2)}) collective-permute-start(bf16[256,1024]{1,0:T(8,128)(2,1)S(1)} %get-tuple-element.22.refs_0_), channel_id=1, source_target_pairs={{0,32},{32,64},{64,96},{96,0},{1,33},{33,65},{65,97},{97,1},{2,34}... | collective-permute-start | bytes 1572872 | tf_op jit(solution)/shard_map/ppermute | solution.py:279
  73.6 20.1 %collective-permute-start.5 = (bf16[256,1024]{1,0:T(8,128)(2,1)S(1)}, bf16[256,1024]{1,0:T(8,128)(2,1)}, u32[]{:S(2)}, u32[]{:S(2)}) collective-permute-start(bf16[256,1024]{1,0:T(8,128)(2,1)S(1)} %get-tuple-element.22.refs_0_), channel_id=1, source_target_pairs={{0,64},{32,96},{64,0},{96,32},{1,65},{33,97},{65,1},{97,33},{2,66}... | collective-permute-start | bytes 1572872 | tf_op jit(solution)/shard_map/ppermute | solution.py:279
  82.8 10.9 %collective-permute-start.11 = (bf16[256,1024]{1,0:T(8,128)(2,1)S(1)}, bf16[256,1024]{1,0:T(8,128)(2,1)}, u32[]{:S(2)}, u32[]{:S(2)}) collective-permute-start(bf16[256,1024]{1,0:T(8,128)(2,1)S(1)} %collective-permute-done.7.refs_5_.refs_1_), channel_id=1, source_target_pairs={{0,1},{1,0},{2,3},{3,2},{4,5},{5,4},{6,7},{7,6},{8,9},{9,8},{10,11... | collective-permute-start | bytes 1572872 | tf_op jit(solution)/shard_map/ppermute | solution.py:27
  82.8 0.9 copy-start.4
  83.6 10.1 %collective-permute-start.12 = (bf16[256,1024]{1,0:T(8,128)(2,1)S(1)}, bf16[256,1024]{1,0:T(8,128)(2,1)}, u32[]{:S(2)}, u32[]{:S(2)}) collective-permute-start(bf16[256,1024]{1,0:T(8,128)(2,1)S(1)} %collective-permute-done.8.refs_6_.refs_2_), channel_id=1, source_target_pairs={{0,1},{1,0},{2,3},{3,2},{4,5},{5,4},{6,7},{7,6},{8,9},{9,8},{10,11... | collective-permute-start | bytes 1572872 | tf_op jit(solution)/shard_map/ppermute | solution.py:27
  84.1 0.8 copy-start.1
  86.7 0.8 copy-start.7
  87.5 6.2 %collective-permute-start.13 = (bf16[256,1024]{1,0:T(8,128)(2,1)}, bf16[256,1024]{1,0:T(8,128)(2,1)}, u32[]{:S(2)}, u32[]{:S(2)}) collective-permute-start(bf16[256,1024]{1,0:T(8,128)(2,1)} %collective-permute-done.9.refs_7_.refs_3_), channel_id=1, source_target_pairs={{0,1},{1,0},{2,3},{3,2},{4,5},{5,4},{6,7},{7,6},{8,9},{9,8},{10,11... | collective-permute-start | bytes 1572872 | tf_op jit(solution)/shard_map/ppermute | solution.py:27
  93.7 1.0 copy-start.2
  94.7 1.0 copy-start.5
  95.8 1.0 copy-start.8
  108.6 9.5 %all-to-all-start.1 = ((f32[8,8,128]{2,1,0:T(8,128)}), f32[8,8,128]{2,1,0:T(8,128)S(1)}, u32[]{:S(2)}, u32[]{:S(2)}) async-start(f32[8,8,128]{2,1,0:T(8,128)} %broadcast_in_dim.11), calls=%async_computation.1 | async-start | bytes 65536 | tf_op jit(solution)/shard_map/all_to_all | solution.py:31
  118.8 13.5 %all-to-all-start.2 = ((f32[16,24,128]{2,1,0:T(8,128)}), f32[16,24,128]{2,1,0:T(8,128)S(1)}, u32[]{:S(2)}, u32[]{:S(2)}) async-start(f32[16,24,128]{2,1,0:T(8,128)} %broadcast_in_dim.12), calls=%async_computation.2 | async-start | bytes 393216 | tf_op jit(solution)/shard_map/all_to_all | solution.py:31
  135.4 16.1 %all-to-all-start.4 = ((f32[8,8,128]{2,1,0:T(8,128)}), f32[8,8,128]{2,1,0:T(8,128)S(1)}, u32[]{:S(2)}, u32[]{:S(2)}) async-start(f32[8,8,128]{2,1,0:T(8,128)} %broadcast_in_dim_broadcast_in_dim_broadcast_in_dim.3), calls=%async_computation.4 | async-start | bytes 65536 | tf_op jit(solution)/shard_map/all_to_all | solution.py:31
  138.8 1.0 copy-start.3
  139.8 1.0 copy-start.6
  151.6 37.0 %all-to-all-start.3 = ((bf16[8,128,1024]{2,1,0:T(8,128)(2,1)}), bf16[8,128,1024]{2,1,0:T(8,128)(2,1)}, u32[]{:S(2)}, u32[]{:S(2)}) async-start(bf16[8,128,1024]{2,1,0:T(8,128)(2,1)} %bitcast.9), calls=%async_computation.3 | async-start | bytes 4194304 | tf_op jit(solution)/shard_map/all_to_all | solution.py:35
  157.3 33.3 %copy-start.11 = (f32[128,1024]{1,0:T(8,128)S(1)}, f32[128,1024]{1,0:T(8,128)}, u32[]{:S(2)}) copy-start(f32[128,1024]{1,0:T(8,128)} %copy-done.10) | copy-start | bytes 1572868
  191.0 8.7 %collective-permute-start.14 = (bf16[128,1024]{1,0:T(8,128)(2,1)S(1)}, bf16[128,1024]{1,0:T(8,128)(2,1)S(1)}, u32[]{:S(2)}, u32[]{:S(2)}) collective-permute-start(bf16[128,1024]{1,0:T(8,128)(2,1)S(1)} %multiply_convert_fusion), channel_id=1, source_target_pairs={{0,2},{2,0},{1,3},{3,1},{4,6},{6,4},{5,7},{7,5},{8,10},{10,8},{9,1... | collective-permute-start | bytes 786440 | tf_op jit(solution)/shard_map/ppermute | solution.py:40
  200.9 12.0 %collective-permute-start.15 = (bf16[256,1024]{1,0:T(8,128)(2,1)}, bf16[256,1024]{1,0:T(8,128)(2,1)S(1)}, u32[]{:S(2)}, u32[]{:S(2)}) collective-permute-start(bf16[256,1024]{1,0:T(8,128)(2,1)} %get-tuple-element.17), channel_id=1, source_target_pairs={{0,12},{4,0},{8,4},{12,8},{1,13},{5,1},{9,5},{13,9},{2,14},{6,2},{... | collective-permute-start | bytes 1572872 | tf_op jit(solution)/shard_map/ppermute | solution.py:43
  201.8 14.7 %collective-permute-start.16 = (bf16[256,1024]{1,0:T(8,128)(2,1)}, bf16[256,1024]{1,0:T(8,128)(2,1)}, u32[]{:S(2)}, u32[]{:S(2)}) collective-permute-start(bf16[256,1024]{1,0:T(8,128)(2,1)} %get-tuple-element.17), channel_id=1, source_target_pairs={{0,4},{4,8},{8,12},{12,0},{1,5},{5,9},{9,13},{13,1},{2,6},{6,10},{... | collective-permute-start | bytes 1572872 | tf_op jit(solution)/shard_map/ppermute | solution.py:44
  212.9 0.8 copy-start.13
  214.4 6.7 %collective-permute-start.17 = (bf16[128,1024]{1,0:T(8,128)(2,1)}, bf16[128,1024]{1,0:T(8,128)(2,1)}, u32[]{:S(2)}, u32[]{:S(2)}) collective-permute-start(bf16[128,1024]{1,0:T(8,128)(2,1)} %slice.30), channel_id=1, source_target_pairs={{0,12},{4,0},{8,4},{12,8},{1,13},{5,1},{9,5},{13,9},{2,14},{6,2},{... | collective-permute-start | bytes 786440 | tf_op jit(solution)/shard_map/ppermute | solution.py:45
  216.5 8.7 %copy-start.18 = (bf16[1024,320]{0,1:T(8,128)(2,1)S(1)}, bf16[1024,320]{0,1:T(8,128)(2,1)}, u32[]{:S(2)}) copy-start(bf16[1024,320]{0,1:T(8,128)(2,1)} %copy-done.17) | copy-start | bytes 1966084
  217.6 7.7 %collective-permute-start.18 = (bf16[128,1024]{1,0:T(8,128)(2,1)S(1)}, bf16[128,1024]{1,0:T(8,128)(2,1)S(1)}, u32[]{:S(2)}, u32[]{:S(2)}) collective-permute-start(bf16[128,1024]{1,0:T(8,128)(2,1)S(1)} %slice.31), channel_id=1, source_target_pairs={{0,4},{4,8},{8,12},{12,0},{1,5},{5,9},{9,13},{13,1},{2,6},{6,10},{... | collective-permute-start | bytes 786440 | tf_op jit(solution)/shard_map/ppermute | solution.py:46
  225.2 3.3 %copy-start.12 = (bf16[1024,1024]{1,0:T(8,128)(2,1)}, bf16[1024,1024]{1,0:T(8,128)(2,1)S(1)}, u32[]{:S(2)}) copy-start(bf16[1024,1024]{1,0:T(8,128)(2,1)S(1)} %constant_dynamic-update-slice_fusion) | copy-start | bytes 6291460
  225.3 1.6 copy-start.16
  226.1 2.4 collective-permute-start.20
  228.5 22.3 %collective-permute-start.19 = (bf16[320,1024]{1,0:T(8,128)(2,1)}, bf16[320,1024]{1,0:T(8,128)(2,1)}, u32[]{:S(2)}, u32[]{:S(2)}) collective-permute-start(bf16[320,1024]{1,0:T(8,128)(2,1)} %fusion.3), channel_id=1, source_target_pairs={{0,1},{1,0},{2,3},{3,2},{4,5},{5,4},{6,7},{7,6},{8,9},{9,8},{10,11... | collective-permute-start | bytes 1966088 | tf_op jit(solution)/shard_map/ppermute | solution.py:27
  230.4 20.4 %copy-start.14 = (bf16[320,1024]{1,0:T(8,128)(2,1)S(1)}, bf16[320,1024]{1,0:T(8,128)(2,1)}, u32[]{:S(2)}) copy-start(bf16[320,1024]{1,0:T(8,128)(2,1)} %param.4) | copy-start | bytes 1966084
  230.4 15.9 %all-to-all-start.5 = ((bf16[8,320,128]{2,1,0:T(8,128)(2,1)}), bf16[8,320,128]{2,1,0:T(8,128)(2,1)S(1)}, u32[]{:S(2)}, u32[]{:S(2)}) async-start(bf16[8,320,128]{2,1,0:T(8,128)(2,1)} %bitcast.42), calls=%async_computation.5 | async-start | bytes 1310720 | tf_op jit(solution)/shard_map/all_to_all | solution.py:35
  247.3 14.5 %all-to-all-start.6 = ((bf16[8,320,128]{2,1,0:T(8,128)(2,1)}), bf16[8,320,128]{2,1,0:T(8,128)(2,1)S(1)}, u32[]{:S(2)}, u32[]{:S(2)}) async-start(bf16[8,320,128]{2,1,0:T(8,128)(2,1)} %broadcast_in_dim.14), calls=%async_computation.6 | async-start | bytes 1310720 | tf_op jit(solution)/shard_map/all_to_all | solution.py:31

commit v4 on v3

v4 whole, which is shorter than its diff:
```python
import jax
import jax.numpy as jnp
from jax import lax
from jax.experimental import pallas as pl
from jax.experimental.pallas import tpu as pltpu
from jax.sharding import Mesh
from jax.sharding import PartitionSpec as P

F32 = jnp.float32
BF16 = jnp.bfloat16
I32 = jnp.int32
SWAP = [(0, 1), (1, 0)]
RING = {s: [(i, (i + s) % 4) for i in range(4)] for s in (1, 2, 3)}
ROWS = 128
PAIR = 256
HALF = 1024
GROUP = 2048
TOTAL = 16384
WIDTH = 1024
VMEM_LIMIT = 20 * 1024 * 1024
YZ, XZ, CUTS = ("y", "zh"), ("x", "zl"), ("y", "zh", "c")
OFFSET = (0, 1, 3, 2)
EXP2_SCALE = 28.853900817779268


def core_swap(value):
    return lax.ppermute(value, "c", SWAP)


def spread(value, axes, count):
    return lax.all_to_all(jnp.broadcast_to(value[None], (count,) + value.shape), axes, 0, 0)


def sum_exchange(parts, axes):
    return jnp.sum(lax.all_to_all(parts, axes, 0, 0).astype(F32), axis=0)


def gather_ring(own, long_axis, short_axis):
    rows = own.shape[0]
    pair = jnp.concatenate([own, lax.ppermute(own, short_axis, SWAP)], 0)
    after = lax.ppermute(pair, long_axis, RING[3])
    before = lax.ppermute(pair, long_axis, RING[1])
    far_top = lax.ppermute(after[:rows], long_axis, RING[3])
    far_low = lax.ppermute(before[rows:], long_axis, RING[1])
    return [pair, after, before, far_top, far_low]


def chunk_of(start, p, which, own_low):
    return lax.rem(start + OFFSET[p], 4) * 2 + (own_low if which == 0 else 1 - own_low)


def key_column(place, p):
    inner = place[4] * HALF + (place[2] * 2 + place[3]) * ROWS
    near, far = (chunk_of(place[0], p, which, place[1]) * GROUP + inner for which in (0, 1))
    at = lax.broadcasted_iota(I32, (PAIR, 1), 0)
    return at % ROWS + jnp.where(at < ROWS, near, far)


def query_core(place, n):
    return place[4] if n < 4 else 1 - place[4]


def query_chunks(place, n):
    return [
        query_core(place, n) * 8 + chunk_of(place[2], n % 4, which, place[3]) for which in (0, 1)
    ]


def score_kernel(place, *refs):
    key_refs, query_refs = refs[:5], refs[5:15]
    mates, w_ref, row_ref, col_ref, keys, queries, lanes, sums, key_sem, query_sem = refs[15:]
    step = pl.program_id(0)

    def key_copy(p):
        rows = PAIR if p < 3 else ROWS
        at = p * PAIR if p < 4 else 3 * PAIR + ROWS
        return pltpu.make_async_copy(key_refs[p], keys.at[pl.ds(at, rows), :], key_sem.at[p])

    def query_copies(n):
        first = n // 4 * 5 + n % 4
        if n % 4 < 3:
            return [pltpu.make_async_copy(query_refs[first], queries.at[n], query_sem.at[first])]
        return [
            pltpu.make_async_copy(
                query_refs[first + i],
                queries.at[n, pl.ds(i * ROWS, ROWS), :],
                query_sem.at[first + i],
            )
            for i in (0, 1)
        ]

    @pl.when(step == 0)
    def _():
        for copy in query_copies(0):
            copy.start()
        for p in range(5):
            key_copy(p).start()
        for n in range(1, 8):
            for copy in query_copies(n):
                copy.start()
        lanes[...] = jnp.zeros_like(lanes)
        sums[...] = jnp.zeros_like(sums)
        for p in range(5):
            key_copy(p).wait()

    def run(n, masked):
        for copy in query_copies(n):
            copy.wait()
        near, far = query_chunks(place, n)
        mate = jnp.concatenate([mates[near], mates[far]], axis=1)
        col = jnp.zeros((8, PAIR), F32)
        pos = jnp.zeros((8, PAIR), F32)
        for p in range(4):
            at = pl.ds(p * PAIR, PAIR)
            scores = lax.dot_general(
                keys[at, :], queries[n], (((1,), (1,)), ((), ())), preferred_element_type=F32
            )
            kid = key_column(place, p)
            weights = jnp.exp2(scores * EXP2_SCALE)
            if masked and p == 0:
                group = (place[0] * 2 + place[1]) * GROUP
                lane = lax.broadcasted_iota(I32, (1, PAIR), 1)
                qid = group + lane % ROWS + jnp.where(lane < ROWS, near, far) * ROWS
                weights = jnp.where(kid != qid, weights, 0.0)
            w_ref[at, :] = weights
            lanes[at, :] += weights[:, :ROWS] + weights[:, ROWS:]
            hits = jnp.where(kid == mate, scores, 0.0)
            col = col + jnp.sum(weights.reshape(PAIR // 8, 8, PAIR), axis=0)
            pos = pos + jnp.sum(hits.reshape(PAIR // 8, 8, PAIR), axis=0)
        col = jnp.sum(col, axis=0, keepdims=True)
        sums[pl.ds(near, 1), :] = col[:, :ROWS]
        sums[pl.ds(far, 1), :] = col[:, ROWS:]
        sums[16:24, :] += pos[:, :ROWS] + pos[:, ROWS:]

    for n in range(8):

        @pl.when(step == n)
        def _(n=n):
            run(n, n == 0)

    @pl.when(step == 7)
    def _():
        for device in range(16):
            col_ref[device] = sums[...]
        for p in range(4):
            for which in (0, 1):
                at = pl.ds(p * PAIR + which * ROWS, ROWS)
                row_ref[pl.ds(chunk_of(place[0], p, which, place[1]), 1), :] = jnp.sum(
                    lanes[at, :].T, axis=0, keepdims=True
                )


def grad_kernel(place, w_ref, r0, r1, r2, r3, cols_ref, mates, *refs):
    query_refs, (out_ref, queries, query_sem, rk_ref, rq_ref) = refs[:10], refs[10:]
    step = pl.program_id(0)

    def query_copy(i):
        half, n = i // 5, i % 5
        rows = PAIR if n < 3 else ROWS
        at = half * HALF + (n * PAIR if n < 4 else 3 * PAIR + ROWS)
        return pltpu.make_async_copy(
            query_refs[i], queries.at[pl.ds(at, rows), :], query_sem.at[i]
        )

    @pl.when(step == 0)
    def _():
        for i in range(10):
            query_copy(i).start()
        den = cols_ref[0, 0:16, :]
        for device in range(1, 16):
            den = den + cols_ref[device, 0:16, :]
        rq_ref[...] = 20.0 / den
        rk_ref[...] = 20.0 / (r0[...] + r1[...] + r2[...] + r3[...])
        for i in range(10):
            query_copy(i).wait()

    def column(chunk):
        return jnp.broadcast_to(rk_ref[pl.ds(chunk, 1), :], (ROWS, ROWS)).T

    def run(p):
        kid = key_column(place, p)
        rk = jnp.concatenate(
            [column(chunk_of(place[0], p, which, place[1])) for which in (0, 1)], axis=0
        )
        parts = []
        for n in range(8):
            for which, chunk in enumerate(query_chunks(place, n)):
                start = n * PAIR + which * ROWS
                grads = w_ref[:, start : start + ROWS] * (rk + rq_ref[pl.ds(chunk, 1), :])
                parts.append(jnp.where(kid == mates[chunk], grads - 40.0, grads).astype(BF16))
        total = jnp.dot(
            jnp.concatenate(parts, axis=1), queries[...], preferred_element_type=F32
        ).astype(BF16)
        out_ref[0, place[1]] = total[:ROWS]
        out_ref[0, 1 - place[1]] = total[ROWS:]

    for p in range(4):

        @pl.when(step == p)
        def _(p=p):
            run(p)


def head_kernel(place, mine, theirs, *refs):
    piece_refs, (mine_ref, theirs_ref, all_ref, copy_sem) = refs[:5], refs[5:]
    copies = []
    for p in range(4):
        for which in (0, 1):
            to = pl.multiple_of(chunk_of(place[2], p, which, place[3]) * ROWS, ROWS)
            source = piece_refs[p if p < 3 else 3 + which]
            start = which * ROWS if p < 3 else 0
            copies.append(
                pltpu.make_async_copy(
                    source.at[pl.ds(start, ROWS), :],
                    all_ref.at[pl.ds(to, ROWS), :],
                    copy_sem.at[2 * p + which],
                )
            )
    for copy in copies:
        copy.start()
    for copy in copies:
        copy.wait()
    for source, to in ((theirs, theirs_ref), (mine, mine_ref)):
        total = jnp.dot(source[...], all_ref[...], preferred_element_type=F32).astype(BF16)
        for j in range(8):
            to[j] = total[:, j * ROWS : (j + 1) * ROWS]


def whole(shape):
    return pl.BlockSpec(shape, lambda t, place: (0,) * len(shape))


def score_call(place, keys, queries, mates):
    return pl.pallas_call(
        score_kernel,
        grid_spec=pltpu.PrefetchScalarGridSpec(
            num_scalar_prefetch=1,
            grid=(8,),
            in_specs=[pl.BlockSpec(memory_space=pl.ANY)] * 15 + [whole((16, 1, ROWS))],
            out_specs=[
                pl.BlockSpec((HALF, PAIR), lambda t, place: (0, t)),
                whole((8, ROWS)),
                whole((16, 24, ROWS)),
            ],
            scratch_shapes=[
                pltpu.VMEM((HALF, WIDTH), BF16),
                pltpu.VMEM((8, PAIR, WIDTH), BF16),
                pltpu.VMEM((HALF, ROWS), F32),
                pltpu.VMEM((24, ROWS), F32),
                pltpu.SemaphoreType.DMA((5,)),
                pltpu.SemaphoreType.DMA((10,)),
            ],
        ),
        out_shape=[
            jax.ShapeDtypeStruct((HALF, GROUP), F32),
            jax.ShapeDtypeStruct((8, ROWS), F32),
            jax.ShapeDtypeStruct((16, 24, ROWS), F32),
        ],
        compiler_params=pltpu.CompilerParams(vmem_limit_bytes=VMEM_LIMIT),
        cost_estimate=pl.CostEstimate(
            flops=2 * HALF * GROUP * WIDTH, bytes_accessed=14 << 20, transcendentals=HALF * GROUP
        ),
        name="scores",
    )(place, *keys, *queries, mates)


def grad_call(place, weights, rows, cols, mates, queries):
    return pl.pallas_call(
        grad_kernel,
        grid_spec=pltpu.PrefetchScalarGridSpec(
            num_scalar_prefetch=1,
            grid=(4,),
            in_specs=[pl.BlockSpec((PAIR, GROUP), lambda t, place: (t, 0))]
            + [whole((8, ROWS))] * 4
            + [whole((16, 24, ROWS)), whole((16, 1, ROWS))]
            + [pl.BlockSpec(memory_space=pl.ANY)] * 10,
            out_specs=pl.BlockSpec(
                (1, 2, ROWS, WIDTH),
                lambda t, place: (
                    lax.rem(place[0] + t + jnp.where(t == 2, 1, 0) - jnp.where(t == 3, 1, 0), 4),
                    0,
                    0,
                    0,
                ),
            ),
            scratch_shapes=[
                pltpu.VMEM((GROUP, WIDTH), BF16),
                pltpu.SemaphoreType.DMA((10,)),
                pltpu.VMEM((8, ROWS), F32),
                pltpu.VMEM((16, ROWS), F32),
            ],
        ),
        out_shape=jax.ShapeDtypeStruct((4, 2, ROWS, WIDTH), BF16),
        compiler_params=pltpu.CompilerParams(vmem_limit_bytes=VMEM_LIMIT),
        cost_estimate=pl.CostEstimate(
            flops=2 * HALF * GROUP * WIDTH, bytes_accessed=14 << 20, transcendentals=0
        ),
        name="grads",
    )(place, weights, *rows, cols, mates, *queries)


def head_call(place, mine, theirs, pieces):
    features = mine.shape[0]
    return pl.pallas_call(
        head_kernel,
        grid_spec=pltpu.PrefetchScalarGridSpec(
            num_scalar_prefetch=1,
            grid=(1,),
            in_specs=[whole((features, HALF))] * 2 + [pl.BlockSpec(memory_space=pl.ANY)] * 5,
            out_specs=[whole((8, features, ROWS))] * 2 + [whole((HALF, WIDTH))],
            scratch_shapes=[pltpu.SemaphoreType.DMA((8,))],
        ),
        out_shape=[jax.ShapeDtypeStruct((8, features, ROWS), BF16)] * 2
        + [jax.ShapeDtypeStruct((HALF, WIDTH), BF16)],
        compiler_params=pltpu.CompilerParams(vmem_limit_bytes=VMEM_LIMIT),
        cost_estimate=pl.CostEstimate(
            flops=4 * HALF * features * WIDTH, bytes_accessed=8 << 20, transcendentals=0
        ),
        name="head_parts",
    )(place, mine, theirs, *pieces)


def shards(summaries, head, partner):
    core = lax.axis_index("c")
    place = jnp.stack([lax.axis_index(a) for a in ("x", "zl", "y", "zh", "c")]).astype(I32)
    mates = partner.reshape(16, 1, ROWS)

    turned = summaries.T
    mine = lax.dynamic_slice_in_dim(turned, core * HALF, HALF, 1)
    theirs = core_swap(lax.dynamic_slice_in_dim(turned, (1 - core) * HALF, HALF, 1))
    other_head = core_swap(head)
    first_dims = (((0,), (0,)), ((), ()))
    z_part = lax.dot_general(
        mine, head, first_dims, preferred_element_type=F32
    ) + lax.dot_general(theirs, other_head, first_dims, preferred_element_type=F32)
    z = sum_exchange(z_part.astype(BF16).reshape(8, ROWS, WIDTH), YZ)
    inv = lax.rsqrt(jnp.sum(z * z, axis=1, keepdims=True) + 1e-06)
    unit = z * inv
    emb = unit.astype(BF16)

    keys = gather_ring(emb, "x", "zl")
    queries = gather_ring(emb, "y", "zh")
    queries = queries + [core_swap(piece) for piece in queries]
    weights, row_part, col_part = score_call(place, keys, queries, mates)

    cols = lax.all_to_all(col_part, CUTS, 0, 0)
    row_part = row_part + lax.ppermute(row_part, "zl", SWAP)
    rows = [row_part] + [lax.ppermute(row_part, "x", RING[s]) for s in (1, 3, 2)]
    grad_part = grad_call(place, weights, rows, cols, mates, queries)
    grad_emb = sum_exchange(grad_part.reshape(8, ROWS, WIDTH), XZ)
    grad_z = (inv * (grad_emb - unit * jnp.sum(unit * grad_emb, axis=1, keepdims=True))).astype(BF16)

    head_mine, head_theirs, grad_half = head_call(place, mine, theirs, gather_ring(grad_z, "y", "zh"))
    head_part = head_mine.astype(F32) + core_swap(head_theirs).astype(F32)

    cols = jnp.sum(cols, axis=0)
    loss = jnp.sum(jnp.log(cols[:16])) - 20.0 * jnp.sum(cols[16:])
    terms = []
    for _ in range(3):
        terms.append(lax.reduce_precision(loss, 8, 7))
        loss = loss - terms[-1]
    rider = jnp.stack(terms + [jnp.zeros((), F32)] * 13).astype(BF16)
    rider = jnp.broadcast_to(rider[None, :, None], (8, 16, ROWS))
    pieces = lax.all_to_all(jnp.concatenate([head_part.astype(BF16), rider], 1), XZ, 0, 0)
    pieces = jnp.sum(pieces.astype(F32), axis=0)
    features = head.shape[0]
    loss = jnp.sum(pieces[features:, 0]) / TOTAL
    head_sum = pieces[:features].astype(BF16)
    grad_head = spread(head_sum, XZ, 8).transpose(1, 0, 2).reshape(features, WIDTH).astype(F32)

    last_dims = (((1,), (1,)), ((), ()))
    out_theirs = lax.dot_general(
        other_head, grad_half, last_dims, preferred_element_type=F32
    ).astype(BF16)
    out_mine = lax.dot_general(head, grad_half, last_dims, preferred_element_type=F32).astype(BF16)
    got = core_swap(out_theirs)
    first = core == 0
    out = jnp.concatenate([jnp.where(first, out_mine, got), jnp.where(first, got, out_mine)], 1)
    return loss, out.T, grad_head


def solution(mesh):
    fine = Mesh(mesh.devices.reshape(4, 2, 4, 2, 2), ("x", "zl", "y", "zh", "c"))
    return jax.shard_map(
        shards,
        mesh=fine,
        in_specs=(P(XZ, CUTS), P(CUTS, None), P(XZ)),
        out_specs=(P(), P(XZ, CUTS), P(CUTS, None)),
        check_vma=False,
    )
```

time: 265 us -> 244 us (0.921)
  waiting for transfers between devices: 119 us -> 74.8 us
  blocking collectives: 36 us -> 63 us
  starting transfers between devices: 44.4 us -> 40.6 us
  matrix products: 9.74 us -> 6.35 us
  between operations: 4.82 us -> 8.2 us
    all_to_all x2, waiting for transfers between devices: 42.3 us -> 10.4 us  [the longest x1 10.4 us: shards(): lax.all_to_all(jnp.concatenate([head_part.astype(BF16), rider], 1), XZ, 0...]
    all_to_all x1 -> x2, blocking collectives: 36 us -> 63 us  [sum_exchange(): return jnp.sum(lax.all_to_all(parts, axes, 0, 0).astype(F32), axis=0)]
    ppermute x9 -> x7, waiting for transfers between devices: 41.2 us -> 24.2 us  [the longest x3 15.5 us: gather_ring(): pair = jnp.concatenate([own, lax.ppermute(own, short_axis, SWAP)], 0)]
    all_to_all x4 -> x1, waiting for transfers between devices: 20.4 us -> 5.85 us  [spread(): lax.all_to_all(jnp.broadcast_to(value[None], (count,) + value.shape), axe...]
    all_to_all x4 -> x1, starting transfers between devices: 15.1 us -> 3.54 us  [spread(): lax.all_to_all(jnp.broadcast_to(value[None], (count,) + value.shape), axe...]
    ppermute x1 -> x3, waiting for transfers between devices: 3.13 us -> 12.8 us  [gather_ring(): far_low = lax.ppermute(before[rows:], long_axis, RING[1])]
    ppermute x1 -> x3, starting transfers between devices: 2.1 us -> 8.76 us  [gather_ring(): far_top = lax.ppermute(after[:rows], long_axis, RING[3])]
    ppermute x1 -> x3, starting transfers between devices: 0.93 us -> 7.33 us  [gather_ring(): after = lax.ppermute(pair, long_axis, RING[3])]
  transfers between devices with their start and end apart: 27 -> 31, of which waited for: 17 -> 18; matrix products, arithmetic and copies ran while one was open for 6% -> 5% of each run, Pallas kernels for 4% -> 0%
where the time goes in v4:
time: 244 us; the launch traced here: 243 us
  waiting for transfers between devices  74.8 us (31%)
  blocking collectives  63 us (26%)
  starting transfers between devices  40.6 us (17%)
  local copies, waits for them, and re-layouts  21.1 us (9%)
  Pallas kernels  21.1 us (9%)
  between operations  8.2 us (3%)
  other arithmetic  7.69 us (3%)
  matrix products  6.35 us (3%)
    all_to_all x2, blocking collectives, sum_exchange(): return jnp.sum(lax.all_to_all(parts, axes, 0, 0).astype(F32), axis=0)  63 us
    ppermute x3, waiting for transfers between devices, gather_ring(): after = lax.ppermute(pair, long_axis, RING[3])  16 us
    unnamed x44, local copies, waits for them, and re-layouts  16 us
    ppermute x3, waiting for transfers between devices, gather_ring(): pair = jnp.concatenate([own, lax.ppermute(own, short_axis, SWAP)], 0)  15.5 us
    ppermute x3, waiting for transfers between devices, gather_ring(): far_low = lax.ppermute(before[rows:], long_axis, RING[1])  12.8 us
    pallas_call x1, Pallas kernels, score_call(): pl.pallas_call(score_kernel, grid_spec=pltpu.PrefetchScalarGridSpec(num_s...  10.7 us
    all_to_all x1, waiting for transfers between devices, shards(): lax.all_to_all(jnp.concatenate([head_part.astype(BF16), rider], 1), XZ, 0...  10.4 us
    ppermute x3, starting transfers between devices, gather_ring(): far_top = lax.ppermute(after[:rows], long_axis, RING[3])  8.76 us
  transfers between devices with their start and end apart: 31, of which 18 were waited for; matrix products, arithmetic and copies ran while one was open for 5% of the time, Pallas kernels for 0%

profile of v4, /device:TPU:0, one launch (start us, length us, event | category | flops | bytes accessed | tf_op | source)
XLA Modules:
  0.0 242.8 jit_solution(3216722803054265442)
XLA Ops:
  0.7 1.5 dynamic-slice_bitcast_fusion
  2.8 1.3 fusion.2
  5.3 1.4 add_convert_fusion
  6.7 36.1 %all_to_all.25 = bf16[8,128,1024]{2,1,0:T(8,128)(2,1)S(1)} all-to-all(bf16[8,128,1024]{2,1,0:T(8,128)(2,1)S(1)} %bitcast.37), channel_id=1, replica_groups=mesh['x'=4,'zl'=2,'y'=4,'zh'=2,'c'=2] {'y','zh'}, dimensions={0} | all-to-all | bytes 4194304 | tf_op jit(solution)/shard_map/all_to_all | solution.py:35
  43.3 1.3 collective-permute-start.7
  44.6 1.0 collective-permute-start.2
  45.6 8.5 %collective-permute-done.7 = bf16[128,1024]{1,0:T(8,128)(2,1)S(1)} collective-permute-done((bf16[128,1024]{1,0:T(8,128)(2,1)S(1)}, bf16[128,1024]{1,0:T(8,128)(2,1)S(1)}, u32[]{:S(2)}, u32[]{:S(2)}) %collective-permute-start.7) | collective-permute-done | bytes 262176 | tf_op jit(solution)/shard_map/ppermute | solution.py:40
  54.2 2.3 collective-permute-done.2
  56.6 2.8 %collective-permute-start.3 = (bf16[256,1024]{1,0:T(8,128)(2,1)S(1)}, bf16[256,1024]{1,0:T(8,128)(2,1)S(1)}, u32[]{:S(2)}, u32[]{:S(2)}) collective-permute-start(bf16[256,1024]{1,0:T(8,128)(2,1)S(1)} %get-tuple-element.20.refs_0_), channel_id=1, source_target_pairs={{0,96},{32,0},{64,32},{96,64},{1,97},{33,1},{65,33},{97,65},{2,98}... | collective-permute-start | bytes 1572872 | tf_op jit(solution)/shard_map/ppermute | solution.py:41
  59.4 1.2 collective-permute-start.8
  61.4 7.4 %collective-permute-done.3.refs_1_ = bf16[256,1024]{1,0:T(8,128)(2,1)S(1)} collective-permute-done((bf16[256,1024]{1,0:T(8,128)(2,1)S(1)}, bf16[256,1024]{1,0:T(8,128)(2,1)S(1)}, u32[]{:S(2)}, u32[]{:S(2)}) %collective-permute-start.3) | collective-permute-done | bytes 524320 | tf_op jit(solution)/shard_map/ppermute | solution.py:41
  68.8 3.8 %collective-permute-start.5 = (bf16[128,1024]{1,0:T(8,128)(2,1)S(1)}, bf16[128,1024]{1,0:T(8,128)(2,1)S(1)}, u32[]{:S(2)}, u32[]{:S(2)}) collective-permute-start(bf16[128,1024]{1,0:T(8,128)(2,1)S(1)} %slice.41), channel_id=1, source_target_pairs={{0,96},{32,0},{64,32},{96,64},{1,97},{33,1},{65,33},{97,65},{2,98}... | collective-permute-start | bytes 786440 | tf_op jit(solution)/shard_map/ppermute | solution.py:43
  72.6 1.2 collective-permute-start.10
  79.1 6.0 %collective-permute-done.11.refs_9_.refs_4_ = bf16[128,1024]{1,0:T(8,128)(2,1)} collective-permute-done((bf16[128,1024]{1,0:T(8,128)(2,1)S(1)}, bf16[128,1024]{1,0:T(8,128)(2,1)}, u32[]{:S(2)}, u32[]{:S(2)}) %collective-permute-start.11) | collective-permute-done | bytes 262176 | tf_op jit(solution)/shard_map/ppermute | solution.py:44
  85.2 2.9 %collective-permute-done.6.refs_4_ = bf16[128,1024]{1,0:T(8,128)(2,1)} collective-permute-done((bf16[128,1024]{1,0:T(8,128)(2,1)}, bf16[128,1024]{1,0:T(8,128)(2,1)}, u32[]{:S(2)}, u32[]{:S(2)}) %collective-permute-start.6) | collective-permute-done | bytes 262176 | tf_op jit(solution)/shard_map/ppermute | solution.py:44
  88.2 1.0 copy-done.1
  89.2 1.0 copy-done.3
  90.2 1.0 copy-done.5
  92.2 10.7 %scores.1 = (f32[1024,2048]{1,0:T(8,128)S(1)}, f32[8,128]{1,0:T(8,128)S(1)}, f32[16,24,128]{2,1,0:T(8,128)}) custom-call(s32[5]{0:T(128)S(1)} %stack.39.place, bf16[256,1024]{1,0:T(8,128)(2,1)S(1)} %get-tuple-element.20.refs_0_, bf16[256,1024]{1,0:T(8,128)(2,1)S(1)} %copy-done.1, bf16[256,1024]{1,0:T(8,128)(2,1)S(1)} %copy-done.3, ...), custom_call_target="tpu_custom_call" | custom-call | flops 4294967296 | bytes 14680064 | tf_op jit(solution)/shard_map/scores/pallas_call | solution.py:234
  103.0 3.3 %copy-done.10 = f32[1024,2048]{1,0:T(8,128)} copy-done((f32[1024,2048]{1,0:T(8,128)}, f32[1024,2048]{1,0:T(8,128)S(1)}, u32[]{:S(2)}) %copy-start.10) | copy-done | bytes 8388632
  106.2 5.0 %all-to-all-start.1 = ((f32[16,24,128]{2,1,0:T(8,128)}), f32[16,24,128]{2,1,0:T(8,128)S(1)}, u32[]{:S(2)}, u32[]{:S(2)}) async-start(f32[16,24,128]{2,1,0:T(8,128)} %get-tuple-element.11), calls=%async_computation.1 | async-start | bytes 393216 | tf_op jit(solution)/shard_map/all_to_all | solution.py:346
  111.4 3.6 %collective-permute-done.17 = f32[8,128]{1,0:T(8,128)S(1)} collective-permute-done((f32[8,128]{1,0:T(8,128)S(1)}, f32[8,128]{1,0:T(8,128)S(1)}, u32[]{:S(2)}, u32[]{:S(2)}) %collective-permute-start.17) | collective-permute-done | bytes 4128 | tf_op jit(solution)/shard_map/ppermute | solution.py:347
  115.0 3.2 %collective-permute-start.19 = (f32[8,128]{1,0:T(8,128)S(1)}, f32[8,128]{1,0:T(8,128)S(1)}, u32[]{:S(2)}, u32[]{:S(2)}) collective-permute-start(f32[8,128]{1,0:T(8,128)S(1)} %add.31.r0), channel_id=1, source_target_pairs={{0,96},{32,0},{64,32},{96,64},{1,97},{33,1},{65,33},{97,65},{2,98}... | collective-permute-start | bytes 12296 | tf_op jit(solution)/shard_map/ppermute | solution.py:348
  118.2 1.6 collective-permute-done.18.r1
  119.8 3.5 %collective-permute-done.20.r3 = f32[8,128]{1,0:T(8,128)S(1)} collective-permute-done((f32[8,128]{1,0:T(8,128)S(1)}, f32[8,128]{1,0:T(8,128)S(1)}, u32[]{:S(2)}, u32[]{:S(2)}) %collective-permute-start.20) | collective-permute-done | bytes 4128 | tf_op jit(solution)/shard_map/ppermute | solution.py:348
  123.3 1.0 copy-done.6
  124.4 3.4 %copy-done.11 = f32[1024,2048]{1,0:T(8,128)S(1)} copy-done((f32[1024,2048]{1,0:T(8,128)S(1)}, f32[1024,2048]{1,0:T(8,128)}, u32[]{:S(2)}) %copy-start.11) | copy-done | bytes 8388632
  127.8 8.0 %grads.1 = bf16[4,2,128,1024]{3,2,1,0:T(8,128)(2,1)S(1)} custom-call(s32[5]{0:T(128)S(1)} %stack.39.place, f32[1024,2048]{1,0:T(8,128)S(1)} %copy-done.11, f32[8,128]{1,0:T(8,128)S(1)} %add.31.r0, f32[8,128]{1,0:T(8,128)S(1)} %collective-permute-done.18.r1, f32[8,128]{1,0:T(8,128)S(1)} %collective-permute-done.19.r2, ...), custom_call_target="tpu_custom_call" | custom-call | flops 4294967296 | bytes 14680064 | tf_op jit(solution)/shard_map/grads/pallas_call | solution.py:268
  135.7 27.0 %all_to_all.26 = bf16[8,128,1024]{2,1,0:T(8,128)(2,1)S(1)} all-to-all(bf16[8,128,1024]{2,1,0:T(8,128)(2,1)S(1)} %bitcast.34), channel_id=1, replica_groups=mesh['x'=4,'zl'=2,'y'=4,'zh'=2,'c'=2] {'x','zl'}, dimensions={0} | all-to-all | bytes 4194304 | tf_op jit(solution)/shard_map/all_to_all | solution.py:35
  164.1 3.3 %collective-permute-start.21 = (bf16[128,1024]{1,0:T(8,128)(2,1)S(1)}, bf16[128,1024]{1,0:T(8,128)(2,1)S(1)}, u32[]{:S(2)}, u32[]{:S(2)}) collective-permute-start(bf16[128,1024]{1,0:T(8,128)(2,1)S(1)} %multiply_convert_fusion), channel_id=1, source_target_pairs={{0,2},{2,0},{1,3},{3,1},{4,6},{6,4},{5,7},{7,5},{8,10},{10,8},{9,1... | collective-permute-start | bytes 786440 | tf_op jit(solution)/shard_map/ppermute | solution.py:40
  167.4 4.7 %collective-permute-done.21 = bf16[128,1024]{1,0:T(8,128)(2,1)S(1)} collective-permute-done((bf16[128,1024]{1,0:T(8,128)(2,1)S(1)}, bf16[128,1024]{1,0:T(8,128)(2,1)S(1)}, u32[]{:S(2)}, u32[]{:S(2)}) %collective-permute-start.21) | collective-permute-done | bytes 262176 | tf_op jit(solution)/shard_map/ppermute | solution.py:40
  172.1 3.3 %collective-permute-start.22 = (bf16[256,1024]{1,0:T(8,128)(2,1)S(1)}, bf16[256,1024]{1,0:T(8,128)(2,1)S(1)}, u32[]{:S(2)}, u32[]{:S(2)}) collective-permute-start(bf16[256,1024]{1,0:T(8,128)(2,1)S(1)} %pad_maximum_fusion.3.refs_0_), channel_id=1, source_target_pairs={{0,12},{4,0},{8,4},{12,8},{1,13},{5,1},{9,5},{13,9},{2,14},{6,2},{... | collective-permute-start | bytes 1572872 | tf_op jit(solution)/shard_map/ppermute | solution.py:41
  175.4 8.6 %collective-permute-done.22.refs_1_ = bf16[256,1024]{1,0:T(8,128)(2,1)S(1)} collective-permute-done((bf16[256,1024]{1,0:T(8,128)(2,1)S(1)}, bf16[256,1024]{1,0:T(8,128)(2,1)S(1)}, u32[]{:S(2)}, u32[]{:S(2)}) %collective-permute-start.22) | collective-permute-done | bytes 524320 | tf_op jit(solution)/shard_map/ppermute | solution.py:41
  184.1 3.8 %collective-permute-start.24 = (bf16[128,1024]{1,0:T(8,128)(2,1)S(1)}, bf16[128,1024]{1,0:T(8,128)(2,1)S(1)}, u32[]{:S(2)}, u32[]{:S(2)}) collective-permute-start(bf16[128,1024]{1,0:T(8,128)(2,1)S(1)} %slice.45), channel_id=1, source_target_pairs={{0,12},{4,0},{8,4},{12,8},{1,13},{5,1},{9,5},{13,9},{2,14},{6,2},{... | collective-permute-start | bytes 786440 | tf_op jit(solution)/shard_map/ppermute | solution.py:43
  188.1 3.7 %collective-permute-done.24.refs_3_ = bf16[128,1024]{1,0:T(8,128)(2,1)S(1)} collective-permute-done((bf16[128,1024]{1,0:T(8,128)(2,1)S(1)}, bf16[128,1024]{1,0:T(8,128)(2,1)S(1)}, u32[]{:S(2)}, u32[]{:S(2)}) %collective-permute-start.24) | collective-permute-done | bytes 262176 | tf_op jit(solution)/shard_map/ppermute | solution.py:43
  191.7 3.9 %collective-permute-done.25.refs_4_ = bf16[128,1024]{1,0:T(8,128)(2,1)S(1)} collective-permute-done((bf16[128,1024]{1,0:T(8,128)(2,1)S(1)}, bf16[128,1024]{1,0:T(8,128)(2,1)S(1)}, u32[]{:S(2)}, u32[]{:S(2)}) %collective-permute-start.25) | collective-permute-done | bytes 262176 | tf_op jit(solution)/shard_map/ppermute | solution.py:44
  195.6 2.3 head_parts.1
  198.0 1.3 copy-done.12
  207.0 1.0 pad_maximum_fusion
  208.1 3.5 %all-to-all-start.3 = ((bf16[8,336,128]{2,1,0:T(8,128)(2,1)}), bf16[8,336,128]{2,1,0:T(8,128)(2,1)S(1)}, u32[]{:S(2)}, u32[]{:S(2)}) async-start(bf16[8,336,128]{2,1,0:T(8,128)(2,1)} %pad_maximum_fusion), calls=%async_computation.3 | async-start | bytes 1376256 | tf_op jit(solution)/shard_map/all_to_all | solution.py:364
  211.6 1.7 fusion.1
  213.9 10.4 %all-to-all-done.3 = bf16[8,336,128]{2,1,0:T(8,128)(2,1)S(1)} async-done(((bf16[8,336,128]{2,1,0:T(8,128)(2,1)}), bf16[8,336,128]{2,1,0:T(8,128)(2,1)S(1)}, u32[]{:S(2)}, u32[]{:S(2)}) %all-to-all-start.3) | async-done | bytes 688160 | tf_op jit(solution)/shard_map/all_to_all | solution.py:364
  226.0 3.5 %all-to-all-start.4 = ((bf16[8,320,128]{2,1,0:T(8,128)(2,1)}), bf16[8,320,128]{2,1,0:T(8,128)(2,1)S(1)}, u32[]{:S(2)}, u32[]{:S(2)}) async-start(bf16[8,320,128]{2,1,0:T(8,128)(2,1)} %broadcast_in_dim.5), calls=%async_computation.4 | async-start | bytes 1310720 | tf_op jit(solution)/shard_map/all_to_all | solution.py:31
  229.5 2.0 broadcast_select_fusion.1
  231.5 1.2 maximum_bitcast_fusion
  232.7 1.3 slice_reduce_fusion
  234.6 5.9 %all-to-all-done.4 = bf16[8,320,128]{2,1,0:T(8,128)(2,1)S(1)} async-done(((bf16[8,320,128]{2,1,0:T(8,128)(2,1)}), bf16[8,320,128]{2,1,0:T(8,128)(2,1)S(1)}, u32[]{:S(2)}, u32[]{:S(2)}) %all-to-all-start.4) | async-done | bytes 655392 | tf_op jit(solution)/shard_map/all_to_all | solution.py:31
  240.5 1.2 copy_bitcast_fusion
  (100 shorter events, 15.8 us)
Async XLA Ops:
  0.6 2.1 copy-start.16
  0.6 1.6 copy-start.17
  2.2 2.2 collective-permute-start
  2.3 3.0 %collective-permute-start.1 = (bf16[320,1024]{1,0:T(8,128)(2,1)S(1)}, bf16[320,1024]{1,0:T(8,128)(2,1)S(1)}, u32[]{:S(2)}, u32[]{:S(2)}) collective-permute-start(bf16[320,1024]{1,0:T(8,128)(2,1)S(1)} %copy-done.17), channel_id=1, source_target_pairs={{0,1},{1,0},{2,3},{3,2},{4,5},{5,4},{6,7},{7,6},{8,9},{9,8},{10,11... | collective-permute-start | bytes 1966088 | tf_op jit(solution)/shard_map/ppermute | solution.py:27
  5.3 1.4 copy-start.19
  43.1 11.1 %copy-start.14 = (f32[128,1024]{1,0:T(8,128)}, f32[128,1024]{1,0:T(8,128)S(1)}, u32[]{:S(2)}) copy-start(f32[128,1024]{1,0:T(8,128)S(1)} %convert_reduce_fusion.1) | copy-start | bytes 1572868
  43.3 44.8 %copy-start.9 = (s32[2048]{0:T(1024)S(1)}, s32[2048]{0:T(1024)}, u32[]{:S(2)}) copy-start(s32[2048]{0:T(1024)} %param.5) | copy-start | bytes 24580
  43.3 10.8 %collective-permute-start.7 = (bf16[128,1024]{1,0:T(8,128)(2,1)S(1)}, bf16[128,1024]{1,0:T(8,128)(2,1)S(1)}, u32[]{:S(2)}, u32[]{:S(2)}) collective-permute-start(bf16[128,1024]{1,0:T(8,128)(2,1)S(1)} %multiply_convert_fusion.1), channel_id=1, source_target_pairs={{0,2},{2,0},{1,3},{3,1},{4,6},{6,4},{5,7},{7,5},{8,10},{10,8},{9,1... | collective-permute-start | bytes 786440 | tf_op jit(solution)/shard_map/ppermute | solution.py:40
  44.6 11.8 %collective-permute-start.2 = (bf16[128,1024]{1,0:T(8,128)(2,1)S(1)}, bf16[128,1024]{1,0:T(8,128)(2,1)S(1)}, u32[]{:S(2)}, u32[]{:S(2)}) collective-permute-start(bf16[128,1024]{1,0:T(8,128)(2,1)S(1)} %multiply_convert_fusion.1), channel_id=1, source_target_pairs={{0,16},{16,0},{1,17},{17,1},{2,18},{18,2},{3,19},{19,3},{4,20},{20... | collective-permute-start | bytes 786440 | tf_op jit(solution)/shard_map/ppermute | solution.py:40
  56.6 12.3 %collective-permute-start.3 = (bf16[256,1024]{1,0:T(8,128)(2,1)S(1)}, bf16[256,1024]{1,0:T(8,128)(2,1)S(1)}, u32[]{:S(2)}, u32[]{:S(2)}) collective-permute-start(bf16[256,1024]{1,0:T(8,128)(2,1)S(1)} %get-tuple-element.20.refs_0_), channel_id=1, source_target_pairs={{0,96},{32,0},{64,32},{96,64},{1,97},{33,1},{65,33},{97,65},{2,98}... | collective-permute-start | bytes 1572872 | tf_op jit(solution)/shard_map/ppermute | solution.py:41
  59.4 13.2 %collective-permute-start.8 = (bf16[256,1024]{1,0:T(8,128)(2,1)S(1)}, bf16[256,1024]{1,0:T(8,128)(2,1)S(1)}, u32[]{:S(2)}, u32[]{:S(2)}) collective-permute-start(bf16[256,1024]{1,0:T(8,128)(2,1)S(1)} %get-tuple-element.19.refs_5_.refs_0_), channel_id=1, source_target_pairs={{0,12},{4,0},{8,4},{12,8},{1,13},{5,1},{9,5},{13,9},{2,14},{6,2},{... | collective-permute-start | bytes 1572872 | tf_op jit(solution)/shard_map/ppermute | solution.py:41
  60.6 13.3 %collective-permute-start.9 = (bf16[256,1024]{1,0:T(8,128)(2,1)S(1)}, bf16[256,1024]{1,0:T(8,128)(2,1)}, u32[]{:S(2)}, u32[]{:S(2)}) collective-permute-start(bf16[256,1024]{1,0:T(8,128)(2,1)S(1)} %get-tuple-element.19.refs_5_.refs_0_), channel_id=1, source_target_pairs={{0,4},{4,8},{8,12},{12,0},{1,5},{5,9},{9,13},{13,1},{2,6},{6,10},{... | collective-permute-start | bytes 1572872 | tf_op jit(solution)/shard_map/ppermute | solution.py:42
  61.4 13.4 %collective-permute-start.4 = (bf16[256,1024]{1,0:T(8,128)(2,1)S(1)}, bf16[256,1024]{1,0:T(8,128)(2,1)S(1)}, u32[]{:S(2)}, u32[]{:S(2)}) collective-permute-start(bf16[256,1024]{1,0:T(8,128)(2,1)S(1)} %get-tuple-element.20.refs_0_), channel_id=1, source_target_pairs={{0,32},{32,64},{64,96},{96,0},{1,33},{33,65},{65,97},{97,1},{2,34}... | collective-permute-start | bytes 1572872 | tf_op jit(solution)/shard_map/ppermute | solution.py:42
  61.4 14.0 %collective-permute-start.12 = (bf16[256,1024]{1,0:T(8,128)(2,1)S(1)}, bf16[256,1024]{1,0:T(8,128)(2,1)S(1)}, u32[]{:S(2)}, u32[]{:S(2)}) collective-permute-start(bf16[256,1024]{1,0:T(8,128)(2,1)S(1)} %get-tuple-element.19.refs_5_.refs_0_), channel_id=1, source_target_pairs={{0,1},{1,0},{2,3},{3,2},{4,5},{5,4},{6,7},{7,6},{8,9},{9,8},{10,11... | collective-permute-start | bytes 1572872 | tf_op jit(solution)/shard_map/ppermute | solution.py:27
  68.8 6.6 %copy-start = (bf16[256,1024]{1,0:T(8,128)(2,1)}, bf16[256,1024]{1,0:T(8,128)(2,1)S(1)}, u32[]{:S(2)}) copy-start(bf16[256,1024]{1,0:T(8,128)(2,1)S(1)} %collective-permute-done.3.refs_1_) | copy-start | bytes 1572868
  68.8 9.1 %collective-permute-start.5 = (bf16[128,1024]{1,0:T(8,128)(2,1)S(1)}, bf16[128,1024]{1,0:T(8,128)(2,1)S(1)}, u32[]{:S(2)}, u32[]{:S(2)}) collective-permute-start(bf16[128,1024]{1,0:T(8,128)(2,1)S(1)} %slice.41), channel_id=1, source_target_pairs={{0,96},{32,0},{64,32},{96,64},{1,97},{33,1},{65,33},{97,65},{2,98}... | collective-permute-start | bytes 786440 | tf_op jit(solution)/shard_map/ppermute | solution.py:43
  72.6 6.4 %collective-permute-start.10 = (bf16[128,1024]{1,0:T(8,128)(2,1)S(1)}, bf16[128,1024]{1,0:T(8,128)(2,1)S(1)}, u32[]{:S(2)}, u32[]{:S(2)}) collective-permute-start(bf16[128,1024]{1,0:T(8,128)(2,1)S(1)} %slice.43), channel_id=1, source_target_pairs={{0,12},{4,0},{8,4},{12,8},{1,13},{5,1},{9,5},{13,9},{2,14},{6,2},{... | collective-permute-start | bytes 786440 | tf_op jit(solution)/shard_map/ppermute | solution.py:43
  73.9 14.2 %collective-permute-start.13 = (bf16[256,1024]{1,0:T(8,128)(2,1)S(1)}, bf16[256,1024]{1,0:T(8,128)(2,1)}, u32[]{:S(2)}, u32[]{:S(2)}) collective-permute-start(bf16[256,1024]{1,0:T(8,128)(2,1)S(1)} %collective-permute-done.8.refs_6_.refs_1_), channel_id=1, source_target_pairs={{0,1},{1,0},{2,3},{3,2},{4,5},{5,4},{6,7},{7,6},{8,9},{9,8},{10,11... | collective-permute-start | bytes 1572872 | tf_op jit(solution)/shard_map/ppermute | solution.py:27
  74.9 13.3 %collective-permute-start.14 = (bf16[256,1024]{1,0:T(8,128)(2,1)}, bf16[256,1024]{1,0:T(8,128)(2,1)}, u32[]{:S(2)}, u32[]{:S(2)}) collective-permute-start(bf16[256,1024]{1,0:T(8,128)(2,1)} %collective-permute-done.9.refs_7_.refs_2_), channel_id=1, source_target_pairs={{0,1},{1,0},{2,3},{3,2},{4,5},{5,4},{6,7},{7,6},{8,9},{9,8},{10,11... | collective-permute-start | bytes 1572872 | tf_op jit(solution)/shard_map/ppermute | solution.py:27
  75.5 1.7 copy-start.4
  75.5 9.6 %collective-permute-start.11 = (bf16[128,1024]{1,0:T(8,128)(2,1)S(1)}, bf16[128,1024]{1,0:T(8,128)(2,1)}, u32[]{:S(2)}, u32[]{:S(2)}) collective-permute-start(bf16[128,1024]{1,0:T(8,128)(2,1)S(1)} %slice.44), channel_id=1, source_target_pairs={{0,4},{4,8},{8,12},{12,0},{1,5},{5,9},{9,13},{13,1},{2,6},{6,10},{... | collective-permute-start | bytes 786440 | tf_op jit(solution)/shard_map/ppermute | solution.py:44
  78.6 9.5 %collective-permute-start.6 = (bf16[128,1024]{1,0:T(8,128)(2,1)}, bf16[128,1024]{1,0:T(8,128)(2,1)}, u32[]{:S(2)}, u32[]{:S(2)}) collective-permute-start(bf16[128,1024]{1,0:T(8,128)(2,1)} %slice.42), channel_id=1, source_target_pairs={{0,32},{32,64},{64,96},{96,0},{1,33},{33,65},{65,97},{97,1},{2,34}... | collective-permute-start | bytes 786440 | tf_op jit(solution)/shard_map/ppermute | solution.py:44
  79.1 9.0 %collective-permute-start.15 = (bf16[128,1024]{1,0:T(8,128)(2,1)S(1)}, bf16[128,1024]{1,0:T(8,128)(2,1)}, u32[]{:S(2)}, u32[]{:S(2)}) collective-permute-start(bf16[128,1024]{1,0:T(8,128)(2,1)S(1)} %collective-permute-done.10.refs_8_.refs_3_), channel_id=1, source_target_pairs={{0,1},{1,0},{2,3},{3,2},{4,5},{5,4},{6,7},{7,6},{8,9},{9,8},{10,11... | collective-permute-start | bytes 786440 | tf_op jit(solution)/shard_map/ppermute | solution.py:27
  85.1 3.0 %collective-permute-start.16 = (bf16[128,1024]{1,0:T(8,128)(2,1)}, bf16[128,1024]{1,0:T(8,128)(2,1)}, u32[]{:S(2)}, u32[]{:S(2)}) collective-permute-start(bf16[128,1024]{1,0:T(8,128)(2,1)} %collective-permute-done.11.refs_9_.refs_4_), channel_id=1, source_target_pairs={{0,1},{1,0},{2,3},{3,2},{4,5},{5,4},{6,7},{7,6},{8,9},{9,8},{10,11... | collective-permute-start | bytes 786440 | tf_op jit(solution)/shard_map/ppermute | solution.py:27
  88.1 1.0 copy-start.1
  89.2 1.0 copy-start.3
  103.0 3.3 %copy-start.10 = (f32[1024,2048]{1,0:T(8,128)}, f32[1024,2048]{1,0:T(8,128)S(1)}, u32[]{:S(2)}) copy-start(f32[1024,2048]{1,0:T(8,128)S(1)} %get-tuple-element.9.w_ref) | copy-start | bytes 25165828
  106.2 17.1 %all-to-all-start.1 = ((f32[16,24,128]{2,1,0:T(8,128)}), f32[16,24,128]{2,1,0:T(8,128)S(1)}, u32[]{:S(2)}, u32[]{:S(2)}) async-start(f32[16,24,128]{2,1,0:T(8,128)} %get-tuple-element.11), calls=%async_computation.1 | async-start | bytes 393216 | tf_op jit(solution)/shard_map/all_to_all | solution.py:346
  111.3 3.7 %collective-permute-start.17 = (f32[8,128]{1,0:T(8,128)S(1)}, f32[8,128]{1,0:T(8,128)S(1)}, u32[]{:S(2)}, u32[]{:S(2)}) collective-permute-start(f32[8,128]{1,0:T(8,128)S(1)} %get-tuple-element.10), channel_id=1, source_target_pairs={{0,16},{16,0},{1,17},{17,1},{2,18},{18,2},{3,19},{19,3},{4,20},{20... | collective-permute-start | bytes 12296 | tf_op jit(solution)/shard_map/ppermute | solution.py:347
  115.0 4.8 %collective-permute-start.18 = (f32[8,128]{1,0:T(8,128)S(1)}, f32[8,128]{1,0:T(8,128)S(1)}, u32[]{:S(2)}, u32[]{:S(2)}) collective-permute-start(f32[8,128]{1,0:T(8,128)S(1)} %add.31.r0), channel_id=1, source_target_pairs={{0,32},{32,64},{64,96},{96,0},{1,33},{33,65},{65,97},{97,1},{2,34}... | collective-permute-start | bytes 12296 | tf_op jit(solution)/shard_map/ppermute | solution.py:348
  115.0 4.8 %collective-permute-start.19 = (f32[8,128]{1,0:T(8,128)S(1)}, f32[8,128]{1,0:T(8,128)S(1)}, u32[]{:S(2)}, u32[]{:S(2)}) collective-permute-start(f32[8,128]{1,0:T(8,128)S(1)} %add.31.r0), channel_id=1, source_target_pairs={{0,96},{32,0},{64,32},{96,64},{1,97},{33,1},{65,33},{97,65},{2,98}... | collective-permute-start | bytes 12296 | tf_op jit(solution)/shard_map/ppermute | solution.py:348
  118.2 5.1 %collective-permute-start.20 = (f32[8,128]{1,0:T(8,128)S(1)}, f32[8,128]{1,0:T(8,128)S(1)}, u32[]{:S(2)}, u32[]{:S(2)}) collective-permute-start(f32[8,128]{1,0:T(8,128)S(1)} %add.31.r0), channel_id=1, source_target_pairs={{0,64},{32,96},{64,0},{96,32},{1,65},{33,97},{65,1},{97,33},{2,66}... | collective-permute-start | bytes 12296 | tf_op jit(solution)/shard_map/ppermute | solution.py:348
  123.3 1.0 copy-start.6
  124.4 3.4 %copy-start.11 = (f32[1024,2048]{1,0:T(8,128)S(1)}, f32[1024,2048]{1,0:T(8,128)}, u32[]{:S(2)}) copy-start(f32[1024,2048]{1,0:T(8,128)} %copy-done.10) | copy-start | bytes 25165828
  162.7 1.0 copy-start.15
  164.1 8.0 %collective-permute-start.21 = (bf16[128,1024]{1,0:T(8,128)(2,1)S(1)}, bf16[128,1024]{1,0:T(8,128)(2,1)S(1)}, u32[]{:S(2)}, u32[]{:S(2)}) collective-permute-start(bf16[128,1024]{1,0:T(8,128)(2,1)S(1)} %multiply_convert_fusion), channel_id=1, source_target_pairs={{0,2},{2,0},{1,3},{3,1},{4,6},{6,4},{5,7},{7,5},{8,10},{10,8},{9,1... | collective-permute-start | bytes 786440 | tf_op jit(solution)/shard_map/ppermute | solution.py:40
  172.1 12.0 %collective-permute-start.22 = (bf16[256,1024]{1,0:T(8,128)(2,1)S(1)}, bf16[256,1024]{1,0:T(8,128)(2,1)S(1)}, u32[]{:S(2)}, u32[]{:S(2)}) collective-permute-start(bf16[256,1024]{1,0:T(8,128)(2,1)S(1)} %pad_maximum_fusion.3.refs_0_), channel_id=1, source_target_pairs={{0,12},{4,0},{8,4},{12,8},{1,13},{5,1},{9,5},{13,9},{2,14},{6,2},{... | collective-permute-start | bytes 1572872 | tf_op jit(solution)/shard_map/ppermute | solution.py:41
  175.4 12.5 %collective-permute-start.23 = (bf16[256,1024]{1,0:T(8,128)(2,1)S(1)}, bf16[256,1024]{1,0:T(8,128)(2,1)S(1)}, u32[]{:S(2)}, u32[]{:S(2)}) collective-permute-start(bf16[256,1024]{1,0:T(8,128)(2,1)S(1)} %pad_maximum_fusion.3.refs_0_), channel_id=1, source_target_pairs={{0,4},{4,8},{8,12},{12,0},{1,5},{5,9},{9,13},{13,1},{2,6},{6,10},{... | collective-permute-start | bytes 1572872 | tf_op jit(solution)/shard_map/ppermute | solution.py:42
  184.1 7.7 %collective-permute-start.24 = (bf16[128,1024]{1,0:T(8,128)(2,1)S(1)}, bf16[128,1024]{1,0:T(8,128)(2,1)S(1)}, u32[]{:S(2)}, u32[]{:S(2)}) collective-permute-start(bf16[128,1024]{1,0:T(8,128)(2,1)S(1)} %slice.45), channel_id=1, source_target_pairs={{0,12},{4,0},{8,4},{12,8},{1,13},{5,1},{9,5},{13,9},{2,14},{6,2},{... | collective-permute-start | bytes 786440 | tf_op jit(solution)/shard_map/ppermute | solution.py:43
  188.0 7.7 %collective-permute-start.25 = (bf16[128,1024]{1,0:T(8,128)(2,1)S(1)}, bf16[128,1024]{1,0:T(8,128)(2,1)S(1)}, u32[]{:S(2)}, u32[]{:S(2)}) collective-permute-start(bf16[128,1024]{1,0:T(8,128)(2,1)S(1)} %slice.46), channel_id=1, source_target_pairs={{0,4},{4,8},{8,12},{12,0},{1,5},{5,9},{9,13},{13,1},{2,6},{6,10},{... | collective-permute-start | bytes 786440 | tf_op jit(solution)/shard_map/ppermute | solution.py:44
  198.0 1.4 copy-start.12
  199.3 7.5 %collective-permute-start.26 = (bf16[8,320,128]{2,1,0:T(8,128)(2,1)S(1)}, bf16[8,320,128]{2,1,0:T(8,128)(2,1)S(1)}, u32[]{:S(2)}, u32[]{:S(2)}) collective-permute-start(bf16[8,320,128]{2,1,0:T(8,128)(2,1)S(1)} %get-tuple-element.13), channel_id=1, source_target_pairs={{0,1},{1,0},{2,3},{3,2},{4,5},{5,4},{6,7},{7,6},{8,9},{9,8},{10,11... | collective-permute-start | bytes 1966088 | tf_op jit(solution)/shard_map/ppermute | solution.py:27
  206.8 4.8 %copy-start.20 = (bf16[320,1024]{1,0:T(8,128)(2,1)S(1)}, bf16[320,1024]{1,0:T(8,128)(2,1)}, u32[]{:S(2)}) copy-start(bf16[320,1024]{1,0:T(8,128)(2,1)} %copy-done.19) | copy-start | bytes 1966084
  207.0 4.6 %copy-start.13 = (bf16[1024,1024]{1,0:T(8,128)(2,1)S(1)}, bf16[1024,1024]{1,0:T(8,128)(2,1)}, u32[]{:S(2)}) copy-start(bf16[1024,1024]{1,0:T(8,128)(2,1)} %copy-done.12) | copy-start | bytes 6291460
  208.1 16.2 %all-to-all-start.3 = ((bf16[8,336,128]{2,1,0:T(8,128)(2,1)}), bf16[8,336,128]{2,1,0:T(8,128)(2,1)S(1)}, u32[]{:S(2)}, u32[]{:S(2)}) async-start(bf16[8,336,128]{2,1,0:T(8,128)(2,1)} %pad_maximum_fusion), calls=%async_computation.3 | async-start | bytes 1376256 | tf_op jit(solution)/shard_map/all_to_all | solution.py:364
  213.4 16.2 %copy-start.18 = (bf16[320,1024]{1,0:T(8,128)(2,1)S(1)}, bf16[320,1024]{1,0:T(8,128)(2,1)}, u32[]{:S(2)}) copy-start(bf16[320,1024]{1,0:T(8,128)(2,1)} %param.4) | copy-start | bytes 1966084
  213.4 16.2 %collective-permute-start.27 = (bf16[320,1024]{1,0:T(8,128)(2,1)}, bf16[320,1024]{1,0:T(8,128)(2,1)}, u32[]{:S(2)}, u32[]{:S(2)}) collective-permute-start(bf16[320,1024]{1,0:T(8,128)(2,1)} %fusion.1), channel_id=1, source_target_pairs={{0,1},{1,0},{2,3},{3,2},{4,5},{5,4},{6,7},{7,6},{8,9},{9,8},{10,11... | collective-permute-start | bytes 1966088 | tf_op jit(solution)/shard_map/ppermute | solution.py:27
  226.0 14.5 %all-to-all-start.4 = ((bf16[8,320,128]{2,1,0:T(8,128)(2,1)}), bf16[8,320,128]{2,1,0:T(8,128)(2,1)S(1)}, u32[]{:S(2)}, u32[]{:S(2)}) async-start(bf16[8,320,128]{2,1,0:T(8,128)(2,1)} %broadcast_in_dim.5), calls=%async_computation.4 | async-start | bytes 1310720 | tf_op jit(solution)/shard_map/all_to_all | solution.py:31
  (5 other events, 4.2 us)

commit v5 on v4

--- a/solution.py
+++ b/solution.py
@@ -17,7 +17,7 @@
 GROUP = 2048
 TOTAL = 16384
 WIDTH = 1024
-VMEM_LIMIT = 20 * 1024 * 1024
+VMEM_LIMIT = 24 * 1024 * 1024
 YZ, XZ, CUTS = ("y", "zh"), ("x", "zl"), ("y", "zh", "c")
 OFFSET = (0, 1, 3, 2)
 EXP2_SCALE = 28.853900817779268
@@ -36,13 +36,14 @@
 
 
 def gather_ring(own, long_axis, short_axis):
-    rows = own.shape[0]
-    pair = jnp.concatenate([own, lax.ppermute(own, short_axis, SWAP)], 0)
-    after = lax.ppermute(pair, long_axis, RING[3])
-    before = lax.ppermute(pair, long_axis, RING[1])
-    far_top = lax.ppermute(after[:rows], long_axis, RING[3])
-    far_low = lax.ppermute(before[rows:], long_axis, RING[1])
-    return [pair, after, before, far_top, far_low]
+    other = lax.ppermute(own, short_axis, SWAP)
+    after_own = lax.ppermute(own, long_axis, RING[3])
+    before_own = lax.ppermute(own, long_axis, RING[1])
+    far_own = lax.ppermute(after_own, long_axis, RING[3])
+    after_other = lax.ppermute(other, long_axis, RING[3])
+    before_other = lax.ppermute(other, long_axis, RING[1])
+    far_other = lax.ppermute(before_other, long_axis, RING[1])
+    return [own, other, after_own, after_other, before_own, before_other, far_own, far_other]
 
 
 def chunk_of(start, p, which, own_low):
@@ -67,45 +68,49 @@
 
 
 def score_kernel(place, *refs):
-    key_refs, query_refs = refs[:5], refs[5:15]
-    mates, w_ref, row_ref, col_ref, keys, queries, lanes, sums, key_sem, query_sem = refs[15:]
+    key_refs, query_refs = refs[:8], refs[8:24]
+    (mates, w_ref, row_ref, col_ref, keys, queries, held, lanes, sums, key_sem, query_sem, out_sem) = refs[24:]
     step = pl.program_id(0)
 
-    def key_copy(p):
-        rows = PAIR if p < 3 else ROWS
-        at = p * PAIR if p < 4 else 3 * PAIR + ROWS
-        return pltpu.make_async_copy(key_refs[p], keys.at[pl.ds(at, rows), :], key_sem.at[p])
+    def key_copy(i):
+        return pltpu.make_async_copy(
+            key_refs[i], keys.at[pl.ds(i * ROWS, ROWS), :], key_sem.at[i]
+        )
 
     def query_copies(n):
-        first = n // 4 * 5 + n % 4
-        if n % 4 < 3:
-            return [pltpu.make_async_copy(query_refs[first], queries.at[n], query_sem.at[first])]
         return [
             pltpu.make_async_copy(
-                query_refs[first + i],
+                query_refs[2 * n + i],
                 queries.at[n, pl.ds(i * ROWS, ROWS), :],
-                query_sem.at[first + i],
+                query_sem.at[2 * n + i],
             )
             for i in (0, 1)
         ]
+
+    def out_copy(n):
+        return pltpu.make_async_copy(
+            held.at[n % 2], w_ref.at[:, pl.ds(n * PAIR, PAIR)], out_sem.at[n % 2]
+        )
 
     @pl.when(step == 0)
     def _():
         for copy in query_copies(0):
             copy.start()
-        for p in range(5):
-            key_copy(p).start()
+        for i in range(8):
+            key_copy(i).start()
         for n in range(1, 8):
             for copy in query_copies(n):
                 copy.start()
         lanes[...] = jnp.zeros_like(lanes)
         sums[...] = jnp.zeros_like(sums)
-        for p in range(5):
-            key_copy(p).wait()
+        for i in range(8):
+            key_copy(i).wait()
 
     def run(n, masked):
         for copy in query_copies(n):
             copy.wait()
+        if n >= 2:
+            out_copy(n - 2).wait()
         near, far = query_chunks(place, n)
         mate = jnp.concatenate([mates[near], mates[far]], axis=1)
         col = jnp.zeros((8, PAIR), F32)
@@ -122,7 +127,7 @@
                 lane = lax.broadcasted_iota(I32, (1, PAIR), 1)
                 qid = group + lane % ROWS + jnp.where(lane < ROWS, near, far) * ROWS
                 weights = jnp.where(kid != qid, weights, 0.0)
-            w_ref[at, :] = weights
+            held[n % 2, at, :] = weights
             lanes[at, :] += weights[:, :ROWS] + weights[:, ROWS:]
             hits = jnp.where(kid == mate, scores, 0.0)
             col = col + jnp.sum(weights.reshape(PAIR // 8, 8, PAIR), axis=0)
@@ -131,6 +136,7 @@
         sums[pl.ds(near, 1), :] = col[:, :ROWS]
         sums[pl.ds(far, 1), :] = col[:, ROWS:]
         sums[16:24, :] += pos[:, :ROWS] + pos[:, ROWS:]
+        out_copy(n).start()
 
     for n in range(8):
 
@@ -148,36 +154,55 @@
                 row_ref[pl.ds(chunk_of(place[0], p, which, place[1]), 1), :] = jnp.sum(
                     lanes[at, :].T, axis=0, keepdims=True
                 )
+        out_copy(6).wait()
+        out_copy(7).wait()
 
 
 def grad_kernel(place, w_ref, r0, r1, r2, r3, cols_ref, mates, *refs):
-    query_refs, (out_ref, queries, query_sem, rk_ref, rq_ref) = refs[:10], refs[10:]
+    query_refs, (out_ref, rider_ref, weights, queries, w_sem, query_sem, rk_ref, rq_ref) = refs[:16], refs[16:]
     step = pl.program_id(0)
 
+    def w_copy(p):
+        return pltpu.make_async_copy(
+            w_ref.at[pl.ds(p * PAIR, PAIR), :], weights.at[p], w_sem.at[p]
+        )
+
     def query_copy(i):
-        half, n = i // 5, i % 5
-        rows = PAIR if n < 3 else ROWS
-        at = half * HALF + (n * PAIR if n < 4 else 3 * PAIR + ROWS)
         return pltpu.make_async_copy(
-            query_refs[i], queries.at[pl.ds(at, rows), :], query_sem.at[i]
+            query_refs[i], queries.at[pl.ds(i * ROWS, ROWS), :], query_sem.at[i]
         )
 
     @pl.when(step == 0)
     def _():
-        for i in range(10):
+        w_copy(0).start()
+        for i in range(16):
             query_copy(i).start()
-        den = cols_ref[0, 0:16, :]
+        for p in range(1, 4):
+            w_copy(p).start()
+        cols = cols_ref[0]
         for device in range(1, 16):
-            den = den + cols_ref[device, 0:16, :]
+            cols = cols + cols_ref[device]
+        den = cols[:16]
         rq_ref[...] = 20.0 / den
         rk_ref[...] = 20.0 / (r0[...] + r1[...] + r2[...] + r3[...])
-        for i in range(10):
+        logs = jnp.sum(jnp.log(den), axis=0, keepdims=True)
+        logs = logs - 20.0 * jnp.sum(cols[16:], axis=0, keepdims=True)
+        loss = jnp.broadcast_to(jnp.sum(logs, axis=1, keepdims=True), (16, ROWS))
+        row = lax.broadcasted_iota(I32, (16, ROWS), 0)
+        rider = jnp.zeros((16, ROWS), F32)
+        for i in range(3):
+            term = loss.astype(BF16).astype(F32)
+            rider = jnp.where(row == i, term, rider)
+            loss = loss - term
+        rider_ref[...] = rider.astype(BF16)
+        for i in range(16):
             query_copy(i).wait()
 
     def column(chunk):
         return jnp.broadcast_to(rk_ref[pl.ds(chunk, 1), :], (ROWS, ROWS)).T
 
     def run(p):
+        w_copy(p).wait()
         kid = key_column(place, p)
         rk = jnp.concatenate(
             [column(chunk_of(place[0], p, which, place[1])) for which in (0, 1)], axis=0
@@ -186,7 +211,7 @@
         for n in range(8):
             for which, chunk in enumerate(query_chunks(place, n)):
                 start = n * PAIR + which * ROWS
-                grads = w_ref[:, start : start + ROWS] * (rk + rq_ref[pl.ds(chunk, 1), :])
+                grads = weights[p, :, start : start + ROWS] * (rk + rq_ref[pl.ds(chunk, 1), :])
                 parts.append(jnp.where(kid == mates[chunk], grads - 40.0, grads).astype(BF16))
         total = jnp.dot(
             jnp.concatenate(parts, axis=1), queries[...], preferred_element_type=F32
@@ -201,29 +226,26 @@
             run(p)
 
 
-def head_kernel(place, mine, theirs, *refs):
-    piece_refs, (mine_ref, theirs_ref, all_ref, copy_sem) = refs[:5], refs[5:]
+def head_kernel(place, mine, theirs, rider, *refs):
+    piece_refs, (mine_ref, theirs_ref, all_ref, copy_sem) = refs[:8], refs[8:]
+    features = mine.shape[0]
     copies = []
-    for p in range(4):
-        for which in (0, 1):
-            to = pl.multiple_of(chunk_of(place[2], p, which, place[3]) * ROWS, ROWS)
-            source = piece_refs[p if p < 3 else 3 + which]
-            start = which * ROWS if p < 3 else 0
-            copies.append(
-                pltpu.make_async_copy(
-                    source.at[pl.ds(start, ROWS), :],
-                    all_ref.at[pl.ds(to, ROWS), :],
-                    copy_sem.at[2 * p + which],
-                )
-            )
+    for i in range(8):
+        to = pl.multiple_of(chunk_of(place[2], i // 2, i % 2, place[3]) * ROWS, ROWS)
+        copies.append(
+            pltpu.make_async_copy(piece_refs[i], all_ref.at[pl.ds(to, ROWS), :], copy_sem.at[i])
+        )
     for copy in copies:
         copy.start()
+    for j in range(8):
+        mine_ref[j, features:] = rider[...]
+        theirs_ref[j, features:] = jnp.zeros_like(rider)
     for copy in copies:
         copy.wait()
     for source, to in ((theirs, theirs_ref), (mine, mine_ref)):
         total = jnp.dot(source[...], all_ref[...], preferred_element_type=F32).astype(BF16)
         for j in range(8):
-            to[j] = total[:, j * ROWS : (j + 1) * ROWS]
+            to[j, :features] = total[:, j * ROWS : (j + 1) * ROWS]
 
 
 def whole(shape):
@@ -236,19 +258,21 @@
         grid_spec=pltpu.PrefetchScalarGridSpec(
             num_scalar_prefetch=1,
             grid=(8,),
-            in_specs=[pl.BlockSpec(memory_space=pl.ANY)] * 15 + [whole((16, 1, ROWS))],
+            in_specs=[pl.BlockSpec(memory_space=pltpu.HBM)] * 24 + [whole((16, 1, ROWS))],
             out_specs=[
-                pl.BlockSpec((HALF, PAIR), lambda t, place: (0, t)),
+                pl.BlockSpec(memory_space=pltpu.HBM),
                 whole((8, ROWS)),
                 whole((16, 24, ROWS)),
             ],
             scratch_shapes=[
                 pltpu.VMEM((HALF, WIDTH), BF16),
                 pltpu.VMEM((8, PAIR, WIDTH), BF16),
+                pltpu.VMEM((2, HALF, PAIR), F32),
                 pltpu.VMEM((HALF, ROWS), F32),
                 pltpu.VMEM((24, ROWS), F32),
-                pltpu.SemaphoreType.DMA((5,)),
-                pltpu.SemaphoreType.DMA((10,)),
+                pltpu.SemaphoreType.DMA((8,)),
+                pltpu.SemaphoreType.DMA((16,)),
+                pltpu.SemaphoreType.DMA((2,)),
             ],
         ),
         out_shape=[
@@ -270,11 +294,11 @@
         grid_spec=pltpu.PrefetchScalarGridSpec(
             num_scalar_prefetch=1,
             grid=(4,),
-            in_specs=[pl.BlockSpec((PAIR, GROUP), lambda t, place: (t, 0))]
+            in_specs=[pl.BlockSpec(memory_space=pltpu.HBM)]
             + [whole((8, ROWS))] * 4
             + [whole((16, 24, ROWS)), whole((16, 1, ROWS))]
-            + [pl.BlockSpec(memory_space=pl.ANY)] * 10,
-            out_specs=pl.BlockSpec(
+            + [pl.BlockSpec(memory_space=pltpu.HBM)] * 16,
+            out_specs=[pl.BlockSpec(
                 (1, 2, ROWS, WIDTH),
                 lambda t, place: (
                     lax.rem(place[0] + t + jnp.where(t == 2, 1, 0) - jnp.where(t == 3, 1, 0), 4),
@@ -282,15 +306,20 @@
                     0,
                     0,
                 ),
-            ),
+            ), whole((16, ROWS))],
             scratch_shapes=[
+                pltpu.VMEM((4, PAIR, GROUP), F32),
                 pltpu.VMEM((GROUP, WIDTH), BF16),
-                pltpu.SemaphoreType.DMA((10,)),
+                pltpu.SemaphoreType.DMA((4,)),
+                pltpu.SemaphoreType.DMA((16,)),
                 pltpu.VMEM((8, ROWS), F32),
                 pltpu.VMEM((16, ROWS), F32),
             ],
         ),
-        out_shape=jax.ShapeDtypeStruct((4, 2, ROWS, WIDTH), BF16),
+        out_shape=[
+            jax.ShapeDtypeStruct((4, 2, ROWS, WIDTH), BF16),
+            jax.ShapeDtypeStruct((16, ROWS), BF16),
+        ],
         compiler_params=pltpu.CompilerParams(vmem_limit_bytes=VMEM_LIMIT),
         cost_estimate=pl.CostEstimate(
             flops=2 * HALF * GROUP * WIDTH, bytes_accessed=14 << 20, transcendentals=0
@@ -299,25 +328,27 @@
     )(place, weights, *rows, cols, mates, *queries)
 
 
-def head_call(place, mine, theirs, pieces):
+def head_call(place, mine, theirs, rider, pieces):
     features = mine.shape[0]
     return pl.pallas_call(
         head_kernel,
         grid_spec=pltpu.PrefetchScalarGridSpec(
             num_scalar_prefetch=1,
             grid=(1,),
-            in_specs=[whole((features, HALF))] * 2 + [pl.BlockSpec(memory_space=pl.ANY)] * 5,
-            out_specs=[whole((8, features, ROWS))] * 2 + [whole((HALF, WIDTH))],
+            in_specs=[whole((features, HALF))] * 2
+            + [whole((16, ROWS))]
+            + [pl.BlockSpec(memory_space=pltpu.HBM)] * 8,
+            out_specs=[whole((8, features + 16, ROWS))] * 2 + [whole((HALF, WIDTH))],
             scratch_shapes=[pltpu.SemaphoreType.DMA((8,))],
         ),
-        out_shape=[jax.ShapeDtypeStruct((8, features, ROWS), BF16)] * 2
+        out_shape=[jax.ShapeDtypeStruct((8, features + 16, ROWS), BF16)] * 2
         + [jax.ShapeDtypeStruct((HALF, WIDTH), BF16)],
         compiler_params=pltpu.CompilerParams(vmem_limit_bytes=VMEM_LIMIT),
         cost_estimate=pl.CostEstimate(
             flops=4 * HALF * features * WIDTH, bytes_accessed=8 << 20, transcendentals=0
         ),
         name="head_parts",
-    )(place, mine, theirs, *pieces)
+    )(place, mine, theirs, rider, *pieces)
 
 
 def shards(summaries, head, partner):
@@ -346,22 +377,16 @@
     cols = lax.all_to_all(col_part, CUTS, 0, 0)
     row_part = row_part + lax.ppermute(row_part, "zl", SWAP)
     rows = [row_part] + [lax.ppermute(row_part, "x", RING[s]) for s in (1, 3, 2)]
-    grad_part = grad_call(place, weights, rows, cols, mates, queries)
+    grad_part, rider = grad_call(place, weights, rows, cols, mates, queries)
     grad_emb = sum_exchange(grad_part.reshape(8, ROWS, WIDTH), XZ)
     grad_z = (inv * (grad_emb - unit * jnp.sum(unit * grad_emb, axis=1, keepdims=True))).astype(BF16)
 
-    head_mine, head_theirs, grad_half = head_call(place, mine, theirs, gather_ring(grad_z, "y", "zh"))
+    head_mine, head_theirs, grad_half = head_call(
+        place, mine, theirs, rider, gather_ring(grad_z, "y", "zh")
+    )
     head_part = head_mine.astype(F32) + core_swap(head_theirs).astype(F32)
 
-    cols = jnp.sum(cols, axis=0)
-    loss = jnp.sum(jnp.log(cols[:16])) - 20.0 * jnp.sum(cols[16:])
-    terms = []
-    for _ in range(3):
-        terms.append(lax.reduce_precision(loss, 8, 7))
-        loss = loss - terms[-1]
-    rider = jnp.stack(terms + [jnp.zeros((), F32)] * 13).astype(BF16)
-    rider = jnp.broadcast_to(rider[None, :, None], (8, 16, ROWS))
-    pieces = lax.all_to_all(jnp.concatenate([head_part.astype(BF16), rider], 1), XZ, 0, 0)
+    pieces = lax.all_to_all(head_part.astype(BF16), XZ, 0, 0)
     pieces = jnp.sum(pieces.astype(F32), axis=0)
     features = head.shape[0]
     loss = jnp.sum(pieces[features:, 0]) / TOTAL

time: 244 us -> 232 us (0.951)
  waiting for transfers between devices: 74.8 us -> 54.5 us
  starting transfers between devices: 40.6 us -> 49.8 us
  between operations: 8.2 us -> 2.71 us
    ppermute x15 -> x21, waiting for transfers between devices: 48.6 us -> 30.5 us  [the longest x3 11.7 us: gather_ring(): far_other = lax.ppermute(before_other, long_axis, RING[1])]
    ppermute x15 -> x21, starting transfers between devices: 23.5 us -> 33.7 us  [the longest x3 8.03 us: gather_ring(): after_own = lax.ppermute(own, long_axis, RING[3])]
    unnamed x44 -> x48, local copies, waits for them, and re-layouts: 16 us -> 20.9 us
  transfers between devices with their start and end apart: 31 -> 40, of which waited for: 18 -> 20; matrix products, arithmetic and copies ran while one was open for 5% -> 5% of each run, Pallas kernels for 0% -> 0%
where the time goes in v5:
time: 232 us; the launch traced here: 231 us
  blocking collectives  64.2 us (28%)
  waiting for transfers between devices  54.5 us (23%)
  starting transfers between devices  49.8 us (21%)
  local copies, waits for them, and re-layouts  23.4 us (10%)
  Pallas kernels  21.6 us (9%)
  matrix products  8.5 us (4%)
  other arithmetic  6.12 us (3%)
  between operations  2.71 us (1%)
    all_to_all x2, blocking collectives, sum_exchange(): return jnp.sum(lax.all_to_all(parts, axes, 0, 0).astype(F32), axis=0)  64.2 us
    unnamed x48, local copies, waits for them, and re-layouts  20.9 us
    ppermute x3, waiting for transfers between devices, gather_ring(): far_other = lax.ppermute(before_other, long_axis, RING[1])  11.7 us
    pallas_call x1, Pallas kernels, score_call(): pl.pallas_call(score_kernel, grid_spec=pltpu.PrefetchScalarGridSpec(num_s...  11.4 us
    all_to_all x1, waiting for transfers between devices, shards(): pieces = lax.all_to_all(head_part.astype(BF16), XZ, 0, 0)  8.91 us
    ppermute x3, starting transfers between devices, gather_ring(): after_own = lax.ppermute(own, long_axis, RING[3])  8.03 us
    pallas_call x1, Pallas kernels, grad_call(): pl.pallas_call(grad_kernel, grid_spec=pltpu.PrefetchScalarGridSpec(num_sc...  7.9 us
    ppermute x3, starting transfers between devices, gather_ring(): after_other = lax.ppermute(other, long_axis, RING[3])  7.62 us
  transfers between devices with their start and end apart: 40, of which 20 were waited for; matrix products, arithmetic and copies ran while one was open for 5% of the time, Pallas kernels for 0%

profile of v5, /device:TPU:0, one launch (start us, length us, event | category | flops | bytes accessed | tf_op | source)
XLA Modules:
  0.0 230.9 jit_solution(16423550058857046925)
XLA Ops:
  0.8 1.5 dynamic-slice_bitcast_fusion
  2.7 1.3 fusion.2
  4.4 2.4 %add_convert_fusion = bf16[1024,1024]{1,0:T(8,128)(2,1)S(1)} fusion(f32[1024,1024]{1,0:T(8,128)S(1)} %fusion.2, bf16[320,1024]{1,0:T(8,128)(2,1)S(1)} %collective-permute-done.theirs, bf16[320,1024]{1,0:T(8,128)(2,1)} %collective-permute-done.1), kind=kOutput, calls=%fused_computation.2 | convolution fusion | flops 673185792 | bytes 7602176 | tf_op jit(solution)/shard_map/dot_general | solution.py:366
  6.9 36.3 %all_to_all.25 = bf16[8,128,1024]{2,1,0:T(8,128)(2,1)S(1)} all-to-all(bf16[8,128,1024]{2,1,0:T(8,128)(2,1)S(1)} %bitcast.34), channel_id=1, replica_groups=mesh['x'=4,'zl'=2,'y'=4,'zh'=2,'c'=2] {'y','zh'}, dimensions={0} | all-to-all | bytes 4194304 | tf_op jit(solution)/shard_map/all_to_all | solution.py:35
  44.8 3.1 %collective-permute-start.10 = (bf16[128,1024]{1,0:T(8,128)(2,1)S(1)}, bf16[128,1024]{1,0:T(8,128)(2,1)S(1)}, u32[]{:S(2)}, u32[]{:S(2)}) collective-permute-start(bf16[128,1024]{1,0:T(8,128)(2,1)S(1)} %multiply_convert_fusion.1.refs_0_.refs_8_), channel_id=1, source_target_pairs={{0,12},{4,0},{8,4},{12,8},{1,13},{5,1},{9,5},{13,9},{2,14},{6,2},{... | collective-permute-start | bytes 786440 | tf_op jit(solution)/shard_map/ppermute | solution.py:40
  47.8 1.2 collective-permute-start.9
  49.0 1.5 collective-permute-start.5
  50.5 1.7 collective-permute-start.3
  52.3 2.2 collective-permute-done.12.refs_12_.refs_4_
  55.5 1.9 collective-permute-done.9.refs_9_.refs_1_
  59.0 3.3 %collective-permute-done.2.refs_1_ = bf16[128,1024]{1,0:T(8,128)(2,1)S(1)} collective-permute-done((bf16[128,1024]{1,0:T(8,128)(2,1)S(1)}, bf16[128,1024]{1,0:T(8,128)(2,1)S(1)}, u32[]{:S(2)}, u32[]{:S(2)}) %collective-permute-start.2) | collective-permute-done | bytes 262176 | tf_op jit(solution)/shard_map/ppermute | solution.py:39
  62.3 3.2 %collective-permute-start.11 = (bf16[128,1024]{1,0:T(8,128)(2,1)S(1)}, bf16[128,1024]{1,0:T(8,128)(2,1)}, u32[]{:S(2)}, u32[]{:S(2)}) collective-permute-start(bf16[128,1024]{1,0:T(8,128)(2,1)S(1)} %collective-permute-done.9.refs_9_.refs_1_), channel_id=1, source_target_pairs={{0,12},{4,0},{8,4},{12,8},{1,13},{5,1},{9,5},{13,9},{2,14},{6,2},{... | collective-permute-start | bytes 786440 | tf_op jit(solution)/shard_map/ppermute | solution.py:43
  65.6 2.8 %collective-permute-start.7 = (bf16[128,1024]{1,0:T(8,128)(2,1)S(1)}, bf16[128,1024]{1,0:T(8,128)(2,1)S(1)}, u32[]{:S(2)}, u32[]{:S(2)}) collective-permute-start(bf16[128,1024]{1,0:T(8,128)(2,1)S(1)} %collective-permute-done.3.refs_2_), channel_id=1, source_target_pairs={{0,96},{32,0},{64,32},{96,64},{1,97},{33,1},{65,33},{97,65},{2,98}... | collective-permute-start | bytes 786440 | tf_op jit(solution)/shard_map/ppermute | solution.py:42
  69.7 3.2 %collective-permute-start.4 = (bf16[128,1024]{1,0:T(8,128)(2,1)S(1)}, bf16[128,1024]{1,0:T(8,128)(2,1)S(1)}, u32[]{:S(2)}, u32[]{:S(2)}) collective-permute-start(bf16[128,1024]{1,0:T(8,128)(2,1)S(1)} %collective-permute-done.2.refs_1_), channel_id=1, source_target_pairs={{0,96},{32,0},{64,32},{96,64},{1,97},{33,1},{65,33},{97,65},{2,98}... | collective-permute-start | bytes 786440 | tf_op jit(solution)/shard_map/ppermute | solution.py:43
  75.0 1.7 collective-permute-done.6.refs_5_
  78.5 1.2 collective-permute-start.8
  79.8 1.8 collective-permute-done.15.refs_15_.refs_7_
  81.7 6.0 %collective-permute-done.8.refs_7_ = bf16[128,1024]{1,0:T(8,128)(2,1)} collective-permute-done((bf16[128,1024]{1,0:T(8,128)(2,1)}, bf16[128,1024]{1,0:T(8,128)(2,1)}, u32[]{:S(2)}, u32[]{:S(2)}) %collective-permute-start.8) | collective-permute-done | bytes 262176 | tf_op jit(solution)/shard_map/ppermute | solution.py:45
  93.4 11.4 %scores.1 = (f32[1024,2048]{1,0:T(8,128)S(1)}, f32[8,128]{1,0:T(8,128)S(1)}, f32[16,24,128]{2,1,0:T(8,128)}) custom-call(s32[5]{0:T(128)S(1)} %stack.23.place, bf16[128,1024]{1,0:T(8,128)(2,1)S(1)} %multiply_convert_fusion.1.refs_0_.refs_8_, bf16[128,1024]{1,0:T(8,128)(2,1)S(1)} %copy-done.8, bf16[128,1024]{1,0:T(8,128)(2,1)S(1)} %copy-done.6, ...), custom_call_target="tpu_custom_call" | custom-call | flops 4294967296 | bytes 14680064 | tf_op jit(solution)/shard_map/scores/pallas_call | solution.py:256
  104.8 3.3 %copy-done.14 = f32[1024,2048]{1,0:T(8,128)} copy-done((f32[1024,2048]{1,0:T(8,128)}, f32[1024,2048]{1,0:T(8,128)S(1)}, u32[]{:S(2)}) %copy-start.14) | copy-done | bytes 8388632
  108.1 4.6 %all-to-all-start.1 = ((f32[16,24,128]{2,1,0:T(8,128)}), f32[16,24,128]{2,1,0:T(8,128)S(1)}, u32[]{:S(2)}, u32[]{:S(2)}) async-start(f32[16,24,128]{2,1,0:T(8,128)} %get-tuple-element.13), calls=%async_computation.1 | async-start | bytes 393216 | tf_op jit(solution)/shard_map/all_to_all | solution.py:377
  113.3 3.1 %collective-permute-done.24 = f32[8,128]{1,0:T(8,128)S(1)} collective-permute-done((f32[8,128]{1,0:T(8,128)S(1)}, f32[8,128]{1,0:T(8,128)S(1)}, u32[]{:S(2)}, u32[]{:S(2)}) %collective-permute-start.24) | collective-permute-done | bytes 4128 | tf_op jit(solution)/shard_map/ppermute | solution.py:378
  116.8 1.2 collective-permute-start.26
  118.9 2.6 %collective-permute-done.27.r3 = f32[8,128]{1,0:T(8,128)S(1)} collective-permute-done((f32[8,128]{1,0:T(8,128)S(1)}, f32[8,128]{1,0:T(8,128)S(1)}, u32[]{:S(2)}, u32[]{:S(2)}) %collective-permute-start.27) | collective-permute-done | bytes 4128 | tf_op jit(solution)/shard_map/ppermute | solution.py:379
  121.4 1.4 collective-permute-done.25.r1
  123.9 3.4 %copy-done.15 = f32[1024,2048]{1,0:T(8,128)S(1)} copy-done((f32[1024,2048]{1,0:T(8,128)S(1)}, f32[1024,2048]{1,0:T(8,128)}, u32[]{:S(2)}) %copy-start.15) | copy-done | bytes 8388632
  127.2 7.9 %grads.1 = (bf16[4,2,128,1024]{3,2,1,0:T(8,128)(2,1)S(1)}, bf16[16,128]{1,0:T(8,128)(2,1)S(1)}) custom-call(s32[5]{0:T(128)S(1)} %stack.23.place, f32[1024,2048]{1,0:T(8,128)S(1)} %copy-done.15, f32[8,128]{1,0:T(8,128)S(1)} %add.31.r0, f32[8,128]{1,0:T(8,128)S(1)} %collective-permute-done.25.r1, f32[8,128]{1,0:T(8,128)S(1)} %collective-permute-done.26.r2, ...), custom_call_target="tpu_custom_call" | custom-call | flops 4294967296 | bytes 14680064 | tf_op jit(solution)/shard_map/grads/pallas_call | solution.py:292
  135.1 27.9 %all_to_all.26 = bf16[8,128,1024]{2,1,0:T(8,128)(2,1)S(1)} all-to-all(bf16[8,128,1024]{2,1,0:T(8,128)(2,1)S(1)} %bitcast.31), channel_id=1, replica_groups=mesh['x'=4,'zl'=2,'y'=4,'zh'=2,'c'=2] {'x','zl'}, dimensions={0} | all-to-all | bytes 4194304 | tf_op jit(solution)/shard_map/all_to_all | solution.py:35
  164.5 2.9 %collective-permute-start.28 = (bf16[128,1024]{1,0:T(8,128)(2,1)S(1)}, bf16[128,1024]{1,0:T(8,128)(2,1)S(1)}, u32[]{:S(2)}, u32[]{:S(2)}) collective-permute-start(bf16[128,1024]{1,0:T(8,128)(2,1)S(1)} %multiply_convert_fusion.refs_0_), channel_id=1, source_target_pairs={{0,2},{2,0},{1,3},{3,1},{4,6},{6,4},{5,7},{7,5},{8,10},{10,8},{9,1... | collective-permute-start | bytes 786440 | tf_op jit(solution)/shard_map/ppermute | solution.py:39
  167.3 3.2 %collective-permute-start.29 = (bf16[128,1024]{1,0:T(8,128)(2,1)S(1)}, bf16[128,1024]{1,0:T(8,128)(2,1)S(1)}, u32[]{:S(2)}, u32[]{:S(2)}) collective-permute-start(bf16[128,1024]{1,0:T(8,128)(2,1)S(1)} %multiply_convert_fusion.refs_0_), channel_id=1, source_target_pairs={{0,12},{4,0},{8,4},{12,8},{1,13},{5,1},{9,5},{13,9},{2,14},{6,2},{... | collective-permute-start | bytes 786440 | tf_op jit(solution)/shard_map/ppermute | solution.py:40
  170.6 1.9 collective-permute-done.28.refs_1_
  173.6 2.1 collective-permute-start.31
  177.1 3.7 %collective-permute-start.33 = (bf16[128,1024]{1,0:T(8,128)(2,1)S(1)}, bf16[128,1024]{1,0:T(8,128)(2,1)S(1)}, u32[]{:S(2)}, u32[]{:S(2)}) collective-permute-start(bf16[128,1024]{1,0:T(8,128)(2,1)S(1)} %collective-permute-done.29.refs_2_), channel_id=1, source_target_pairs={{0,12},{4,0},{8,4},{12,8},{1,13},{5,1},{9,5},{13,9},{2,14},{6,2},{... | collective-permute-start | bytes 786440 | tf_op jit(solution)/shard_map/ppermute | solution.py:42
  180.8 2.1 collective-permute-done.32.refs_5_
  182.9 3.7 %collective-permute-done.31.refs_4_ = bf16[128,1024]{1,0:T(8,128)(2,1)S(1)} collective-permute-done((bf16[128,1024]{1,0:T(8,128)(2,1)S(1)}, bf16[128,1024]{1,0:T(8,128)(2,1)S(1)}, u32[]{:S(2)}, u32[]{:S(2)}) %collective-permute-start.31) | collective-permute-done | bytes 262176 | tf_op jit(solution)/shard_map/ppermute | solution.py:41
  186.6 3.9 %collective-permute-done.34.refs_7_ = bf16[128,1024]{1,0:T(8,128)(2,1)S(1)} collective-permute-done((bf16[128,1024]{1,0:T(8,128)(2,1)S(1)}, bf16[128,1024]{1,0:T(8,128)(2,1)S(1)}, u32[]{:S(2)}, u32[]{:S(2)}) %collective-permute-start.34) | collective-permute-done | bytes 262176 | tf_op jit(solution)/shard_map/ppermute | solution.py:45
  190.5 2.3 %head_parts.1 = (bf16[8,336,128]{2,1,0:T(8,128)(2,1)S(1)}, bf16[8,336,128]{2,1,0:T(8,128)(2,1)S(1)}, bf16[1024,1024]{1,0:T(8,128)(2,1)S(1)}) custom-call(s32[5]{0:T(128)S(1)} %stack.23.place, bf16[320,1024]{1,0:T(8,128)(2,1)S(1)} %get-tuple-element.22.mine, bf16[320,1024]{1,0:T(8,128)(2,1)S(1)} %collective-permute-done.theirs, ...), custom_call_target="tpu_custom_call" | custom-call | flops 1342177280 | bytes 8388608 | tf_op jit(solution)/shard_map/head_parts/pallas_call | solution.py:333
  192.8 1.3 copy-done.16
  194.2 2.1 collective-permute-done.35
  197.3 3.5 %all-to-all-start.3 = ((bf16[8,336,128]{2,1,0:T(8,128)(2,1)}), bf16[8,336,128]{2,1,0:T(8,128)(2,1)S(1)}, u32[]{:S(2)}, u32[]{:S(2)}) async-start(bf16[8,336,128]{2,1,0:T(8,128)(2,1)} %add_convert_fusion.1), calls=%async_computation.3 | async-start | bytes 1376256 | tf_op jit(solution)/shard_map/all_to_all | solution.py:389
  200.9 2.8 %fusion.1 = bf16[320,1024]{1,0:T(8,128)(2,1)} fusion(bf16[1024,1024]{1,0:T(8,128)(2,1)S(1)} %copy-done.17, bf16[320,1024]{1,0:T(8,128)(2,1)} %collective-permute-done.1), kind=kOutput, calls=%fused_computation.11 | convolution fusion | flops 671416320 | bytes 3407872 | tf_op jit(solution)/shard_map/dot_general | solution.py:397
  203.8 8.9 %all-to-all-done.3 = bf16[8,336,128]{2,1,0:T(8,128)(2,1)S(1)} async-done(((bf16[8,336,128]{2,1,0:T(8,128)(2,1)}), bf16[8,336,128]{2,1,0:T(8,128)(2,1)S(1)}, u32[]{:S(2)}, u32[]{:S(2)}) %all-to-all-start.3) | async-done | bytes 688160 | tf_op jit(solution)/shard_map/all_to_all | solution.py:389
  214.5 3.5 %all-to-all-start.4 = ((bf16[8,320,128]{2,1,0:T(8,128)(2,1)}), bf16[8,320,128]{2,1,0:T(8,128)(2,1)S(1)}, u32[]{:S(2)}, u32[]{:S(2)}) async-start(bf16[8,320,128]{2,1,0:T(8,128)(2,1)} %broadcast_in_dim.2), calls=%async_computation.4 | async-start | bytes 1310720 | tf_op jit(solution)/shard_map/all_to_all | solution.py:31
  218.0 2.0 broadcast_select_fusion.1
  220.0 1.2 maximum_bitcast_fusion
  221.2 1.3 slice_reduce_fusion
  223.1 5.4 %all-to-all-done.4 = bf16[8,320,128]{2,1,0:T(8,128)(2,1)S(1)} async-done(((bf16[8,320,128]{2,1,0:T(8,128)(2,1)}), bf16[8,320,128]{2,1,0:T(8,128)(2,1)S(1)}, u32[]{:S(2)}, u32[]{:S(2)}) %all-to-all-start.4) | async-done | bytes 655392 | tf_op jit(solution)/shard_map/all_to_all | solution.py:31
  228.6 1.2 copy_bitcast_fusion
  (106 shorter events, 26.0 us)
Async XLA Ops:
  0.6 2.1 copy-start.21
  0.6 2.1 copy-start.20
  0.7 3.4 %collective-permute-start.1 = (bf16[320,1024]{1,0:T(8,128)(2,1)}, bf16[320,1024]{1,0:T(8,128)(2,1)}, u32[]{:S(2)}, u32[]{:S(2)}) collective-permute-start(bf16[320,1024]{1,0:T(8,128)(2,1)} %param.4), channel_id=1, source_target_pairs={{0,1},{1,0},{2,3},{3,2},{4,5},{5,4},{6,7},{7,6},{8,9},{9,8},{10,11... | collective-permute-start | bytes 1966088 | tf_op jit(solution)/shard_map/ppermute | solution.py:27
  2.3 2.2 collective-permute-start
  43.2 44.5 %copy-start.13 = (s32[2048]{0:T(1024)S(1)}, s32[2048]{0:T(1024)}, u32[]{:S(2)}) copy-start(s32[2048]{0:T(1024)} %param.5) | copy-start | bytes 24580
  44.4 6.1 %collective-permute-start.16 = (bf16[128,1024]{1,0:T(8,128)(2,1)S(1)}, bf16[128,1024]{1,0:T(8,128)(2,1)S(1)}, u32[]{:S(2)}, u32[]{:S(2)}) collective-permute-start(bf16[128,1024]{1,0:T(8,128)(2,1)S(1)} %multiply_convert_fusion.1.refs_0_.refs_8_), channel_id=1, source_target_pairs={{0,1},{1,0},{2,3},{3,2},{4,5},{5,4},{6,7},{7,6},{8,9},{9,8},{10,11... | collective-permute-start | bytes 786440 | tf_op jit(solution)/shard_map/ppermute | solution.py:27
  44.5 9.9 %collective-permute-start.12 = (bf16[128,1024]{1,0:T(8,128)(2,1)S(1)}, bf16[128,1024]{1,0:T(8,128)(2,1)S(1)}, u32[]{:S(2)}, u32[]{:S(2)}) collective-permute-start(bf16[128,1024]{1,0:T(8,128)(2,1)S(1)} %multiply_convert_fusion.1.refs_0_.refs_8_), channel_id=1, source_target_pairs={{0,4},{4,8},{8,12},{12,0},{1,5},{5,9},{9,13},{13,1},{2,6},{6,10},{... | collective-permute-start | bytes 786440 | tf_op jit(solution)/shard_map/ppermute | solution.py:41
  44.8 10.7 %collective-permute-start.10 = (bf16[128,1024]{1,0:T(8,128)(2,1)S(1)}, bf16[128,1024]{1,0:T(8,128)(2,1)S(1)}, u32[]{:S(2)}, u32[]{:S(2)}) collective-permute-start(bf16[128,1024]{1,0:T(8,128)(2,1)S(1)} %multiply_convert_fusion.1.refs_0_.refs_8_), channel_id=1, source_target_pairs={{0,12},{4,0},{8,4},{12,8},{1,13},{5,1},{9,5},{13,9},{2,14},{6,2},{... | collective-permute-start | bytes 786440 | tf_op jit(solution)/shard_map/ppermute | solution.py:40
  47.8 9.6 %collective-permute-start.9 = (bf16[128,1024]{1,0:T(8,128)(2,1)S(1)}, bf16[128,1024]{1,0:T(8,128)(2,1)S(1)}, u32[]{:S(2)}, u32[]{:S(2)}) collective-permute-start(bf16[128,1024]{1,0:T(8,128)(2,1)S(1)} %multiply_convert_fusion.1.refs_0_.refs_8_), channel_id=1, source_target_pairs={{0,2},{2,0},{1,3},{3,1},{4,6},{6,4},{5,7},{7,5},{8,10},{10,8},{9,1... | collective-permute-start | bytes 786440 | tf_op jit(solution)/shard_map/ppermute | solution.py:39
  49.0 9.0 %collective-permute-start.5 = (bf16[128,1024]{1,0:T(8,128)(2,1)S(1)}, bf16[128,1024]{1,0:T(8,128)(2,1)S(1)}, u32[]{:S(2)}, u32[]{:S(2)}) collective-permute-start(bf16[128,1024]{1,0:T(8,128)(2,1)S(1)} %multiply_convert_fusion.1.refs_0_.refs_8_), channel_id=1, source_target_pairs={{0,32},{32,64},{64,96},{96,0},{1,33},{33,65},{65,97},{97,1},{2,34}... | collective-permute-start | bytes 786440 | tf_op jit(solution)/shard_map/ppermute | solution.py:41
  50.5 8.5 %collective-permute-start.3 = (bf16[128,1024]{1,0:T(8,128)(2,1)S(1)}, bf16[128,1024]{1,0:T(8,128)(2,1)S(1)}, u32[]{:S(2)}, u32[]{:S(2)}) collective-permute-start(bf16[128,1024]{1,0:T(8,128)(2,1)S(1)} %multiply_convert_fusion.1.refs_0_.refs_8_), channel_id=1, source_target_pairs={{0,96},{32,0},{64,32},{96,64},{1,97},{33,1},{65,33},{97,65},{2,98}... | collective-permute-start | bytes 786440 | tf_op jit(solution)/shard_map/ppermute | solution.py:40
  54.4 7.9 %collective-permute-start.2 = (bf16[128,1024]{1,0:T(8,128)(2,1)S(1)}, bf16[128,1024]{1,0:T(8,128)(2,1)S(1)}, u32[]{:S(2)}, u32[]{:S(2)}) collective-permute-start(bf16[128,1024]{1,0:T(8,128)(2,1)S(1)} %multiply_convert_fusion.1.refs_0_.refs_8_), channel_id=1, source_target_pairs={{0,16},{16,0},{1,17},{17,1},{2,18},{18,2},{3,19},{19,3},{4,20},{20... | collective-permute-start | bytes 786440 | tf_op jit(solution)/shard_map/ppermute | solution.py:39
  55.5 6.8 %collective-permute-start.20 = (bf16[128,1024]{1,0:T(8,128)(2,1)S(1)}, bf16[128,1024]{1,0:T(8,128)(2,1)S(1)}, u32[]{:S(2)}, u32[]{:S(2)}) collective-permute-start(bf16[128,1024]{1,0:T(8,128)(2,1)S(1)} %collective-permute-done.12.refs_12_.refs_4_), channel_id=1, source_target_pairs={{0,1},{1,0},{2,3},{3,2},{4,5},{5,4},{6,7},{7,6},{8,9},{9,8},{10,11... | collective-permute-start | bytes 786440 | tf_op jit(solution)/shard_map/ppermute | solution.py:27
  57.4 8.1 %collective-permute-start.18 = (bf16[128,1024]{1,0:T(8,128)(2,1)S(1)}, bf16[128,1024]{1,0:T(8,128)(2,1)S(1)}, u32[]{:S(2)}, u32[]{:S(2)}) collective-permute-start(bf16[128,1024]{1,0:T(8,128)(2,1)S(1)} %collective-permute-done.10.refs_10_.refs_2_), channel_id=1, source_target_pairs={{0,1},{1,0},{2,3},{3,2},{4,5},{5,4},{6,7},{7,6},{8,9},{9,8},{10,11... | collective-permute-start | bytes 786440 | tf_op jit(solution)/shard_map/ppermute | solution.py:27
  58.8 10.3 %collective-permute-start.14 = (bf16[128,1024]{1,0:T(8,128)(2,1)S(1)}, bf16[128,1024]{1,0:T(8,128)(2,1)}, u32[]{:S(2)}, u32[]{:S(2)}) collective-permute-start(bf16[128,1024]{1,0:T(8,128)(2,1)S(1)} %collective-permute-done.10.refs_10_.refs_2_), channel_id=1, source_target_pairs={{0,12},{4,0},{8,4},{12,8},{1,13},{5,1},{9,5},{13,9},{2,14},{6,2},{... | collective-permute-start | bytes 786440 | tf_op jit(solution)/shard_map/ppermute | solution.py:42
  59.0 10.0 %collective-permute-start.17 = (bf16[128,1024]{1,0:T(8,128)(2,1)S(1)}, bf16[128,1024]{1,0:T(8,128)(2,1)S(1)}, u32[]{:S(2)}, u32[]{:S(2)}) collective-permute-start(bf16[128,1024]{1,0:T(8,128)(2,1)S(1)} %collective-permute-done.9.refs_9_.refs_1_), channel_id=1, source_target_pairs={{0,1},{1,0},{2,3},{3,2},{4,5},{5,4},{6,7},{7,6},{8,9},{9,8},{10,11... | collective-permute-start | bytes 786440 | tf_op jit(solution)/shard_map/ppermute | solution.py:27
  62.3 11.4 %collective-permute-start.13 = (bf16[128,1024]{1,0:T(8,128)(2,1)S(1)}, bf16[128,1024]{1,0:T(8,128)(2,1)}, u32[]{:S(2)}, u32[]{:S(2)}) collective-permute-start(bf16[128,1024]{1,0:T(8,128)(2,1)S(1)} %collective-permute-done.9.refs_9_.refs_1_), channel_id=1, source_target_pairs={{0,4},{4,8},{8,12},{12,0},{1,5},{5,9},{9,13},{13,1},{2,6},{6,10},{... | collective-permute-start | bytes 786440 | tf_op jit(solution)/shard_map/ppermute | solution.py:44
  62.3 11.4 %collective-permute-start.11 = (bf16[128,1024]{1,0:T(8,128)(2,1)S(1)}, bf16[128,1024]{1,0:T(8,128)(2,1)}, u32[]{:S(2)}, u32[]{:S(2)}) collective-permute-start(bf16[128,1024]{1,0:T(8,128)(2,1)S(1)} %collective-permute-done.9.refs_9_.refs_1_), channel_id=1, source_target_pairs={{0,12},{4,0},{8,4},{12,8},{1,13},{5,1},{9,5},{13,9},{2,14},{6,2},{... | collective-permute-start | bytes 786440 | tf_op jit(solution)/shard_map/ppermute | solution.py:43
  65.6 8.2 %collective-permute-start.7 = (bf16[128,1024]{1,0:T(8,128)(2,1)S(1)}, bf16[128,1024]{1,0:T(8,128)(2,1)S(1)}, u32[]{:S(2)}, u32[]{:S(2)}) collective-permute-start(bf16[128,1024]{1,0:T(8,128)(2,1)S(1)} %collective-permute-done.3.refs_2_), channel_id=1, source_target_pairs={{0,96},{32,0},{64,32},{96,64},{1,97},{33,1},{65,33},{97,65},{2,98}... | collective-permute-start | bytes 786440 | tf_op jit(solution)/shard_map/ppermute | solution.py:42
  69.0 7.7 %collective-permute-start.6 = (bf16[128,1024]{1,0:T(8,128)(2,1)S(1)}, bf16[128,1024]{1,0:T(8,128)(2,1)}, u32[]{:S(2)}, u32[]{:S(2)}) collective-permute-start(bf16[128,1024]{1,0:T(8,128)(2,1)S(1)} %collective-permute-done.2.refs_1_), channel_id=1, source_target_pairs={{0,32},{32,64},{64,96},{96,0},{1,33},{33,65},{65,97},{97,1},{2,34}... | collective-permute-start | bytes 786440 | tf_op jit(solution)/shard_map/ppermute | solution.py:44
  69.7 8.1 %collective-permute-start.4 = (bf16[128,1024]{1,0:T(8,128)(2,1)S(1)}, bf16[128,1024]{1,0:T(8,128)(2,1)S(1)}, u32[]{:S(2)}, u32[]{:S(2)}) collective-permute-start(bf16[128,1024]{1,0:T(8,128)(2,1)S(1)} %collective-permute-done.2.refs_1_), channel_id=1, source_target_pairs={{0,96},{32,0},{64,32},{96,64},{1,97},{33,1},{65,33},{97,65},{2,98}... | collective-permute-start | bytes 786440 | tf_op jit(solution)/shard_map/ppermute | solution.py:43
  73.7 7.9 %collective-permute-start.15 = (bf16[128,1024]{1,0:T(8,128)(2,1)}, bf16[128,1024]{1,0:T(8,128)(2,1)}, u32[]{:S(2)}, u32[]{:S(2)}) collective-permute-start(bf16[128,1024]{1,0:T(8,128)(2,1)} %collective-permute-done.13.refs_13_.refs_5_), channel_id=1, source_target_pairs={{0,4},{4,8},{8,12},{12,0},{1,5},{5,9},{9,13},{13,1},{2,6},{6,10},{... | collective-permute-start | bytes 786440 | tf_op jit(solution)/shard_map/ppermute | solution.py:45
  73.7 8.0 %collective-permute-start.21 = (bf16[128,1024]{1,0:T(8,128)(2,1)}, bf16[128,1024]{1,0:T(8,128)(2,1)}, u32[]{:S(2)}, u32[]{:S(2)}) collective-permute-start(bf16[128,1024]{1,0:T(8,128)(2,1)} %collective-permute-done.13.refs_13_.refs_5_), channel_id=1, source_target_pairs={{0,1},{1,0},{2,3},{3,2},{4,5},{5,4},{6,7},{7,6},{8,9},{9,8},{10,11... | collective-permute-start | bytes 786440 | tf_op jit(solution)/shard_map/ppermute | solution.py:27
  74.5 7.2 %collective-permute-start.22 = (bf16[128,1024]{1,0:T(8,128)(2,1)}, bf16[128,1024]{1,0:T(8,128)(2,1)}, u32[]{:S(2)}, u32[]{:S(2)}) collective-permute-start(bf16[128,1024]{1,0:T(8,128)(2,1)} %collective-permute-done.14.refs_14_.refs_6_), channel_id=1, source_target_pairs={{0,1},{1,0},{2,3},{3,2},{4,5},{5,4},{6,7},{7,6},{8,9},{9,8},{10,11... | collective-permute-start | bytes 786440 | tf_op jit(solution)/shard_map/ppermute | solution.py:27
  76.7 5.0 %collective-permute-start.19 = (bf16[128,1024]{1,0:T(8,128)(2,1)}, bf16[128,1024]{1,0:T(8,128)(2,1)}, u32[]{:S(2)}, u32[]{:S(2)}) collective-permute-start(bf16[128,1024]{1,0:T(8,128)(2,1)} %collective-permute-done.11.refs_11_.refs_3_), channel_id=1, source_target_pairs={{0,1},{1,0},{2,3},{3,2},{4,5},{5,4},{6,7},{7,6},{8,9},{9,8},{10,11... | collective-permute-start | bytes 786440 | tf_op jit(solution)/shard_map/ppermute | solution.py:27
  78.5 9.1 %collective-permute-start.8 = (bf16[128,1024]{1,0:T(8,128)(2,1)}, bf16[128,1024]{1,0:T(8,128)(2,1)}, u32[]{:S(2)}, u32[]{:S(2)}) collective-permute-start(bf16[128,1024]{1,0:T(8,128)(2,1)} %collective-permute-done.6.refs_5_), channel_id=1, source_target_pairs={{0,32},{32,64},{64,96},{96,0},{1,33},{33,65},{65,97},{97,1},{2,34}... | collective-permute-start | bytes 786440 | tf_op jit(solution)/shard_map/ppermute | solution.py:45
  81.6 6.1 %collective-permute-start.23 = (bf16[128,1024]{1,0:T(8,128)(2,1)}, bf16[128,1024]{1,0:T(8,128)(2,1)}, u32[]{:S(2)}, u32[]{:S(2)}) collective-permute-start(bf16[128,1024]{1,0:T(8,128)(2,1)} %collective-permute-done.15.refs_15_.refs_7_), channel_id=1, source_target_pairs={{0,1},{1,0},{2,3},{3,2},{4,5},{5,4},{6,7},{7,6},{8,9},{9,8},{10,11... | collective-permute-start | bytes 786440 | tf_op jit(solution)/shard_map/ppermute | solution.py:27
  104.8 3.3 %copy-start.14 = (f32[1024,2048]{1,0:T(8,128)}, f32[1024,2048]{1,0:T(8,128)S(1)}, u32[]{:S(2)}) copy-start(f32[1024,2048]{1,0:T(8,128)S(1)} %get-tuple-element.11.w_ref) | copy-start | bytes 25165828
  108.1 14.8 %all-to-all-start.1 = ((f32[16,24,128]{2,1,0:T(8,128)}), f32[16,24,128]{2,1,0:T(8,128)S(1)}, u32[]{:S(2)}, u32[]{:S(2)}) async-start(f32[16,24,128]{2,1,0:T(8,128)} %get-tuple-element.13), calls=%async_computation.1 | async-start | bytes 393216 | tf_op jit(solution)/shard_map/all_to_all | solution.py:377
  112.6 3.7 %collective-permute-start.24 = (f32[8,128]{1,0:T(8,128)S(1)}, f32[8,128]{1,0:T(8,128)S(1)}, u32[]{:S(2)}, u32[]{:S(2)}) collective-permute-start(f32[8,128]{1,0:T(8,128)S(1)} %get-tuple-element.12), channel_id=1, source_target_pairs={{0,16},{16,0},{1,17},{17,1},{2,18},{18,2},{3,19},{19,3},{4,20},{20... | collective-permute-start | bytes 12296 | tf_op jit(solution)/shard_map/ppermute | solution.py:378
  116.3 5.1 %collective-permute-start.27 = (f32[8,128]{1,0:T(8,128)S(1)}, f32[8,128]{1,0:T(8,128)S(1)}, u32[]{:S(2)}, u32[]{:S(2)}) collective-permute-start(f32[8,128]{1,0:T(8,128)S(1)} %add.31.r0), channel_id=1, source_target_pairs={{0,64},{32,96},{64,0},{96,32},{1,65},{33,97},{65,1},{97,33},{2,66}... | collective-permute-start | bytes 12296 | tf_op jit(solution)/shard_map/ppermute | solution.py:379
  116.8 4.6 %collective-permute-start.26 = (f32[8,128]{1,0:T(8,128)S(1)}, f32[8,128]{1,0:T(8,128)S(1)}, u32[]{:S(2)}, u32[]{:S(2)}) collective-permute-start(f32[8,128]{1,0:T(8,128)S(1)} %add.31.r0), channel_id=1, source_target_pairs={{0,96},{32,0},{64,32},{96,64},{1,97},{33,1},{65,33},{97,65},{2,98}... | collective-permute-start | bytes 12296 | tf_op jit(solution)/shard_map/ppermute | solution.py:379
  118.1 4.8 %collective-permute-start.25 = (f32[8,128]{1,0:T(8,128)S(1)}, f32[8,128]{1,0:T(8,128)S(1)}, u32[]{:S(2)}, u32[]{:S(2)}) collective-permute-start(f32[8,128]{1,0:T(8,128)S(1)} %add.31.r0), channel_id=1, source_target_pairs={{0,32},{32,64},{64,96},{96,0},{1,33},{33,65},{65,97},{97,1},{2,34}... | collective-permute-start | bytes 12296 | tf_op jit(solution)/shard_map/ppermute | solution.py:379
  123.9 3.4 %copy-start.15 = (f32[1024,2048]{1,0:T(8,128)S(1)}, f32[1024,2048]{1,0:T(8,128)}, u32[]{:S(2)}) copy-start(f32[1024,2048]{1,0:T(8,128)} %copy-done.14) | copy-start | bytes 25165828
  164.5 8.0 %collective-permute-start.28 = (bf16[128,1024]{1,0:T(8,128)(2,1)S(1)}, bf16[128,1024]{1,0:T(8,128)(2,1)S(1)}, u32[]{:S(2)}, u32[]{:S(2)}) collective-permute-start(bf16[128,1024]{1,0:T(8,128)(2,1)S(1)} %multiply_convert_fusion.refs_0_), channel_id=1, source_target_pairs={{0,2},{2,0},{1,3},{3,1},{4,6},{6,4},{5,7},{7,5},{8,10},{10,8},{9,1... | collective-permute-start | bytes 786440 | tf_op jit(solution)/shard_map/ppermute | solution.py:39
  167.3 9.7 %collective-permute-start.29 = (bf16[128,1024]{1,0:T(8,128)(2,1)S(1)}, bf16[128,1024]{1,0:T(8,128)(2,1)S(1)}, u32[]{:S(2)}, u32[]{:S(2)}) collective-permute-start(bf16[128,1024]{1,0:T(8,128)(2,1)S(1)} %multiply_convert_fusion.refs_0_), channel_id=1, source_target_pairs={{0,12},{4,0},{8,4},{12,8},{1,13},{5,1},{9,5},{13,9},{2,14},{6,2},{... | collective-permute-start | bytes 786440 | tf_op jit(solution)/shard_map/ppermute | solution.py:40
  172.4 10.5 %collective-permute-start.32 = (bf16[128,1024]{1,0:T(8,128)(2,1)S(1)}, bf16[128,1024]{1,0:T(8,128)(2,1)S(1)}, u32[]{:S(2)}, u32[]{:S(2)}) collective-permute-start(bf16[128,1024]{1,0:T(8,128)(2,1)S(1)} %collective-permute-done.28.refs_1_), channel_id=1, source_target_pairs={{0,4},{4,8},{8,12},{12,0},{1,5},{5,9},{9,13},{13,1},{2,6},{6,10},{... | collective-permute-start | bytes 786440 | tf_op jit(solution)/shard_map/ppermute | solution.py:44
  173.6 13.0 %collective-permute-start.31 = (bf16[128,1024]{1,0:T(8,128)(2,1)S(1)}, bf16[128,1024]{1,0:T(8,128)(2,1)S(1)}, u32[]{:S(2)}, u32[]{:S(2)}) collective-permute-start(bf16[128,1024]{1,0:T(8,128)(2,1)S(1)} %multiply_convert_fusion.refs_0_), channel_id=1, source_target_pairs={{0,4},{4,8},{8,12},{12,0},{1,5},{5,9},{9,13},{13,1},{2,6},{6,10},{... | collective-permute-start | bytes 786440 | tf_op jit(solution)/shard_map/ppermute | solution.py:41
  175.7 10.9 %collective-permute-start.30 = (bf16[128,1024]{1,0:T(8,128)(2,1)S(1)}, bf16[128,1024]{1,0:T(8,128)(2,1)S(1)}, u32[]{:S(2)}, u32[]{:S(2)}) collective-permute-start(bf16[128,1024]{1,0:T(8,128)(2,1)S(1)} %collective-permute-done.28.refs_1_), channel_id=1, source_target_pairs={{0,12},{4,0},{8,4},{12,8},{1,13},{5,1},{9,5},{13,9},{2,14},{6,2},{... | collective-permute-start | bytes 786440 | tf_op jit(solution)/shard_map/ppermute | solution.py:43
  177.1 9.5 %collective-permute-start.33 = (bf16[128,1024]{1,0:T(8,128)(2,1)S(1)}, bf16[128,1024]{1,0:T(8,128)(2,1)S(1)}, u32[]{:S(2)}, u32[]{:S(2)}) collective-permute-start(bf16[128,1024]{1,0:T(8,128)(2,1)S(1)} %collective-permute-done.29.refs_2_), channel_id=1, source_target_pairs={{0,12},{4,0},{8,4},{12,8},{1,13},{5,1},{9,5},{13,9},{2,14},{6,2},{... | collective-permute-start | bytes 786440 | tf_op jit(solution)/shard_map/ppermute | solution.py:42
  182.9 7.6 %collective-permute-start.34 = (bf16[128,1024]{1,0:T(8,128)(2,1)S(1)}, bf16[128,1024]{1,0:T(8,128)(2,1)S(1)}, u32[]{:S(2)}, u32[]{:S(2)}) collective-permute-start(bf16[128,1024]{1,0:T(8,128)(2,1)S(1)} %collective-permute-done.32.refs_5_), channel_id=1, source_target_pairs={{0,4},{4,8},{8,12},{12,0},{1,5},{5,9},{9,13},{13,1},{2,6},{6,10},{... | collective-permute-start | bytes 786440 | tf_op jit(solution)/shard_map/ppermute | solution.py:45
  192.8 1.3 copy-start.16
  194.2 6.7 %copy-start.17 = (bf16[1024,1024]{1,0:T(8,128)(2,1)S(1)}, bf16[1024,1024]{1,0:T(8,128)(2,1)}, u32[]{:S(2)}) copy-start(bf16[1024,1024]{1,0:T(8,128)(2,1)} %copy-done.16) | copy-start | bytes 6291460
  194.2 2.1 collective-permute-start.35
  197.3 15.4 %all-to-all-start.3 = ((bf16[8,336,128]{2,1,0:T(8,128)(2,1)}), bf16[8,336,128]{2,1,0:T(8,128)(2,1)S(1)}, u32[]{:S(2)}, u32[]{:S(2)}) async-start(bf16[8,336,128]{2,1,0:T(8,128)(2,1)} %add_convert_fusion.1), calls=%async_computation.3 | async-start | bytes 1376256 | tf_op jit(solution)/shard_map/all_to_all | solution.py:389
  203.7 14.3 %copy-start.22 = (bf16[320,1024]{1,0:T(8,128)(2,1)S(1)}, bf16[320,1024]{1,0:T(8,128)(2,1)}, u32[]{:S(2)}) copy-start(bf16[320,1024]{1,0:T(8,128)(2,1)} %param.4) | copy-start | bytes 1966084
  203.7 14.3 %collective-permute-start.36 = (bf16[320,1024]{1,0:T(8,128)(2,1)}, bf16[320,1024]{1,0:T(8,128)(2,1)}, u32[]{:S(2)}, u32[]{:S(2)}) collective-permute-start(bf16[320,1024]{1,0:T(8,128)(2,1)} %fusion.1), channel_id=1, source_target_pairs={{0,1},{1,0},{2,3},{3,2},{4,5},{5,4},{6,7},{7,6},{8,9},{9,8},{10,11... | collective-permute-start | bytes 1966088 | tf_op jit(solution)/shard_map/ppermute | solution.py:27
  214.5 14.1 %all-to-all-start.4 = ((bf16[8,320,128]{2,1,0:T(8,128)(2,1)}), bf16[8,320,128]{2,1,0:T(8,128)(2,1)S(1)}, u32[]{:S(2)}, u32[]{:S(2)}) async-start(bf16[8,320,128]{2,1,0:T(8,128)(2,1)} %broadcast_in_dim.2), calls=%async_computation.4 | async-start | bytes 1310720 | tf_op jit(solution)/shard_map/all_to_all | solution.py:31
  (16 other events, 13.4 us)

commit v6 on v5

--- a/solution.py
+++ b/solution.py
@@ -17,10 +17,13 @@
 GROUP = 2048
 TOTAL = 16384
 WIDTH = 1024
-VMEM_LIMIT = 24 * 1024 * 1024
 YZ, XZ, CUTS = ("y", "zh"), ("x", "zl"), ("y", "zh", "c")
 OFFSET = (0, 1, 3, 2)
 EXP2_SCALE = 28.853900817779268
+
+
+def in_hbm(value):
+    return pltpu.with_memory_space_constraint(value, pltpu.HBM)
 
 
 def core_swap(value):
@@ -69,7 +72,8 @@
 
 def score_kernel(place, *refs):
     key_refs, query_refs = refs[:8], refs[8:24]
-    (mates, w_ref, row_ref, col_ref, keys, queries, held, lanes, sums, key_sem, query_sem, out_sem) = refs[24:]
+    (mates, w_ref, row_ref, col_ref, all_ref) = refs[24:29]
+    (keys, queries, held, lanes, sums, key_sem, query_sem, out_sem, all_sem) = refs[29:]
     step = pl.program_id(0)
 
     def key_copy(i):
@@ -86,6 +90,11 @@
             )
             for i in (0, 1)
         ]
+
+    def all_copy(n):
+        return pltpu.make_async_copy(
+            queries.at[n], all_ref.at[pl.ds(n * PAIR, PAIR), :], all_sem.at[n]
+        )
 
     def out_copy(n):
         return pltpu.make_async_copy(
@@ -109,6 +118,7 @@
     def run(n, masked):
         for copy in query_copies(n):
             copy.wait()
+        all_copy(n).start()
         if n >= 2:
             out_copy(n - 2).wait()
         near, far = query_chunks(place, n)
@@ -156,10 +166,12 @@
                 )
         out_copy(6).wait()
         out_copy(7).wait()
-
-
-def grad_kernel(place, w_ref, r0, r1, r2, r3, cols_ref, mates, *refs):
-    query_refs, (out_ref, rider_ref, weights, queries, w_sem, query_sem, rk_ref, rq_ref) = refs[:16], refs[16:]
+        for n in range(8):
+            all_copy(n).wait()
+
+
+def grad_kernel(place, w_ref, query_ref, r0, r1, r2, r3, cols_ref, mates, *refs):
+    out_ref, rider_ref, weights, queries, w_sem, query_sem, rk_ref, rq_ref = refs
     step = pl.program_id(0)
 
     def w_copy(p):
@@ -167,16 +179,12 @@
             w_ref.at[pl.ds(p * PAIR, PAIR), :], weights.at[p], w_sem.at[p]
         )
 
-    def query_copy(i):
-        return pltpu.make_async_copy(
-            query_refs[i], queries.at[pl.ds(i * ROWS, ROWS), :], query_sem.at[i]
-        )
+    query_copy = pltpu.make_async_copy(query_ref, queries, query_sem)
 
     @pl.when(step == 0)
     def _():
         w_copy(0).start()
-        for i in range(16):
-            query_copy(i).start()
+        query_copy.start()
         for p in range(1, 4):
             w_copy(p).start()
         cols = cols_ref[0]
@@ -195,8 +203,7 @@
             rider = jnp.where(row == i, term, rider)
             loss = loss - term
         rider_ref[...] = rider.astype(BF16)
-        for i in range(16):
-            query_copy(i).wait()
+        query_copy.wait()
 
     def column(chunk):
         return jnp.broadcast_to(rk_ref[pl.ds(chunk, 1), :], (ROWS, ROWS)).T
@@ -258,11 +265,12 @@
         grid_spec=pltpu.PrefetchScalarGridSpec(
             num_scalar_prefetch=1,
             grid=(8,),
-            in_specs=[pl.BlockSpec(memory_space=pltpu.HBM)] * 24 + [whole((16, 1, ROWS))],
+            in_specs=[pl.BlockSpec(memory_space=pl.ANY)] * 24 + [whole((16, 1, ROWS))],
             out_specs=[
                 pl.BlockSpec(memory_space=pltpu.HBM),
                 whole((8, ROWS)),
                 whole((16, 24, ROWS)),
+                pl.BlockSpec(memory_space=pltpu.HBM),
             ],
             scratch_shapes=[
                 pltpu.VMEM((HALF, WIDTH), BF16),
@@ -273,14 +281,16 @@
                 pltpu.SemaphoreType.DMA((8,)),
                 pltpu.SemaphoreType.DMA((16,)),
                 pltpu.SemaphoreType.DMA((2,)),
+                pltpu.SemaphoreType.DMA((8,)),
             ],
         ),
         out_shape=[
-            jax.ShapeDtypeStruct((HALF, GROUP), F32),
+            pltpu.HBM((HALF, GROUP), F32),
             jax.ShapeDtypeStruct((8, ROWS), F32),
             jax.ShapeDtypeStruct((16, 24, ROWS), F32),
+            pltpu.HBM((GROUP, WIDTH), BF16),
         ],
-        compiler_params=pltpu.CompilerParams(vmem_limit_bytes=VMEM_LIMIT),
+        compiler_params=pltpu.CompilerParams(vmem_limit_bytes=12 << 20),
         cost_estimate=pl.CostEstimate(
             flops=2 * HALF * GROUP * WIDTH, bytes_accessed=14 << 20, transcendentals=HALF * GROUP
         ),
@@ -294,10 +304,9 @@
         grid_spec=pltpu.PrefetchScalarGridSpec(
             num_scalar_prefetch=1,
             grid=(4,),
-            in_specs=[pl.BlockSpec(memory_space=pltpu.HBM)]
+            in_specs=[pl.BlockSpec(memory_space=pltpu.HBM)] * 2
             + [whole((8, ROWS))] * 4
-            + [whole((16, 24, ROWS)), whole((16, 1, ROWS))]
-            + [pl.BlockSpec(memory_space=pltpu.HBM)] * 16,
+            + [whole((16, 24, ROWS)), whole((16, 1, ROWS))],
             out_specs=[pl.BlockSpec(
                 (1, 2, ROWS, WIDTH),
                 lambda t, place: (
@@ -311,7 +320,7 @@
                 pltpu.VMEM((4, PAIR, GROUP), F32),
                 pltpu.VMEM((GROUP, WIDTH), BF16),
                 pltpu.SemaphoreType.DMA((4,)),
-                pltpu.SemaphoreType.DMA((16,)),
+                pltpu.SemaphoreType.DMA,
                 pltpu.VMEM((8, ROWS), F32),
                 pltpu.VMEM((16, ROWS), F32),
             ],
@@ -320,12 +329,12 @@
             jax.ShapeDtypeStruct((4, 2, ROWS, WIDTH), BF16),
             jax.ShapeDtypeStruct((16, ROWS), BF16),
         ],
-        compiler_params=pltpu.CompilerParams(vmem_limit_bytes=VMEM_LIMIT),
+        compiler_params=pltpu.CompilerParams(vmem_limit_bytes=18 << 20),
         cost_estimate=pl.CostEstimate(
             flops=2 * HALF * GROUP * WIDTH, bytes_accessed=14 << 20, transcendentals=0
         ),
         name="grads",
-    )(place, weights, *rows, cols, mates, *queries)
+    )(place, in_hbm(weights), in_hbm(queries), *rows, cols, mates)
 
 
 def head_call(place, mine, theirs, rider, pieces):
@@ -337,13 +346,13 @@
             grid=(1,),
             in_specs=[whole((features, HALF))] * 2
             + [whole((16, ROWS))]
-            + [pl.BlockSpec(memory_space=pltpu.HBM)] * 8,
+            + [pl.BlockSpec(memory_space=pl.ANY)] * 8,
             out_specs=[whole((8, features + 16, ROWS))] * 2 + [whole((HALF, WIDTH))],
             scratch_shapes=[pltpu.SemaphoreType.DMA((8,))],
         ),
         out_shape=[jax.ShapeDtypeStruct((8, features + 16, ROWS), BF16)] * 2
-        + [jax.ShapeDtypeStruct((HALF, WIDTH), BF16)],
-        compiler_params=pltpu.CompilerParams(vmem_limit_bytes=VMEM_LIMIT),
+        + [pltpu.HBM((HALF, WIDTH), BF16)],
+        compiler_params=pltpu.CompilerParams(vmem_limit_bytes=10 << 20),
         cost_estimate=pl.CostEstimate(
             flops=4 * HALF * features * WIDTH, bytes_accessed=8 << 20, transcendentals=0
         ),
@@ -364,7 +373,8 @@
     z_part = lax.dot_general(
         mine, head, first_dims, preferred_element_type=F32
     ) + lax.dot_general(theirs, other_head, first_dims, preferred_element_type=F32)
-    z = sum_exchange(z_part.astype(BF16).reshape(8, ROWS, WIDTH), YZ)
+    z_part, place, mates = lax.optimization_barrier((z_part.astype(BF16), place, mates))
+    z = sum_exchange(z_part.reshape(8, ROWS, WIDTH), YZ)
     inv = lax.rsqrt(jnp.sum(z * z, axis=1, keepdims=True) + 1e-06)
     unit = z * inv
     emb = unit.astype(BF16)
@@ -372,7 +382,7 @@
     keys = gather_ring(emb, "x", "zl")
     queries = gather_ring(emb, "y", "zh")
     queries = queries + [core_swap(piece) for piece in queries]
-    weights, row_part, col_part = score_call(place, keys, queries, mates)
+    weights, row_part, col_part, queries = score_call(place, keys, queries, mates)
 
     cols = lax.all_to_all(col_part, CUTS, 0, 0)
     row_part = row_part + lax.ppermute(row_part, "zl", SWAP)

time: 232 us -> 215 us (0.927)
  local copies, waits for them, and re-layouts: 23.4 us -> 2.5 us
    unnamed x48 -> x6, local copies, waits for them, and re-layouts: 20.9 us -> 0.01 us
    ppermute x3, waiting for transfers between devices: 0.01 us -> 3.31 us  [gather_ring(): far_own = lax.ppermute(after_own, long_axis, RING[3])]
  transfers between devices with their start and end apart: 40 -> 40, of which waited for: 20 -> 20; matrix products, arithmetic and copies ran while one was open for 5% -> 6% of each run, Pallas kernels for 0% -> 0%
where the time goes in v6:
time: 215 us
  blocking collectives  63.9 us (30%)
  waiting for transfers between devices  55.7 us (26%)
  starting transfers between devices  51 us (24%)
  Pallas kernels  23.5 us (11%)
  matrix products  9.93 us (5%)
  other arithmetic  5.42 us (3%)
  between operations  2.65 us (1%)
  local copies, waits for them, and re-layouts  2.5 us (1%)
    all_to_all x2, blocking collectives, sum_exchange(): return jnp.sum(lax.all_to_all(parts, axes, 0, 0).astype(F32), axis=0)  63.9 us
    pallas_call x1, Pallas kernels, score_call(): pl.pallas_call(score_kernel, grid_spec=pltpu.PrefetchScalarGridSpec(num_s...  10.8 us
    ppermute x3, waiting for transfers between devices, gather_ring(): far_other = lax.ppermute(before_other, long_axis, RING[1])  10.7 us
    pallas_call x1, Pallas kernels, grad_call(): pl.pallas_call(grad_kernel, grid_spec=pltpu.PrefetchScalarGridSpec(num_sc...  10.1 us
    all_to_all x1, waiting for transfers between devices, shards(): pieces = lax.all_to_all(head_part.astype(BF16), XZ, 0, 0)  9.03 us
    ppermute x3, starting transfers between devices, gather_ring(): after_other = lax.ppermute(other, long_axis, RING[3])  8.05 us
    ppermute x3, starting transfers between devices, gather_ring(): after_own = lax.ppermute(own, long_axis, RING[3])  7.87 us
    ppermute x3, waiting for transfers between devices, gather_ring(): other = lax.ppermute(own, short_axis, SWAP)  7.41 us
  transfers between devices with their start and end apart: 40, of which 20 were waited for; matrix products, arithmetic and copies ran while one was open for 6% of the time, Pallas kernels for 0%

profile of v6, /device:TPU:0, one launch (start us, length us, event | category | flops | bytes accessed | tf_op | source)
XLA Modules:
  0.0 214.5 jit_solution(12703626089541982773)
XLA Ops:
  0.7 1.5 dynamic-slice_bitcast_fusion.1
  2.8 2.4 %fusion.2 = f32[1024,1024]{1,0:T(8,128)S(1)} fusion(bf16[320,1024]{1,0:T(8,128)(2,1)} %param.4, bf16[2048,320]{0,1:T(8,128)(2,1)S(1)} %copy-done.1, s32[]{:T(128)S(6)} %select_n.18), kind=kOutput, calls=%fused_computation.16 | convolution fusion | flops 671088640 | bytes 5505028 | tf_op jit(solution)/shard_map/dot_general | solution.py:373
  5.2 2.4 %add_convert_fusion = bf16[1024,1024]{1,0:T(8,128)(2,1)S(1)} fusion(f32[1024,1024]{1,0:T(8,128)S(1)} %fusion.2, bf16[320,1024]{1,0:T(8,128)(2,1)S(1)} %collective-permute-done.theirs, bf16[320,1024]{1,0:T(8,128)(2,1)} %collective-permute-done.1), kind=kOutput, calls=%fused_computation.2 | convolution fusion | flops 673185792 | bytes 7602176 | tf_op jit(solution)/shard_map/dot_general | solution.py:375
  7.6 36.0 %all_to_all.25 = bf16[8,128,1024]{2,1,0:T(8,128)(2,1)S(1)} all-to-all(bf16[8,128,1024]{2,1,0:T(8,128)(2,1)S(1)} %bitcast.34), channel_id=1, replica_groups=mesh['x'=4,'zl'=2,'y'=4,'zh'=2,'c'=2] {'y','zh'}, dimensions={0} | all-to-all | bytes 4194304 | tf_op jit(solution)/shard_map/all_to_all | solution.py:38
  44.7 3.0 %collective-permute-start.10 = (bf16[128,1024]{1,0:T(8,128)(2,1)S(1)}, bf16[128,1024]{1,0:T(8,128)(2,1)S(1)}, u32[]{:S(2)}, u32[]{:S(2)}) collective-permute-start(bf16[128,1024]{1,0:T(8,128)(2,1)S(1)} %multiply_convert_fusion.1.refs_0_.refs_8_), channel_id=1, source_target_pairs={{0,12},{4,0},{8,4},{12,8},{1,13},{5,1},{9,5},{13,9},{2,14},{6,2},{... | collective-permute-start | bytes 786440 | tf_op jit(solution)/shard_map/ppermute | solution.py:43
  47.6 1.2 collective-permute-start.9
  48.8 1.5 collective-permute-start.5
  50.3 1.7 collective-permute-start.3
  52.1 2.2 %collective-permute-done.12.refs_12_ = bf16[128,1024]{1,0:T(8,128)(2,1)S(1)} collective-permute-done((bf16[128,1024]{1,0:T(8,128)(2,1)S(1)}, bf16[128,1024]{1,0:T(8,128)(2,1)S(1)}, u32[]{:S(2)}, u32[]{:S(2)}) %collective-permute-start.12) | collective-permute-done | bytes 262176 | tf_op jit(solution)/shard_map/ppermute | solution.py:44
  55.3 1.9 collective-permute-done.9.refs_9_
  58.2 4.0 %collective-permute-done.2.refs_1_ = bf16[128,1024]{1,0:T(8,128)(2,1)S(1)} collective-permute-done((bf16[128,1024]{1,0:T(8,128)(2,1)S(1)}, bf16[128,1024]{1,0:T(8,128)(2,1)S(1)}, u32[]{:S(2)}, u32[]{:S(2)}) %collective-permute-start.2) | collective-permute-done | bytes 262176 | tf_op jit(solution)/shard_map/ppermute | solution.py:42
  62.1 3.2 %collective-permute-start.11 = (bf16[128,1024]{1,0:T(8,128)(2,1)S(1)}, bf16[128,1024]{1,0:T(8,128)(2,1)S(1)}, u32[]{:S(2)}, u32[]{:S(2)}) collective-permute-start(bf16[128,1024]{1,0:T(8,128)(2,1)S(1)} %collective-permute-done.9.refs_9_), channel_id=1, source_target_pairs={{0,12},{4,0},{8,4},{12,8},{1,13},{5,1},{9,5},{13,9},{2,14},{6,2},{... | collective-permute-start | bytes 786440 | tf_op jit(solution)/shard_map/ppermute | solution.py:46
  65.4 2.8 %collective-permute-start.7 = (bf16[128,1024]{1,0:T(8,128)(2,1)S(1)}, bf16[128,1024]{1,0:T(8,128)(2,1)S(1)}, u32[]{:S(2)}, u32[]{:S(2)}) collective-permute-start(bf16[128,1024]{1,0:T(8,128)(2,1)S(1)} %collective-permute-done.3.refs_2_), channel_id=1, source_target_pairs={{0,96},{32,0},{64,32},{96,64},{1,97},{33,1},{65,33},{97,65},{2,98}... | collective-permute-start | bytes 786440 | tf_op jit(solution)/shard_map/ppermute | solution.py:45
  68.1 3.2 %collective-permute-start.4 = (bf16[128,1024]{1,0:T(8,128)(2,1)S(1)}, bf16[128,1024]{1,0:T(8,128)(2,1)S(1)}, u32[]{:S(2)}, u32[]{:S(2)}) collective-permute-start(bf16[128,1024]{1,0:T(8,128)(2,1)S(1)} %collective-permute-done.2.refs_1_), channel_id=1, source_target_pairs={{0,96},{32,0},{64,32},{96,64},{1,97},{33,1},{65,33},{97,65},{2,98}... | collective-permute-start | bytes 786440 | tf_op jit(solution)/shard_map/ppermute | solution.py:46
  71.6 3.3 %collective-permute-done.7.refs_6_ = bf16[128,1024]{1,0:T(8,128)(2,1)S(1)} collective-permute-done((bf16[128,1024]{1,0:T(8,128)(2,1)S(1)}, bf16[128,1024]{1,0:T(8,128)(2,1)S(1)}, u32[]{:S(2)}, u32[]{:S(2)}) %collective-permute-start.7) | collective-permute-done | bytes 262176 | tf_op jit(solution)/shard_map/ppermute | solution.py:45
  75.7 1.9 collective-permute-done.4.refs_3_
  77.7 1.2 collective-permute-start.8
  79.0 6.7 %collective-permute-done.8.refs_7_ = bf16[128,1024]{1,0:T(8,128)(2,1)S(1)} collective-permute-done((bf16[128,1024]{1,0:T(8,128)(2,1)S(1)}, bf16[128,1024]{1,0:T(8,128)(2,1)S(1)}, u32[]{:S(2)}, u32[]{:S(2)}) %collective-permute-start.8) | collective-permute-done | bytes 262176 | tf_op jit(solution)/shard_map/ppermute | solution.py:48
  85.7 10.8 %scores.1 = (f32[1024,2048]{1,0:T(8,128)}, f32[8,128]{1,0:T(8,128)S(1)}, f32[16,24,128]{2,1,0:T(8,128)}, bf16[2048,1024]{1,0:T(8,128)(2,1)}) custom-call(s32[5]{0:T(128)S(1)} %stack.23.place, bf16[128,1024]{1,0:T(8,128)(2,1)S(1)} %multiply_convert_fusion.1.refs_0_.refs_8_, bf16[128,1024]{1,0:T(8,128)(2,1)S(1)} %collective-permute-done.2.refs_1_, ...), custom_call_target="tpu_custom_call" | custom-call | flops 4294967296 | bytes 14680064 | tf_op jit(solution)/shard_map/scores/pallas_call | solution.py:263
  96.6 4.0 %all-to-all-start.1 = ((f32[16,24,128]{2,1,0:T(8,128)}), f32[16,24,128]{2,1,0:T(8,128)S(1)}, u32[]{:S(2)}, u32[]{:S(2)}) async-start(f32[16,24,128]{2,1,0:T(8,128)} %get-tuple-element.21), calls=%async_computation.1 | async-start | bytes 393216 | tf_op jit(solution)/shard_map/all_to_all | solution.py:387
  100.6 1.1 collective-permute-start.24
  101.7 2.6 %collective-permute-done.24 = f32[8,128]{1,0:T(8,128)S(1)} collective-permute-done((f32[8,128]{1,0:T(8,128)S(1)}, f32[8,128]{1,0:T(8,128)S(1)}, u32[]{:S(2)}, u32[]{:S(2)}) %collective-permute-start.24) | collective-permute-done | bytes 4128 | tf_op jit(solution)/shard_map/ppermute | solution.py:388
  104.3 1.1 collective-permute-start.27
  105.3 1.1 collective-permute-start.26
  107.4 2.0 collective-permute-done.27.r3
  109.4 1.9 collective-permute-done.25.r1
  111.3 10.1 %grads.1 = (bf16[4,2,128,1024]{3,2,1,0:T(8,128)(2,1)S(1)}, bf16[16,128]{1,0:T(8,128)(2,1)S(1)}) custom-call(s32[5]{0:T(128)S(1)} %stack.23.place, f32[1024,2048]{1,0:T(8,128)} %get-tuple-element.18.w_ref, bf16[2048,1024]{1,0:T(8,128)(2,1)} %get-tuple-element.19.query_ref, f32[8,128]{1,0:T(8,128)S(1)} %add.31.r0, f32[8,128]{1,0:T(8,128)S(1)} %collective-permute-done.25.r1, ...), custom_call_target="tpu_custom_call" | custom-call | flops 4294967296 | bytes 14680064 | tf_op jit(solution)/shard_map/grads/pallas_call | solution.py:302
  121.4 27.8 %all_to_all.26 = bf16[8,128,1024]{2,1,0:T(8,128)(2,1)S(1)} all-to-all(bf16[8,128,1024]{2,1,0:T(8,128)(2,1)S(1)} %bitcast.31), channel_id=1, replica_groups=mesh['x'=4,'zl'=2,'y'=4,'zh'=2,'c'=2] {'x','zl'}, dimensions={0} | all-to-all | bytes 4194304 | tf_op jit(solution)/shard_map/all_to_all | solution.py:38
  150.0 3.3 %collective-permute-start.28 = (bf16[128,1024]{1,0:T(8,128)(2,1)S(1)}, bf16[128,1024]{1,0:T(8,128)(2,1)S(1)}, u32[]{:S(2)}, u32[]{:S(2)}) collective-permute-start(bf16[128,1024]{1,0:T(8,128)(2,1)S(1)} %multiply_convert_fusion.refs_0_), channel_id=1, source_target_pairs={{0,2},{2,0},{1,3},{3,1},{4,6},{6,4},{5,7},{7,5},{8,10},{10,8},{9,1... | collective-permute-start | bytes 786440 | tf_op jit(solution)/shard_map/ppermute | solution.py:42
  153.3 3.1 %collective-permute-start.29 = (bf16[128,1024]{1,0:T(8,128)(2,1)S(1)}, bf16[128,1024]{1,0:T(8,128)(2,1)S(1)}, u32[]{:S(2)}, u32[]{:S(2)}) collective-permute-start(bf16[128,1024]{1,0:T(8,128)(2,1)S(1)} %multiply_convert_fusion.refs_0_), channel_id=1, source_target_pairs={{0,12},{4,0},{8,4},{12,8},{1,13},{5,1},{9,5},{13,9},{2,14},{6,2},{... | collective-permute-start | bytes 786440 | tf_op jit(solution)/shard_map/ppermute | solution.py:43
  156.5 1.5 collective-permute-done.28.refs_1_
  158.0 1.6 collective-permute-start.32
  159.6 1.7 collective-permute-start.31
  161.2 1.6 collective-permute-start.30
  162.8 3.4 %collective-permute-start.33 = (bf16[128,1024]{1,0:T(8,128)(2,1)S(1)}, bf16[128,1024]{1,0:T(8,128)(2,1)S(1)}, u32[]{:S(2)}, u32[]{:S(2)}) collective-permute-start(bf16[128,1024]{1,0:T(8,128)(2,1)S(1)} %collective-permute-done.29.refs_2_), channel_id=1, source_target_pairs={{0,12},{4,0},{8,4},{12,8},{1,13},{5,1},{9,5},{13,9},{2,14},{6,2},{... | collective-permute-start | bytes 786440 | tf_op jit(solution)/shard_map/ppermute | solution.py:45
  166.2 2.0 collective-permute-done.32.refs_5_
  168.8 3.1 %collective-permute-done.31.refs_4_ = bf16[128,1024]{1,0:T(8,128)(2,1)S(1)} collective-permute-done((bf16[128,1024]{1,0:T(8,128)(2,1)S(1)}, bf16[128,1024]{1,0:T(8,128)(2,1)S(1)}, u32[]{:S(2)}, u32[]{:S(2)}) %collective-permute-start.31) | collective-permute-done | bytes 262176 | tf_op jit(solution)/shard_map/ppermute | solution.py:44
  172.0 3.9 %collective-permute-done.34.refs_7_ = bf16[128,1024]{1,0:T(8,128)(2,1)S(1)} collective-permute-done((bf16[128,1024]{1,0:T(8,128)(2,1)S(1)}, bf16[128,1024]{1,0:T(8,128)(2,1)S(1)}, u32[]{:S(2)}, u32[]{:S(2)}) %collective-permute-start.34) | collective-permute-done | bytes 262176 | tf_op jit(solution)/shard_map/ppermute | solution.py:48
  175.8 2.5 %head_parts.1 = (bf16[8,336,128]{2,1,0:T(8,128)(2,1)S(1)}, bf16[8,336,128]{2,1,0:T(8,128)(2,1)S(1)}, bf16[1024,1024]{1,0:T(8,128)(2,1)}) custom-call(s32[5]{0:T(128)S(1)} %stack.23.place, bf16[320,1024]{1,0:T(8,128)(2,1)S(1)} %get-tuple-element.29.mine, bf16[320,1024]{1,0:T(8,128)(2,1)S(1)} %collective-permute-done.theirs, ...), custom_call_target="tpu_custom_call" | custom-call | flops 1342177280 | bytes 8388608 | tf_op jit(solution)/shard_map/head_parts/pallas_call | solution.py:342
  178.5 2.1 collective-permute-done.35
  181.6 3.5 %all-to-all-start.3 = ((bf16[8,336,128]{2,1,0:T(8,128)(2,1)}), bf16[8,336,128]{2,1,0:T(8,128)(2,1)S(1)}, u32[]{:S(2)}, u32[]{:S(2)}) async-start(bf16[8,336,128]{2,1,0:T(8,128)(2,1)} %add_convert_fusion.1), calls=%async_computation.3 | async-start | bytes 1376256 | tf_op jit(solution)/shard_map/all_to_all | solution.py:399
  185.2 2.6 %fusion.1 = bf16[320,1024]{1,0:T(8,128)(2,1)S(1)} fusion(bf16[1024,1024]{1,0:T(8,128)(2,1)} %get-tuple-element.26, bf16[320,1024]{1,0:T(8,128)(2,1)} %collective-permute-done.1), kind=kOutput, calls=%fused_computation.11 | convolution fusion | flops 671416320 | bytes 3407872 | tf_op jit(solution)/shard_map/dot_general | solution.py:407
  188.0 9.0 %all-to-all-done.3 = bf16[8,336,128]{2,1,0:T(8,128)(2,1)S(1)} async-done(((bf16[8,336,128]{2,1,0:T(8,128)(2,1)}), bf16[8,336,128]{2,1,0:T(8,128)(2,1)S(1)}, u32[]{:S(2)}, u32[]{:S(2)}) %all-to-all-start.3) | async-done | bytes 688160 | tf_op jit(solution)/shard_map/all_to_all | solution.py:399
  198.1 3.5 %all-to-all-start.4 = ((bf16[8,320,128]{2,1,0:T(8,128)(2,1)}), bf16[8,320,128]{2,1,0:T(8,128)(2,1)S(1)}, u32[]{:S(2)}, u32[]{:S(2)}) async-start(bf16[8,320,128]{2,1,0:T(8,128)(2,1)} %broadcast_in_dim.2), calls=%async_computation.4 | async-start | bytes 1310720 | tf_op jit(solution)/shard_map/all_to_all | solution.py:34
  201.7 2.5 %broadcast_select_fusion.1 = (bf16[320,1024]{1,0:T(8,128)(2,1)S(1)}, bf16[320,1024]{1,0:T(8,128)(2,1)S(1)}) fusion(bf16[320,1024]{1,0:T(8,128)(2,1)S(1)} %collective-permute-done.36, pred[]{:T(512)S(6)} %eq.3, bf16[1024,1024]{1,0:T(8,128)(2,1)} %get-tuple-element.26, bf16[320,1024]{1,0:T(8,128)(2,1)S(1)} %copy-done.2), kind=kOutput, calls=%fused_computation.14 | convolution fusion | flops 672071680 | bytes 4718593 | tf_op jit(solution)/shard_map/dot_general | solution.py:410
  204.2 1.2 maximum_bitcast_fusion
  206.6 5.6 %all-to-all-done.4 = bf16[8,320,128]{2,1,0:T(8,128)(2,1)S(1)} async-done(((bf16[8,320,128]{2,1,0:T(8,128)(2,1)}), bf16[8,320,128]{2,1,0:T(8,128)(2,1)S(1)}, u32[]{:S(2)}, u32[]{:S(2)}) %all-to-all-start.4) | async-done | bytes 655392 | tf_op jit(solution)/shard_map/all_to_all | solution.py:34
  212.2 1.2 copy_bitcast_fusion
  (64 shorter events, 9.9 us)
Async XLA Ops:
  0.6 2.1 %copy-start.1 = (bf16[2048,320]{0,1:T(8,128)(2,1)S(1)}, bf16[2048,320]{0,1:T(8,128)(2,1)}, u32[]{:S(2)}) copy-start(bf16[2048,320]{0,1:T(8,128)(2,1)} %param.3) | copy-start | bytes 3932164
  0.6 4.5 %collective-permute-start.1 = (bf16[320,1024]{1,0:T(8,128)(2,1)}, bf16[320,1024]{1,0:T(8,128)(2,1)}, u32[]{:S(2)}, u32[]{:S(2)}) collective-permute-start(bf16[320,1024]{1,0:T(8,128)(2,1)} %param.4), channel_id=1, source_target_pairs={{0,1},{1,0},{2,3},{3,2},{4,5},{5,4},{6,7},{7,6},{8,9},{9,8},{10,11... | collective-permute-start | bytes 1966088 | tf_op jit(solution)/shard_map/ppermute | solution.py:30
  2.2 3.0 %collective-permute-start = (bf16[320,1024]{1,0:T(8,128)(2,1)S(1)}, bf16[320,1024]{1,0:T(8,128)(2,1)S(1)}, u32[]{:S(2)}, u32[]{:S(2)}) collective-permute-start(bf16[320,1024]{1,0:T(8,128)(2,1)S(1)} %get-tuple-element.30), channel_id=1, source_target_pairs={{0,1},{1,0},{2,3},{3,2},{4,5},{5,4},{6,7},{7,6},{8,9},{9,8},{10,11... | collective-permute-start | bytes 1966088 | tf_op jit(solution)/shard_map/ppermute | solution.py:30
  43.6 42.1 %copy-start = (s32[2048]{0:T(1024)S(1)}, s32[2048]{0:T(1024)}, u32[]{:S(2)}) copy-start(s32[2048]{0:T(1024)} %param.5) | copy-start | bytes 24580
  44.2 6.1 %collective-permute-start.16 = (bf16[128,1024]{1,0:T(8,128)(2,1)S(1)}, bf16[128,1024]{1,0:T(8,128)(2,1)S(1)}, u32[]{:S(2)}, u32[]{:S(2)}) collective-permute-start(bf16[128,1024]{1,0:T(8,128)(2,1)S(1)} %multiply_convert_fusion.1.refs_0_.refs_8_), channel_id=1, source_target_pairs={{0,1},{1,0},{2,3},{3,2},{4,5},{5,4},{6,7},{7,6},{8,9},{9,8},{10,11... | collective-permute-start | bytes 786440 | tf_op jit(solution)/shard_map/ppermute | solution.py:30
  44.3 9.9 %collective-permute-start.12 = (bf16[128,1024]{1,0:T(8,128)(2,1)S(1)}, bf16[128,1024]{1,0:T(8,128)(2,1)S(1)}, u32[]{:S(2)}, u32[]{:S(2)}) collective-permute-start(bf16[128,1024]{1,0:T(8,128)(2,1)S(1)} %multiply_convert_fusion.1.refs_0_.refs_8_), channel_id=1, source_target_pairs={{0,4},{4,8},{8,12},{12,0},{1,5},{5,9},{9,13},{13,1},{2,6},{6,10},{... | collective-permute-start | bytes 786440 | tf_op jit(solution)/shard_map/ppermute | solution.py:44
  44.7 10.6 %collective-permute-start.10 = (bf16[128,1024]{1,0:T(8,128)(2,1)S(1)}, bf16[128,1024]{1,0:T(8,128)(2,1)S(1)}, u32[]{:S(2)}, u32[]{:S(2)}) collective-permute-start(bf16[128,1024]{1,0:T(8,128)(2,1)S(1)} %multiply_convert_fusion.1.refs_0_.refs_8_), channel_id=1, source_target_pairs={{0,12},{4,0},{8,4},{12,8},{1,13},{5,1},{9,5},{13,9},{2,14},{6,2},{... | collective-permute-start | bytes 786440 | tf_op jit(solution)/shard_map/ppermute | solution.py:43
  47.6 9.6 %collective-permute-start.9 = (bf16[128,1024]{1,0:T(8,128)(2,1)S(1)}, bf16[128,1024]{1,0:T(8,128)(2,1)S(1)}, u32[]{:S(2)}, u32[]{:S(2)}) collective-permute-start(bf16[128,1024]{1,0:T(8,128)(2,1)S(1)} %multiply_convert_fusion.1.refs_0_.refs_8_), channel_id=1, source_target_pairs={{0,2},{2,0},{1,3},{3,1},{4,6},{6,4},{5,7},{7,5},{8,10},{10,8},{9,1... | collective-permute-start | bytes 786440 | tf_op jit(solution)/shard_map/ppermute | solution.py:42
  48.8 9.0 %collective-permute-start.5 = (bf16[128,1024]{1,0:T(8,128)(2,1)S(1)}, bf16[128,1024]{1,0:T(8,128)(2,1)S(1)}, u32[]{:S(2)}, u32[]{:S(2)}) collective-permute-start(bf16[128,1024]{1,0:T(8,128)(2,1)S(1)} %multiply_convert_fusion.1.refs_0_.refs_8_), channel_id=1, source_target_pairs={{0,32},{32,64},{64,96},{96,0},{1,33},{33,65},{65,97},{97,1},{2,34}... | collective-permute-start | bytes 786440 | tf_op jit(solution)/shard_map/ppermute | solution.py:44
  50.3 7.8 %collective-permute-start.3 = (bf16[128,1024]{1,0:T(8,128)(2,1)S(1)}, bf16[128,1024]{1,0:T(8,128)(2,1)S(1)}, u32[]{:S(2)}, u32[]{:S(2)}) collective-permute-start(bf16[128,1024]{1,0:T(8,128)(2,1)S(1)} %multiply_convert_fusion.1.refs_0_.refs_8_), channel_id=1, source_target_pairs={{0,96},{32,0},{64,32},{96,64},{1,97},{33,1},{65,33},{97,65},{2,98}... | collective-permute-start | bytes 786440 | tf_op jit(solution)/shard_map/ppermute | solution.py:43
  54.3 7.9 %collective-permute-start.2 = (bf16[128,1024]{1,0:T(8,128)(2,1)S(1)}, bf16[128,1024]{1,0:T(8,128)(2,1)S(1)}, u32[]{:S(2)}, u32[]{:S(2)}) collective-permute-start(bf16[128,1024]{1,0:T(8,128)(2,1)S(1)} %multiply_convert_fusion.1.refs_0_.refs_8_), channel_id=1, source_target_pairs={{0,16},{16,0},{1,17},{17,1},{2,18},{18,2},{3,19},{19,3},{4,20},{20... | collective-permute-start | bytes 786440 | tf_op jit(solution)/shard_map/ppermute | solution.py:42
  55.3 6.8 %collective-permute-start.20 = (bf16[128,1024]{1,0:T(8,128)(2,1)S(1)}, bf16[128,1024]{1,0:T(8,128)(2,1)S(1)}, u32[]{:S(2)}, u32[]{:S(2)}) collective-permute-start(bf16[128,1024]{1,0:T(8,128)(2,1)S(1)} %collective-permute-done.12.refs_12_), channel_id=1, source_target_pairs={{0,1},{1,0},{2,3},{3,2},{4,5},{5,4},{6,7},{7,6},{8,9},{9,8},{10,11... | collective-permute-start | bytes 786440 | tf_op jit(solution)/shard_map/ppermute | solution.py:30
  57.2 8.1 %collective-permute-start.18 = (bf16[128,1024]{1,0:T(8,128)(2,1)S(1)}, bf16[128,1024]{1,0:T(8,128)(2,1)S(1)}, u32[]{:S(2)}, u32[]{:S(2)}) collective-permute-start(bf16[128,1024]{1,0:T(8,128)(2,1)S(1)} %collective-permute-done.10.refs_10_), channel_id=1, source_target_pairs={{0,1},{1,0},{2,3},{3,2},{4,5},{5,4},{6,7},{7,6},{8,9},{9,8},{10,11... | collective-permute-start | bytes 786440 | tf_op jit(solution)/shard_map/ppermute | solution.py:30
  57.9 10.3 %collective-permute-start.14 = (bf16[128,1024]{1,0:T(8,128)(2,1)S(1)}, bf16[128,1024]{1,0:T(8,128)(2,1)S(1)}, u32[]{:S(2)}, u32[]{:S(2)}) collective-permute-start(bf16[128,1024]{1,0:T(8,128)(2,1)S(1)} %collective-permute-done.10.refs_10_), channel_id=1, source_target_pairs={{0,12},{4,0},{8,4},{12,8},{1,13},{5,1},{9,5},{13,9},{2,14},{6,2},{... | collective-permute-start | bytes 786440 | tf_op jit(solution)/shard_map/ppermute | solution.py:45
  58.2 10.0 %collective-permute-start.17 = (bf16[128,1024]{1,0:T(8,128)(2,1)S(1)}, bf16[128,1024]{1,0:T(8,128)(2,1)S(1)}, u32[]{:S(2)}, u32[]{:S(2)}) collective-permute-start(bf16[128,1024]{1,0:T(8,128)(2,1)S(1)} %collective-permute-done.9.refs_9_), channel_id=1, source_target_pairs={{0,1},{1,0},{2,3},{3,2},{4,5},{5,4},{6,7},{7,6},{8,9},{9,8},{10,11... | collective-permute-start | bytes 786440 | tf_op jit(solution)/shard_map/ppermute | solution.py:30
  62.1 9.2 %collective-permute-start.13 = (bf16[128,1024]{1,0:T(8,128)(2,1)S(1)}, bf16[128,1024]{1,0:T(8,128)(2,1)S(1)}, u32[]{:S(2)}, u32[]{:S(2)}) collective-permute-start(bf16[128,1024]{1,0:T(8,128)(2,1)S(1)} %collective-permute-done.9.refs_9_), channel_id=1, source_target_pairs={{0,4},{4,8},{8,12},{12,0},{1,5},{5,9},{9,13},{13,1},{2,6},{6,10},{... | collective-permute-start | bytes 786440 | tf_op jit(solution)/shard_map/ppermute | solution.py:47
  62.1 9.4 %collective-permute-start.11 = (bf16[128,1024]{1,0:T(8,128)(2,1)S(1)}, bf16[128,1024]{1,0:T(8,128)(2,1)S(1)}, u32[]{:S(2)}, u32[]{:S(2)}) collective-permute-start(bf16[128,1024]{1,0:T(8,128)(2,1)S(1)} %collective-permute-done.9.refs_9_), channel_id=1, source_target_pairs={{0,12},{4,0},{8,4},{12,8},{1,13},{5,1},{9,5},{13,9},{2,14},{6,2},{... | collective-permute-start | bytes 786440 | tf_op jit(solution)/shard_map/ppermute | solution.py:46
  65.4 9.5 %collective-permute-start.7 = (bf16[128,1024]{1,0:T(8,128)(2,1)S(1)}, bf16[128,1024]{1,0:T(8,128)(2,1)S(1)}, u32[]{:S(2)}, u32[]{:S(2)}) collective-permute-start(bf16[128,1024]{1,0:T(8,128)(2,1)S(1)} %collective-permute-done.3.refs_2_), channel_id=1, source_target_pairs={{0,96},{32,0},{64,32},{96,64},{1,97},{33,1},{65,33},{97,65},{2,98}... | collective-permute-start | bytes 786440 | tf_op jit(solution)/shard_map/ppermute | solution.py:45
  68.1 7.6 %collective-permute-start.6 = (bf16[128,1024]{1,0:T(8,128)(2,1)S(1)}, bf16[128,1024]{1,0:T(8,128)(2,1)S(1)}, u32[]{:S(2)}, u32[]{:S(2)}) collective-permute-start(bf16[128,1024]{1,0:T(8,128)(2,1)S(1)} %collective-permute-done.2.refs_1_), channel_id=1, source_target_pairs={{0,32},{32,64},{64,96},{96,0},{1,33},{33,65},{65,97},{97,1},{2,34}... | collective-permute-start | bytes 786440 | tf_op jit(solution)/shard_map/ppermute | solution.py:47
  68.1 9.5 %collective-permute-start.4 = (bf16[128,1024]{1,0:T(8,128)(2,1)S(1)}, bf16[128,1024]{1,0:T(8,128)(2,1)S(1)}, u32[]{:S(2)}, u32[]{:S(2)}) collective-permute-start(bf16[128,1024]{1,0:T(8,128)(2,1)S(1)} %collective-permute-done.2.refs_1_), channel_id=1, source_target_pairs={{0,96},{32,0},{64,32},{96,64},{1,97},{33,1},{65,33},{97,65},{2,98}... | collective-permute-start | bytes 786440 | tf_op jit(solution)/shard_map/ppermute | solution.py:46
  71.4 7.6 %collective-permute-start.15 = (bf16[128,1024]{1,0:T(8,128)(2,1)S(1)}, bf16[128,1024]{1,0:T(8,128)(2,1)S(1)}, u32[]{:S(2)}, u32[]{:S(2)}) collective-permute-start(bf16[128,1024]{1,0:T(8,128)(2,1)S(1)} %collective-permute-done.13.refs_13_), channel_id=1, source_target_pairs={{0,4},{4,8},{8,12},{12,0},{1,5},{5,9},{9,13},{13,1},{2,6},{6,10},{... | collective-permute-start | bytes 786440 | tf_op jit(solution)/shard_map/ppermute | solution.py:48
  71.6 7.4 %collective-permute-start.21 = (bf16[128,1024]{1,0:T(8,128)(2,1)S(1)}, bf16[128,1024]{1,0:T(8,128)(2,1)S(1)}, u32[]{:S(2)}, u32[]{:S(2)}) collective-permute-start(bf16[128,1024]{1,0:T(8,128)(2,1)S(1)} %collective-permute-done.13.refs_13_), channel_id=1, source_target_pairs={{0,1},{1,0},{2,3},{3,2},{4,5},{5,4},{6,7},{7,6},{8,9},{9,8},{10,11... | collective-permute-start | bytes 786440 | tf_op jit(solution)/shard_map/ppermute | solution.py:30
  74.9 4.1 %collective-permute-start.22 = (bf16[128,1024]{1,0:T(8,128)(2,1)S(1)}, bf16[128,1024]{1,0:T(8,128)(2,1)S(1)}, u32[]{:S(2)}, u32[]{:S(2)}) collective-permute-start(bf16[128,1024]{1,0:T(8,128)(2,1)S(1)} %collective-permute-done.14.refs_14_), channel_id=1, source_target_pairs={{0,1},{1,0},{2,3},{3,2},{4,5},{5,4},{6,7},{7,6},{8,9},{9,8},{10,11... | collective-permute-start | bytes 786440 | tf_op jit(solution)/shard_map/ppermute | solution.py:30
  75.7 3.3 %collective-permute-start.19 = (bf16[128,1024]{1,0:T(8,128)(2,1)S(1)}, bf16[128,1024]{1,0:T(8,128)(2,1)S(1)}, u32[]{:S(2)}, u32[]{:S(2)}) collective-permute-start(bf16[128,1024]{1,0:T(8,128)(2,1)S(1)} %collective-permute-done.11.refs_11_), channel_id=1, source_target_pairs={{0,1},{1,0},{2,3},{3,2},{4,5},{5,4},{6,7},{7,6},{8,9},{9,8},{10,11... | collective-permute-start | bytes 786440 | tf_op jit(solution)/shard_map/ppermute | solution.py:30
  77.7 8.0 %collective-permute-start.8 = (bf16[128,1024]{1,0:T(8,128)(2,1)S(1)}, bf16[128,1024]{1,0:T(8,128)(2,1)S(1)}, u32[]{:S(2)}, u32[]{:S(2)}) collective-permute-start(bf16[128,1024]{1,0:T(8,128)(2,1)S(1)} %collective-permute-done.6.refs_5_), channel_id=1, source_target_pairs={{0,32},{32,64},{64,96},{96,0},{1,33},{33,65},{65,97},{97,1},{2,34}... | collective-permute-start | bytes 786440 | tf_op jit(solution)/shard_map/ppermute | solution.py:48
  79.0 6.8 %collective-permute-start.23 = (bf16[128,1024]{1,0:T(8,128)(2,1)S(1)}, bf16[128,1024]{1,0:T(8,128)(2,1)S(1)}, u32[]{:S(2)}, u32[]{:S(2)}) collective-permute-start(bf16[128,1024]{1,0:T(8,128)(2,1)S(1)} %collective-permute-done.15.refs_15_), channel_id=1, source_target_pairs={{0,1},{1,0},{2,3},{3,2},{4,5},{5,4},{6,7},{7,6},{8,9},{9,8},{10,11... | collective-permute-start | bytes 786440 | tf_op jit(solution)/shard_map/ppermute | solution.py:30
  96.6 14.7 %all-to-all-start.1 = ((f32[16,24,128]{2,1,0:T(8,128)}), f32[16,24,128]{2,1,0:T(8,128)S(1)}, u32[]{:S(2)}, u32[]{:S(2)}) async-start(f32[16,24,128]{2,1,0:T(8,128)} %get-tuple-element.21), calls=%async_computation.1 | async-start | bytes 393216 | tf_op jit(solution)/shard_map/all_to_all | solution.py:387
  100.6 3.7 %collective-permute-start.24 = (f32[8,128]{1,0:T(8,128)S(1)}, f32[8,128]{1,0:T(8,128)S(1)}, u32[]{:S(2)}, u32[]{:S(2)}) collective-permute-start(f32[8,128]{1,0:T(8,128)S(1)} %get-tuple-element.20), channel_id=1, source_target_pairs={{0,16},{16,0},{1,17},{17,1},{2,18},{18,2},{3,19},{19,3},{4,20},{20... | collective-permute-start | bytes 12296 | tf_op jit(solution)/shard_map/ppermute | solution.py:388
  104.3 5.1 %collective-permute-start.27 = (f32[8,128]{1,0:T(8,128)S(1)}, f32[8,128]{1,0:T(8,128)S(1)}, u32[]{:S(2)}, u32[]{:S(2)}) collective-permute-start(f32[8,128]{1,0:T(8,128)S(1)} %add.31.r0), channel_id=1, source_target_pairs={{0,64},{32,96},{64,0},{96,32},{1,65},{33,97},{65,1},{97,33},{2,66}... | collective-permute-start | bytes 12296 | tf_op jit(solution)/shard_map/ppermute | solution.py:389
  105.3 4.0 %collective-permute-start.26 = (f32[8,128]{1,0:T(8,128)S(1)}, f32[8,128]{1,0:T(8,128)S(1)}, u32[]{:S(2)}, u32[]{:S(2)}) collective-permute-start(f32[8,128]{1,0:T(8,128)S(1)} %add.31.r0), channel_id=1, source_target_pairs={{0,96},{32,0},{64,32},{96,64},{1,97},{33,1},{65,33},{97,65},{2,98}... | collective-permute-start | bytes 12296 | tf_op jit(solution)/shard_map/ppermute | solution.py:389
  106.5 4.8 %collective-permute-start.25 = (f32[8,128]{1,0:T(8,128)S(1)}, f32[8,128]{1,0:T(8,128)S(1)}, u32[]{:S(2)}, u32[]{:S(2)}) collective-permute-start(f32[8,128]{1,0:T(8,128)S(1)} %add.31.r0), channel_id=1, source_target_pairs={{0,32},{32,64},{64,96},{96,0},{1,33},{33,65},{65,97},{97,1},{2,34}... | collective-permute-start | bytes 12296 | tf_op jit(solution)/shard_map/ppermute | solution.py:389
  150.0 8.0 %collective-permute-start.28 = (bf16[128,1024]{1,0:T(8,128)(2,1)S(1)}, bf16[128,1024]{1,0:T(8,128)(2,1)S(1)}, u32[]{:S(2)}, u32[]{:S(2)}) collective-permute-start(bf16[128,1024]{1,0:T(8,128)(2,1)S(1)} %multiply_convert_fusion.refs_0_), channel_id=1, source_target_pairs={{0,2},{2,0},{1,3},{3,1},{4,6},{6,4},{5,7},{7,5},{8,10},{10,8},{9,1... | collective-permute-start | bytes 786440 | tf_op jit(solution)/shard_map/ppermute | solution.py:42
  153.3 9.5 %collective-permute-start.29 = (bf16[128,1024]{1,0:T(8,128)(2,1)S(1)}, bf16[128,1024]{1,0:T(8,128)(2,1)S(1)}, u32[]{:S(2)}, u32[]{:S(2)}) collective-permute-start(bf16[128,1024]{1,0:T(8,128)(2,1)S(1)} %multiply_convert_fusion.refs_0_), channel_id=1, source_target_pairs={{0,12},{4,0},{8,4},{12,8},{1,13},{5,1},{9,5},{13,9},{2,14},{6,2},{... | collective-permute-start | bytes 786440 | tf_op jit(solution)/shard_map/ppermute | solution.py:43
  158.0 10.3 %collective-permute-start.32 = (bf16[128,1024]{1,0:T(8,128)(2,1)S(1)}, bf16[128,1024]{1,0:T(8,128)(2,1)S(1)}, u32[]{:S(2)}, u32[]{:S(2)}) collective-permute-start(bf16[128,1024]{1,0:T(8,128)(2,1)S(1)} %collective-permute-done.28.refs_1_), channel_id=1, source_target_pairs={{0,4},{4,8},{8,12},{12,0},{1,5},{5,9},{9,13},{13,1},{2,6},{6,10},{... | collective-permute-start | bytes 786440 | tf_op jit(solution)/shard_map/ppermute | solution.py:47
  159.6 12.4 %collective-permute-start.31 = (bf16[128,1024]{1,0:T(8,128)(2,1)S(1)}, bf16[128,1024]{1,0:T(8,128)(2,1)S(1)}, u32[]{:S(2)}, u32[]{:S(2)}) collective-permute-start(bf16[128,1024]{1,0:T(8,128)(2,1)S(1)} %multiply_convert_fusion.refs_0_), channel_id=1, source_target_pairs={{0,4},{4,8},{8,12},{12,0},{1,5},{5,9},{9,13},{13,1},{2,6},{6,10},{... | collective-permute-start | bytes 786440 | tf_op jit(solution)/shard_map/ppermute | solution.py:44
  161.2 10.7 %collective-permute-start.30 = (bf16[128,1024]{1,0:T(8,128)(2,1)S(1)}, bf16[128,1024]{1,0:T(8,128)(2,1)S(1)}, u32[]{:S(2)}, u32[]{:S(2)}) collective-permute-start(bf16[128,1024]{1,0:T(8,128)(2,1)S(1)} %collective-permute-done.28.refs_1_), channel_id=1, source_target_pairs={{0,12},{4,0},{8,4},{12,8},{1,13},{5,1},{9,5},{13,9},{2,14},{6,2},{... | collective-permute-start | bytes 786440 | tf_op jit(solution)/shard_map/ppermute | solution.py:46
  162.8 9.1 %collective-permute-start.33 = (bf16[128,1024]{1,0:T(8,128)(2,1)S(1)}, bf16[128,1024]{1,0:T(8,128)(2,1)S(1)}, u32[]{:S(2)}, u32[]{:S(2)}) collective-permute-start(bf16[128,1024]{1,0:T(8,128)(2,1)S(1)} %collective-permute-done.29.refs_2_), channel_id=1, source_target_pairs={{0,12},{4,0},{8,4},{12,8},{1,13},{5,1},{9,5},{13,9},{2,14},{6,2},{... | collective-permute-start | bytes 786440 | tf_op jit(solution)/shard_map/ppermute | solution.py:45
  168.3 7.6 %collective-permute-start.34 = (bf16[128,1024]{1,0:T(8,128)(2,1)S(1)}, bf16[128,1024]{1,0:T(8,128)(2,1)S(1)}, u32[]{:S(2)}, u32[]{:S(2)}) collective-permute-start(bf16[128,1024]{1,0:T(8,128)(2,1)S(1)} %collective-permute-done.32.refs_5_), channel_id=1, source_target_pairs={{0,4},{4,8},{8,12},{12,0},{1,5},{5,9},{9,13},{13,1},{2,6},{6,10},{... | collective-permute-start | bytes 786440 | tf_op jit(solution)/shard_map/ppermute | solution.py:48
  178.4 2.2 %collective-permute-start.35 = (bf16[8,336,128]{2,1,0:T(8,128)(2,1)S(1)}, bf16[8,336,128]{2,1,0:T(8,128)(2,1)S(1)}, u32[]{:S(2)}, u32[]{:S(2)}) collective-permute-start(bf16[8,336,128]{2,1,0:T(8,128)(2,1)S(1)} %get-tuple-element.25), channel_id=1, source_target_pairs={{0,1},{1,0},{2,3},{3,2},{4,5},{5,4},{6,7},{7,6},{8,9},{9,8},{10,11... | collective-permute-start | bytes 2064392 | tf_op jit(solution)/shard_map/ppermute | solution.py:30
  181.6 15.4 %all-to-all-start.3 = ((bf16[8,336,128]{2,1,0:T(8,128)(2,1)}), bf16[8,336,128]{2,1,0:T(8,128)(2,1)S(1)}, u32[]{:S(2)}, u32[]{:S(2)}) async-start(bf16[8,336,128]{2,1,0:T(8,128)(2,1)} %add_convert_fusion.1), calls=%async_computation.3 | async-start | bytes 1376256 | tf_op jit(solution)/shard_map/all_to_all | solution.py:399
  187.8 13.9 %copy-start.2 = (bf16[320,1024]{1,0:T(8,128)(2,1)S(1)}, bf16[320,1024]{1,0:T(8,128)(2,1)}, u32[]{:S(2)}) copy-start(bf16[320,1024]{1,0:T(8,128)(2,1)} %param.4) | copy-start | bytes 1966084
  187.8 13.8 %collective-permute-start.36 = (bf16[320,1024]{1,0:T(8,128)(2,1)S(1)}, bf16[320,1024]{1,0:T(8,128)(2,1)S(1)}, u32[]{:S(2)}, u32[]{:S(2)}) collective-permute-start(bf16[320,1024]{1,0:T(8,128)(2,1)S(1)} %fusion.1), channel_id=1, source_target_pairs={{0,1},{1,0},{2,3},{3,2},{4,5},{5,4},{6,7},{7,6},{8,9},{9,8},{10,11... | collective-permute-start | bytes 1966088 | tf_op jit(solution)/shard_map/ppermute | solution.py:30
  198.1 14.1 %all-to-all-start.4 = ((bf16[8,320,128]{2,1,0:T(8,128)(2,1)}), bf16[8,320,128]{2,1,0:T(8,128)(2,1)S(1)}, u32[]{:S(2)}, u32[]{:S(2)}) async-start(bf16[8,320,128]{2,1,0:T(8,128)(2,1)} %broadcast_in_dim.2), calls=%async_computation.4 | async-start | bytes 1310720 | tf_op jit(solution)/shard_map/all_to_all | solution.py:34

commit v7 on v6

--- a/solution.py
+++ b/solution.py
@@ -125,11 +125,12 @@
         mate = jnp.concatenate([mates[near], mates[far]], axis=1)
         col = jnp.zeros((8, PAIR), F32)
         pos = jnp.zeros((8, PAIR), F32)
+        block = lax.dot_general(
+            keys[...], queries[n], (((1,), (1,)), ((), ())), preferred_element_type=F32
+        )
         for p in range(4):
             at = pl.ds(p * PAIR, PAIR)
-            scores = lax.dot_general(
-                keys[at, :], queries[n], (((1,), (1,)), ((), ())), preferred_element_type=F32
-            )
+            scores = block[p * PAIR : (p + 1) * PAIR]
             kid = key_column(place, p)
             weights = jnp.exp2(scores * EXP2_SCALE)
             if masked and p == 0:
@@ -233,26 +234,31 @@
             run(p)
 
 
-def head_kernel(place, mine, theirs, rider, *refs):
-    piece_refs, (mine_ref, theirs_ref, all_ref, copy_sem) = refs[:8], refs[8:]
-    features = mine.shape[0]
+def head_kernel(place, summaries, rider, *refs):
+    piece_refs, (head_ref, all_ref, rows, copy_sem, out_sem) = refs[:16], refs[16:]
+    features = summaries.shape[0]
     copies = []
-    for i in range(8):
-        to = pl.multiple_of(chunk_of(place[2], i // 2, i % 2, place[3]) * ROWS, ROWS)
-        copies.append(
-            pltpu.make_async_copy(piece_refs[i], all_ref.at[pl.ds(to, ROWS), :], copy_sem.at[i])
-        )
+    for n in range(8):
+        for i, chunk in enumerate(query_chunks(place, n)):
+            to = pl.multiple_of(chunk * ROWS, ROWS)
+            at = 2 * n + i
+            copies.append(
+                pltpu.make_async_copy(
+                    piece_refs[at], rows.at[pl.ds(to, ROWS), :], copy_sem.at[at]
+                )
+            )
     for copy in copies:
         copy.start()
     for j in range(8):
-        mine_ref[j, features:] = rider[...]
-        theirs_ref[j, features:] = jnp.zeros_like(rider)
+        head_ref[j, features:] = rider[...]
     for copy in copies:
         copy.wait()
-    for source, to in ((theirs, theirs_ref), (mine, mine_ref)):
-        total = jnp.dot(source[...], all_ref[...], preferred_element_type=F32).astype(BF16)
-        for j in range(8):
-            to[j, :features] = total[:, j * ROWS : (j + 1) * ROWS]
+    out = pltpu.make_async_copy(rows, all_ref, out_sem)
+    out.start()
+    total = jnp.dot(summaries[...], rows[...], preferred_element_type=F32).astype(BF16)
+    for j in range(8):
+        head_ref[j, :features] = total[:, j * ROWS : (j + 1) * ROWS]
+    out.wait()
 
 
 def whole(shape):
@@ -337,27 +343,32 @@
     )(place, in_hbm(weights), in_hbm(queries), *rows, cols, mates)
 
 
-def head_call(place, mine, theirs, rider, pieces):
-    features = mine.shape[0]
+def head_call(place, summaries, rider, pieces):
+    features = summaries.shape[0]
     return pl.pallas_call(
         head_kernel,
         grid_spec=pltpu.PrefetchScalarGridSpec(
             num_scalar_prefetch=1,
             grid=(1,),
-            in_specs=[whole((features, HALF))] * 2
-            + [whole((16, ROWS))]
-            + [pl.BlockSpec(memory_space=pl.ANY)] * 8,
-            out_specs=[whole((8, features + 16, ROWS))] * 2 + [whole((HALF, WIDTH))],
-            scratch_shapes=[pltpu.SemaphoreType.DMA((8,))],
-        ),
-        out_shape=[jax.ShapeDtypeStruct((8, features + 16, ROWS), BF16)] * 2
-        + [pltpu.HBM((HALF, WIDTH), BF16)],
-        compiler_params=pltpu.CompilerParams(vmem_limit_bytes=10 << 20),
+            in_specs=[whole((features, GROUP)), whole((16, ROWS))]
+            + [pl.BlockSpec(memory_space=pl.ANY)] * 16,
+            out_specs=[whole((8, features + 16, ROWS)), pl.BlockSpec(memory_space=pltpu.HBM)],
+            scratch_shapes=[
+                pltpu.VMEM((GROUP, WIDTH), BF16),
+                pltpu.SemaphoreType.DMA((16,)),
+                pltpu.SemaphoreType.DMA,
+            ],
+        ),
+        out_shape=[
+            jax.ShapeDtypeStruct((8, features + 16, ROWS), BF16),
+            pltpu.HBM((GROUP, WIDTH), BF16),
+        ],
+        compiler_params=pltpu.CompilerParams(vmem_limit_bytes=20 << 20),
         cost_estimate=pl.CostEstimate(
-            flops=4 * HALF * features * WIDTH, bytes_accessed=8 << 20, transcendentals=0
+            flops=2 * GROUP * features * WIDTH, bytes_accessed=10 << 20, transcendentals=0
         ),
         name="head_parts",
-    )(place, mine, theirs, rider, *pieces)
+    )(place, summaries, rider, *pieces)
 
 
 def shards(summaries, head, partner):
@@ -391,12 +402,10 @@
     grad_emb = sum_exchange(grad_part.reshape(8, ROWS, WIDTH), XZ)
     grad_z = (inv * (grad_emb - unit * jnp.sum(unit * grad_emb, axis=1, keepdims=True))).astype(BF16)
 
-    head_mine, head_theirs, grad_half = head_call(
-        place, mine, theirs, rider, gather_ring(grad_z, "y", "zh")
-    )
-    head_part = head_mine.astype(F32) + core_swap(head_theirs).astype(F32)
-
-    pieces = lax.all_to_all(head_part.astype(BF16), XZ, 0, 0)
+    pieces = gather_ring(grad_z, "y", "zh")
+    pieces = pieces + [core_swap(piece) for piece in pieces]
+    head_part, grad_group = head_call(place, turned, rider, pieces)
+    pieces = lax.all_to_all(head_part, XZ, 0, 0)
     pieces = jnp.sum(pieces.astype(F32), axis=0)
     features = head.shape[0]
     loss = jnp.sum(pieces[features:, 0]) / TOTAL
@@ -404,13 +413,7 @@
     grad_head = spread(head_sum, XZ, 8).transpose(1, 0, 2).reshape(features, WIDTH).astype(F32)
 
     last_dims = (((1,), (1,)), ((), ()))
-    out_theirs = lax.dot_general(
-        other_head, grad_half, last_dims, preferred_element_type=F32
-    ).astype(BF16)
-    out_mine = lax.dot_general(head, grad_half, last_dims, preferred_element_type=F32).astype(BF16)
-    got = core_swap(out_theirs)
-    first = core == 0
-    out = jnp.concatenate([jnp.where(first, out_mine, got), jnp.where(first, got, out_mine)], 1)
+    out = lax.dot_general(head, grad_group, last_dims, preferred_element_type=F32).astype(BF16)
     return loss, out.T, grad_head
 
 

time: 215 us -> 212 us (0.986)
  blocking collectives: 63.9 us -> 78.6 us
  waiting for transfers between devices: 55.7 us -> 46.8 us
  starting transfers between devices: 51 us -> 45.6 us
  other arithmetic: 5.42 us -> 3.22 us
    all_to_all x0 -> x1, blocking collectives: none -> 14.7 us  [shards(): pieces = lax.all_to_all(head_part, XZ, 0, 0)]
    all_to_all x1 -> x0, waiting for transfers between devices: 9.03 us -> none  [shards(): pieces = lax.all_to_all(head_part.astype(BF16), XZ, 0, 0)]
    ppermute x3, waiting for transfers between devices: 2.15 us -> 6.97 us  [gather_ring(): after_other = lax.ppermute(other, long_axis, RING[3])]
    ppermute x3, waiting for transfers between devices: 10.7 us -> 6.81 us  [gather_ring(): far_other = lax.ppermute(before_other, long_axis, RING[1])]
    ppermute x3, waiting for transfers between devices: 3.31 us -> 7.17 us  [gather_ring(): far_own = lax.ppermute(after_own, long_axis, RING[3])]
    all_to_all x1 -> x0, starting transfers between devices: 3.54 us -> none  [shards(): pieces = lax.all_to_all(head_part.astype(BF16), XZ, 0, 0)]
    dot_general x2 -> x1, matrix products: 5.11 us -> 4.81 us  [shards(): lax.dot_general(head, grad_group, last_dims, preferred_element_type=F32)]
  transfers between devices with their start and end apart: 40 -> 45, of which waited for: 20 -> 23; matrix products, arithmetic and copies ran while one was open for 6% -> 4% of each run, Pallas kernels for 0% -> 0%
where the time goes in v7:
time: 212 us; the launch traced here: 211 us
  blocking collectives  78.6 us (37%)
  waiting for transfers between devices  46.8 us (22%)
  starting transfers between devices  45.6 us (22%)
  Pallas kernels  23.5 us (11%)
  matrix products  8.73 us (4%)
  other arithmetic  3.22 us (2%)
  between operations  2.61 us (1%)
  local copies, waits for them, and re-layouts  2.17 us (1%)
    all_to_all x2, blocking collectives, sum_exchange(): return jnp.sum(lax.all_to_all(parts, axes, 0, 0).astype(F32), axis=0)  63.9 us
    all_to_all x1, blocking collectives, shards(): pieces = lax.all_to_all(head_part, XZ, 0, 0)  14.7 us
    pallas_call x1, Pallas kernels, score_call(): pl.pallas_call(score_kernel, grid_spec=pltpu.PrefetchScalarGridSpec(num_s...  10.3 us
    pallas_call x1, Pallas kernels, grad_call(): pl.pallas_call(grad_kernel, grid_spec=pltpu.PrefetchScalarGridSpec(num_sc...  10.1 us
    ppermute x3, waiting for transfers between devices, gather_ring(): other = lax.ppermute(own, short_axis, SWAP)  7.27 us
    ppermute x3, starting transfers between devices, gather_ring(): after_other = lax.ppermute(other, long_axis, RING[3])  7.2 us
    ppermute x3, waiting for transfers between devices, gather_ring(): far_own = lax.ppermute(after_own, long_axis, RING[3])  7.17 us
    ppermute x3, waiting for transfers between devices, gather_ring(): after_other = lax.ppermute(other, long_axis, RING[3])  6.97 us
  transfers between devices with their start and end apart: 45, of which 23 were waited for; matrix products, arithmetic and copies ran while one was open for 4% of the time, Pallas kernels for 0%

profile of v7, /device:TPU:0, one launch (start us, length us, event | category | flops | bytes accessed | tf_op | source)
XLA Modules:
  0.0 211.2 jit_solution(8855206355973363493)
XLA Ops:
  0.6 1.1 dynamic-slice_bitcast_fusion
  2.4 2.6 %fusion = f32[1024,1024]{1,0:T(8,128)S(1)} fusion(bf16[320,1024]{1,0:T(8,128)(2,1)} %param.4, bf16[2048,320]{0,1:T(8,128)(2,1)} %param.3, s32[]{:T(128)S(6)} %select_n.6), kind=kOutput, calls=%fused_computation.8 | convolution fusion | flops 671088640 | bytes 5505028 | tf_op jit(solution)/shard_map/dot_general | solution.py:384
  5.1 1.3 add_convert_fusion
  6.5 36.1 %all_to_all.25 = bf16[8,128,1024]{2,1,0:T(8,128)(2,1)S(1)} all-to-all(bf16[8,128,1024]{2,1,0:T(8,128)(2,1)S(1)} %bitcast.26), channel_id=1, replica_groups=mesh['x'=4,'zl'=2,'y'=4,'zh'=2,'c'=2] {'y','zh'}, dimensions={0} | all-to-all | bytes 4194304 | tf_op jit(solution)/shard_map/all_to_all | solution.py:38
  43.5 3.0 %collective-permute-start.10 = (bf16[128,1024]{1,0:T(8,128)(2,1)S(1)}, bf16[128,1024]{1,0:T(8,128)(2,1)S(1)}, u32[]{:S(2)}, u32[]{:S(2)}) collective-permute-start(bf16[128,1024]{1,0:T(8,128)(2,1)S(1)} %multiply_convert_fusion.1.refs_0_.refs_8_), channel_id=1, source_target_pairs={{0,12},{4,0},{8,4},{12,8},{1,13},{5,1},{9,5},{13,9},{2,14},{6,2},{... | collective-permute-start | bytes 786440 | tf_op jit(solution)/shard_map/ppermute | solution.py:43
  46.5 1.2 collective-permute-start.9
  47.7 1.5 collective-permute-start.5
  49.2 1.7 collective-permute-start.3
  50.9 2.2 %collective-permute-done.12.refs_12_ = bf16[128,1024]{1,0:T(8,128)(2,1)S(1)} collective-permute-done((bf16[128,1024]{1,0:T(8,128)(2,1)S(1)}, bf16[128,1024]{1,0:T(8,128)(2,1)S(1)}, u32[]{:S(2)}, u32[]{:S(2)}) %collective-permute-start.12) | collective-permute-done | bytes 262176 | tf_op jit(solution)/shard_map/ppermute | solution.py:44
  53.1 1.0 collective-permute-start.2
  54.1 1.9 collective-permute-done.9.refs_9_
  57.0 4.0 %collective-permute-done.2.refs_1_ = bf16[128,1024]{1,0:T(8,128)(2,1)S(1)} collective-permute-done((bf16[128,1024]{1,0:T(8,128)(2,1)S(1)}, bf16[128,1024]{1,0:T(8,128)(2,1)S(1)}, u32[]{:S(2)}, u32[]{:S(2)}) %collective-permute-start.2) | collective-permute-done | bytes 262176 | tf_op jit(solution)/shard_map/ppermute | solution.py:42
  61.0 3.2 %collective-permute-start.11 = (bf16[128,1024]{1,0:T(8,128)(2,1)S(1)}, bf16[128,1024]{1,0:T(8,128)(2,1)S(1)}, u32[]{:S(2)}, u32[]{:S(2)}) collective-permute-start(bf16[128,1024]{1,0:T(8,128)(2,1)S(1)} %collective-permute-done.9.refs_9_), channel_id=1, source_target_pairs={{0,12},{4,0},{8,4},{12,8},{1,13},{5,1},{9,5},{13,9},{2,14},{6,2},{... | collective-permute-start | bytes 786440 | tf_op jit(solution)/shard_map/ppermute | solution.py:46
  64.2 2.8 %collective-permute-start.7 = (bf16[128,1024]{1,0:T(8,128)(2,1)S(1)}, bf16[128,1024]{1,0:T(8,128)(2,1)S(1)}, u32[]{:S(2)}, u32[]{:S(2)}) collective-permute-start(bf16[128,1024]{1,0:T(8,128)(2,1)S(1)} %collective-permute-done.3.refs_2_), channel_id=1, source_target_pairs={{0,96},{32,0},{64,32},{96,64},{1,97},{33,1},{65,33},{97,65},{2,98}... | collective-permute-start | bytes 786440 | tf_op jit(solution)/shard_map/ppermute | solution.py:45
  67.0 3.2 %collective-permute-start.4 = (bf16[128,1024]{1,0:T(8,128)(2,1)S(1)}, bf16[128,1024]{1,0:T(8,128)(2,1)S(1)}, u32[]{:S(2)}, u32[]{:S(2)}) collective-permute-start(bf16[128,1024]{1,0:T(8,128)(2,1)S(1)} %collective-permute-done.2.refs_1_), channel_id=1, source_target_pairs={{0,96},{32,0},{64,32},{96,64},{1,97},{33,1},{65,33},{97,65},{2,98}... | collective-permute-start | bytes 786440 | tf_op jit(solution)/shard_map/ppermute | solution.py:46
  70.4 3.3 %collective-permute-done.7.refs_6_ = bf16[128,1024]{1,0:T(8,128)(2,1)S(1)} collective-permute-done((bf16[128,1024]{1,0:T(8,128)(2,1)S(1)}, bf16[128,1024]{1,0:T(8,128)(2,1)S(1)}, u32[]{:S(2)}, u32[]{:S(2)}) %collective-permute-start.7) | collective-permute-done | bytes 262176 | tf_op jit(solution)/shard_map/ppermute | solution.py:45
  74.6 1.9 collective-permute-done.4.refs_3_
  76.5 1.2 collective-permute-start.8
  77.8 6.7 %collective-permute-done.8.refs_7_ = bf16[128,1024]{1,0:T(8,128)(2,1)S(1)} collective-permute-done((bf16[128,1024]{1,0:T(8,128)(2,1)S(1)}, bf16[128,1024]{1,0:T(8,128)(2,1)S(1)}, u32[]{:S(2)}, u32[]{:S(2)}) %collective-permute-start.8) | collective-permute-done | bytes 262176 | tf_op jit(solution)/shard_map/ppermute | solution.py:48
  84.6 10.3 %scores.1 = (f32[1024,2048]{1,0:T(8,128)}, f32[8,128]{1,0:T(8,128)S(1)}, f32[16,24,128]{2,1,0:T(8,128)}, bf16[2048,1024]{1,0:T(8,128)(2,1)}) custom-call(s32[5]{0:T(128)S(1)} %stack.23.place, bf16[128,1024]{1,0:T(8,128)(2,1)S(1)} %multiply_convert_fusion.1.refs_0_.refs_8_, bf16[128,1024]{1,0:T(8,128)(2,1)S(1)} %collective-permute-done.2.refs_1_, ...), custom_call_target="tpu_custom_call" | custom-call | flops 4294967296 | bytes 14680064 | tf_op jit(solution)/shard_map/scores/pallas_call | solution.py:269
  94.9 4.0 %all-to-all-start.1 = ((f32[16,24,128]{2,1,0:T(8,128)}), f32[16,24,128]{2,1,0:T(8,128)S(1)}, u32[]{:S(2)}, u32[]{:S(2)}) async-start(f32[16,24,128]{2,1,0:T(8,128)} %get-tuple-element.20), calls=%async_computation.1 | async-start | bytes 393216 | tf_op jit(solution)/shard_map/all_to_all | solution.py:398
  98.9 1.1 collective-permute-start.24
  100.0 2.6 %collective-permute-done.24 = f32[8,128]{1,0:T(8,128)S(1)} collective-permute-done((f32[8,128]{1,0:T(8,128)S(1)}, f32[8,128]{1,0:T(8,128)S(1)}, u32[]{:S(2)}, u32[]{:S(2)}) %collective-permute-start.24) | collective-permute-done | bytes 4128 | tf_op jit(solution)/shard_map/ppermute | solution.py:399
  102.6 1.1 collective-permute-start.27
  103.7 1.1 collective-permute-start.26
  104.8 0.9 collective-permute-start.25
  105.7 2.0 collective-permute-done.27.r3
  107.7 1.9 collective-permute-done.25.r1
  109.6 10.1 %grads.1 = (bf16[4,2,128,1024]{3,2,1,0:T(8,128)(2,1)S(1)}, bf16[16,128]{1,0:T(8,128)(2,1)S(1)}) custom-call(s32[5]{0:T(128)S(1)} %stack.23.place, f32[1024,2048]{1,0:T(8,128)} %get-tuple-element.17.w_ref, bf16[2048,1024]{1,0:T(8,128)(2,1)} %get-tuple-element.18.query_ref, f32[8,128]{1,0:T(8,128)S(1)} %add.28.r0, f32[8,128]{1,0:T(8,128)S(1)} %collective-permute-done.25.r1, ...), custom_call_target="tpu_custom_call" | custom-call | flops 4294967296 | bytes 14680064 | tf_op jit(solution)/shard_map/grads/pallas_call | solution.py:308
  119.8 27.8 %all_to_all.26 = bf16[8,128,1024]{2,1,0:T(8,128)(2,1)S(1)} all-to-all(bf16[8,128,1024]{2,1,0:T(8,128)(2,1)S(1)} %bitcast.23), channel_id=1, replica_groups=mesh['x'=4,'zl'=2,'y'=4,'zh'=2,'c'=2] {'x','zl'}, dimensions={0} | all-to-all | bytes 4194304 | tf_op jit(solution)/shard_map/all_to_all | solution.py:38
  148.3 3.6 %collective-permute-start.28 = (bf16[128,1024]{1,0:T(8,128)(2,1)S(1)}, bf16[128,1024]{1,0:T(8,128)(2,1)S(1)}, u32[]{:S(2)}, u32[]{:S(2)}) collective-permute-start(bf16[128,1024]{1,0:T(8,128)(2,1)S(1)} %multiply_convert_fusion.refs_0_), channel_id=1, source_target_pairs={{0,2},{2,0},{1,3},{3,1},{4,6},{6,4},{5,7},{7,5},{8,10},{10,8},{9,1... | collective-permute-start | bytes 786440 | tf_op jit(solution)/shard_map/ppermute | solution.py:42
  151.9 1.5 collective-permute-start.31
  153.4 1.8 collective-permute-start.29
  155.2 1.4 collective-permute-done.28.refs_1_
  156.5 1.6 collective-permute-start.32
  158.1 1.4 collective-permute-done.31.refs_4_
  160.0 3.1 %collective-permute-start.33 = (bf16[128,1024]{1,0:T(8,128)(2,1)S(1)}, bf16[128,1024]{1,0:T(8,128)(2,1)S(1)}, u32[]{:S(2)}, u32[]{:S(2)}) collective-permute-start(bf16[128,1024]{1,0:T(8,128)(2,1)S(1)} %collective-permute-done.29.refs_2_), channel_id=1, source_target_pairs={{0,12},{4,0},{8,4},{12,8},{1,13},{5,1},{9,5},{13,9},{2,14},{6,2},{... | collective-permute-start | bytes 786440 | tf_op jit(solution)/shard_map/ppermute | solution.py:45
  163.8 1.3 collective-permute-done.32.refs_5_
  165.9 3.9 %collective-permute-done.33.refs_6_ = bf16[128,1024]{1,0:T(8,128)(2,1)S(1)} collective-permute-done((bf16[128,1024]{1,0:T(8,128)(2,1)S(1)}, bf16[128,1024]{1,0:T(8,128)(2,1)S(1)}, u32[]{:S(2)}, u32[]{:S(2)}) %collective-permute-start.33) | collective-permute-done | bytes 262176 | tf_op jit(solution)/shard_map/ppermute | solution.py:45
  169.8 4.8 %collective-permute-done.30.refs_3_ = bf16[128,1024]{1,0:T(8,128)(2,1)S(1)} collective-permute-done((bf16[128,1024]{1,0:T(8,128)(2,1)S(1)}, bf16[128,1024]{1,0:T(8,128)(2,1)S(1)}, u32[]{:S(2)}, u32[]{:S(2)}) %collective-permute-start.30) | collective-permute-done | bytes 262176 | tf_op jit(solution)/shard_map/ppermute | solution.py:46
  175.1 1.0 collective-permute-done.38.refs_11_
  176.5 3.0 %head_parts.1 = (bf16[8,336,128]{2,1,0:T(8,128)(2,1)S(1)}, bf16[2048,1024]{1,0:T(8,128)(2,1)}) custom-call(s32[5]{0:T(128)S(1)} %stack.23.place, bf16[320,2048]{1,0:T(8,128)(2,1)S(1)} %bitcast.22, bf16[16,128]{1,0:T(8,128)(2,1)S(1)} %get-tuple-element.21.rider, bf16[128,1024]{1,0:T(8,128)(2,1)S(1)} %multiply_convert_fusion.refs_0_, ...), custom_call_target="tpu_custom_call" | custom-call | flops 1342177280 | bytes 10485760 | tf_op jit(solution)/shard_map/head_parts/pallas_call | solution.py:348
  179.6 14.7 %all_to_all.27 = bf16[8,336,128]{2,1,0:T(8,128)(2,1)S(1)} all-to-all(bf16[8,336,128]{2,1,0:T(8,128)(2,1)S(1)} %get-tuple-element.23), channel_id=1, replica_groups=mesh['x'=4,'zl'=2,'y'=4,'zh'=2,'c'=2] {'x','zl'}, dimensions={0} | all-to-all | bytes 1376256 | tf_op jit(solution)/shard_map/all_to_all | solution.py:408
  194.4 0.9 broadcast_in_dim.2
  195.3 3.5 %all-to-all-start.4 = ((bf16[8,320,128]{2,1,0:T(8,128)(2,1)}), bf16[8,320,128]{2,1,0:T(8,128)(2,1)S(1)}, u32[]{:S(2)}, u32[]{:S(2)}) async-start(bf16[8,320,128]{2,1,0:T(8,128)(2,1)} %broadcast_in_dim.2), calls=%async_computation.4 | async-start | bytes 1310720 | tf_op jit(solution)/shard_map/all_to_all | solution.py:34
  198.9 4.8 %convolution_convert_fusion = bf16[2048,320]{0,1:T(8,128)(2,1)} fusion(bf16[2048,1024]{1,0:T(8,128)(2,1)} %get-tuple-element.24, bf16[320,1024]{1,0:T(8,128)(2,1)S(1)} %copy-done.2), kind=kOutput, calls=%fused_computation.3 | convolution fusion | flops 1342832640 | bytes 6160384 | tf_op jit(solution)/shard_map/dot_general | solution.py:416
  205.0 3.9 %all-to-all-done.4 = bf16[8,320,128]{2,1,0:T(8,128)(2,1)S(1)} async-done(((bf16[8,320,128]{2,1,0:T(8,128)(2,1)}), bf16[8,320,128]{2,1,0:T(8,128)(2,1)S(1)}, u32[]{:S(2)}, u32[]{:S(2)}) %all-to-all-start.4) | async-done | bytes 655392 | tf_op jit(solution)/shard_map/all_to_all | solution.py:34
  208.9 1.2 copy_bitcast_fusion
  (72 shorter events, 8.2 us)
Async XLA Ops:
  1.8 3.3 %collective-permute-start = (bf16[320,1024]{1,0:T(8,128)(2,1)S(1)}, bf16[320,1024]{1,0:T(8,128)(2,1)S(1)}, u32[]{:S(2)}, u32[]{:S(2)}) collective-permute-start(bf16[320,1024]{1,0:T(8,128)(2,1)S(1)} %dynamic-slice_bitcast_fusion), channel_id=1, source_target_pairs={{0,1},{1,0},{2,3},{3,2},{4,5},{5,4},{6,7},{7,6},{8,9},{9,8},{10,11... | collective-permute-start | bytes 1966088 | tf_op jit(solution)/shard_map/ppermute | solution.py:30
  1.9 3.2 %collective-permute-start.1 = (bf16[320,1024]{1,0:T(8,128)(2,1)}, bf16[320,1024]{1,0:T(8,128)(2,1)S(1)}, u32[]{:S(2)}, u32[]{:S(2)}) collective-permute-start(bf16[320,1024]{1,0:T(8,128)(2,1)} %param.4), channel_id=1, source_target_pairs={{0,1},{1,0},{2,3},{3,2},{4,5},{5,4},{6,7},{7,6},{8,9},{9,8},{10,11... | collective-permute-start | bytes 1966088 | tf_op jit(solution)/shard_map/ppermute | solution.py:30
  42.5 42.1 %copy-start.1 = (s32[2048]{0:T(1024)S(1)}, s32[2048]{0:T(1024)}, u32[]{:S(2)}) copy-start(s32[2048]{0:T(1024)} %param.5) | copy-start | bytes 24580
  43.1 6.1 %collective-permute-start.16 = (bf16[128,1024]{1,0:T(8,128)(2,1)S(1)}, bf16[128,1024]{1,0:T(8,128)(2,1)S(1)}, u32[]{:S(2)}, u32[]{:S(2)}) collective-permute-start(bf16[128,1024]{1,0:T(8,128)(2,1)S(1)} %multiply_convert_fusion.1.refs_0_.refs_8_), channel_id=1, source_target_pairs={{0,1},{1,0},{2,3},{3,2},{4,5},{5,4},{6,7},{7,6},{8,9},{9,8},{10,11... | collective-permute-start | bytes 786440 | tf_op jit(solution)/shard_map/ppermute | solution.py:30
  43.2 9.9 %collective-permute-start.12 = (bf16[128,1024]{1,0:T(8,128)(2,1)S(1)}, bf16[128,1024]{1,0:T(8,128)(2,1)S(1)}, u32[]{:S(2)}, u32[]{:S(2)}) collective-permute-start(bf16[128,1024]{1,0:T(8,128)(2,1)S(1)} %multiply_convert_fusion.1.refs_0_.refs_8_), channel_id=1, source_target_pairs={{0,4},{4,8},{8,12},{12,0},{1,5},{5,9},{9,13},{13,1},{2,6},{6,10},{... | collective-permute-start | bytes 786440 | tf_op jit(solution)/shard_map/ppermute | solution.py:44
  43.5 10.6 %collective-permute-start.10 = (bf16[128,1024]{1,0:T(8,128)(2,1)S(1)}, bf16[128,1024]{1,0:T(8,128)(2,1)S(1)}, u32[]{:S(2)}, u32[]{:S(2)}) collective-permute-start(bf16[128,1024]{1,0:T(8,128)(2,1)S(1)} %multiply_convert_fusion.1.refs_0_.refs_8_), channel_id=1, source_target_pairs={{0,12},{4,0},{8,4},{12,8},{1,13},{5,1},{9,5},{13,9},{2,14},{6,2},{... | collective-permute-start | bytes 786440 | tf_op jit(solution)/shard_map/ppermute | solution.py:43
  46.5 9.6 %collective-permute-start.9 = (bf16[128,1024]{1,0:T(8,128)(2,1)S(1)}, bf16[128,1024]{1,0:T(8,128)(2,1)S(1)}, u32[]{:S(2)}, u32[]{:S(2)}) collective-permute-start(bf16[128,1024]{1,0:T(8,128)(2,1)S(1)} %multiply_convert_fusion.1.refs_0_.refs_8_), channel_id=1, source_target_pairs={{0,2},{2,0},{1,3},{3,1},{4,6},{6,4},{5,7},{7,5},{8,10},{10,8},{9,1... | collective-permute-start | bytes 786440 | tf_op jit(solution)/shard_map/ppermute | solution.py:42
  47.7 9.0 %collective-permute-start.5 = (bf16[128,1024]{1,0:T(8,128)(2,1)S(1)}, bf16[128,1024]{1,0:T(8,128)(2,1)S(1)}, u32[]{:S(2)}, u32[]{:S(2)}) collective-permute-start(bf16[128,1024]{1,0:T(8,128)(2,1)S(1)} %multiply_convert_fusion.1.refs_0_.refs_8_), channel_id=1, source_target_pairs={{0,32},{32,64},{64,96},{96,0},{1,33},{33,65},{65,97},{97,1},{2,34}... | collective-permute-start | bytes 786440 | tf_op jit(solution)/shard_map/ppermute | solution.py:44
  49.2 7.8 %collective-permute-start.3 = (bf16[128,1024]{1,0:T(8,128)(2,1)S(1)}, bf16[128,1024]{1,0:T(8,128)(2,1)S(1)}, u32[]{:S(2)}, u32[]{:S(2)}) collective-permute-start(bf16[128,1024]{1,0:T(8,128)(2,1)S(1)} %multiply_convert_fusion.1.refs_0_.refs_8_), channel_id=1, source_target_pairs={{0,96},{32,0},{64,32},{96,64},{1,97},{33,1},{65,33},{97,65},{2,98}... | collective-permute-start | bytes 786440 | tf_op jit(solution)/shard_map/ppermute | solution.py:43
  53.1 7.9 %collective-permute-start.2 = (bf16[128,1024]{1,0:T(8,128)(2,1)S(1)}, bf16[128,1024]{1,0:T(8,128)(2,1)S(1)}, u32[]{:S(2)}, u32[]{:S(2)}) collective-permute-start(bf16[128,1024]{1,0:T(8,128)(2,1)S(1)} %multiply_convert_fusion.1.refs_0_.refs_8_), channel_id=1, source_target_pairs={{0,16},{16,0},{1,17},{17,1},{2,18},{18,2},{3,19},{19,3},{4,20},{20... | collective-permute-start | bytes 786440 | tf_op jit(solution)/shard_map/ppermute | solution.py:42
  54.1 6.8 %collective-permute-start.20 = (bf16[128,1024]{1,0:T(8,128)(2,1)S(1)}, bf16[128,1024]{1,0:T(8,128)(2,1)S(1)}, u32[]{:S(2)}, u32[]{:S(2)}) collective-permute-start(bf16[128,1024]{1,0:T(8,128)(2,1)S(1)} %collective-permute-done.12.refs_12_), channel_id=1, source_target_pairs={{0,1},{1,0},{2,3},{3,2},{4,5},{5,4},{6,7},{7,6},{8,9},{9,8},{10,11... | collective-permute-start | bytes 786440 | tf_op jit(solution)/shard_map/ppermute | solution.py:30
  56.1 8.1 %collective-permute-start.18 = (bf16[128,1024]{1,0:T(8,128)(2,1)S(1)}, bf16[128,1024]{1,0:T(8,128)(2,1)S(1)}, u32[]{:S(2)}, u32[]{:S(2)}) collective-permute-start(bf16[128,1024]{1,0:T(8,128)(2,1)S(1)} %collective-permute-done.10.refs_10_), channel_id=1, source_target_pairs={{0,1},{1,0},{2,3},{3,2},{4,5},{5,4},{6,7},{7,6},{8,9},{9,8},{10,11... | collective-permute-start | bytes 786440 | tf_op jit(solution)/shard_map/ppermute | solution.py:30
  56.7 10.3 %collective-permute-start.14 = (bf16[128,1024]{1,0:T(8,128)(2,1)S(1)}, bf16[128,1024]{1,0:T(8,128)(2,1)S(1)}, u32[]{:S(2)}, u32[]{:S(2)}) collective-permute-start(bf16[128,1024]{1,0:T(8,128)(2,1)S(1)} %collective-permute-done.10.refs_10_), channel_id=1, source_target_pairs={{0,12},{4,0},{8,4},{12,8},{1,13},{5,1},{9,5},{13,9},{2,14},{6,2},{... | collective-permute-start | bytes 786440 | tf_op jit(solution)/shard_map/ppermute | solution.py:45
  57.0 10.0 %collective-permute-start.17 = (bf16[128,1024]{1,0:T(8,128)(2,1)S(1)}, bf16[128,1024]{1,0:T(8,128)(2,1)S(1)}, u32[]{:S(2)}, u32[]{:S(2)}) collective-permute-start(bf16[128,1024]{1,0:T(8,128)(2,1)S(1)} %collective-permute-done.9.refs_9_), channel_id=1, source_target_pairs={{0,1},{1,0},{2,3},{3,2},{4,5},{5,4},{6,7},{7,6},{8,9},{9,8},{10,11... | collective-permute-start | bytes 786440 | tf_op jit(solution)/shard_map/ppermute | solution.py:30
  61.0 9.3 %collective-permute-start.13 = (bf16[128,1024]{1,0:T(8,128)(2,1)S(1)}, bf16[128,1024]{1,0:T(8,128)(2,1)S(1)}, u32[]{:S(2)}, u32[]{:S(2)}) collective-permute-start(bf16[128,1024]{1,0:T(8,128)(2,1)S(1)} %collective-permute-done.9.refs_9_), channel_id=1, source_target_pairs={{0,4},{4,8},{8,12},{12,0},{1,5},{5,9},{9,13},{13,1},{2,6},{6,10},{... | collective-permute-start | bytes 786440 | tf_op jit(solution)/shard_map/ppermute | solution.py:47
  61.0 9.4 %collective-permute-start.11 = (bf16[128,1024]{1,0:T(8,128)(2,1)S(1)}, bf16[128,1024]{1,0:T(8,128)(2,1)S(1)}, u32[]{:S(2)}, u32[]{:S(2)}) collective-permute-start(bf16[128,1024]{1,0:T(8,128)(2,1)S(1)} %collective-permute-done.9.refs_9_), channel_id=1, source_target_pairs={{0,12},{4,0},{8,4},{12,8},{1,13},{5,1},{9,5},{13,9},{2,14},{6,2},{... | collective-permute-start | bytes 786440 | tf_op jit(solution)/shard_map/ppermute | solution.py:46
  64.2 9.5 %collective-permute-start.7 = (bf16[128,1024]{1,0:T(8,128)(2,1)S(1)}, bf16[128,1024]{1,0:T(8,128)(2,1)S(1)}, u32[]{:S(2)}, u32[]{:S(2)}) collective-permute-start(bf16[128,1024]{1,0:T(8,128)(2,1)S(1)} %collective-permute-done.3.refs_2_), channel_id=1, source_target_pairs={{0,96},{32,0},{64,32},{96,64},{1,97},{33,1},{65,33},{97,65},{2,98}... | collective-permute-start | bytes 786440 | tf_op jit(solution)/shard_map/ppermute | solution.py:45
  67.0 7.6 %collective-permute-start.6 = (bf16[128,1024]{1,0:T(8,128)(2,1)S(1)}, bf16[128,1024]{1,0:T(8,128)(2,1)S(1)}, u32[]{:S(2)}, u32[]{:S(2)}) collective-permute-start(bf16[128,1024]{1,0:T(8,128)(2,1)S(1)} %collective-permute-done.2.refs_1_), channel_id=1, source_target_pairs={{0,32},{32,64},{64,96},{96,0},{1,33},{33,65},{65,97},{97,1},{2,34}... | collective-permute-start | bytes 786440 | tf_op jit(solution)/shard_map/ppermute | solution.py:47
  67.0 9.5 %collective-permute-start.4 = (bf16[128,1024]{1,0:T(8,128)(2,1)S(1)}, bf16[128,1024]{1,0:T(8,128)(2,1)S(1)}, u32[]{:S(2)}, u32[]{:S(2)}) collective-permute-start(bf16[128,1024]{1,0:T(8,128)(2,1)S(1)} %collective-permute-done.2.refs_1_), channel_id=1, source_target_pairs={{0,96},{32,0},{64,32},{96,64},{1,97},{33,1},{65,33},{97,65},{2,98}... | collective-permute-start | bytes 786440 | tf_op jit(solution)/shard_map/ppermute | solution.py:46
  70.2 7.6 %collective-permute-start.15 = (bf16[128,1024]{1,0:T(8,128)(2,1)S(1)}, bf16[128,1024]{1,0:T(8,128)(2,1)S(1)}, u32[]{:S(2)}, u32[]{:S(2)}) collective-permute-start(bf16[128,1024]{1,0:T(8,128)(2,1)S(1)} %collective-permute-done.13.refs_13_), channel_id=1, source_target_pairs={{0,4},{4,8},{8,12},{12,0},{1,5},{5,9},{9,13},{13,1},{2,6},{6,10},{... | collective-permute-start | bytes 786440 | tf_op jit(solution)/shard_map/ppermute | solution.py:48
  70.4 7.4 %collective-permute-start.21 = (bf16[128,1024]{1,0:T(8,128)(2,1)S(1)}, bf16[128,1024]{1,0:T(8,128)(2,1)S(1)}, u32[]{:S(2)}, u32[]{:S(2)}) collective-permute-start(bf16[128,1024]{1,0:T(8,128)(2,1)S(1)} %collective-permute-done.13.refs_13_), channel_id=1, source_target_pairs={{0,1},{1,0},{2,3},{3,2},{4,5},{5,4},{6,7},{7,6},{8,9},{9,8},{10,11... | collective-permute-start | bytes 786440 | tf_op jit(solution)/shard_map/ppermute | solution.py:30
  73.7 4.1 %collective-permute-start.22 = (bf16[128,1024]{1,0:T(8,128)(2,1)S(1)}, bf16[128,1024]{1,0:T(8,128)(2,1)S(1)}, u32[]{:S(2)}, u32[]{:S(2)}) collective-permute-start(bf16[128,1024]{1,0:T(8,128)(2,1)S(1)} %collective-permute-done.14.refs_14_), channel_id=1, source_target_pairs={{0,1},{1,0},{2,3},{3,2},{4,5},{5,4},{6,7},{7,6},{8,9},{9,8},{10,11... | collective-permute-start | bytes 786440 | tf_op jit(solution)/shard_map/ppermute | solution.py:30
  74.6 3.3 %collective-permute-start.19 = (bf16[128,1024]{1,0:T(8,128)(2,1)S(1)}, bf16[128,1024]{1,0:T(8,128)(2,1)S(1)}, u32[]{:S(2)}, u32[]{:S(2)}) collective-permute-start(bf16[128,1024]{1,0:T(8,128)(2,1)S(1)} %collective-permute-done.11.refs_11_), channel_id=1, source_target_pairs={{0,1},{1,0},{2,3},{3,2},{4,5},{5,4},{6,7},{7,6},{8,9},{9,8},{10,11... | collective-permute-start | bytes 786440 | tf_op jit(solution)/shard_map/ppermute | solution.py:30
  76.5 8.0 %collective-permute-start.8 = (bf16[128,1024]{1,0:T(8,128)(2,1)S(1)}, bf16[128,1024]{1,0:T(8,128)(2,1)S(1)}, u32[]{:S(2)}, u32[]{:S(2)}) collective-permute-start(bf16[128,1024]{1,0:T(8,128)(2,1)S(1)} %collective-permute-done.6.refs_5_), channel_id=1, source_target_pairs={{0,32},{32,64},{64,96},{96,0},{1,33},{33,65},{65,97},{97,1},{2,34}... | collective-permute-start | bytes 786440 | tf_op jit(solution)/shard_map/ppermute | solution.py:48
  77.8 6.8 %collective-permute-start.23 = (bf16[128,1024]{1,0:T(8,128)(2,1)S(1)}, bf16[128,1024]{1,0:T(8,128)(2,1)S(1)}, u32[]{:S(2)}, u32[]{:S(2)}) collective-permute-start(bf16[128,1024]{1,0:T(8,128)(2,1)S(1)} %collective-permute-done.15.refs_15_), channel_id=1, source_target_pairs={{0,1},{1,0},{2,3},{3,2},{4,5},{5,4},{6,7},{7,6},{8,9},{9,8},{10,11... | collective-permute-start | bytes 786440 | tf_op jit(solution)/shard_map/ppermute | solution.py:30
  94.9 14.7 %all-to-all-start.1 = ((f32[16,24,128]{2,1,0:T(8,128)}), f32[16,24,128]{2,1,0:T(8,128)S(1)}, u32[]{:S(2)}, u32[]{:S(2)}) async-start(f32[16,24,128]{2,1,0:T(8,128)} %get-tuple-element.20), calls=%async_computation.1 | async-start | bytes 393216 | tf_op jit(solution)/shard_map/all_to_all | solution.py:398
  98.9 3.7 %collective-permute-start.24 = (f32[8,128]{1,0:T(8,128)S(1)}, f32[8,128]{1,0:T(8,128)S(1)}, u32[]{:S(2)}, u32[]{:S(2)}) collective-permute-start(f32[8,128]{1,0:T(8,128)S(1)} %get-tuple-element.19), channel_id=1, source_target_pairs={{0,16},{16,0},{1,17},{17,1},{2,18},{18,2},{3,19},{19,3},{4,20},{20... | collective-permute-start | bytes 12296 | tf_op jit(solution)/shard_map/ppermute | solution.py:399
  102.6 5.1 %collective-permute-start.27 = (f32[8,128]{1,0:T(8,128)S(1)}, f32[8,128]{1,0:T(8,128)S(1)}, u32[]{:S(2)}, u32[]{:S(2)}) collective-permute-start(f32[8,128]{1,0:T(8,128)S(1)} %add.28.r0), channel_id=1, source_target_pairs={{0,64},{32,96},{64,0},{96,32},{1,65},{33,97},{65,1},{97,33},{2,66}... | collective-permute-start | bytes 12296 | tf_op jit(solution)/shard_map/ppermute | solution.py:400
  103.7 4.0 %collective-permute-start.26 = (f32[8,128]{1,0:T(8,128)S(1)}, f32[8,128]{1,0:T(8,128)S(1)}, u32[]{:S(2)}, u32[]{:S(2)}) collective-permute-start(f32[8,128]{1,0:T(8,128)S(1)} %add.28.r0), channel_id=1, source_target_pairs={{0,96},{32,0},{64,32},{96,64},{1,97},{33,1},{65,33},{97,65},{2,98}... | collective-permute-start | bytes 12296 | tf_op jit(solution)/shard_map/ppermute | solution.py:400
  104.8 4.8 %collective-permute-start.25 = (f32[8,128]{1,0:T(8,128)S(1)}, f32[8,128]{1,0:T(8,128)S(1)}, u32[]{:S(2)}, u32[]{:S(2)}) collective-permute-start(f32[8,128]{1,0:T(8,128)S(1)} %add.28.r0), channel_id=1, source_target_pairs={{0,32},{32,64},{64,96},{96,0},{1,33},{33,65},{65,97},{97,1},{2,34}... | collective-permute-start | bytes 12296 | tf_op jit(solution)/shard_map/ppermute | solution.py:400
  147.6 28.9 %copy-start = (bf16[2048,320]{0,1:T(8,128)(2,1)S(1)}, bf16[2048,320]{0,1:T(8,128)(2,1)}, u32[]{:S(2)}) copy-start(bf16[2048,320]{0,1:T(8,128)(2,1)} %param.3) | copy-start | bytes 3932164
  148.3 8.2 %collective-permute-start.28 = (bf16[128,1024]{1,0:T(8,128)(2,1)S(1)}, bf16[128,1024]{1,0:T(8,128)(2,1)S(1)}, u32[]{:S(2)}, u32[]{:S(2)}) collective-permute-start(bf16[128,1024]{1,0:T(8,128)(2,1)S(1)} %multiply_convert_fusion.refs_0_), channel_id=1, source_target_pairs={{0,2},{2,0},{1,3},{3,1},{4,6},{6,4},{5,7},{7,5},{8,10},{10,8},{9,1... | collective-permute-start | bytes 786440 | tf_op jit(solution)/shard_map/ppermute | solution.py:42
  151.9 7.6 %collective-permute-start.31 = (bf16[128,1024]{1,0:T(8,128)(2,1)S(1)}, bf16[128,1024]{1,0:T(8,128)(2,1)S(1)}, u32[]{:S(2)}, u32[]{:S(2)}) collective-permute-start(bf16[128,1024]{1,0:T(8,128)(2,1)S(1)} %multiply_convert_fusion.refs_0_), channel_id=1, source_target_pairs={{0,4},{4,8},{8,12},{12,0},{1,5},{5,9},{9,13},{13,1},{2,6},{6,10},{... | collective-permute-start | bytes 786440 | tf_op jit(solution)/shard_map/ppermute | solution.py:44
  153.4 6.4 %collective-permute-start.29 = (bf16[128,1024]{1,0:T(8,128)(2,1)S(1)}, bf16[128,1024]{1,0:T(8,128)(2,1)S(1)}, u32[]{:S(2)}, u32[]{:S(2)}) collective-permute-start(bf16[128,1024]{1,0:T(8,128)(2,1)S(1)} %multiply_convert_fusion.refs_0_), channel_id=1, source_target_pairs={{0,12},{4,0},{8,4},{12,8},{1,13},{5,1},{9,5},{13,9},{2,14},{6,2},{... | collective-permute-start | bytes 786440 | tf_op jit(solution)/shard_map/ppermute | solution.py:43
  155.2 7.9 %collective-permute-start.35 = (bf16[128,1024]{1,0:T(8,128)(2,1)S(1)}, bf16[128,1024]{1,0:T(8,128)(2,1)S(1)}, u32[]{:S(2)}, u32[]{:S(2)}) collective-permute-start(bf16[128,1024]{1,0:T(8,128)(2,1)S(1)} %multiply_convert_fusion.refs_0_), channel_id=1, source_target_pairs={{0,1},{1,0},{2,3},{3,2},{4,5},{5,4},{6,7},{7,6},{8,9},{9,8},{10,11... | collective-permute-start | bytes 786440 | tf_op jit(solution)/shard_map/ppermute | solution.py:30
  156.5 8.6 %collective-permute-start.32 = (bf16[128,1024]{1,0:T(8,128)(2,1)S(1)}, bf16[128,1024]{1,0:T(8,128)(2,1)S(1)}, u32[]{:S(2)}, u32[]{:S(2)}) collective-permute-start(bf16[128,1024]{1,0:T(8,128)(2,1)S(1)} %collective-permute-done.28.refs_1_), channel_id=1, source_target_pairs={{0,4},{4,8},{8,12},{12,0},{1,5},{5,9},{9,13},{13,1},{2,6},{6,10},{... | collective-permute-start | bytes 786440 | tf_op jit(solution)/shard_map/ppermute | solution.py:47
  159.5 5.9 %collective-permute-start.39 = (bf16[128,1024]{1,0:T(8,128)(2,1)S(1)}, bf16[128,1024]{1,0:T(8,128)(2,1)S(1)}, u32[]{:S(2)}, u32[]{:S(2)}) collective-permute-start(bf16[128,1024]{1,0:T(8,128)(2,1)S(1)} %collective-permute-done.31.refs_4_), channel_id=1, source_target_pairs={{0,1},{1,0},{2,3},{3,2},{4,5},{5,4},{6,7},{7,6},{8,9},{9,8},{10,11... | collective-permute-start | bytes 786440 | tf_op jit(solution)/shard_map/ppermute | solution.py:30
  159.8 5.6 %collective-permute-start.37 = (bf16[128,1024]{1,0:T(8,128)(2,1)S(1)}, bf16[128,1024]{1,0:T(8,128)(2,1)S(1)}, u32[]{:S(2)}, u32[]{:S(2)}) collective-permute-start(bf16[128,1024]{1,0:T(8,128)(2,1)S(1)} %collective-permute-done.29.refs_2_), channel_id=1, source_target_pairs={{0,1},{1,0},{2,3},{3,2},{4,5},{5,4},{6,7},{7,6},{8,9},{9,8},{10,11... | collective-permute-start | bytes 786440 | tf_op jit(solution)/shard_map/ppermute | solution.py:30
  160.0 9.8 %collective-permute-start.33 = (bf16[128,1024]{1,0:T(8,128)(2,1)S(1)}, bf16[128,1024]{1,0:T(8,128)(2,1)S(1)}, u32[]{:S(2)}, u32[]{:S(2)}) collective-permute-start(bf16[128,1024]{1,0:T(8,128)(2,1)S(1)} %collective-permute-done.29.refs_2_), channel_id=1, source_target_pairs={{0,12},{4,0},{8,4},{12,8},{1,13},{5,1},{9,5},{13,9},{2,14},{6,2},{... | collective-permute-start | bytes 786440 | tf_op jit(solution)/shard_map/ppermute | solution.py:45
  163.1 11.5 %collective-permute-start.30 = (bf16[128,1024]{1,0:T(8,128)(2,1)S(1)}, bf16[128,1024]{1,0:T(8,128)(2,1)S(1)}, u32[]{:S(2)}, u32[]{:S(2)}) collective-permute-start(bf16[128,1024]{1,0:T(8,128)(2,1)S(1)} %collective-permute-done.28.refs_1_), channel_id=1, source_target_pairs={{0,12},{4,0},{8,4},{12,8},{1,13},{5,1},{9,5},{13,9},{2,14},{6,2},{... | collective-permute-start | bytes 786440 | tf_op jit(solution)/shard_map/ppermute | solution.py:46
  165.1 9.5 %collective-permute-start.34 = (bf16[128,1024]{1,0:T(8,128)(2,1)S(1)}, bf16[128,1024]{1,0:T(8,128)(2,1)S(1)}, u32[]{:S(2)}, u32[]{:S(2)}) collective-permute-start(bf16[128,1024]{1,0:T(8,128)(2,1)S(1)} %collective-permute-done.32.refs_5_), channel_id=1, source_target_pairs={{0,4},{4,8},{8,12},{12,0},{1,5},{5,9},{9,13},{13,1},{2,6},{6,10},{... | collective-permute-start | bytes 786440 | tf_op jit(solution)/shard_map/ppermute | solution.py:48
  165.4 9.7 %collective-permute-start.36 = (bf16[128,1024]{1,0:T(8,128)(2,1)S(1)}, bf16[128,1024]{1,0:T(8,128)(2,1)S(1)}, u32[]{:S(2)}, u32[]{:S(2)}) collective-permute-start(bf16[128,1024]{1,0:T(8,128)(2,1)S(1)} %collective-permute-done.28.refs_1_), channel_id=1, source_target_pairs={{0,1},{1,0},{2,3},{3,2},{4,5},{5,4},{6,7},{7,6},{8,9},{9,8},{10,11... | collective-permute-start | bytes 786440 | tf_op jit(solution)/shard_map/ppermute | solution.py:30
  165.4 9.7 %collective-permute-start.40 = (bf16[128,1024]{1,0:T(8,128)(2,1)S(1)}, bf16[128,1024]{1,0:T(8,128)(2,1)S(1)}, u32[]{:S(2)}, u32[]{:S(2)}) collective-permute-start(bf16[128,1024]{1,0:T(8,128)(2,1)S(1)} %collective-permute-done.32.refs_5_), channel_id=1, source_target_pairs={{0,1},{1,0},{2,3},{3,2},{4,5},{5,4},{6,7},{7,6},{8,9},{9,8},{10,11... | collective-permute-start | bytes 786440 | tf_op jit(solution)/shard_map/ppermute | solution.py:30
  169.8 5.3 %collective-permute-start.41 = (bf16[128,1024]{1,0:T(8,128)(2,1)S(1)}, bf16[128,1024]{1,0:T(8,128)(2,1)S(1)}, u32[]{:S(2)}, u32[]{:S(2)}) collective-permute-start(bf16[128,1024]{1,0:T(8,128)(2,1)S(1)} %collective-permute-done.33.refs_6_), channel_id=1, source_target_pairs={{0,1},{1,0},{2,3},{3,2},{4,5},{5,4},{6,7},{7,6},{8,9},{9,8},{10,11... | collective-permute-start | bytes 786440 | tf_op jit(solution)/shard_map/ppermute | solution.py:30
  174.6 1.5 collective-permute-start.38
  174.6 1.9 collective-permute-start.42
  179.6 19.3 %copy-start.2 = (bf16[320,1024]{1,0:T(8,128)(2,1)S(1)}, bf16[320,1024]{1,0:T(8,128)(2,1)}, u32[]{:S(2)}) copy-start(bf16[320,1024]{1,0:T(8,128)(2,1)} %param.4) | copy-start | bytes 1966084
  195.3 13.5 %all-to-all-start.4 = ((bf16[8,320,128]{2,1,0:T(8,128)(2,1)}), bf16[8,320,128]{2,1,0:T(8,128)(2,1)S(1)}, u32[]{:S(2)}, u32[]{:S(2)}) async-start(bf16[8,320,128]{2,1,0:T(8,128)(2,1)} %broadcast_in_dim.2), calls=%async_computation.4 | async-start | bytes 1310720 | tf_op jit(solution)/shard_map/all_to_all | solution.py:34

commit v8 on v7

--- a/solution.py
+++ b/solution.py
@@ -72,8 +72,8 @@
 
 def score_kernel(place, *refs):
     key_refs, query_refs = refs[:8], refs[8:24]
-    (mates, w_ref, row_ref, col_ref, all_ref) = refs[24:29]
-    (keys, queries, held, lanes, sums, key_sem, query_sem, out_sem, all_sem) = refs[29:]
+    (mates, w_ref, row_ref, hit_ref, col_ref, all_ref) = refs[24:30]
+    (keys, queries, held, lanes, hit_lanes, sums, key_sem, query_sem, out_sem, all_sem) = refs[30:]
     step = pl.program_id(0)
 
     def key_copy(i):
@@ -111,7 +111,7 @@
             for copy in query_copies(n):
                 copy.start()
         lanes[...] = jnp.zeros_like(lanes)
-        sums[...] = jnp.zeros_like(sums)
+        hit_lanes[...] = jnp.zeros_like(hit_lanes)
         for i in range(8):
             key_copy(i).wait()
 
@@ -124,7 +124,6 @@
         near, far = query_chunks(place, n)
         mate = jnp.concatenate([mates[near], mates[far]], axis=1)
         col = jnp.zeros((8, PAIR), F32)
-        pos = jnp.zeros((8, PAIR), F32)
         block = lax.dot_general(
             keys[...], queries[n], (((1,), (1,)), ((), ())), preferred_element_type=F32
         )
@@ -138,15 +137,14 @@
                 lane = lax.broadcasted_iota(I32, (1, PAIR), 1)
                 qid = group + lane % ROWS + jnp.where(lane < ROWS, near, far) * ROWS
                 weights = jnp.where(kid != qid, weights, 0.0)
-            held[n % 2, at, :] = weights
+            held[n % 2, at, :] = weights.astype(BF16)
             lanes[at, :] += weights[:, :ROWS] + weights[:, ROWS:]
-            hits = jnp.where(kid == mate, scores, 0.0)
+            hits = jnp.where(kid == mate, weights, 0.0)
+            hit_lanes[at, :] += hits[:, :ROWS] + hits[:, ROWS:]
             col = col + jnp.sum(weights.reshape(PAIR // 8, 8, PAIR), axis=0)
-            pos = pos + jnp.sum(hits.reshape(PAIR // 8, 8, PAIR), axis=0)
         col = jnp.sum(col, axis=0, keepdims=True)
         sums[pl.ds(near, 1), :] = col[:, :ROWS]
         sums[pl.ds(far, 1), :] = col[:, ROWS:]
-        sums[16:24, :] += pos[:, :ROWS] + pos[:, ROWS:]
         out_copy(n).start()
 
     for n in range(8):
@@ -157,23 +155,27 @@
 
     @pl.when(step == 7)
     def _():
-        for device in range(16):
-            col_ref[device] = sums[...]
         for p in range(4):
             for which in (0, 1):
                 at = pl.ds(p * PAIR + which * ROWS, ROWS)
-                row_ref[pl.ds(chunk_of(place[0], p, which, place[1]), 1), :] = jnp.sum(
-                    lanes[at, :].T, axis=0, keepdims=True
+                chunk = chunk_of(place[0], p, which, place[1])
+                hits = jnp.sum(hit_lanes[at, :].T, axis=0, keepdims=True)
+                hit_ref[pl.ds(chunk, 1), :] = hits
+                row_ref[pl.ds(chunk, 1), :] = jnp.sum(lanes[at, :].T, axis=0, keepdims=True)
+                found = hits > 0.0
+                sums[16 + 2 * p + which : 17 + 2 * p + which, :] = jnp.where(
+                    found, jnp.log(jnp.where(found, hits, 1.0)), 0.0
                 )
+        for device in range(16):
+            col_ref[device] = sums[...]
         out_copy(6).wait()
         out_copy(7).wait()
         for n in range(8):
             all_copy(n).wait()
 
 
-def grad_kernel(place, w_ref, query_ref, r0, r1, r2, r3, cols_ref, mates, *refs):
+def grad_kernel(place, w_ref, query_ref, hit_ref, r0, r1, r2, r3, cols_ref, mates, *refs):
     out_ref, rider_ref, weights, queries, w_sem, query_sem, rk_ref, rq_ref = refs
-    step = pl.program_id(0)
 
     def w_copy(p):
         return pltpu.make_async_copy(
@@ -182,56 +184,56 @@
 
     query_copy = pltpu.make_async_copy(query_ref, queries, query_sem)
 
-    @pl.when(step == 0)
-    def _():
-        w_copy(0).start()
-        query_copy.start()
-        for p in range(1, 4):
-            w_copy(p).start()
-        cols = cols_ref[0]
-        for device in range(1, 16):
-            cols = cols + cols_ref[device]
-        den = cols[:16]
-        rq_ref[...] = 20.0 / den
-        rk_ref[...] = 20.0 / (r0[...] + r1[...] + r2[...] + r3[...])
-        logs = jnp.sum(jnp.log(den), axis=0, keepdims=True)
-        logs = logs - 20.0 * jnp.sum(cols[16:], axis=0, keepdims=True)
-        loss = jnp.broadcast_to(jnp.sum(logs, axis=1, keepdims=True), (16, ROWS))
-        row = lax.broadcasted_iota(I32, (16, ROWS), 0)
-        rider = jnp.zeros((16, ROWS), F32)
-        for i in range(3):
-            term = loss.astype(BF16).astype(F32)
-            rider = jnp.where(row == i, term, rider)
-            loss = loss - term
-        rider_ref[...] = rider.astype(BF16)
-        query_copy.wait()
-
-    def column(chunk):
-        return jnp.broadcast_to(rk_ref[pl.ds(chunk, 1), :], (ROWS, ROWS)).T
+    w_copy(0).start()
+    query_copy.start()
+    for p in range(1, 4):
+        w_copy(p).start()
+    cols = cols_ref[0]
+    for device in range(1, 16):
+        cols = cols + cols_ref[device]
+    den = cols[:16]
+    rq_ref[...] = 20.0 / den
+    rk_ref[...] = 20.0 / (r0[...] + r1[...] + r2[...] + r3[...])
+    logs = jnp.sum(jnp.log(den), axis=0, keepdims=True)
+    logs = logs - jnp.sum(cols[16:], axis=0, keepdims=True)
+    loss = jnp.broadcast_to(jnp.sum(logs, axis=1, keepdims=True), (16, ROWS))
+    row = lax.broadcasted_iota(I32, (16, ROWS), 0)
+    rider = jnp.zeros((16, ROWS), F32)
+    for i in range(3):
+        term = loss.astype(BF16).astype(F32)
+        rider = jnp.where(row == i, term, rider)
+        loss = loss - term
+    rider_ref[...] = rider.astype(BF16)
+
+    def columns(source, p):
+        chunks = [chunk_of(place[0], p, which, place[1]) for which in (0, 1)]
+        return jnp.concatenate(
+            [jnp.broadcast_to(source[pl.ds(chunk, 1), :], (ROWS, ROWS)).T for chunk in chunks], axis=0
+        )
 
     def run(p):
         w_copy(p).wait()
         kid = key_column(place, p)
-        rk = jnp.concatenate(
-            [column(chunk_of(place[0], p, which, place[1])) for which in (0, 1)], axis=0
-        )
+        rk, hit_weights = columns(rk_ref, p), columns(hit_ref, p)
         parts = []
         for n in range(8):
             for which, chunk in enumerate(query_chunks(place, n)):
                 start = n * PAIR + which * ROWS
-                grads = weights[p, :, start : start + ROWS] * (rk + rq_ref[pl.ds(chunk, 1), :])
-                parts.append(jnp.where(kid == mates[chunk], grads - 40.0, grads).astype(BF16))
+                hit = kid == mates[chunk]
+                chosen = jnp.where(hit, hit_weights, weights[p, :, start : start + ROWS].astype(F32))
+                grads = chosen * (rk + rq_ref[pl.ds(chunk, 1), :])
+                parts.append(jnp.where(hit, grads - 40.0, grads).astype(BF16))
+        if p == 0:
+            query_copy.wait()
         total = jnp.dot(
             jnp.concatenate(parts, axis=1), queries[...], preferred_element_type=F32
         ).astype(BF16)
-        out_ref[0, place[1]] = total[:ROWS]
-        out_ref[0, 1 - place[1]] = total[ROWS:]
+        at = lax.rem(place[0] + OFFSET[p], 4)
+        out_ref[at, place[1]] = total[:ROWS]
+        out_ref[at, 1 - place[1]] = total[ROWS:]
 
     for p in range(4):
-
-        @pl.when(step == p)
-        def _(p=p):
-            run(p)
+        run(p)
 
 
 def head_kernel(place, summaries, rider, *refs):
@@ -275,13 +277,15 @@
             out_specs=[
                 pl.BlockSpec(memory_space=pltpu.HBM),
                 whole((8, ROWS)),
+                whole((8, ROWS)),
                 whole((16, 24, ROWS)),
                 pl.BlockSpec(memory_space=pltpu.HBM),
             ],
             scratch_shapes=[
                 pltpu.VMEM((HALF, WIDTH), BF16),
                 pltpu.VMEM((8, PAIR, WIDTH), BF16),
-                pltpu.VMEM((2, HALF, PAIR), F32),
+                pltpu.VMEM((2, HALF, PAIR), BF16),
+                pltpu.VMEM((HALF, ROWS), F32),
                 pltpu.VMEM((HALF, ROWS), F32),
                 pltpu.VMEM((24, ROWS), F32),
                 pltpu.SemaphoreType.DMA((8,)),
@@ -291,7 +295,8 @@
             ],
         ),
         out_shape=[
-            pltpu.HBM((HALF, GROUP), F32),
+            pltpu.HBM((HALF, GROUP), BF16),
+            jax.ShapeDtypeStruct((8, ROWS), F32),
             jax.ShapeDtypeStruct((8, ROWS), F32),
             jax.ShapeDtypeStruct((16, 24, ROWS), F32),
             pltpu.HBM((GROUP, WIDTH), BF16),
@@ -304,26 +309,18 @@
     )(place, *keys, *queries, mates)
 
 
-def grad_call(place, weights, rows, cols, mates, queries):
+def grad_call(place, weights, hits, rows, cols, mates, queries):
     return pl.pallas_call(
         grad_kernel,
         grid_spec=pltpu.PrefetchScalarGridSpec(
             num_scalar_prefetch=1,
-            grid=(4,),
+            grid=(1,),
             in_specs=[pl.BlockSpec(memory_space=pltpu.HBM)] * 2
-            + [whole((8, ROWS))] * 4
+            + [whole((8, ROWS))] * 5
             + [whole((16, 24, ROWS)), whole((16, 1, ROWS))],
-            out_specs=[pl.BlockSpec(
-                (1, 2, ROWS, WIDTH),
-                lambda t, place: (
-                    lax.rem(place[0] + t + jnp.where(t == 2, 1, 0) - jnp.where(t == 3, 1, 0), 4),
-                    0,
-                    0,
-                    0,
-                ),
-            ), whole((16, ROWS))],
+            out_specs=[whole((4, 2, ROWS, WIDTH)), whole((16, ROWS))],
             scratch_shapes=[
-                pltpu.VMEM((4, PAIR, GROUP), F32),
+                pltpu.VMEM((4, PAIR, GROUP), BF16),
                 pltpu.VMEM((GROUP, WIDTH), BF16),
                 pltpu.SemaphoreType.DMA((4,)),
                 pltpu.SemaphoreType.DMA,
@@ -340,7 +337,7 @@
             flops=2 * HALF * GROUP * WIDTH, bytes_accessed=14 << 20, transcendentals=0
         ),
         name="grads",
-    )(place, in_hbm(weights), in_hbm(queries), *rows, cols, mates)
+    )(place, in_hbm(weights), in_hbm(queries), hits, *rows, cols, mates)
 
 
 def head_call(place, summaries, rider, pieces):
@@ -393,12 +390,12 @@
     keys = gather_ring(emb, "x", "zl")
     queries = gather_ring(emb, "y", "zh")
     queries = queries + [core_swap(piece) for piece in queries]
-    weights, row_part, col_part, queries = score_call(place, keys, queries, mates)
+    weights, row_part, hits, col_part, queries = score_call(place, keys, queries, mates)
 
     cols = lax.all_to_all(col_part, CUTS, 0, 0)
     row_part = row_part + lax.ppermute(row_part, "zl", SWAP)
     rows = [row_part] + [lax.ppermute(row_part, "x", RING[s]) for s in (1, 3, 2)]
-    grad_part, rider = grad_call(place, weights, rows, cols, mates, queries)
+    grad_part, rider = grad_call(place, weights, hits, rows, cols, mates, queries)
     grad_emb = sum_exchange(grad_part.reshape(8, ROWS, WIDTH), XZ)
     grad_z = (inv * (grad_emb - unit * jnp.sum(unit * grad_emb, axis=1, keepdims=True))).astype(BF16)
 

time: 212 us -> 211 us (level)
  no operation moved by 1% of the time
where the time goes in v8:
time: 211 us; the launch traced here: 210 us
  blocking collectives  78.6 us (37%)
  waiting for transfers between devices  46.7 us (22%)
  starting transfers between devices  45.6 us (22%)
  Pallas kernels  21.9 us (10%)
  matrix products  8.73 us (4%)
  other arithmetic  3.22 us (2%)
  between operations  2.61 us (1%)
  local copies, waits for them, and re-layouts  2.17 us (1%)
    all_to_all x2, blocking collectives, sum_exchange(): return jnp.sum(lax.all_to_all(parts, axes, 0, 0).astype(F32), axis=0)  63.9 us
    all_to_all x1, blocking collectives, shards(): pieces = lax.all_to_all(head_part, XZ, 0, 0)  14.7 us
    pallas_call x1, Pallas kernels, score_call(): pl.pallas_call(score_kernel, grid_spec=pltpu.PrefetchScalarGridSpec(num_s...  9.76 us
    pallas_call x1, Pallas kernels, grad_call(): pl.pallas_call(grad_kernel, grid_spec=pltpu.PrefetchScalarGridSpec(num_sc...  9.1 us
    ppermute x3, starting transfers between devices, gather_ring(): after_other = lax.ppermute(other, long_axis, RING[3])  7.26 us
    ppermute x3, waiting for transfers between devices, gather_ring(): far_own = lax.ppermute(after_own, long_axis, RING[3])  7.14 us
    ppermute x3, waiting for transfers between devices, gather_ring(): other = lax.ppermute(own, short_axis, SWAP)  7.09 us
    ppermute x3, waiting for transfers between devices, gather_ring(): after_other = lax.ppermute(other, long_axis, RING[3])  7.02 us
  transfers between devices with their start and end apart: 45, of which 23 were waited for; matrix products, arithmetic and copies ran while one was open for 4% of the time, Pallas kernels for 0%

profile of v8, /device:TPU:0, one launch (start us, length us, event | category | flops | bytes accessed | tf_op | source)
XLA Modules:
  0.0 209.6 jit_solution(4752814844716793322)
XLA Ops:
  0.6 1.1 dynamic-slice_bitcast_fusion
  2.4 2.6 %fusion = f32[1024,1024]{1,0:T(8,128)S(1)} fusion(bf16[320,1024]{1,0:T(8,128)(2,1)} %param.4, bf16[2048,320]{0,1:T(8,128)(2,1)} %param.3, s32[]{:T(128)S(6)} %select_n.6), kind=kOutput, calls=%fused_computation.8 | convolution fusion | flops 671088640 | bytes 5505028 | tf_op jit(solution)/shard_map/dot_general | solution.py:381
  5.1 1.3 add_convert_fusion
  6.5 36.1 %all_to_all.25 = bf16[8,128,1024]{2,1,0:T(8,128)(2,1)S(1)} all-to-all(bf16[8,128,1024]{2,1,0:T(8,128)(2,1)S(1)} %bitcast.26), channel_id=1, replica_groups=mesh['x'=4,'zl'=2,'y'=4,'zh'=2,'c'=2] {'y','zh'}, dimensions={0} | all-to-all | bytes 4194304 | tf_op jit(solution)/shard_map/all_to_all | solution.py:38
  43.5 3.0 %collective-permute-start.10 = (bf16[128,1024]{1,0:T(8,128)(2,1)S(1)}, bf16[128,1024]{1,0:T(8,128)(2,1)S(1)}, u32[]{:S(2)}, u32[]{:S(2)}) collective-permute-start(bf16[128,1024]{1,0:T(8,128)(2,1)S(1)} %multiply_convert_fusion.1.refs_0_.refs_8_), channel_id=1, source_target_pairs={{0,12},{4,0},{8,4},{12,8},{1,13},{5,1},{9,5},{13,9},{2,14},{6,2},{... | collective-permute-start | bytes 786440 | tf_op jit(solution)/shard_map/ppermute | solution.py:43
  46.5 1.2 collective-permute-start.9
  47.7 1.5 collective-permute-start.5
  49.2 1.7 collective-permute-start.3
  50.9 2.2 %collective-permute-done.12.refs_12_ = bf16[128,1024]{1,0:T(8,128)(2,1)S(1)} collective-permute-done((bf16[128,1024]{1,0:T(8,128)(2,1)S(1)}, bf16[128,1024]{1,0:T(8,128)(2,1)S(1)}, u32[]{:S(2)}, u32[]{:S(2)}) %collective-permute-start.12) | collective-permute-done | bytes 262176 | tf_op jit(solution)/shard_map/ppermute | solution.py:44
  53.1 1.0 collective-permute-start.2
  54.1 1.9 collective-permute-done.9.refs_9_
  57.0 4.0 %collective-permute-done.2.refs_1_ = bf16[128,1024]{1,0:T(8,128)(2,1)S(1)} collective-permute-done((bf16[128,1024]{1,0:T(8,128)(2,1)S(1)}, bf16[128,1024]{1,0:T(8,128)(2,1)S(1)}, u32[]{:S(2)}, u32[]{:S(2)}) %collective-permute-start.2) | collective-permute-done | bytes 262176 | tf_op jit(solution)/shard_map/ppermute | solution.py:42
  61.0 3.2 %collective-permute-start.11 = (bf16[128,1024]{1,0:T(8,128)(2,1)S(1)}, bf16[128,1024]{1,0:T(8,128)(2,1)S(1)}, u32[]{:S(2)}, u32[]{:S(2)}) collective-permute-start(bf16[128,1024]{1,0:T(8,128)(2,1)S(1)} %collective-permute-done.9.refs_9_), channel_id=1, source_target_pairs={{0,12},{4,0},{8,4},{12,8},{1,13},{5,1},{9,5},{13,9},{2,14},{6,2},{... | collective-permute-start | bytes 786440 | tf_op jit(solution)/shard_map/ppermute | solution.py:46
  64.2 2.8 %collective-permute-start.7 = (bf16[128,1024]{1,0:T(8,128)(2,1)S(1)}, bf16[128,1024]{1,0:T(8,128)(2,1)S(1)}, u32[]{:S(2)}, u32[]{:S(2)}) collective-permute-start(bf16[128,1024]{1,0:T(8,128)(2,1)S(1)} %collective-permute-done.3.refs_2_), channel_id=1, source_target_pairs={{0,96},{32,0},{64,32},{96,64},{1,97},{33,1},{65,33},{97,65},{2,98}... | collective-permute-start | bytes 786440 | tf_op jit(solution)/shard_map/ppermute | solution.py:45
  67.0 3.2 %collective-permute-start.4 = (bf16[128,1024]{1,0:T(8,128)(2,1)S(1)}, bf16[128,1024]{1,0:T(8,128)(2,1)S(1)}, u32[]{:S(2)}, u32[]{:S(2)}) collective-permute-start(bf16[128,1024]{1,0:T(8,128)(2,1)S(1)} %collective-permute-done.2.refs_1_), channel_id=1, source_target_pairs={{0,96},{32,0},{64,32},{96,64},{1,97},{33,1},{65,33},{97,65},{2,98}... | collective-permute-start | bytes 786440 | tf_op jit(solution)/shard_map/ppermute | solution.py:46
  70.4 3.3 %collective-permute-done.7.refs_6_ = bf16[128,1024]{1,0:T(8,128)(2,1)S(1)} collective-permute-done((bf16[128,1024]{1,0:T(8,128)(2,1)S(1)}, bf16[128,1024]{1,0:T(8,128)(2,1)S(1)}, u32[]{:S(2)}, u32[]{:S(2)}) %collective-permute-start.7) | collective-permute-done | bytes 262176 | tf_op jit(solution)/shard_map/ppermute | solution.py:45
  74.6 1.9 collective-permute-done.4.refs_3_
  76.5 1.2 collective-permute-start.8
  77.8 6.7 %collective-permute-done.8.refs_7_ = bf16[128,1024]{1,0:T(8,128)(2,1)S(1)} collective-permute-done((bf16[128,1024]{1,0:T(8,128)(2,1)S(1)}, bf16[128,1024]{1,0:T(8,128)(2,1)S(1)}, u32[]{:S(2)}, u32[]{:S(2)}) %collective-permute-start.8) | collective-permute-done | bytes 262176 | tf_op jit(solution)/shard_map/ppermute | solution.py:48
  84.6 9.8 %scores.1 = (bf16[1024,2048]{1,0:T(8,128)(2,1)}, f32[8,128]{1,0:T(8,128)S(1)}, f32[8,128]{1,0:T(8,128)S(1)}, f32[16,24,128]{2,1,0:T(8,128)}, bf16[2048,1024]{1,0:T(8,128)(2,1)}) custom-call(s32[5]{0:T(128)S(1)} %stack.23.place, bf16[128,1024]{1,0:T(8,128)(2,1)S(1)} %multiply_convert_fusion.1.refs_0_.refs_8_, ...), custom_call_target="tpu_custom_call" | custom-call | flops 4294967296 | bytes 14680064 | tf_op jit(solution)/shard_map/scores/pallas_call | solution.py:271
  94.3 4.0 %all-to-all-start.1 = ((f32[16,24,128]{2,1,0:T(8,128)}), f32[16,24,128]{2,1,0:T(8,128)S(1)}, u32[]{:S(2)}, u32[]{:S(2)}) async-start(f32[16,24,128]{2,1,0:T(8,128)} %get-tuple-element.22), calls=%async_computation.1 | async-start | bytes 393216 | tf_op jit(solution)/shard_map/all_to_all | solution.py:395
  98.4 1.1 collective-permute-start.24
  99.4 2.6 %collective-permute-done.24 = f32[8,128]{1,0:T(8,128)S(1)} collective-permute-done((f32[8,128]{1,0:T(8,128)S(1)}, f32[8,128]{1,0:T(8,128)S(1)}, u32[]{:S(2)}, u32[]{:S(2)}) %collective-permute-start.24) | collective-permute-done | bytes 4128 | tf_op jit(solution)/shard_map/ppermute | solution.py:396
  102.0 1.1 collective-permute-start.27
  103.1 1.1 collective-permute-start.26
  104.3 0.9 collective-permute-start.25
  105.1 2.0 collective-permute-done.27.r3
  107.2 1.9 collective-permute-done.25.r1
  109.1 9.1 %grads.1 = (bf16[4,2,128,1024]{3,2,1,0:T(8,128)(2,1)S(1)}, bf16[16,128]{1,0:T(8,128)(2,1)S(1)}) custom-call(s32[5]{0:T(128)S(1)} %stack.23.place, bf16[1024,2048]{1,0:T(8,128)(2,1)} %get-tuple-element.18.w_ref, bf16[2048,1024]{1,0:T(8,128)(2,1)} %get-tuple-element.19.query_ref, f32[8,128]{1,0:T(8,128)S(1)} %get-tuple-element.20.hit_ref, ...), custom_call_target="tpu_custom_call" | custom-call | flops 4294967296 | bytes 14680064 | tf_op jit(solution)/shard_map/grads/pallas_call | solution.py:313
  118.2 27.8 %all_to_all.26 = bf16[8,128,1024]{2,1,0:T(8,128)(2,1)S(1)} all-to-all(bf16[8,128,1024]{2,1,0:T(8,128)(2,1)S(1)} %bitcast.23), channel_id=1, replica_groups=mesh['x'=4,'zl'=2,'y'=4,'zh'=2,'c'=2] {'x','zl'}, dimensions={0} | all-to-all | bytes 4194304 | tf_op jit(solution)/shard_map/all_to_all | solution.py:38
  146.8 3.5 %collective-permute-start.28 = (bf16[128,1024]{1,0:T(8,128)(2,1)S(1)}, bf16[128,1024]{1,0:T(8,128)(2,1)S(1)}, u32[]{:S(2)}, u32[]{:S(2)}) collective-permute-start(bf16[128,1024]{1,0:T(8,128)(2,1)S(1)} %multiply_convert_fusion.refs_0_), channel_id=1, source_target_pairs={{0,2},{2,0},{1,3},{3,1},{4,6},{6,4},{5,7},{7,5},{8,10},{10,8},{9,1... | collective-permute-start | bytes 786440 | tf_op jit(solution)/shard_map/ppermute | solution.py:42
  150.3 1.5 collective-permute-start.31
  151.7 1.8 collective-permute-start.29
  153.5 1.2 collective-permute-done.28.refs_1_
  154.7 1.6 collective-permute-start.32
  156.3 1.6 collective-permute-done.31.refs_4_
  158.4 3.0 %collective-permute-start.33 = (bf16[128,1024]{1,0:T(8,128)(2,1)S(1)}, bf16[128,1024]{1,0:T(8,128)(2,1)S(1)}, u32[]{:S(2)}, u32[]{:S(2)}) collective-permute-start(bf16[128,1024]{1,0:T(8,128)(2,1)S(1)} %collective-permute-done.29.refs_2_), channel_id=1, source_target_pairs={{0,12},{4,0},{8,4},{12,8},{1,13},{5,1},{9,5},{13,9},{2,14},{6,2},{... | collective-permute-start | bytes 786440 | tf_op jit(solution)/shard_map/ppermute | solution.py:45
  162.2 1.3 collective-permute-done.32.refs_5_
  164.3 3.8 %collective-permute-done.33.refs_6_ = bf16[128,1024]{1,0:T(8,128)(2,1)S(1)} collective-permute-done((bf16[128,1024]{1,0:T(8,128)(2,1)S(1)}, bf16[128,1024]{1,0:T(8,128)(2,1)S(1)}, u32[]{:S(2)}, u32[]{:S(2)}) %collective-permute-start.33) | collective-permute-done | bytes 262176 | tf_op jit(solution)/shard_map/ppermute | solution.py:45
  168.1 4.9 %collective-permute-done.30.refs_3_ = bf16[128,1024]{1,0:T(8,128)(2,1)S(1)} collective-permute-done((bf16[128,1024]{1,0:T(8,128)(2,1)S(1)}, bf16[128,1024]{1,0:T(8,128)(2,1)S(1)}, u32[]{:S(2)}, u32[]{:S(2)}) %collective-permute-start.30) | collective-permute-done | bytes 262176 | tf_op jit(solution)/shard_map/ppermute | solution.py:46
  173.5 1.0 collective-permute-done.38.refs_11_
  174.9 3.0 %head_parts.1 = (bf16[8,336,128]{2,1,0:T(8,128)(2,1)S(1)}, bf16[2048,1024]{1,0:T(8,128)(2,1)}) custom-call(s32[5]{0:T(128)S(1)} %stack.23.place, bf16[320,2048]{1,0:T(8,128)(2,1)S(1)} %bitcast.22, bf16[16,128]{1,0:T(8,128)(2,1)S(1)} %get-tuple-element.23.rider, bf16[128,1024]{1,0:T(8,128)(2,1)S(1)} %multiply_convert_fusion.refs_0_, ...), custom_call_target="tpu_custom_call" | custom-call | flops 1342177280 | bytes 10485760 | tf_op jit(solution)/shard_map/head_parts/pallas_call | solution.py:345
  177.9 14.7 %all_to_all.27 = bf16[8,336,128]{2,1,0:T(8,128)(2,1)S(1)} all-to-all(bf16[8,336,128]{2,1,0:T(8,128)(2,1)S(1)} %get-tuple-element.25), channel_id=1, replica_groups=mesh['x'=4,'zl'=2,'y'=4,'zh'=2,'c'=2] {'x','zl'}, dimensions={0} | all-to-all | bytes 1376256 | tf_op jit(solution)/shard_map/all_to_all | solution.py:405
  192.8 0.9 broadcast_in_dim.2
  193.7 3.5 %all-to-all-start.4 = ((bf16[8,320,128]{2,1,0:T(8,128)(2,1)}), bf16[8,320,128]{2,1,0:T(8,128)(2,1)S(1)}, u32[]{:S(2)}, u32[]{:S(2)}) async-start(bf16[8,320,128]{2,1,0:T(8,128)(2,1)} %broadcast_in_dim.2), calls=%async_computation.4 | async-start | bytes 1310720 | tf_op jit(solution)/shard_map/all_to_all | solution.py:34
  197.3 4.8 %convolution_convert_fusion = bf16[2048,320]{0,1:T(8,128)(2,1)} fusion(bf16[2048,1024]{1,0:T(8,128)(2,1)} %get-tuple-element.26, bf16[320,1024]{1,0:T(8,128)(2,1)S(1)} %copy-done.2), kind=kOutput, calls=%fused_computation.3 | convolution fusion | flops 1342832640 | bytes 6160384 | tf_op jit(solution)/shard_map/dot_general | solution.py:413
  203.3 3.9 %all-to-all-done.4 = bf16[8,320,128]{2,1,0:T(8,128)(2,1)S(1)} async-done(((bf16[8,320,128]{2,1,0:T(8,128)(2,1)}), bf16[8,320,128]{2,1,0:T(8,128)(2,1)S(1)}, u32[]{:S(2)}, u32[]{:S(2)}) %all-to-all-start.4) | async-done | bytes 655392 | tf_op jit(solution)/shard_map/all_to_all | solution.py:34
  207.2 1.2 copy_bitcast_fusion
  (72 shorter events, 8.2 us)
Async XLA Ops:
  1.8 3.3 %collective-permute-start = (bf16[320,1024]{1,0:T(8,128)(2,1)S(1)}, bf16[320,1024]{1,0:T(8,128)(2,1)S(1)}, u32[]{:S(2)}, u32[]{:S(2)}) collective-permute-start(bf16[320,1024]{1,0:T(8,128)(2,1)S(1)} %dynamic-slice_bitcast_fusion), channel_id=1, source_target_pairs={{0,1},{1,0},{2,3},{3,2},{4,5},{5,4},{6,7},{7,6},{8,9},{9,8},{10,11... | collective-permute-start | bytes 1966088 | tf_op jit(solution)/shard_map/ppermute | solution.py:30
  1.9 3.2 %collective-permute-start.1 = (bf16[320,1024]{1,0:T(8,128)(2,1)}, bf16[320,1024]{1,0:T(8,128)(2,1)S(1)}, u32[]{:S(2)}, u32[]{:S(2)}) collective-permute-start(bf16[320,1024]{1,0:T(8,128)(2,1)} %param.4), channel_id=1, source_target_pairs={{0,1},{1,0},{2,3},{3,2},{4,5},{5,4},{6,7},{7,6},{8,9},{9,8},{10,11... | collective-permute-start | bytes 1966088 | tf_op jit(solution)/shard_map/ppermute | solution.py:30
  42.5 42.1 %copy-start.1 = (s32[2048]{0:T(1024)S(1)}, s32[2048]{0:T(1024)}, u32[]{:S(2)}) copy-start(s32[2048]{0:T(1024)} %param.5) | copy-start | bytes 24580
  43.1 6.1 %collective-permute-start.16 = (bf16[128,1024]{1,0:T(8,128)(2,1)S(1)}, bf16[128,1024]{1,0:T(8,128)(2,1)S(1)}, u32[]{:S(2)}, u32[]{:S(2)}) collective-permute-start(bf16[128,1024]{1,0:T(8,128)(2,1)S(1)} %multiply_convert_fusion.1.refs_0_.refs_8_), channel_id=1, source_target_pairs={{0,1},{1,0},{2,3},{3,2},{4,5},{5,4},{6,7},{7,6},{8,9},{9,8},{10,11... | collective-permute-start | bytes 786440 | tf_op jit(solution)/shard_map/ppermute | solution.py:30
  43.2 9.9 %collective-permute-start.12 = (bf16[128,1024]{1,0:T(8,128)(2,1)S(1)}, bf16[128,1024]{1,0:T(8,128)(2,1)S(1)}, u32[]{:S(2)}, u32[]{:S(2)}) collective-permute-start(bf16[128,1024]{1,0:T(8,128)(2,1)S(1)} %multiply_convert_fusion.1.refs_0_.refs_8_), channel_id=1, source_target_pairs={{0,4},{4,8},{8,12},{12,0},{1,5},{5,9},{9,13},{13,1},{2,6},{6,10},{... | collective-permute-start | bytes 786440 | tf_op jit(solution)/shard_map/ppermute | solution.py:44
  43.5 10.6 %collective-permute-start.10 = (bf16[128,1024]{1,0:T(8,128)(2,1)S(1)}, bf16[128,1024]{1,0:T(8,128)(2,1)S(1)}, u32[]{:S(2)}, u32[]{:S(2)}) collective-permute-start(bf16[128,1024]{1,0:T(8,128)(2,1)S(1)} %multiply_convert_fusion.1.refs_0_.refs_8_), channel_id=1, source_target_pairs={{0,12},{4,0},{8,4},{12,8},{1,13},{5,1},{9,5},{13,9},{2,14},{6,2},{... | collective-permute-start | bytes 786440 | tf_op jit(solution)/shard_map/ppermute | solution.py:43
  46.5 9.6 %collective-permute-start.9 = (bf16[128,1024]{1,0:T(8,128)(2,1)S(1)}, bf16[128,1024]{1,0:T(8,128)(2,1)S(1)}, u32[]{:S(2)}, u32[]{:S(2)}) collective-permute-start(bf16[128,1024]{1,0:T(8,128)(2,1)S(1)} %multiply_convert_fusion.1.refs_0_.refs_8_), channel_id=1, source_target_pairs={{0,2},{2,0},{1,3},{3,1},{4,6},{6,4},{5,7},{7,5},{8,10},{10,8},{9,1... | collective-permute-start | bytes 786440 | tf_op jit(solution)/shard_map/ppermute | solution.py:42
  47.7 9.0 %collective-permute-start.5 = (bf16[128,1024]{1,0:T(8,128)(2,1)S(1)}, bf16[128,1024]{1,0:T(8,128)(2,1)S(1)}, u32[]{:S(2)}, u32[]{:S(2)}) collective-permute-start(bf16[128,1024]{1,0:T(8,128)(2,1)S(1)} %multiply_convert_fusion.1.refs_0_.refs_8_), channel_id=1, source_target_pairs={{0,32},{32,64},{64,96},{96,0},{1,33},{33,65},{65,97},{97,1},{2,34}... | collective-permute-start | bytes 786440 | tf_op jit(solution)/shard_map/ppermute | solution.py:44
  49.2 7.8 %collective-permute-start.3 = (bf16[128,1024]{1,0:T(8,128)(2,1)S(1)}, bf16[128,1024]{1,0:T(8,128)(2,1)S(1)}, u32[]{:S(2)}, u32[]{:S(2)}) collective-permute-start(bf16[128,1024]{1,0:T(8,128)(2,1)S(1)} %multiply_convert_fusion.1.refs_0_.refs_8_), channel_id=1, source_target_pairs={{0,96},{32,0},{64,32},{96,64},{1,97},{33,1},{65,33},{97,65},{2,98}... | collective-permute-start | bytes 786440 | tf_op jit(solution)/shard_map/ppermute | solution.py:43
  53.1 7.9 %collective-permute-start.2 = (bf16[128,1024]{1,0:T(8,128)(2,1)S(1)}, bf16[128,1024]{1,0:T(8,128)(2,1)S(1)}, u32[]{:S(2)}, u32[]{:S(2)}) collective-permute-start(bf16[128,1024]{1,0:T(8,128)(2,1)S(1)} %multiply_convert_fusion.1.refs_0_.refs_8_), channel_id=1, source_target_pairs={{0,16},{16,0},{1,17},{17,1},{2,18},{18,2},{3,19},{19,3},{4,20},{20... | collective-permute-start | bytes 786440 | tf_op jit(solution)/shard_map/ppermute | solution.py:42
  54.1 6.8 %collective-permute-start.20 = (bf16[128,1024]{1,0:T(8,128)(2,1)S(1)}, bf16[128,1024]{1,0:T(8,128)(2,1)S(1)}, u32[]{:S(2)}, u32[]{:S(2)}) collective-permute-start(bf16[128,1024]{1,0:T(8,128)(2,1)S(1)} %collective-permute-done.12.refs_12_), channel_id=1, source_target_pairs={{0,1},{1,0},{2,3},{3,2},{4,5},{5,4},{6,7},{7,6},{8,9},{9,8},{10,11... | collective-permute-start | bytes 786440 | tf_op jit(solution)/shard_map/ppermute | solution.py:30
  56.1 8.1 %collective-permute-start.18 = (bf16[128,1024]{1,0:T(8,128)(2,1)S(1)}, bf16[128,1024]{1,0:T(8,128)(2,1)S(1)}, u32[]{:S(2)}, u32[]{:S(2)}) collective-permute-start(bf16[128,1024]{1,0:T(8,128)(2,1)S(1)} %collective-permute-done.10.refs_10_), channel_id=1, source_target_pairs={{0,1},{1,0},{2,3},{3,2},{4,5},{5,4},{6,7},{7,6},{8,9},{9,8},{10,11... | collective-permute-start | bytes 786440 | tf_op jit(solution)/shard_map/ppermute | solution.py:30
  56.7 10.3 %collective-permute-start.14 = (bf16[128,1024]{1,0:T(8,128)(2,1)S(1)}, bf16[128,1024]{1,0:T(8,128)(2,1)S(1)}, u32[]{:S(2)}, u32[]{:S(2)}) collective-permute-start(bf16[128,1024]{1,0:T(8,128)(2,1)S(1)} %collective-permute-done.10.refs_10_), channel_id=1, source_target_pairs={{0,12},{4,0},{8,4},{12,8},{1,13},{5,1},{9,5},{13,9},{2,14},{6,2},{... | collective-permute-start | bytes 786440 | tf_op jit(solution)/shard_map/ppermute | solution.py:45
  57.0 10.0 %collective-permute-start.17 = (bf16[128,1024]{1,0:T(8,128)(2,1)S(1)}, bf16[128,1024]{1,0:T(8,128)(2,1)S(1)}, u32[]{:S(2)}, u32[]{:S(2)}) collective-permute-start(bf16[128,1024]{1,0:T(8,128)(2,1)S(1)} %collective-permute-done.9.refs_9_), channel_id=1, source_target_pairs={{0,1},{1,0},{2,3},{3,2},{4,5},{5,4},{6,7},{7,6},{8,9},{9,8},{10,11... | collective-permute-start | bytes 786440 | tf_op jit(solution)/shard_map/ppermute | solution.py:30
  61.0 9.3 %collective-permute-start.13 = (bf16[128,1024]{1,0:T(8,128)(2,1)S(1)}, bf16[128,1024]{1,0:T(8,128)(2,1)S(1)}, u32[]{:S(2)}, u32[]{:S(2)}) collective-permute-start(bf16[128,1024]{1,0:T(8,128)(2,1)S(1)} %collective-permute-done.9.refs_9_), channel_id=1, source_target_pairs={{0,4},{4,8},{8,12},{12,0},{1,5},{5,9},{9,13},{13,1},{2,6},{6,10},{... | collective-permute-start | bytes 786440 | tf_op jit(solution)/shard_map/ppermute | solution.py:47
  61.0 9.4 %collective-permute-start.11 = (bf16[128,1024]{1,0:T(8,128)(2,1)S(1)}, bf16[128,1024]{1,0:T(8,128)(2,1)S(1)}, u32[]{:S(2)}, u32[]{:S(2)}) collective-permute-start(bf16[128,1024]{1,0:T(8,128)(2,1)S(1)} %collective-permute-done.9.refs_9_), channel_id=1, source_target_pairs={{0,12},{4,0},{8,4},{12,8},{1,13},{5,1},{9,5},{13,9},{2,14},{6,2},{... | collective-permute-start | bytes 786440 | tf_op jit(solution)/shard_map/ppermute | solution.py:46
  64.2 9.5 %collective-permute-start.7 = (bf16[128,1024]{1,0:T(8,128)(2,1)S(1)}, bf16[128,1024]{1,0:T(8,128)(2,1)S(1)}, u32[]{:S(2)}, u32[]{:S(2)}) collective-permute-start(bf16[128,1024]{1,0:T(8,128)(2,1)S(1)} %collective-permute-done.3.refs_2_), channel_id=1, source_target_pairs={{0,96},{32,0},{64,32},{96,64},{1,97},{33,1},{65,33},{97,65},{2,98}... | collective-permute-start | bytes 786440 | tf_op jit(solution)/shard_map/ppermute | solution.py:45
  67.0 7.6 %collective-permute-start.6 = (bf16[128,1024]{1,0:T(8,128)(2,1)S(1)}, bf16[128,1024]{1,0:T(8,128)(2,1)S(1)}, u32[]{:S(2)}, u32[]{:S(2)}) collective-permute-start(bf16[128,1024]{1,0:T(8,128)(2,1)S(1)} %collective-permute-done.2.refs_1_), channel_id=1, source_target_pairs={{0,32},{32,64},{64,96},{96,0},{1,33},{33,65},{65,97},{97,1},{2,34}... | collective-permute-start | bytes 786440 | tf_op jit(solution)/shard_map/ppermute | solution.py:47
  67.0 9.5 %collective-permute-start.4 = (bf16[128,1024]{1,0:T(8,128)(2,1)S(1)}, bf16[128,1024]{1,0:T(8,128)(2,1)S(1)}, u32[]{:S(2)}, u32[]{:S(2)}) collective-permute-start(bf16[128,1024]{1,0:T(8,128)(2,1)S(1)} %collective-permute-done.2.refs_1_), channel_id=1, source_target_pairs={{0,96},{32,0},{64,32},{96,64},{1,97},{33,1},{65,33},{97,65},{2,98}... | collective-permute-start | bytes 786440 | tf_op jit(solution)/shard_map/ppermute | solution.py:46
  70.2 7.6 %collective-permute-start.15 = (bf16[128,1024]{1,0:T(8,128)(2,1)S(1)}, bf16[128,1024]{1,0:T(8,128)(2,1)S(1)}, u32[]{:S(2)}, u32[]{:S(2)}) collective-permute-start(bf16[128,1024]{1,0:T(8,128)(2,1)S(1)} %collective-permute-done.13.refs_13_), channel_id=1, source_target_pairs={{0,4},{4,8},{8,12},{12,0},{1,5},{5,9},{9,13},{13,1},{2,6},{6,10},{... | collective-permute-start | bytes 786440 | tf_op jit(solution)/shard_map/ppermute | solution.py:48
  70.4 7.4 %collective-permute-start.21 = (bf16[128,1024]{1,0:T(8,128)(2,1)S(1)}, bf16[128,1024]{1,0:T(8,128)(2,1)S(1)}, u32[]{:S(2)}, u32[]{:S(2)}) collective-permute-start(bf16[128,1024]{1,0:T(8,128)(2,1)S(1)} %collective-permute-done.13.refs_13_), channel_id=1, source_target_pairs={{0,1},{1,0},{2,3},{3,2},{4,5},{5,4},{6,7},{7,6},{8,9},{9,8},{10,11... | collective-permute-start | bytes 786440 | tf_op jit(solution)/shard_map/ppermute | solution.py:30
  73.7 4.1 %collective-permute-start.22 = (bf16[128,1024]{1,0:T(8,128)(2,1)S(1)}, bf16[128,1024]{1,0:T(8,128)(2,1)S(1)}, u32[]{:S(2)}, u32[]{:S(2)}) collective-permute-start(bf16[128,1024]{1,0:T(8,128)(2,1)S(1)} %collective-permute-done.14.refs_14_), channel_id=1, source_target_pairs={{0,1},{1,0},{2,3},{3,2},{4,5},{5,4},{6,7},{7,6},{8,9},{9,8},{10,11... | collective-permute-start | bytes 786440 | tf_op jit(solution)/shard_map/ppermute | solution.py:30
  74.6 3.3 %collective-permute-start.19 = (bf16[128,1024]{1,0:T(8,128)(2,1)S(1)}, bf16[128,1024]{1,0:T(8,128)(2,1)S(1)}, u32[]{:S(2)}, u32[]{:S(2)}) collective-permute-start(bf16[128,1024]{1,0:T(8,128)(2,1)S(1)} %collective-permute-done.11.refs_11_), channel_id=1, source_target_pairs={{0,1},{1,0},{2,3},{3,2},{4,5},{5,4},{6,7},{7,6},{8,9},{9,8},{10,11... | collective-permute-start | bytes 786440 | tf_op jit(solution)/shard_map/ppermute | solution.py:30
  76.5 8.0 %collective-permute-start.8 = (bf16[128,1024]{1,0:T(8,128)(2,1)S(1)}, bf16[128,1024]{1,0:T(8,128)(2,1)S(1)}, u32[]{:S(2)}, u32[]{:S(2)}) collective-permute-start(bf16[128,1024]{1,0:T(8,128)(2,1)S(1)} %collective-permute-done.6.refs_5_), channel_id=1, source_target_pairs={{0,32},{32,64},{64,96},{96,0},{1,33},{33,65},{65,97},{97,1},{2,34}... | collective-permute-start | bytes 786440 | tf_op jit(solution)/shard_map/ppermute | solution.py:48
  77.8 6.8 %collective-permute-start.23 = (bf16[128,1024]{1,0:T(8,128)(2,1)S(1)}, bf16[128,1024]{1,0:T(8,128)(2,1)S(1)}, u32[]{:S(2)}, u32[]{:S(2)}) collective-permute-start(bf16[128,1024]{1,0:T(8,128)(2,1)S(1)} %collective-permute-done.15.refs_15_), channel_id=1, source_target_pairs={{0,1},{1,0},{2,3},{3,2},{4,5},{5,4},{6,7},{7,6},{8,9},{9,8},{10,11... | collective-permute-start | bytes 786440 | tf_op jit(solution)/shard_map/ppermute | solution.py:30
  94.3 14.7 %all-to-all-start.1 = ((f32[16,24,128]{2,1,0:T(8,128)}), f32[16,24,128]{2,1,0:T(8,128)S(1)}, u32[]{:S(2)}, u32[]{:S(2)}) async-start(f32[16,24,128]{2,1,0:T(8,128)} %get-tuple-element.22), calls=%async_computation.1 | async-start | bytes 393216 | tf_op jit(solution)/shard_map/all_to_all | solution.py:395
  98.4 3.7 %collective-permute-start.24 = (f32[8,128]{1,0:T(8,128)S(1)}, f32[8,128]{1,0:T(8,128)S(1)}, u32[]{:S(2)}, u32[]{:S(2)}) collective-permute-start(f32[8,128]{1,0:T(8,128)S(1)} %get-tuple-element.21), channel_id=1, source_target_pairs={{0,16},{16,0},{1,17},{17,1},{2,18},{18,2},{3,19},{19,3},{4,20},{20... | collective-permute-start | bytes 12296 | tf_op jit(solution)/shard_map/ppermute | solution.py:396
  102.0 5.1 %collective-permute-start.27 = (f32[8,128]{1,0:T(8,128)S(1)}, f32[8,128]{1,0:T(8,128)S(1)}, u32[]{:S(2)}, u32[]{:S(2)}) collective-permute-start(f32[8,128]{1,0:T(8,128)S(1)} %add.28.r0), channel_id=1, source_target_pairs={{0,64},{32,96},{64,0},{96,32},{1,65},{33,97},{65,1},{97,33},{2,66}... | collective-permute-start | bytes 12296 | tf_op jit(solution)/shard_map/ppermute | solution.py:397
  103.1 4.0 %collective-permute-start.26 = (f32[8,128]{1,0:T(8,128)S(1)}, f32[8,128]{1,0:T(8,128)S(1)}, u32[]{:S(2)}, u32[]{:S(2)}) collective-permute-start(f32[8,128]{1,0:T(8,128)S(1)} %add.28.r0), channel_id=1, source_target_pairs={{0,96},{32,0},{64,32},{96,64},{1,97},{33,1},{65,33},{97,65},{2,98}... | collective-permute-start | bytes 12296 | tf_op jit(solution)/shard_map/ppermute | solution.py:397
  104.3 4.8 %collective-permute-start.25 = (f32[8,128]{1,0:T(8,128)S(1)}, f32[8,128]{1,0:T(8,128)S(1)}, u32[]{:S(2)}, u32[]{:S(2)}) collective-permute-start(f32[8,128]{1,0:T(8,128)S(1)} %add.28.r0), channel_id=1, source_target_pairs={{0,32},{32,64},{64,96},{96,0},{1,33},{33,65},{65,97},{97,1},{2,34}... | collective-permute-start | bytes 12296 | tf_op jit(solution)/shard_map/ppermute | solution.py:397
  146.0 28.9 %copy-start = (bf16[2048,320]{0,1:T(8,128)(2,1)S(1)}, bf16[2048,320]{0,1:T(8,128)(2,1)}, u32[]{:S(2)}) copy-start(bf16[2048,320]{0,1:T(8,128)(2,1)} %param.3) | copy-start | bytes 3932164
  146.8 8.0 %collective-permute-start.28 = (bf16[128,1024]{1,0:T(8,128)(2,1)S(1)}, bf16[128,1024]{1,0:T(8,128)(2,1)S(1)}, u32[]{:S(2)}, u32[]{:S(2)}) collective-permute-start(bf16[128,1024]{1,0:T(8,128)(2,1)S(1)} %multiply_convert_fusion.refs_0_), channel_id=1, source_target_pairs={{0,2},{2,0},{1,3},{3,1},{4,6},{6,4},{5,7},{7,5},{8,10},{10,8},{9,1... | collective-permute-start | bytes 786440 | tf_op jit(solution)/shard_map/ppermute | solution.py:42
  150.3 7.6 %collective-permute-start.31 = (bf16[128,1024]{1,0:T(8,128)(2,1)S(1)}, bf16[128,1024]{1,0:T(8,128)(2,1)S(1)}, u32[]{:S(2)}, u32[]{:S(2)}) collective-permute-start(bf16[128,1024]{1,0:T(8,128)(2,1)S(1)} %multiply_convert_fusion.refs_0_), channel_id=1, source_target_pairs={{0,4},{4,8},{8,12},{12,0},{1,5},{5,9},{9,13},{13,1},{2,6},{6,10},{... | collective-permute-start | bytes 786440 | tf_op jit(solution)/shard_map/ppermute | solution.py:44
  151.7 6.4 %collective-permute-start.29 = (bf16[128,1024]{1,0:T(8,128)(2,1)S(1)}, bf16[128,1024]{1,0:T(8,128)(2,1)S(1)}, u32[]{:S(2)}, u32[]{:S(2)}) collective-permute-start(bf16[128,1024]{1,0:T(8,128)(2,1)S(1)} %multiply_convert_fusion.refs_0_), channel_id=1, source_target_pairs={{0,12},{4,0},{8,4},{12,8},{1,13},{5,1},{9,5},{13,9},{2,14},{6,2},{... | collective-permute-start | bytes 786440 | tf_op jit(solution)/shard_map/ppermute | solution.py:43
  153.5 7.9 %collective-permute-start.35 = (bf16[128,1024]{1,0:T(8,128)(2,1)S(1)}, bf16[128,1024]{1,0:T(8,128)(2,1)S(1)}, u32[]{:S(2)}, u32[]{:S(2)}) collective-permute-start(bf16[128,1024]{1,0:T(8,128)(2,1)S(1)} %multiply_convert_fusion.refs_0_), channel_id=1, source_target_pairs={{0,1},{1,0},{2,3},{3,2},{4,5},{5,4},{6,7},{7,6},{8,9},{9,8},{10,11... | collective-permute-start | bytes 786440 | tf_op jit(solution)/shard_map/ppermute | solution.py:30
  154.7 8.8 %collective-permute-start.32 = (bf16[128,1024]{1,0:T(8,128)(2,1)S(1)}, bf16[128,1024]{1,0:T(8,128)(2,1)S(1)}, u32[]{:S(2)}, u32[]{:S(2)}) collective-permute-start(bf16[128,1024]{1,0:T(8,128)(2,1)S(1)} %collective-permute-done.28.refs_1_), channel_id=1, source_target_pairs={{0,4},{4,8},{8,12},{12,0},{1,5},{5,9},{9,13},{13,1},{2,6},{6,10},{... | collective-permute-start | bytes 786440 | tf_op jit(solution)/shard_map/ppermute | solution.py:47
  157.9 5.9 %collective-permute-start.39 = (bf16[128,1024]{1,0:T(8,128)(2,1)S(1)}, bf16[128,1024]{1,0:T(8,128)(2,1)S(1)}, u32[]{:S(2)}, u32[]{:S(2)}) collective-permute-start(bf16[128,1024]{1,0:T(8,128)(2,1)S(1)} %collective-permute-done.31.refs_4_), channel_id=1, source_target_pairs={{0,1},{1,0},{2,3},{3,2},{4,5},{5,4},{6,7},{7,6},{8,9},{9,8},{10,11... | collective-permute-start | bytes 786440 | tf_op jit(solution)/shard_map/ppermute | solution.py:30
  158.1 5.6 %collective-permute-start.37 = (bf16[128,1024]{1,0:T(8,128)(2,1)S(1)}, bf16[128,1024]{1,0:T(8,128)(2,1)S(1)}, u32[]{:S(2)}, u32[]{:S(2)}) collective-permute-start(bf16[128,1024]{1,0:T(8,128)(2,1)S(1)} %collective-permute-done.29.refs_2_), channel_id=1, source_target_pairs={{0,1},{1,0},{2,3},{3,2},{4,5},{5,4},{6,7},{7,6},{8,9},{9,8},{10,11... | collective-permute-start | bytes 786440 | tf_op jit(solution)/shard_map/ppermute | solution.py:30
  158.4 9.7 %collective-permute-start.33 = (bf16[128,1024]{1,0:T(8,128)(2,1)S(1)}, bf16[128,1024]{1,0:T(8,128)(2,1)S(1)}, u32[]{:S(2)}, u32[]{:S(2)}) collective-permute-start(bf16[128,1024]{1,0:T(8,128)(2,1)S(1)} %collective-permute-done.29.refs_2_), channel_id=1, source_target_pairs={{0,12},{4,0},{8,4},{12,8},{1,13},{5,1},{9,5},{13,9},{2,14},{6,2},{... | collective-permute-start | bytes 786440 | tf_op jit(solution)/shard_map/ppermute | solution.py:45
  161.4 11.5 %collective-permute-start.30 = (bf16[128,1024]{1,0:T(8,128)(2,1)S(1)}, bf16[128,1024]{1,0:T(8,128)(2,1)S(1)}, u32[]{:S(2)}, u32[]{:S(2)}) collective-permute-start(bf16[128,1024]{1,0:T(8,128)(2,1)S(1)} %collective-permute-done.28.refs_1_), channel_id=1, source_target_pairs={{0,12},{4,0},{8,4},{12,8},{1,13},{5,1},{9,5},{13,9},{2,14},{6,2},{... | collective-permute-start | bytes 786440 | tf_op jit(solution)/shard_map/ppermute | solution.py:46
  163.5 9.5 %collective-permute-start.34 = (bf16[128,1024]{1,0:T(8,128)(2,1)S(1)}, bf16[128,1024]{1,0:T(8,128)(2,1)S(1)}, u32[]{:S(2)}, u32[]{:S(2)}) collective-permute-start(bf16[128,1024]{1,0:T(8,128)(2,1)S(1)} %collective-permute-done.32.refs_5_), channel_id=1, source_target_pairs={{0,4},{4,8},{8,12},{12,0},{1,5},{5,9},{9,13},{13,1},{2,6},{6,10},{... | collective-permute-start | bytes 786440 | tf_op jit(solution)/shard_map/ppermute | solution.py:48
  163.7 9.7 %collective-permute-start.36 = (bf16[128,1024]{1,0:T(8,128)(2,1)S(1)}, bf16[128,1024]{1,0:T(8,128)(2,1)S(1)}, u32[]{:S(2)}, u32[]{:S(2)}) collective-permute-start(bf16[128,1024]{1,0:T(8,128)(2,1)S(1)} %collective-permute-done.28.refs_1_), channel_id=1, source_target_pairs={{0,1},{1,0},{2,3},{3,2},{4,5},{5,4},{6,7},{7,6},{8,9},{9,8},{10,11... | collective-permute-start | bytes 786440 | tf_op jit(solution)/shard_map/ppermute | solution.py:30
  163.8 9.7 %collective-permute-start.40 = (bf16[128,1024]{1,0:T(8,128)(2,1)S(1)}, bf16[128,1024]{1,0:T(8,128)(2,1)S(1)}, u32[]{:S(2)}, u32[]{:S(2)}) collective-permute-start(bf16[128,1024]{1,0:T(8,128)(2,1)S(1)} %collective-permute-done.32.refs_5_), channel_id=1, source_target_pairs={{0,1},{1,0},{2,3},{3,2},{4,5},{5,4},{6,7},{7,6},{8,9},{9,8},{10,11... | collective-permute-start | bytes 786440 | tf_op jit(solution)/shard_map/ppermute | solution.py:30
  168.1 5.4 %collective-permute-start.41 = (bf16[128,1024]{1,0:T(8,128)(2,1)S(1)}, bf16[128,1024]{1,0:T(8,128)(2,1)S(1)}, u32[]{:S(2)}, u32[]{:S(2)}) collective-permute-start(bf16[128,1024]{1,0:T(8,128)(2,1)S(1)} %collective-permute-done.33.refs_6_), channel_id=1, source_target_pairs={{0,1},{1,0},{2,3},{3,2},{4,5},{5,4},{6,7},{7,6},{8,9},{9,8},{10,11... | collective-permute-start | bytes 786440 | tf_op jit(solution)/shard_map/ppermute | solution.py:30
  173.0 1.5 collective-permute-start.38
  173.0 1.9 collective-permute-start.42
  177.9 19.3 %copy-start.2 = (bf16[320,1024]{1,0:T(8,128)(2,1)S(1)}, bf16[320,1024]{1,0:T(8,128)(2,1)}, u32[]{:S(2)}) copy-start(bf16[320,1024]{1,0:T(8,128)(2,1)} %param.4) | copy-start | bytes 1966084
  193.7 13.5 %all-to-all-start.4 = ((bf16[8,320,128]{2,1,0:T(8,128)(2,1)}), bf16[8,320,128]{2,1,0:T(8,128)(2,1)S(1)}, u32[]{:S(2)}, u32[]{:S(2)}) async-start(bf16[8,320,128]{2,1,0:T(8,128)(2,1)} %broadcast_in_dim.2), calls=%async_computation.4 | async-start | bytes 1310720 | tf_op jit(solution)/shard_map/all_to_all | solution.py:34

commit v9 on v8

--- a/solution.py
+++ b/solution.py
@@ -38,14 +38,17 @@
     return jnp.sum(lax.all_to_all(parts, axes, 0, 0).astype(F32), axis=0)
 
 
-def gather_ring(own, long_axis, short_axis):
+def gather_ring(own, long_axis, short_axis, direct=False):
     other = lax.ppermute(own, short_axis, SWAP)
     after_own = lax.ppermute(own, long_axis, RING[3])
     before_own = lax.ppermute(own, long_axis, RING[1])
     far_own = lax.ppermute(after_own, long_axis, RING[3])
     after_other = lax.ppermute(other, long_axis, RING[3])
     before_other = lax.ppermute(other, long_axis, RING[1])
-    far_other = lax.ppermute(before_other, long_axis, RING[1])
+    if direct:
+        far_other = lax.ppermute(other, long_axis, RING[2])
+    else:
+        far_other = lax.ppermute(before_other, long_axis, RING[1])
     return [own, other, after_own, after_other, before_own, before_other, far_own, far_other]
 
 
@@ -387,7 +390,7 @@
     unit = z * inv
     emb = unit.astype(BF16)
 
-    keys = gather_ring(emb, "x", "zl")
+    keys = gather_ring(emb, "x", "zl", direct=True)
     queries = gather_ring(emb, "y", "zh")
     queries = queries + [core_swap(piece) for piece in queries]
     weights, row_part, hits, col_part, queries = score_call(place, keys, queries, mates)

time: 211 us -> 210 us (level)
  waiting for transfers between devices: 46.7 us -> 43.1 us
  starting transfers between devices: 45.6 us -> 48.8 us
    ppermute x3 -> x2, waiting for transfers between devices: 6.81 us -> 0.01 us  [gather_ring(): far_other = lax.ppermute(before_other, long_axis, RING[1])]
where the time goes in v9:
time: 210 us; the launch traced here: 209 us
  blocking collectives  78.5 us (37%)
  starting transfers between devices  48.8 us (23%)
  waiting for transfers between devices  43.1 us (21%)
  Pallas kernels  21.9 us (10%)
  matrix products  8.73 us (4%)
  other arithmetic  3.22 us (2%)
  between operations  2.62 us (1%)
  local copies, waits for them, and re-layouts  2.17 us (1%)
    all_to_all x2, blocking collectives, sum_exchange(): return jnp.sum(lax.all_to_all(parts, axes, 0, 0).astype(F32), axis=0)  63.8 us
    all_to_all x1, blocking collectives, shards(): pieces = lax.all_to_all(head_part, XZ, 0, 0)  14.7 us
    pallas_call x1, Pallas kernels, score_call(): pl.pallas_call(score_kernel, grid_spec=pltpu.PrefetchScalarGridSpec(num_s...  9.8 us
    pallas_call x1, Pallas kernels, grad_call(): pl.pallas_call(grad_kernel, grid_spec=pltpu.PrefetchScalarGridSpec(num_sc...  9.1 us
    ppermute x3, waiting for transfers between devices, gather_ring(): far_own = lax.ppermute(after_own, long_axis, RING[3])  8.02 us
    ppermute x3, waiting for transfers between devices, gather_ring(): after_other = lax.ppermute(other, long_axis, RING[3])  7.67 us
    ppermute x3, waiting for transfers between devices, gather_ring(): other = lax.ppermute(own, short_axis, SWAP)  7.02 us
    ppermute x3, starting transfers between devices, gather_ring(): after_other = lax.ppermute(other, long_axis, RING[3])  6.91 us
  transfers between devices with their start and end apart: 45, of which 23 were waited for; matrix products, arithmetic and copies ran while one was open for 4% of the time, Pallas kernels for 0%

profile of v9, /device:TPU:0, one launch (start us, length us, event | category | flops | bytes accessed | tf_op | source)
XLA Modules:
  0.0 209.0 jit_solution(18377071119911410468)
XLA Ops:
  0.6 1.1 dynamic-slice_bitcast_fusion
  2.4 2.6 %fusion = f32[1024,1024]{1,0:T(8,128)S(1)} fusion(bf16[320,1024]{1,0:T(8,128)(2,1)} %param.4, bf16[2048,320]{0,1:T(8,128)(2,1)} %param.3, s32[]{:T(128)S(6)} %select_n.6), kind=kOutput, calls=%fused_computation.8 | convolution fusion | flops 671088640 | bytes 5505028 | tf_op jit(solution)/shard_map/dot_general | solution.py:384
  5.1 1.3 add_convert_fusion
  6.5 36.1 %all_to_all.25 = bf16[8,128,1024]{2,1,0:T(8,128)(2,1)S(1)} all-to-all(bf16[8,128,1024]{2,1,0:T(8,128)(2,1)S(1)} %bitcast.26), channel_id=1, replica_groups=mesh['x'=4,'zl'=2,'y'=4,'zh'=2,'c'=2] {'y','zh'}, dimensions={0} | all-to-all | bytes 4194304 | tf_op jit(solution)/shard_map/all_to_all | solution.py:38
  43.5 3.0 %collective-permute-start.10 = (bf16[128,1024]{1,0:T(8,128)(2,1)S(1)}, bf16[128,1024]{1,0:T(8,128)(2,1)S(1)}, u32[]{:S(2)}, u32[]{:S(2)}) collective-permute-start(bf16[128,1024]{1,0:T(8,128)(2,1)S(1)} %multiply_convert_fusion.1.refs_0_.refs_8_), channel_id=1, source_target_pairs={{0,12},{4,0},{8,4},{12,8},{1,13},{5,1},{9,5},{13,9},{2,14},{6,2},{... | collective-permute-start | bytes 786440 | tf_op jit(solution)/shard_map/ppermute | solution.py:43
  46.5 1.2 collective-permute-start.9
  47.7 1.5 collective-permute-start.5
  49.2 1.7 collective-permute-start.3
  50.9 2.2 %collective-permute-done.12.refs_12_ = bf16[128,1024]{1,0:T(8,128)(2,1)S(1)} collective-permute-done((bf16[128,1024]{1,0:T(8,128)(2,1)S(1)}, bf16[128,1024]{1,0:T(8,128)(2,1)S(1)}, u32[]{:S(2)}, u32[]{:S(2)}) %collective-permute-start.12) | collective-permute-done | bytes 262176 | tf_op jit(solution)/shard_map/ppermute | solution.py:44
  53.1 1.0 collective-permute-start.2
  54.1 1.9 collective-permute-done.9.refs_9_
  57.0 4.0 %collective-permute-done.2.refs_1_ = bf16[128,1024]{1,0:T(8,128)(2,1)S(1)} collective-permute-done((bf16[128,1024]{1,0:T(8,128)(2,1)S(1)}, bf16[128,1024]{1,0:T(8,128)(2,1)S(1)}, u32[]{:S(2)}, u32[]{:S(2)}) %collective-permute-start.2) | collective-permute-done | bytes 262176 | tf_op jit(solution)/shard_map/ppermute | solution.py:42
  61.0 3.2 %collective-permute-start.11 = (bf16[128,1024]{1,0:T(8,128)(2,1)S(1)}, bf16[128,1024]{1,0:T(8,128)(2,1)S(1)}, u32[]{:S(2)}, u32[]{:S(2)}) collective-permute-start(bf16[128,1024]{1,0:T(8,128)(2,1)S(1)} %collective-permute-done.9.refs_9_), channel_id=1, source_target_pairs={{0,12},{4,0},{8,4},{12,8},{1,13},{5,1},{9,5},{13,9},{2,14},{6,2},{... | collective-permute-start | bytes 786440 | tf_op jit(solution)/shard_map/ppermute | solution.py:46
  64.2 2.8 %collective-permute-start.7 = (bf16[128,1024]{1,0:T(8,128)(2,1)S(1)}, bf16[128,1024]{1,0:T(8,128)(2,1)S(1)}, u32[]{:S(2)}, u32[]{:S(2)}) collective-permute-start(bf16[128,1024]{1,0:T(8,128)(2,1)S(1)} %collective-permute-done.3.refs_2_), channel_id=1, source_target_pairs={{0,96},{32,0},{64,32},{96,64},{1,97},{33,1},{65,33},{97,65},{2,98}... | collective-permute-start | bytes 786440 | tf_op jit(solution)/shard_map/ppermute | solution.py:45
  67.0 1.2 collective-permute-start.8
  69.2 1.3 collective-permute-done.11.refs_11_
  70.4 2.8 %collective-permute-start.4 = (bf16[128,1024]{1,0:T(8,128)(2,1)S(1)}, bf16[128,1024]{1,0:T(8,128)(2,1)S(1)}, u32[]{:S(2)}, u32[]{:S(2)}) collective-permute-start(bf16[128,1024]{1,0:T(8,128)(2,1)S(1)} %collective-permute-done.2.refs_1_), channel_id=1, source_target_pairs={{0,96},{32,0},{64,32},{96,64},{1,97},{33,1},{65,33},{97,65},{2,98}... | collective-permute-start | bytes 786440 | tf_op jit(solution)/shard_map/ppermute | solution.py:46
  73.2 4.4 %collective-permute-done.7.refs_6_ = bf16[128,1024]{1,0:T(8,128)(2,1)S(1)} collective-permute-done((bf16[128,1024]{1,0:T(8,128)(2,1)S(1)}, bf16[128,1024]{1,0:T(8,128)(2,1)S(1)}, u32[]{:S(2)}, u32[]{:S(2)}) %collective-permute-start.7) | collective-permute-done | bytes 262176 | tf_op jit(solution)/shard_map/ppermute | solution.py:45
  78.1 2.2 %collective-permute-done.6.refs_5_ = bf16[128,1024]{1,0:T(8,128)(2,1)S(1)} collective-permute-done((bf16[128,1024]{1,0:T(8,128)(2,1)S(1)}, bf16[128,1024]{1,0:T(8,128)(2,1)S(1)}, u32[]{:S(2)}, u32[]{:S(2)}) %collective-permute-start.6) | collective-permute-done | bytes 262176 | tf_op jit(solution)/shard_map/ppermute | solution.py:47
  80.7 1.4 collective-permute-done.4.refs_3_
  82.2 9.8 %scores.1 = (bf16[1024,2048]{1,0:T(8,128)(2,1)}, f32[8,128]{1,0:T(8,128)S(1)}, f32[8,128]{1,0:T(8,128)S(1)}, f32[16,24,128]{2,1,0:T(8,128)}, bf16[2048,1024]{1,0:T(8,128)(2,1)}) custom-call(s32[5]{0:T(128)S(1)} %stack.23.place, bf16[128,1024]{1,0:T(8,128)(2,1)S(1)} %multiply_convert_fusion.1.refs_0_.refs_8_, ...), custom_call_target="tpu_custom_call" | custom-call | flops 4294967296 | bytes 14680064 | tf_op jit(solution)/shard_map/scores/pallas_call | solution.py:274
  92.0 4.0 %all-to-all-start.1 = ((f32[16,24,128]{2,1,0:T(8,128)}), f32[16,24,128]{2,1,0:T(8,128)S(1)}, u32[]{:S(2)}, u32[]{:S(2)}) async-start(f32[16,24,128]{2,1,0:T(8,128)} %get-tuple-element.22), calls=%async_computation.1 | async-start | bytes 393216 | tf_op jit(solution)/shard_map/all_to_all | solution.py:398
  96.0 1.3 collective-permute-start.24
  97.3 2.4 %collective-permute-done.24 = f32[8,128]{1,0:T(8,128)S(1)} collective-permute-done((f32[8,128]{1,0:T(8,128)S(1)}, f32[8,128]{1,0:T(8,128)S(1)}, u32[]{:S(2)}, u32[]{:S(2)}) %collective-permute-start.24) | collective-permute-done | bytes 4128 | tf_op jit(solution)/shard_map/ppermute | solution.py:399
  99.7 2.7 %collective-permute-start.27 = (f32[8,128]{1,0:T(8,128)S(1)}, f32[8,128]{1,0:T(8,128)S(1)}, u32[]{:S(2)}, u32[]{:S(2)}) collective-permute-start(f32[8,128]{1,0:T(8,128)S(1)} %add.28.r0), channel_id=1, source_target_pairs={{0,64},{32,96},{64,0},{96,32},{1,65},{33,97},{65,1},{97,33},{2,66}... | collective-permute-start | bytes 12296 | tf_op jit(solution)/shard_map/ppermute | solution.py:400
  102.4 1.2 collective-permute-start.26
  104.8 1.2 collective-permute-done.26.r2
  106.0 2.5 %collective-permute-done.25.r1 = f32[8,128]{1,0:T(8,128)S(1)} collective-permute-done((f32[8,128]{1,0:T(8,128)S(1)}, f32[8,128]{1,0:T(8,128)S(1)}, u32[]{:S(2)}, u32[]{:S(2)}) %collective-permute-start.25) | collective-permute-done | bytes 4128 | tf_op jit(solution)/shard_map/ppermute | solution.py:400
  108.5 9.1 %grads.1 = (bf16[4,2,128,1024]{3,2,1,0:T(8,128)(2,1)S(1)}, bf16[16,128]{1,0:T(8,128)(2,1)S(1)}) custom-call(s32[5]{0:T(128)S(1)} %stack.23.place, bf16[1024,2048]{1,0:T(8,128)(2,1)} %get-tuple-element.18.w_ref, bf16[2048,1024]{1,0:T(8,128)(2,1)} %get-tuple-element.19.query_ref, f32[8,128]{1,0:T(8,128)S(1)} %get-tuple-element.20.hit_ref, ...), custom_call_target="tpu_custom_call" | custom-call | flops 4294967296 | bytes 14680064 | tf_op jit(solution)/shard_map/grads/pallas_call | solution.py:316
  117.6 27.7 %all_to_all.26 = bf16[8,128,1024]{2,1,0:T(8,128)(2,1)S(1)} all-to-all(bf16[8,128,1024]{2,1,0:T(8,128)(2,1)S(1)} %bitcast.23), channel_id=1, replica_groups=mesh['x'=4,'zl'=2,'y'=4,'zh'=2,'c'=2] {'x','zl'}, dimensions={0} | all-to-all | bytes 4194304 | tf_op jit(solution)/shard_map/all_to_all | solution.py:38
  146.1 3.6 %collective-permute-start.28 = (bf16[128,1024]{1,0:T(8,128)(2,1)S(1)}, bf16[128,1024]{1,0:T(8,128)(2,1)S(1)}, u32[]{:S(2)}, u32[]{:S(2)}) collective-permute-start(bf16[128,1024]{1,0:T(8,128)(2,1)S(1)} %multiply_convert_fusion.refs_0_), channel_id=1, source_target_pairs={{0,2},{2,0},{1,3},{3,1},{4,6},{6,4},{5,7},{7,5},{8,10},{10,8},{9,1... | collective-permute-start | bytes 786440 | tf_op jit(solution)/shard_map/ppermute | solution.py:42
  149.7 1.5 collective-permute-start.31
  151.2 1.7 collective-permute-start.29
  153.0 1.1 collective-permute-done.28.refs_1_
  154.1 1.5 collective-permute-start.32
  155.6 1.7 collective-permute-done.31.refs_4_
  157.8 2.9 %collective-permute-start.33 = (bf16[128,1024]{1,0:T(8,128)(2,1)S(1)}, bf16[128,1024]{1,0:T(8,128)(2,1)S(1)}, u32[]{:S(2)}, u32[]{:S(2)}) collective-permute-start(bf16[128,1024]{1,0:T(8,128)(2,1)S(1)} %collective-permute-done.29.refs_2_), channel_id=1, source_target_pairs={{0,12},{4,0},{8,4},{12,8},{1,13},{5,1},{9,5},{13,9},{2,14},{6,2},{... | collective-permute-start | bytes 786440 | tf_op jit(solution)/shard_map/ppermute | solution.py:45
  160.8 0.9 collective-permute-start.30
  161.7 1.2 collective-permute-done.32.refs_5_
  163.7 3.7 %collective-permute-done.33.refs_6_ = bf16[128,1024]{1,0:T(8,128)(2,1)S(1)} collective-permute-done((bf16[128,1024]{1,0:T(8,128)(2,1)S(1)}, bf16[128,1024]{1,0:T(8,128)(2,1)S(1)}, u32[]{:S(2)}, u32[]{:S(2)}) %collective-permute-start.33) | collective-permute-done | bytes 262176 | tf_op jit(solution)/shard_map/ppermute | solution.py:45
  167.4 5.0 %collective-permute-done.30.refs_3_ = bf16[128,1024]{1,0:T(8,128)(2,1)S(1)} collective-permute-done((bf16[128,1024]{1,0:T(8,128)(2,1)S(1)}, bf16[128,1024]{1,0:T(8,128)(2,1)S(1)}, u32[]{:S(2)}, u32[]{:S(2)}) %collective-permute-start.30) | collective-permute-done | bytes 262176 | tf_op jit(solution)/shard_map/ppermute | solution.py:46
  172.9 1.0 collective-permute-done.38.refs_11_
  174.3 3.0 %head_parts.1 = (bf16[8,336,128]{2,1,0:T(8,128)(2,1)S(1)}, bf16[2048,1024]{1,0:T(8,128)(2,1)}) custom-call(s32[5]{0:T(128)S(1)} %stack.23.place, bf16[320,2048]{1,0:T(8,128)(2,1)S(1)} %bitcast.22, bf16[16,128]{1,0:T(8,128)(2,1)S(1)} %get-tuple-element.23.rider, bf16[128,1024]{1,0:T(8,128)(2,1)S(1)} %multiply_convert_fusion.refs_0_, ...), custom_call_target="tpu_custom_call" | custom-call | flops 1342177280 | bytes 10485760 | tf_op jit(solution)/shard_map/head_parts/pallas_call | solution.py:348
  177.4 14.7 %all_to_all.27 = bf16[8,336,128]{2,1,0:T(8,128)(2,1)S(1)} all-to-all(bf16[8,336,128]{2,1,0:T(8,128)(2,1)S(1)} %get-tuple-element.25), channel_id=1, replica_groups=mesh['x'=4,'zl'=2,'y'=4,'zh'=2,'c'=2] {'x','zl'}, dimensions={0} | all-to-all | bytes 1376256 | tf_op jit(solution)/shard_map/all_to_all | solution.py:408
  193.1 3.5 %all-to-all-start.4 = ((bf16[8,320,128]{2,1,0:T(8,128)(2,1)}), bf16[8,320,128]{2,1,0:T(8,128)(2,1)S(1)}, u32[]{:S(2)}, u32[]{:S(2)}) async-start(bf16[8,320,128]{2,1,0:T(8,128)(2,1)} %broadcast_in_dim.2), calls=%async_computation.4 | async-start | bytes 1310720 | tf_op jit(solution)/shard_map/all_to_all | solution.py:34
  196.7 4.8 %convolution_convert_fusion = bf16[2048,320]{0,1:T(8,128)(2,1)} fusion(bf16[2048,1024]{1,0:T(8,128)(2,1)} %get-tuple-element.26, bf16[320,1024]{1,0:T(8,128)(2,1)S(1)} %copy-done.2), kind=kOutput, calls=%fused_computation.3 | convolution fusion | flops 1342832640 | bytes 6160384 | tf_op jit(solution)/shard_map/dot_general | solution.py:416
  202.8 3.9 %all-to-all-done.4 = bf16[8,320,128]{2,1,0:T(8,128)(2,1)S(1)} async-done(((bf16[8,320,128]{2,1,0:T(8,128)(2,1)}), bf16[8,320,128]{2,1,0:T(8,128)(2,1)S(1)}, u32[]{:S(2)}, u32[]{:S(2)}) %all-to-all-start.4) | async-done | bytes 655392 | tf_op jit(solution)/shard_map/all_to_all | solution.py:34
  206.7 1.2 copy_bitcast_fusion
  (72 shorter events, 10.3 us)
Async XLA Ops:
  1.8 3.3 %collective-permute-start = (bf16[320,1024]{1,0:T(8,128)(2,1)S(1)}, bf16[320,1024]{1,0:T(8,128)(2,1)S(1)}, u32[]{:S(2)}, u32[]{:S(2)}) collective-permute-start(bf16[320,1024]{1,0:T(8,128)(2,1)S(1)} %dynamic-slice_bitcast_fusion), channel_id=1, source_target_pairs={{0,1},{1,0},{2,3},{3,2},{4,5},{5,4},{6,7},{7,6},{8,9},{9,8},{10,11... | collective-permute-start | bytes 1966088 | tf_op jit(solution)/shard_map/ppermute | solution.py:30
  1.9 3.2 %collective-permute-start.1 = (bf16[320,1024]{1,0:T(8,128)(2,1)}, bf16[320,1024]{1,0:T(8,128)(2,1)S(1)}, u32[]{:S(2)}, u32[]{:S(2)}) collective-permute-start(bf16[320,1024]{1,0:T(8,128)(2,1)} %param.4), channel_id=1, source_target_pairs={{0,1},{1,0},{2,3},{3,2},{4,5},{5,4},{6,7},{7,6},{8,9},{9,8},{10,11... | collective-permute-start | bytes 1966088 | tf_op jit(solution)/shard_map/ppermute | solution.py:30
  42.5 39.7 %copy-start.1 = (s32[2048]{0:T(1024)S(1)}, s32[2048]{0:T(1024)}, u32[]{:S(2)}) copy-start(s32[2048]{0:T(1024)} %param.5) | copy-start | bytes 24580
  43.1 6.1 %collective-permute-start.16 = (bf16[128,1024]{1,0:T(8,128)(2,1)S(1)}, bf16[128,1024]{1,0:T(8,128)(2,1)S(1)}, u32[]{:S(2)}, u32[]{:S(2)}) collective-permute-start(bf16[128,1024]{1,0:T(8,128)(2,1)S(1)} %multiply_convert_fusion.1.refs_0_.refs_8_), channel_id=1, source_target_pairs={{0,1},{1,0},{2,3},{3,2},{4,5},{5,4},{6,7},{7,6},{8,9},{9,8},{10,11... | collective-permute-start | bytes 786440 | tf_op jit(solution)/shard_map/ppermute | solution.py:30
  43.2 9.9 %collective-permute-start.12 = (bf16[128,1024]{1,0:T(8,128)(2,1)S(1)}, bf16[128,1024]{1,0:T(8,128)(2,1)S(1)}, u32[]{:S(2)}, u32[]{:S(2)}) collective-permute-start(bf16[128,1024]{1,0:T(8,128)(2,1)S(1)} %multiply_convert_fusion.1.refs_0_.refs_8_), channel_id=1, source_target_pairs={{0,4},{4,8},{8,12},{12,0},{1,5},{5,9},{9,13},{13,1},{2,6},{6,10},{... | collective-permute-start | bytes 786440 | tf_op jit(solution)/shard_map/ppermute | solution.py:44
  43.5 10.6 %collective-permute-start.10 = (bf16[128,1024]{1,0:T(8,128)(2,1)S(1)}, bf16[128,1024]{1,0:T(8,128)(2,1)S(1)}, u32[]{:S(2)}, u32[]{:S(2)}) collective-permute-start(bf16[128,1024]{1,0:T(8,128)(2,1)S(1)} %multiply_convert_fusion.1.refs_0_.refs_8_), channel_id=1, source_target_pairs={{0,12},{4,0},{8,4},{12,8},{1,13},{5,1},{9,5},{13,9},{2,14},{6,2},{... | collective-permute-start | bytes 786440 | tf_op jit(solution)/shard_map/ppermute | solution.py:43
  46.5 9.6 %collective-permute-start.9 = (bf16[128,1024]{1,0:T(8,128)(2,1)S(1)}, bf16[128,1024]{1,0:T(8,128)(2,1)S(1)}, u32[]{:S(2)}, u32[]{:S(2)}) collective-permute-start(bf16[128,1024]{1,0:T(8,128)(2,1)S(1)} %multiply_convert_fusion.1.refs_0_.refs_8_), channel_id=1, source_target_pairs={{0,2},{2,0},{1,3},{3,1},{4,6},{6,4},{5,7},{7,5},{8,10},{10,8},{9,1... | collective-permute-start | bytes 786440 | tf_op jit(solution)/shard_map/ppermute | solution.py:42
  47.7 9.0 %collective-permute-start.5 = (bf16[128,1024]{1,0:T(8,128)(2,1)S(1)}, bf16[128,1024]{1,0:T(8,128)(2,1)S(1)}, u32[]{:S(2)}, u32[]{:S(2)}) collective-permute-start(bf16[128,1024]{1,0:T(8,128)(2,1)S(1)} %multiply_convert_fusion.1.refs_0_.refs_8_), channel_id=1, source_target_pairs={{0,32},{32,64},{64,96},{96,0},{1,33},{33,65},{65,97},{97,1},{2,34}... | collective-permute-start | bytes 786440 | tf_op jit(solution)/shard_map/ppermute | solution.py:44
  49.2 7.8 %collective-permute-start.3 = (bf16[128,1024]{1,0:T(8,128)(2,1)S(1)}, bf16[128,1024]{1,0:T(8,128)(2,1)S(1)}, u32[]{:S(2)}, u32[]{:S(2)}) collective-permute-start(bf16[128,1024]{1,0:T(8,128)(2,1)S(1)} %multiply_convert_fusion.1.refs_0_.refs_8_), channel_id=1, source_target_pairs={{0,96},{32,0},{64,32},{96,64},{1,97},{33,1},{65,33},{97,65},{2,98}... | collective-permute-start | bytes 786440 | tf_op jit(solution)/shard_map/ppermute | solution.py:43
  53.1 7.9 %collective-permute-start.2 = (bf16[128,1024]{1,0:T(8,128)(2,1)S(1)}, bf16[128,1024]{1,0:T(8,128)(2,1)S(1)}, u32[]{:S(2)}, u32[]{:S(2)}) collective-permute-start(bf16[128,1024]{1,0:T(8,128)(2,1)S(1)} %multiply_convert_fusion.1.refs_0_.refs_8_), channel_id=1, source_target_pairs={{0,16},{16,0},{1,17},{17,1},{2,18},{18,2},{3,19},{19,3},{4,20},{20... | collective-permute-start | bytes 786440 | tf_op jit(solution)/shard_map/ppermute | solution.py:42
  54.1 6.8 %collective-permute-start.20 = (bf16[128,1024]{1,0:T(8,128)(2,1)S(1)}, bf16[128,1024]{1,0:T(8,128)(2,1)S(1)}, u32[]{:S(2)}, u32[]{:S(2)}) collective-permute-start(bf16[128,1024]{1,0:T(8,128)(2,1)S(1)} %collective-permute-done.12.refs_12_), channel_id=1, source_target_pairs={{0,1},{1,0},{2,3},{3,2},{4,5},{5,4},{6,7},{7,6},{8,9},{9,8},{10,11... | collective-permute-start | bytes 786440 | tf_op jit(solution)/shard_map/ppermute | solution.py:30
  56.1 8.1 %collective-permute-start.18 = (bf16[128,1024]{1,0:T(8,128)(2,1)S(1)}, bf16[128,1024]{1,0:T(8,128)(2,1)S(1)}, u32[]{:S(2)}, u32[]{:S(2)}) collective-permute-start(bf16[128,1024]{1,0:T(8,128)(2,1)S(1)} %collective-permute-done.10.refs_10_), channel_id=1, source_target_pairs={{0,1},{1,0},{2,3},{3,2},{4,5},{5,4},{6,7},{7,6},{8,9},{9,8},{10,11... | collective-permute-start | bytes 786440 | tf_op jit(solution)/shard_map/ppermute | solution.py:30
  56.7 10.3 %collective-permute-start.14 = (bf16[128,1024]{1,0:T(8,128)(2,1)S(1)}, bf16[128,1024]{1,0:T(8,128)(2,1)S(1)}, u32[]{:S(2)}, u32[]{:S(2)}) collective-permute-start(bf16[128,1024]{1,0:T(8,128)(2,1)S(1)} %collective-permute-done.10.refs_10_), channel_id=1, source_target_pairs={{0,12},{4,0},{8,4},{12,8},{1,13},{5,1},{9,5},{13,9},{2,14},{6,2},{... | collective-permute-start | bytes 786440 | tf_op jit(solution)/shard_map/ppermute | solution.py:45
  57.0 11.2 %collective-permute-start.17 = (bf16[128,1024]{1,0:T(8,128)(2,1)S(1)}, bf16[128,1024]{1,0:T(8,128)(2,1)S(1)}, u32[]{:S(2)}, u32[]{:S(2)}) collective-permute-start(bf16[128,1024]{1,0:T(8,128)(2,1)S(1)} %collective-permute-done.9.refs_9_), channel_id=1, source_target_pairs={{0,1},{1,0},{2,3},{3,2},{4,5},{5,4},{6,7},{7,6},{8,9},{9,8},{10,11... | collective-permute-start | bytes 786440 | tf_op jit(solution)/shard_map/ppermute | solution.py:30
  61.0 8.2 %collective-permute-start.13 = (bf16[128,1024]{1,0:T(8,128)(2,1)S(1)}, bf16[128,1024]{1,0:T(8,128)(2,1)S(1)}, u32[]{:S(2)}, u32[]{:S(2)}) collective-permute-start(bf16[128,1024]{1,0:T(8,128)(2,1)S(1)} %collective-permute-done.9.refs_9_), channel_id=1, source_target_pairs={{0,4},{4,8},{8,12},{12,0},{1,5},{5,9},{9,13},{13,1},{2,6},{6,10},{... | collective-permute-start | bytes 786440 | tf_op jit(solution)/shard_map/ppermute | solution.py:47
  61.0 9.4 %collective-permute-start.11 = (bf16[128,1024]{1,0:T(8,128)(2,1)S(1)}, bf16[128,1024]{1,0:T(8,128)(2,1)S(1)}, u32[]{:S(2)}, u32[]{:S(2)}) collective-permute-start(bf16[128,1024]{1,0:T(8,128)(2,1)S(1)} %collective-permute-done.9.refs_9_), channel_id=1, source_target_pairs={{0,12},{4,0},{8,4},{12,8},{1,13},{5,1},{9,5},{13,9},{2,14},{6,2},{... | collective-permute-start | bytes 786440 | tf_op jit(solution)/shard_map/ppermute | solution.py:46
  64.2 13.3 %collective-permute-start.7 = (bf16[128,1024]{1,0:T(8,128)(2,1)S(1)}, bf16[128,1024]{1,0:T(8,128)(2,1)S(1)}, u32[]{:S(2)}, u32[]{:S(2)}) collective-permute-start(bf16[128,1024]{1,0:T(8,128)(2,1)S(1)} %collective-permute-done.3.refs_2_), channel_id=1, source_target_pairs={{0,96},{32,0},{64,32},{96,64},{1,97},{33,1},{65,33},{97,65},{2,98}... | collective-permute-start | bytes 786440 | tf_op jit(solution)/shard_map/ppermute | solution.py:45
  67.0 10.6 %collective-permute-start.8 = (bf16[128,1024]{1,0:T(8,128)(2,1)S(1)}, bf16[128,1024]{1,0:T(8,128)(2,1)S(1)}, u32[]{:S(2)}, u32[]{:S(2)}) collective-permute-start(bf16[128,1024]{1,0:T(8,128)(2,1)S(1)} %collective-permute-done.2.refs_1_), channel_id=1, source_target_pairs={{0,64},{32,96},{64,0},{96,32},{1,65},{33,97},{65,1},{97,33},{2,66}... | collective-permute-start | bytes 786440 | tf_op jit(solution)/shard_map/ppermute | solution.py:49
  68.2 12.0 %collective-permute-start.6 = (bf16[128,1024]{1,0:T(8,128)(2,1)S(1)}, bf16[128,1024]{1,0:T(8,128)(2,1)S(1)}, u32[]{:S(2)}, u32[]{:S(2)}) collective-permute-start(bf16[128,1024]{1,0:T(8,128)(2,1)S(1)} %collective-permute-done.2.refs_1_), channel_id=1, source_target_pairs={{0,32},{32,64},{64,96},{96,0},{1,33},{33,65},{65,97},{97,1},{2,34}... | collective-permute-start | bytes 786440 | tf_op jit(solution)/shard_map/ppermute | solution.py:47
  69.2 11.1 %collective-permute-start.15 = (bf16[128,1024]{1,0:T(8,128)(2,1)S(1)}, bf16[128,1024]{1,0:T(8,128)(2,1)S(1)}, u32[]{:S(2)}, u32[]{:S(2)}) collective-permute-start(bf16[128,1024]{1,0:T(8,128)(2,1)S(1)} %collective-permute-done.13.refs_13_), channel_id=1, source_target_pairs={{0,4},{4,8},{8,12},{12,0},{1,5},{5,9},{9,13},{13,1},{2,6},{6,10},{... | collective-permute-start | bytes 786440 | tf_op jit(solution)/shard_map/ppermute | solution.py:51
  70.4 11.7 %collective-permute-start.4 = (bf16[128,1024]{1,0:T(8,128)(2,1)S(1)}, bf16[128,1024]{1,0:T(8,128)(2,1)S(1)}, u32[]{:S(2)}, u32[]{:S(2)}) collective-permute-start(bf16[128,1024]{1,0:T(8,128)(2,1)S(1)} %collective-permute-done.2.refs_1_), channel_id=1, source_target_pairs={{0,96},{32,0},{64,32},{96,64},{1,97},{33,1},{65,33},{97,65},{2,98}... | collective-permute-start | bytes 786440 | tf_op jit(solution)/shard_map/ppermute | solution.py:46
  77.6 4.6 %collective-permute-start.21 = (bf16[128,1024]{1,0:T(8,128)(2,1)S(1)}, bf16[128,1024]{1,0:T(8,128)(2,1)S(1)}, u32[]{:S(2)}, u32[]{:S(2)}) collective-permute-start(bf16[128,1024]{1,0:T(8,128)(2,1)S(1)} %collective-permute-done.13.refs_13_), channel_id=1, source_target_pairs={{0,1},{1,0},{2,3},{3,2},{4,5},{5,4},{6,7},{7,6},{8,9},{9,8},{10,11... | collective-permute-start | bytes 786440 | tf_op jit(solution)/shard_map/ppermute | solution.py:30
  77.6 4.6 %collective-permute-start.22 = (bf16[128,1024]{1,0:T(8,128)(2,1)S(1)}, bf16[128,1024]{1,0:T(8,128)(2,1)S(1)}, u32[]{:S(2)}, u32[]{:S(2)}) collective-permute-start(bf16[128,1024]{1,0:T(8,128)(2,1)S(1)} %collective-permute-done.14.refs_14_), channel_id=1, source_target_pairs={{0,1},{1,0},{2,3},{3,2},{4,5},{5,4},{6,7},{7,6},{8,9},{9,8},{10,11... | collective-permute-start | bytes 786440 | tf_op jit(solution)/shard_map/ppermute | solution.py:30
  80.2 1.9 collective-permute-start.19
  80.2 1.9 collective-permute-start.23
  92.0 16.5 %all-to-all-start.1 = ((f32[16,24,128]{2,1,0:T(8,128)}), f32[16,24,128]{2,1,0:T(8,128)S(1)}, u32[]{:S(2)}, u32[]{:S(2)}) async-start(f32[16,24,128]{2,1,0:T(8,128)} %get-tuple-element.22), calls=%async_computation.1 | async-start | bytes 393216 | tf_op jit(solution)/shard_map/all_to_all | solution.py:398
  96.0 3.7 %collective-permute-start.24 = (f32[8,128]{1,0:T(8,128)S(1)}, f32[8,128]{1,0:T(8,128)S(1)}, u32[]{:S(2)}, u32[]{:S(2)}) collective-permute-start(f32[8,128]{1,0:T(8,128)S(1)} %get-tuple-element.21), channel_id=1, source_target_pairs={{0,16},{16,0},{1,17},{17,1},{2,18},{18,2},{3,19},{19,3},{4,20},{20... | collective-permute-start | bytes 12296 | tf_op jit(solution)/shard_map/ppermute | solution.py:399
  99.7 5.1 %collective-permute-start.27 = (f32[8,128]{1,0:T(8,128)S(1)}, f32[8,128]{1,0:T(8,128)S(1)}, u32[]{:S(2)}, u32[]{:S(2)}) collective-permute-start(f32[8,128]{1,0:T(8,128)S(1)} %add.28.r0), channel_id=1, source_target_pairs={{0,64},{32,96},{64,0},{96,32},{1,65},{33,97},{65,1},{97,33},{2,66}... | collective-permute-start | bytes 12296 | tf_op jit(solution)/shard_map/ppermute | solution.py:400
  102.4 3.6 %collective-permute-start.26 = (f32[8,128]{1,0:T(8,128)S(1)}, f32[8,128]{1,0:T(8,128)S(1)}, u32[]{:S(2)}, u32[]{:S(2)}) collective-permute-start(f32[8,128]{1,0:T(8,128)S(1)} %add.28.r0), channel_id=1, source_target_pairs={{0,96},{32,0},{64,32},{96,64},{1,97},{33,1},{65,33},{97,65},{2,98}... | collective-permute-start | bytes 12296 | tf_op jit(solution)/shard_map/ppermute | solution.py:400
  103.7 4.8 %collective-permute-start.25 = (f32[8,128]{1,0:T(8,128)S(1)}, f32[8,128]{1,0:T(8,128)S(1)}, u32[]{:S(2)}, u32[]{:S(2)}) collective-permute-start(f32[8,128]{1,0:T(8,128)S(1)} %add.28.r0), channel_id=1, source_target_pairs={{0,32},{32,64},{64,96},{96,0},{1,33},{33,65},{65,97},{97,1},{2,34}... | collective-permute-start | bytes 12296 | tf_op jit(solution)/shard_map/ppermute | solution.py:400
  145.3 29.0 %copy-start = (bf16[2048,320]{0,1:T(8,128)(2,1)S(1)}, bf16[2048,320]{0,1:T(8,128)(2,1)}, u32[]{:S(2)}) copy-start(bf16[2048,320]{0,1:T(8,128)(2,1)} %param.3) | copy-start | bytes 3932164
  146.1 8.0 %collective-permute-start.28 = (bf16[128,1024]{1,0:T(8,128)(2,1)S(1)}, bf16[128,1024]{1,0:T(8,128)(2,1)S(1)}, u32[]{:S(2)}, u32[]{:S(2)}) collective-permute-start(bf16[128,1024]{1,0:T(8,128)(2,1)S(1)} %multiply_convert_fusion.refs_0_), channel_id=1, source_target_pairs={{0,2},{2,0},{1,3},{3,1},{4,6},{6,4},{5,7},{7,5},{8,10},{10,8},{9,1... | collective-permute-start | bytes 786440 | tf_op jit(solution)/shard_map/ppermute | solution.py:42
  149.7 7.6 %collective-permute-start.31 = (bf16[128,1024]{1,0:T(8,128)(2,1)S(1)}, bf16[128,1024]{1,0:T(8,128)(2,1)S(1)}, u32[]{:S(2)}, u32[]{:S(2)}) collective-permute-start(bf16[128,1024]{1,0:T(8,128)(2,1)S(1)} %multiply_convert_fusion.refs_0_), channel_id=1, source_target_pairs={{0,4},{4,8},{8,12},{12,0},{1,5},{5,9},{9,13},{13,1},{2,6},{6,10},{... | collective-permute-start | bytes 786440 | tf_op jit(solution)/shard_map/ppermute | solution.py:44
  151.2 6.4 %collective-permute-start.29 = (bf16[128,1024]{1,0:T(8,128)(2,1)S(1)}, bf16[128,1024]{1,0:T(8,128)(2,1)S(1)}, u32[]{:S(2)}, u32[]{:S(2)}) collective-permute-start(bf16[128,1024]{1,0:T(8,128)(2,1)S(1)} %multiply_convert_fusion.refs_0_), channel_id=1, source_target_pairs={{0,12},{4,0},{8,4},{12,8},{1,13},{5,1},{9,5},{13,9},{2,14},{6,2},{... | collective-permute-start | bytes 786440 | tf_op jit(solution)/shard_map/ppermute | solution.py:43
  153.0 7.8 %collective-permute-start.35 = (bf16[128,1024]{1,0:T(8,128)(2,1)S(1)}, bf16[128,1024]{1,0:T(8,128)(2,1)S(1)}, u32[]{:S(2)}, u32[]{:S(2)}) collective-permute-start(bf16[128,1024]{1,0:T(8,128)(2,1)S(1)} %multiply_convert_fusion.refs_0_), channel_id=1, source_target_pairs={{0,1},{1,0},{2,3},{3,2},{4,5},{5,4},{6,7},{7,6},{8,9},{9,8},{10,11... | collective-permute-start | bytes 786440 | tf_op jit(solution)/shard_map/ppermute | solution.py:30
  154.1 8.8 %collective-permute-start.32 = (bf16[128,1024]{1,0:T(8,128)(2,1)S(1)}, bf16[128,1024]{1,0:T(8,128)(2,1)S(1)}, u32[]{:S(2)}, u32[]{:S(2)}) collective-permute-start(bf16[128,1024]{1,0:T(8,128)(2,1)S(1)} %collective-permute-done.28.refs_1_), channel_id=1, source_target_pairs={{0,4},{4,8},{8,12},{12,0},{1,5},{5,9},{9,13},{13,1},{2,6},{6,10},{... | collective-permute-start | bytes 786440 | tf_op jit(solution)/shard_map/ppermute | solution.py:47
  157.3 5.9 %collective-permute-start.39 = (bf16[128,1024]{1,0:T(8,128)(2,1)S(1)}, bf16[128,1024]{1,0:T(8,128)(2,1)S(1)}, u32[]{:S(2)}, u32[]{:S(2)}) collective-permute-start(bf16[128,1024]{1,0:T(8,128)(2,1)S(1)} %collective-permute-done.31.refs_4_), channel_id=1, source_target_pairs={{0,1},{1,0},{2,3},{3,2},{4,5},{5,4},{6,7},{7,6},{8,9},{9,8},{10,11... | collective-permute-start | bytes 786440 | tf_op jit(solution)/shard_map/ppermute | solution.py:30
  157.6 5.6 %collective-permute-start.37 = (bf16[128,1024]{1,0:T(8,128)(2,1)S(1)}, bf16[128,1024]{1,0:T(8,128)(2,1)S(1)}, u32[]{:S(2)}, u32[]{:S(2)}) collective-permute-start(bf16[128,1024]{1,0:T(8,128)(2,1)S(1)} %collective-permute-done.29.refs_2_), channel_id=1, source_target_pairs={{0,1},{1,0},{2,3},{3,2},{4,5},{5,4},{6,7},{7,6},{8,9},{9,8},{10,11... | collective-permute-start | bytes 786440 | tf_op jit(solution)/shard_map/ppermute | solution.py:30
  157.8 9.6 %collective-permute-start.33 = (bf16[128,1024]{1,0:T(8,128)(2,1)S(1)}, bf16[128,1024]{1,0:T(8,128)(2,1)S(1)}, u32[]{:S(2)}, u32[]{:S(2)}) collective-permute-start(bf16[128,1024]{1,0:T(8,128)(2,1)S(1)} %collective-permute-done.29.refs_2_), channel_id=1, source_target_pairs={{0,12},{4,0},{8,4},{12,8},{1,13},{5,1},{9,5},{13,9},{2,14},{6,2},{... | collective-permute-start | bytes 786440 | tf_op jit(solution)/shard_map/ppermute | solution.py:45
  160.8 11.6 %collective-permute-start.30 = (bf16[128,1024]{1,0:T(8,128)(2,1)S(1)}, bf16[128,1024]{1,0:T(8,128)(2,1)S(1)}, u32[]{:S(2)}, u32[]{:S(2)}) collective-permute-start(bf16[128,1024]{1,0:T(8,128)(2,1)S(1)} %collective-permute-done.28.refs_1_), channel_id=1, source_target_pairs={{0,12},{4,0},{8,4},{12,8},{1,13},{5,1},{9,5},{13,9},{2,14},{6,2},{... | collective-permute-start | bytes 786440 | tf_op jit(solution)/shard_map/ppermute | solution.py:46
  162.9 9.5 %collective-permute-start.34 = (bf16[128,1024]{1,0:T(8,128)(2,1)S(1)}, bf16[128,1024]{1,0:T(8,128)(2,1)S(1)}, u32[]{:S(2)}, u32[]{:S(2)}) collective-permute-start(bf16[128,1024]{1,0:T(8,128)(2,1)S(1)} %collective-permute-done.32.refs_5_), channel_id=1, source_target_pairs={{0,4},{4,8},{8,12},{12,0},{1,5},{5,9},{9,13},{13,1},{2,6},{6,10},{... | collective-permute-start | bytes 786440 | tf_op jit(solution)/shard_map/ppermute | solution.py:51
  163.2 9.7 %collective-permute-start.36 = (bf16[128,1024]{1,0:T(8,128)(2,1)S(1)}, bf16[128,1024]{1,0:T(8,128)(2,1)S(1)}, u32[]{:S(2)}, u32[]{:S(2)}) collective-permute-start(bf16[128,1024]{1,0:T(8,128)(2,1)S(1)} %collective-permute-done.28.refs_1_), channel_id=1, source_target_pairs={{0,1},{1,0},{2,3},{3,2},{4,5},{5,4},{6,7},{7,6},{8,9},{9,8},{10,11... | collective-permute-start | bytes 786440 | tf_op jit(solution)/shard_map/ppermute | solution.py:30
  163.2 9.7 %collective-permute-start.40 = (bf16[128,1024]{1,0:T(8,128)(2,1)S(1)}, bf16[128,1024]{1,0:T(8,128)(2,1)S(1)}, u32[]{:S(2)}, u32[]{:S(2)}) collective-permute-start(bf16[128,1024]{1,0:T(8,128)(2,1)S(1)} %collective-permute-done.32.refs_5_), channel_id=1, source_target_pairs={{0,1},{1,0},{2,3},{3,2},{4,5},{5,4},{6,7},{7,6},{8,9},{9,8},{10,11... | collective-permute-start | bytes 786440 | tf_op jit(solution)/shard_map/ppermute | solution.py:30
  167.4 5.5 %collective-permute-start.41 = (bf16[128,1024]{1,0:T(8,128)(2,1)S(1)}, bf16[128,1024]{1,0:T(8,128)(2,1)S(1)}, u32[]{:S(2)}, u32[]{:S(2)}) collective-permute-start(bf16[128,1024]{1,0:T(8,128)(2,1)S(1)} %collective-permute-done.33.refs_6_), channel_id=1, source_target_pairs={{0,1},{1,0},{2,3},{3,2},{4,5},{5,4},{6,7},{7,6},{8,9},{9,8},{10,11... | collective-permute-start | bytes 786440 | tf_op jit(solution)/shard_map/ppermute | solution.py:30
  172.4 1.5 collective-permute-start.38
  172.4 1.9 collective-permute-start.42
  177.3 19.3 %copy-start.2 = (bf16[320,1024]{1,0:T(8,128)(2,1)S(1)}, bf16[320,1024]{1,0:T(8,128)(2,1)}, u32[]{:S(2)}) copy-start(bf16[320,1024]{1,0:T(8,128)(2,1)} %param.4) | copy-start | bytes 1966084
  193.1 13.5 %all-to-all-start.4 = ((bf16[8,320,128]{2,1,0:T(8,128)(2,1)}), bf16[8,320,128]{2,1,0:T(8,128)(2,1)S(1)}, u32[]{:S(2)}, u32[]{:S(2)}) async-start(bf16[8,320,128]{2,1,0:T(8,128)(2,1)} %broadcast_in_dim.2), calls=%async_computation.4 | async-start | bytes 1310720 | tf_op jit(solution)/shard_map/all_to_all | solution.py:34

commit v10 on v9

--- a/solution.py
+++ b/solution.py
@@ -242,28 +242,26 @@
 def head_kernel(place, summaries, rider, *refs):
     piece_refs, (head_ref, all_ref, rows, copy_sem, out_sem) = refs[:16], refs[16:]
     features = summaries.shape[0]
-    copies = []
+    copies, outs = [], []
     for n in range(8):
         for i, chunk in enumerate(query_chunks(place, n)):
-            to = pl.multiple_of(chunk * ROWS, ROWS)
+            to = pl.ds(pl.multiple_of(chunk * ROWS, ROWS), ROWS)
             at = 2 * n + i
             copies.append(
-                pltpu.make_async_copy(
-                    piece_refs[at], rows.at[pl.ds(to, ROWS), :], copy_sem.at[at]
-                )
+                pltpu.make_async_copy(piece_refs[at], rows.at[to, :], copy_sem.at[at])
             )
-    for copy in copies:
+            outs.append(pltpu.make_async_copy(piece_refs[at], all_ref.at[to, :], out_sem.at[at]))
+    for copy in copies + outs:
         copy.start()
     for j in range(8):
         head_ref[j, features:] = rider[...]
     for copy in copies:
         copy.wait()
-    out = pltpu.make_async_copy(rows, all_ref, out_sem)
-    out.start()
     total = jnp.dot(summaries[...], rows[...], preferred_element_type=F32).astype(BF16)
     for j in range(8):
         head_ref[j, :features] = total[:, j * ROWS : (j + 1) * ROWS]
-    out.wait()
+    for out in outs:
+        out.wait()
 
 
 def whole(shape):
@@ -356,7 +354,7 @@
             scratch_shapes=[
                 pltpu.VMEM((GROUP, WIDTH), BF16),
                 pltpu.SemaphoreType.DMA((16,)),
-                pltpu.SemaphoreType.DMA,
+                pltpu.SemaphoreType.DMA((16,)),
             ],
         ),
         out_shape=[

time: 210 us -> 210 us (level)
  no operation moved by 1% of the time
where the time goes in v10:
time: 210 us; the launch traced here: 209 us
  blocking collectives  78.5 us (37%)
  starting transfers between devices  48.8 us (23%)
  waiting for transfers between devices  43.1 us (21%)
  Pallas kernels  22 us (10%)
  matrix products  8.72 us (4%)
  other arithmetic  3.22 us (2%)
  between operations  2.62 us (1%)
  local copies, waits for them, and re-layouts  2.17 us (1%)
    all_to_all x2, blocking collectives, sum_exchange(): return jnp.sum(lax.all_to_all(parts, axes, 0, 0).astype(F32), axis=0)  63.8 us
    all_to_all x1, blocking collectives, shards(): pieces = lax.all_to_all(head_part, XZ, 0, 0)  14.8 us
    pallas_call x1, Pallas kernels, score_call(): pl.pallas_call(score_kernel, grid_spec=pltpu.PrefetchScalarGridSpec(num_s...  9.8 us
    pallas_call x1, Pallas kernels, grad_call(): pl.pallas_call(grad_kernel, grid_spec=pltpu.PrefetchScalarGridSpec(num_sc...  9.1 us
    ppermute x3, waiting for transfers between devices, gather_ring(): far_own = lax.ppermute(after_own, long_axis, RING[3])  8.02 us
    ppermute x3, waiting for transfers between devices, gather_ring(): after_other = lax.ppermute(other, long_axis, RING[3])  7.67 us
    ppermute x3, waiting for transfers between devices, gather_ring(): other = lax.ppermute(own, short_axis, SWAP)  7.02 us
    ppermute x3, starting transfers between devices, gather_ring(): after_other = lax.ppermute(other, long_axis, RING[3])  6.91 us
  transfers between devices with their start and end apart: 45, of which 23 were waited for; matrix products, arithmetic and copies ran while one was open for 4% of the time, Pallas kernels for 0%

profile of v10, /device:TPU:0, one launch (start us, length us, event | category | flops | bytes accessed | tf_op | source)
XLA Modules:
  0.0 209.2 jit_solution(2149990653284562669)
XLA Ops:
  0.6 1.1 dynamic-slice_bitcast_fusion
  2.4 2.6 %fusion = f32[1024,1024]{1,0:T(8,128)S(1)} fusion(bf16[320,1024]{1,0:T(8,128)(2,1)} %param.4, bf16[2048,320]{0,1:T(8,128)(2,1)} %param.3, s32[]{:T(128)S(6)} %select_n.6), kind=kOutput, calls=%fused_computation.8 | convolution fusion | flops 671088640 | bytes 5505028 | tf_op jit(solution)/shard_map/dot_general | solution.py:382
  5.1 1.3 add_convert_fusion
  6.5 36.1 %all_to_all.25 = bf16[8,128,1024]{2,1,0:T(8,128)(2,1)S(1)} all-to-all(bf16[8,128,1024]{2,1,0:T(8,128)(2,1)S(1)} %bitcast.26), channel_id=1, replica_groups=mesh['x'=4,'zl'=2,'y'=4,'zh'=2,'c'=2] {'y','zh'}, dimensions={0} | all-to-all | bytes 4194304 | tf_op jit(solution)/shard_map/all_to_all | solution.py:38
  43.5 3.0 %collective-permute-start.10 = (bf16[128,1024]{1,0:T(8,128)(2,1)S(1)}, bf16[128,1024]{1,0:T(8,128)(2,1)S(1)}, u32[]{:S(2)}, u32[]{:S(2)}) collective-permute-start(bf16[128,1024]{1,0:T(8,128)(2,1)S(1)} %multiply_convert_fusion.1.refs_0_.refs_8_), channel_id=1, source_target_pairs={{0,12},{4,0},{8,4},{12,8},{1,13},{5,1},{9,5},{13,9},{2,14},{6,2},{... | collective-permute-start | bytes 786440 | tf_op jit(solution)/shard_map/ppermute | solution.py:43
  46.5 1.2 collective-permute-start.9
  47.7 1.5 collective-permute-start.5
  49.2 1.7 collective-permute-start.3
  50.9 2.2 %collective-permute-done.12.refs_12_ = bf16[128,1024]{1,0:T(8,128)(2,1)S(1)} collective-permute-done((bf16[128,1024]{1,0:T(8,128)(2,1)S(1)}, bf16[128,1024]{1,0:T(8,128)(2,1)S(1)}, u32[]{:S(2)}, u32[]{:S(2)}) %collective-permute-start.12) | collective-permute-done | bytes 262176 | tf_op jit(solution)/shard_map/ppermute | solution.py:44
  53.1 1.0 collective-permute-start.2
  54.1 1.9 collective-permute-done.9.refs_9_
  57.0 4.0 %collective-permute-done.2.refs_1_ = bf16[128,1024]{1,0:T(8,128)(2,1)S(1)} collective-permute-done((bf16[128,1024]{1,0:T(8,128)(2,1)S(1)}, bf16[128,1024]{1,0:T(8,128)(2,1)S(1)}, u32[]{:S(2)}, u32[]{:S(2)}) %collective-permute-start.2) | collective-permute-done | bytes 262176 | tf_op jit(solution)/shard_map/ppermute | solution.py:42
  61.0 3.2 %collective-permute-start.11 = (bf16[128,1024]{1,0:T(8,128)(2,1)S(1)}, bf16[128,1024]{1,0:T(8,128)(2,1)S(1)}, u32[]{:S(2)}, u32[]{:S(2)}) collective-permute-start(bf16[128,1024]{1,0:T(8,128)(2,1)S(1)} %collective-permute-done.9.refs_9_), channel_id=1, source_target_pairs={{0,12},{4,0},{8,4},{12,8},{1,13},{5,1},{9,5},{13,9},{2,14},{6,2},{... | collective-permute-start | bytes 786440 | tf_op jit(solution)/shard_map/ppermute | solution.py:46
  64.2 2.8 %collective-permute-start.7 = (bf16[128,1024]{1,0:T(8,128)(2,1)S(1)}, bf16[128,1024]{1,0:T(8,128)(2,1)S(1)}, u32[]{:S(2)}, u32[]{:S(2)}) collective-permute-start(bf16[128,1024]{1,0:T(8,128)(2,1)S(1)} %collective-permute-done.3.refs_2_), channel_id=1, source_target_pairs={{0,96},{32,0},{64,32},{96,64},{1,97},{33,1},{65,33},{97,65},{2,98}... | collective-permute-start | bytes 786440 | tf_op jit(solution)/shard_map/ppermute | solution.py:45
  67.0 1.2 collective-permute-start.8
  69.2 1.3 collective-permute-done.11.refs_11_
  70.4 2.8 %collective-permute-start.4 = (bf16[128,1024]{1,0:T(8,128)(2,1)S(1)}, bf16[128,1024]{1,0:T(8,128)(2,1)S(1)}, u32[]{:S(2)}, u32[]{:S(2)}) collective-permute-start(bf16[128,1024]{1,0:T(8,128)(2,1)S(1)} %collective-permute-done.2.refs_1_), channel_id=1, source_target_pairs={{0,96},{32,0},{64,32},{96,64},{1,97},{33,1},{65,33},{97,65},{2,98}... | collective-permute-start | bytes 786440 | tf_op jit(solution)/shard_map/ppermute | solution.py:46
  73.2 4.4 %collective-permute-done.7.refs_6_ = bf16[128,1024]{1,0:T(8,128)(2,1)S(1)} collective-permute-done((bf16[128,1024]{1,0:T(8,128)(2,1)S(1)}, bf16[128,1024]{1,0:T(8,128)(2,1)S(1)}, u32[]{:S(2)}, u32[]{:S(2)}) %collective-permute-start.7) | collective-permute-done | bytes 262176 | tf_op jit(solution)/shard_map/ppermute | solution.py:45
  78.1 2.2 %collective-permute-done.6.refs_5_ = bf16[128,1024]{1,0:T(8,128)(2,1)S(1)} collective-permute-done((bf16[128,1024]{1,0:T(8,128)(2,1)S(1)}, bf16[128,1024]{1,0:T(8,128)(2,1)S(1)}, u32[]{:S(2)}, u32[]{:S(2)}) %collective-permute-start.6) | collective-permute-done | bytes 262176 | tf_op jit(solution)/shard_map/ppermute | solution.py:47
  80.7 1.4 collective-permute-done.4.refs_3_
  82.2 9.8 %scores.1 = (bf16[1024,2048]{1,0:T(8,128)(2,1)}, f32[8,128]{1,0:T(8,128)S(1)}, f32[8,128]{1,0:T(8,128)S(1)}, f32[16,24,128]{2,1,0:T(8,128)}, bf16[2048,1024]{1,0:T(8,128)(2,1)}) custom-call(s32[5]{0:T(128)S(1)} %stack.23.place, bf16[128,1024]{1,0:T(8,128)(2,1)S(1)} %multiply_convert_fusion.1.refs_0_.refs_8_, ...), custom_call_target="tpu_custom_call" | custom-call | flops 4294967296 | bytes 14680064 | tf_op jit(solution)/shard_map/scores/pallas_call | solution.py:272
  92.0 4.0 %all-to-all-start.1 = ((f32[16,24,128]{2,1,0:T(8,128)}), f32[16,24,128]{2,1,0:T(8,128)S(1)}, u32[]{:S(2)}, u32[]{:S(2)}) async-start(f32[16,24,128]{2,1,0:T(8,128)} %get-tuple-element.22), calls=%async_computation.1 | async-start | bytes 393216 | tf_op jit(solution)/shard_map/all_to_all | solution.py:396
  96.0 1.3 collective-permute-start.24
  97.3 2.4 %collective-permute-done.24 = f32[8,128]{1,0:T(8,128)S(1)} collective-permute-done((f32[8,128]{1,0:T(8,128)S(1)}, f32[8,128]{1,0:T(8,128)S(1)}, u32[]{:S(2)}, u32[]{:S(2)}) %collective-permute-start.24) | collective-permute-done | bytes 4128 | tf_op jit(solution)/shard_map/ppermute | solution.py:397
  99.7 2.7 %collective-permute-start.27 = (f32[8,128]{1,0:T(8,128)S(1)}, f32[8,128]{1,0:T(8,128)S(1)}, u32[]{:S(2)}, u32[]{:S(2)}) collective-permute-start(f32[8,128]{1,0:T(8,128)S(1)} %add.28.r0), channel_id=1, source_target_pairs={{0,64},{32,96},{64,0},{96,32},{1,65},{33,97},{65,1},{97,33},{2,66}... | collective-permute-start | bytes 12296 | tf_op jit(solution)/shard_map/ppermute | solution.py:398
  102.4 1.2 collective-permute-start.26
  104.8 1.2 collective-permute-done.26.r2
  106.0 2.5 %collective-permute-done.25.r1 = f32[8,128]{1,0:T(8,128)S(1)} collective-permute-done((f32[8,128]{1,0:T(8,128)S(1)}, f32[8,128]{1,0:T(8,128)S(1)}, u32[]{:S(2)}, u32[]{:S(2)}) %collective-permute-start.25) | collective-permute-done | bytes 4128 | tf_op jit(solution)/shard_map/ppermute | solution.py:398
  108.5 9.1 %grads.1 = (bf16[4,2,128,1024]{3,2,1,0:T(8,128)(2,1)S(1)}, bf16[16,128]{1,0:T(8,128)(2,1)S(1)}) custom-call(s32[5]{0:T(128)S(1)} %stack.23.place, bf16[1024,2048]{1,0:T(8,128)(2,1)} %get-tuple-element.18.w_ref, bf16[2048,1024]{1,0:T(8,128)(2,1)} %get-tuple-element.19.query_ref, f32[8,128]{1,0:T(8,128)S(1)} %get-tuple-element.20.hit_ref, ...), custom_call_target="tpu_custom_call" | custom-call | flops 4294967296 | bytes 14680064 | tf_op jit(solution)/shard_map/grads/pallas_call | solution.py:314
  117.6 27.7 %all_to_all.26 = bf16[8,128,1024]{2,1,0:T(8,128)(2,1)S(1)} all-to-all(bf16[8,128,1024]{2,1,0:T(8,128)(2,1)S(1)} %bitcast.23), channel_id=1, replica_groups=mesh['x'=4,'zl'=2,'y'=4,'zh'=2,'c'=2] {'x','zl'}, dimensions={0} | all-to-all | bytes 4194304 | tf_op jit(solution)/shard_map/all_to_all | solution.py:38
  146.1 3.6 %collective-permute-start.28 = (bf16[128,1024]{1,0:T(8,128)(2,1)S(1)}, bf16[128,1024]{1,0:T(8,128)(2,1)S(1)}, u32[]{:S(2)}, u32[]{:S(2)}) collective-permute-start(bf16[128,1024]{1,0:T(8,128)(2,1)S(1)} %multiply_convert_fusion.refs_0_), channel_id=1, source_target_pairs={{0,2},{2,0},{1,3},{3,1},{4,6},{6,4},{5,7},{7,5},{8,10},{10,8},{9,1... | collective-permute-start | bytes 786440 | tf_op jit(solution)/shard_map/ppermute | solution.py:42
  149.7 1.5 collective-permute-start.31
  151.2 1.7 collective-permute-start.29
  153.0 1.1 collective-permute-done.28.refs_1_
  154.1 1.5 collective-permute-start.32
  155.6 1.7 collective-permute-done.31.refs_4_
  157.8 2.9 %collective-permute-start.33 = (bf16[128,1024]{1,0:T(8,128)(2,1)S(1)}, bf16[128,1024]{1,0:T(8,128)(2,1)S(1)}, u32[]{:S(2)}, u32[]{:S(2)}) collective-permute-start(bf16[128,1024]{1,0:T(8,128)(2,1)S(1)} %collective-permute-done.29.refs_2_), channel_id=1, source_target_pairs={{0,12},{4,0},{8,4},{12,8},{1,13},{5,1},{9,5},{13,9},{2,14},{6,2},{... | collective-permute-start | bytes 786440 | tf_op jit(solution)/shard_map/ppermute | solution.py:45
  160.8 0.9 collective-permute-start.30
  161.7 1.2 collective-permute-done.32.refs_5_
  163.7 3.7 %collective-permute-done.33.refs_6_ = bf16[128,1024]{1,0:T(8,128)(2,1)S(1)} collective-permute-done((bf16[128,1024]{1,0:T(8,128)(2,1)S(1)}, bf16[128,1024]{1,0:T(8,128)(2,1)S(1)}, u32[]{:S(2)}, u32[]{:S(2)}) %collective-permute-start.33) | collective-permute-done | bytes 262176 | tf_op jit(solution)/shard_map/ppermute | solution.py:45
  167.4 5.0 %collective-permute-done.30.refs_3_ = bf16[128,1024]{1,0:T(8,128)(2,1)S(1)} collective-permute-done((bf16[128,1024]{1,0:T(8,128)(2,1)S(1)}, bf16[128,1024]{1,0:T(8,128)(2,1)S(1)}, u32[]{:S(2)}, u32[]{:S(2)}) %collective-permute-start.30) | collective-permute-done | bytes 262176 | tf_op jit(solution)/shard_map/ppermute | solution.py:46
  172.9 1.0 collective-permute-done.38.refs_11_
  174.3 3.1 %head_parts.1 = (bf16[8,336,128]{2,1,0:T(8,128)(2,1)S(1)}, bf16[2048,1024]{1,0:T(8,128)(2,1)}) custom-call(s32[5]{0:T(128)S(1)} %stack.23.place, bf16[320,2048]{1,0:T(8,128)(2,1)S(1)} %bitcast.22, bf16[16,128]{1,0:T(8,128)(2,1)S(1)} %get-tuple-element.23.rider, bf16[128,1024]{1,0:T(8,128)(2,1)S(1)} %multiply_convert_fusion.refs_0_, ...), custom_call_target="tpu_custom_call" | custom-call | flops 1342177280 | bytes 10485760 | tf_op jit(solution)/shard_map/head_parts/pallas_call | solution.py:346
  177.5 14.8 %all_to_all.27 = bf16[8,336,128]{2,1,0:T(8,128)(2,1)S(1)} all-to-all(bf16[8,336,128]{2,1,0:T(8,128)(2,1)S(1)} %get-tuple-element.25), channel_id=1, replica_groups=mesh['x'=4,'zl'=2,'y'=4,'zh'=2,'c'=2] {'x','zl'}, dimensions={0} | all-to-all | bytes 1376256 | tf_op jit(solution)/shard_map/all_to_all | solution.py:406
  193.3 3.5 %all-to-all-start.4 = ((bf16[8,320,128]{2,1,0:T(8,128)(2,1)}), bf16[8,320,128]{2,1,0:T(8,128)(2,1)S(1)}, u32[]{:S(2)}, u32[]{:S(2)}) async-start(bf16[8,320,128]{2,1,0:T(8,128)(2,1)} %broadcast_in_dim.2), calls=%async_computation.4 | async-start | bytes 1310720 | tf_op jit(solution)/shard_map/all_to_all | solution.py:34
  196.8 4.8 %convolution_convert_fusion = bf16[2048,320]{0,1:T(8,128)(2,1)} fusion(bf16[2048,1024]{1,0:T(8,128)(2,1)} %get-tuple-element.26, bf16[320,1024]{1,0:T(8,128)(2,1)S(1)} %copy-done.2), kind=kOutput, calls=%fused_computation.3 | convolution fusion | flops 1342832640 | bytes 6160384 | tf_op jit(solution)/shard_map/dot_general | solution.py:414
  202.9 4.0 %all-to-all-done.4 = bf16[8,320,128]{2,1,0:T(8,128)(2,1)S(1)} async-done(((bf16[8,320,128]{2,1,0:T(8,128)(2,1)}), bf16[8,320,128]{2,1,0:T(8,128)(2,1)S(1)}, u32[]{:S(2)}, u32[]{:S(2)}) %all-to-all-start.4) | async-done | bytes 655392 | tf_op jit(solution)/shard_map/all_to_all | solution.py:34
  206.8 1.2 copy_bitcast_fusion
  (72 shorter events, 10.3 us)
Async XLA Ops:
  1.8 3.3 %collective-permute-start = (bf16[320,1024]{1,0:T(8,128)(2,1)S(1)}, bf16[320,1024]{1,0:T(8,128)(2,1)S(1)}, u32[]{:S(2)}, u32[]{:S(2)}) collective-permute-start(bf16[320,1024]{1,0:T(8,128)(2,1)S(1)} %dynamic-slice_bitcast_fusion), channel_id=1, source_target_pairs={{0,1},{1,0},{2,3},{3,2},{4,5},{5,4},{6,7},{7,6},{8,9},{9,8},{10,11... | collective-permute-start | bytes 1966088 | tf_op jit(solution)/shard_map/ppermute | solution.py:30
  1.9 3.2 %collective-permute-start.1 = (bf16[320,1024]{1,0:T(8,128)(2,1)}, bf16[320,1024]{1,0:T(8,128)(2,1)S(1)}, u32[]{:S(2)}, u32[]{:S(2)}) collective-permute-start(bf16[320,1024]{1,0:T(8,128)(2,1)} %param.4), channel_id=1, source_target_pairs={{0,1},{1,0},{2,3},{3,2},{4,5},{5,4},{6,7},{7,6},{8,9},{9,8},{10,11... | collective-permute-start | bytes 1966088 | tf_op jit(solution)/shard_map/ppermute | solution.py:30
  42.5 39.7 %copy-start.1 = (s32[2048]{0:T(1024)S(1)}, s32[2048]{0:T(1024)}, u32[]{:S(2)}) copy-start(s32[2048]{0:T(1024)} %param.5) | copy-start | bytes 24580
  43.1 6.1 %collective-permute-start.16 = (bf16[128,1024]{1,0:T(8,128)(2,1)S(1)}, bf16[128,1024]{1,0:T(8,128)(2,1)S(1)}, u32[]{:S(2)}, u32[]{:S(2)}) collective-permute-start(bf16[128,1024]{1,0:T(8,128)(2,1)S(1)} %multiply_convert_fusion.1.refs_0_.refs_8_), channel_id=1, source_target_pairs={{0,1},{1,0},{2,3},{3,2},{4,5},{5,4},{6,7},{7,6},{8,9},{9,8},{10,11... | collective-permute-start | bytes 786440 | tf_op jit(solution)/shard_map/ppermute | solution.py:30
  43.2 9.9 %collective-permute-start.12 = (bf16[128,1024]{1,0:T(8,128)(2,1)S(1)}, bf16[128,1024]{1,0:T(8,128)(2,1)S(1)}, u32[]{:S(2)}, u32[]{:S(2)}) collective-permute-start(bf16[128,1024]{1,0:T(8,128)(2,1)S(1)} %multiply_convert_fusion.1.refs_0_.refs_8_), channel_id=1, source_target_pairs={{0,4},{4,8},{8,12},{12,0},{1,5},{5,9},{9,13},{13,1},{2,6},{6,10},{... | collective-permute-start | bytes 786440 | tf_op jit(solution)/shard_map/ppermute | solution.py:44
  43.5 10.6 %collective-permute-start.10 = (bf16[128,1024]{1,0:T(8,128)(2,1)S(1)}, bf16[128,1024]{1,0:T(8,128)(2,1)S(1)}, u32[]{:S(2)}, u32[]{:S(2)}) collective-permute-start(bf16[128,1024]{1,0:T(8,128)(2,1)S(1)} %multiply_convert_fusion.1.refs_0_.refs_8_), channel_id=1, source_target_pairs={{0,12},{4,0},{8,4},{12,8},{1,13},{5,1},{9,5},{13,9},{2,14},{6,2},{... | collective-permute-start | bytes 786440 | tf_op jit(solution)/shard_map/ppermute | solution.py:43
  46.5 9.6 %collective-permute-start.9 = (bf16[128,1024]{1,0:T(8,128)(2,1)S(1)}, bf16[128,1024]{1,0:T(8,128)(2,1)S(1)}, u32[]{:S(2)}, u32[]{:S(2)}) collective-permute-start(bf16[128,1024]{1,0:T(8,128)(2,1)S(1)} %multiply_convert_fusion.1.refs_0_.refs_8_), channel_id=1, source_target_pairs={{0,2},{2,0},{1,3},{3,1},{4,6},{6,4},{5,7},{7,5},{8,10},{10,8},{9,1... | collective-permute-start | bytes 786440 | tf_op jit(solution)/shard_map/ppermute | solution.py:42
  47.7 9.0 %collective-permute-start.5 = (bf16[128,1024]{1,0:T(8,128)(2,1)S(1)}, bf16[128,1024]{1,0:T(8,128)(2,1)S(1)}, u32[]{:S(2)}, u32[]{:S(2)}) collective-permute-start(bf16[128,1024]{1,0:T(8,128)(2,1)S(1)} %multiply_convert_fusion.1.refs_0_.refs_8_), channel_id=1, source_target_pairs={{0,32},{32,64},{64,96},{96,0},{1,33},{33,65},{65,97},{97,1},{2,34}... | collective-permute-start | bytes 786440 | tf_op jit(solution)/shard_map/ppermute | solution.py:44
  49.2 7.8 %collective-permute-start.3 = (bf16[128,1024]{1,0:T(8,128)(2,1)S(1)}, bf16[128,1024]{1,0:T(8,128)(2,1)S(1)}, u32[]{:S(2)}, u32[]{:S(2)}) collective-permute-start(bf16[128,1024]{1,0:T(8,128)(2,1)S(1)} %multiply_convert_fusion.1.refs_0_.refs_8_), channel_id=1, source_target_pairs={{0,96},{32,0},{64,32},{96,64},{1,97},{33,1},{65,33},{97,65},{2,98}... | collective-permute-start | bytes 786440 | tf_op jit(solution)/shard_map/ppermute | solution.py:43
  53.1 7.9 %collective-permute-start.2 = (bf16[128,1024]{1,0:T(8,128)(2,1)S(1)}, bf16[128,1024]{1,0:T(8,128)(2,1)S(1)}, u32[]{:S(2)}, u32[]{:S(2)}) collective-permute-start(bf16[128,1024]{1,0:T(8,128)(2,1)S(1)} %multiply_convert_fusion.1.refs_0_.refs_8_), channel_id=1, source_target_pairs={{0,16},{16,0},{1,17},{17,1},{2,18},{18,2},{3,19},{19,3},{4,20},{20... | collective-permute-start | bytes 786440 | tf_op jit(solution)/shard_map/ppermute | solution.py:42
  54.1 6.8 %collective-permute-start.20 = (bf16[128,1024]{1,0:T(8,128)(2,1)S(1)}, bf16[128,1024]{1,0:T(8,128)(2,1)S(1)}, u32[]{:S(2)}, u32[]{:S(2)}) collective-permute-start(bf16[128,1024]{1,0:T(8,128)(2,1)S(1)} %collective-permute-done.12.refs_12_), channel_id=1, source_target_pairs={{0,1},{1,0},{2,3},{3,2},{4,5},{5,4},{6,7},{7,6},{8,9},{9,8},{10,11... | collective-permute-start | bytes 786440 | tf_op jit(solution)/shard_map/ppermute | solution.py:30
  56.1 8.1 %collective-permute-start.18 = (bf16[128,1024]{1,0:T(8,128)(2,1)S(1)}, bf16[128,1024]{1,0:T(8,128)(2,1)S(1)}, u32[]{:S(2)}, u32[]{:S(2)}) collective-permute-start(bf16[128,1024]{1,0:T(8,128)(2,1)S(1)} %collective-permute-done.10.refs_10_), channel_id=1, source_target_pairs={{0,1},{1,0},{2,3},{3,2},{4,5},{5,4},{6,7},{7,6},{8,9},{9,8},{10,11... | collective-permute-start | bytes 786440 | tf_op jit(solution)/shard_map/ppermute | solution.py:30
  56.7 10.3 %collective-permute-start.14 = (bf16[128,1024]{1,0:T(8,128)(2,1)S(1)}, bf16[128,1024]{1,0:T(8,128)(2,1)S(1)}, u32[]{:S(2)}, u32[]{:S(2)}) collective-permute-start(bf16[128,1024]{1,0:T(8,128)(2,1)S(1)} %collective-permute-done.10.refs_10_), channel_id=1, source_target_pairs={{0,12},{4,0},{8,4},{12,8},{1,13},{5,1},{9,5},{13,9},{2,14},{6,2},{... | collective-permute-start | bytes 786440 | tf_op jit(solution)/shard_map/ppermute | solution.py:45
  57.0 11.2 %collective-permute-start.17 = (bf16[128,1024]{1,0:T(8,128)(2,1)S(1)}, bf16[128,1024]{1,0:T(8,128)(2,1)S(1)}, u32[]{:S(2)}, u32[]{:S(2)}) collective-permute-start(bf16[128,1024]{1,0:T(8,128)(2,1)S(1)} %collective-permute-done.9.refs_9_), channel_id=1, source_target_pairs={{0,1},{1,0},{2,3},{3,2},{4,5},{5,4},{6,7},{7,6},{8,9},{9,8},{10,11... | collective-permute-start | bytes 786440 | tf_op jit(solution)/shard_map/ppermute | solution.py:30
  61.0 8.2 %collective-permute-start.13 = (bf16[128,1024]{1,0:T(8,128)(2,1)S(1)}, bf16[128,1024]{1,0:T(8,128)(2,1)S(1)}, u32[]{:S(2)}, u32[]{:S(2)}) collective-permute-start(bf16[128,1024]{1,0:T(8,128)(2,1)S(1)} %collective-permute-done.9.refs_9_), channel_id=1, source_target_pairs={{0,4},{4,8},{8,12},{12,0},{1,5},{5,9},{9,13},{13,1},{2,6},{6,10},{... | collective-permute-start | bytes 786440 | tf_op jit(solution)/shard_map/ppermute | solution.py:47
  61.0 9.4 %collective-permute-start.11 = (bf16[128,1024]{1,0:T(8,128)(2,1)S(1)}, bf16[128,1024]{1,0:T(8,128)(2,1)S(1)}, u32[]{:S(2)}, u32[]{:S(2)}) collective-permute-start(bf16[128,1024]{1,0:T(8,128)(2,1)S(1)} %collective-permute-done.9.refs_9_), channel_id=1, source_target_pairs={{0,12},{4,0},{8,4},{12,8},{1,13},{5,1},{9,5},{13,9},{2,14},{6,2},{... | collective-permute-start | bytes 786440 | tf_op jit(solution)/shard_map/ppermute | solution.py:46
  64.2 13.3 %collective-permute-start.7 = (bf16[128,1024]{1,0:T(8,128)(2,1)S(1)}, bf16[128,1024]{1,0:T(8,128)(2,1)S(1)}, u32[]{:S(2)}, u32[]{:S(2)}) collective-permute-start(bf16[128,1024]{1,0:T(8,128)(2,1)S(1)} %collective-permute-done.3.refs_2_), channel_id=1, source_target_pairs={{0,96},{32,0},{64,32},{96,64},{1,97},{33,1},{65,33},{97,65},{2,98}... | collective-permute-start | bytes 786440 | tf_op jit(solution)/shard_map/ppermute | solution.py:45
  67.0 10.6 %collective-permute-start.8 = (bf16[128,1024]{1,0:T(8,128)(2,1)S(1)}, bf16[128,1024]{1,0:T(8,128)(2,1)S(1)}, u32[]{:S(2)}, u32[]{:S(2)}) collective-permute-start(bf16[128,1024]{1,0:T(8,128)(2,1)S(1)} %collective-permute-done.2.refs_1_), channel_id=1, source_target_pairs={{0,64},{32,96},{64,0},{96,32},{1,65},{33,97},{65,1},{97,33},{2,66}... | collective-permute-start | bytes 786440 | tf_op jit(solution)/shard_map/ppermute | solution.py:49
  68.2 12.0 %collective-permute-start.6 = (bf16[128,1024]{1,0:T(8,128)(2,1)S(1)}, bf16[128,1024]{1,0:T(8,128)(2,1)S(1)}, u32[]{:S(2)}, u32[]{:S(2)}) collective-permute-start(bf16[128,1024]{1,0:T(8,128)(2,1)S(1)} %collective-permute-done.2.refs_1_), channel_id=1, source_target_pairs={{0,32},{32,64},{64,96},{96,0},{1,33},{33,65},{65,97},{97,1},{2,34}... | collective-permute-start | bytes 786440 | tf_op jit(solution)/shard_map/ppermute | solution.py:47
  69.2 11.1 %collective-permute-start.15 = (bf16[128,1024]{1,0:T(8,128)(2,1)S(1)}, bf16[128,1024]{1,0:T(8,128)(2,1)S(1)}, u32[]{:S(2)}, u32[]{:S(2)}) collective-permute-start(bf16[128,1024]{1,0:T(8,128)(2,1)S(1)} %collective-permute-done.13.refs_13_), channel_id=1, source_target_pairs={{0,4},{4,8},{8,12},{12,0},{1,5},{5,9},{9,13},{13,1},{2,6},{6,10},{... | collective-permute-start | bytes 786440 | tf_op jit(solution)/shard_map/ppermute | solution.py:51
  70.4 11.7 %collective-permute-start.4 = (bf16[128,1024]{1,0:T(8,128)(2,1)S(1)}, bf16[128,1024]{1,0:T(8,128)(2,1)S(1)}, u32[]{:S(2)}, u32[]{:S(2)}) collective-permute-start(bf16[128,1024]{1,0:T(8,128)(2,1)S(1)} %collective-permute-done.2.refs_1_), channel_id=1, source_target_pairs={{0,96},{32,0},{64,32},{96,64},{1,97},{33,1},{65,33},{97,65},{2,98}... | collective-permute-start | bytes 786440 | tf_op jit(solution)/shard_map/ppermute | solution.py:46
  77.6 4.6 %collective-permute-start.21 = (bf16[128,1024]{1,0:T(8,128)(2,1)S(1)}, bf16[128,1024]{1,0:T(8,128)(2,1)S(1)}, u32[]{:S(2)}, u32[]{:S(2)}) collective-permute-start(bf16[128,1024]{1,0:T(8,128)(2,1)S(1)} %collective-permute-done.13.refs_13_), channel_id=1, source_target_pairs={{0,1},{1,0},{2,3},{3,2},{4,5},{5,4},{6,7},{7,6},{8,9},{9,8},{10,11... | collective-permute-start | bytes 786440 | tf_op jit(solution)/shard_map/ppermute | solution.py:30
  77.6 4.6 %collective-permute-start.22 = (bf16[128,1024]{1,0:T(8,128)(2,1)S(1)}, bf16[128,1024]{1,0:T(8,128)(2,1)S(1)}, u32[]{:S(2)}, u32[]{:S(2)}) collective-permute-start(bf16[128,1024]{1,0:T(8,128)(2,1)S(1)} %collective-permute-done.14.refs_14_), channel_id=1, source_target_pairs={{0,1},{1,0},{2,3},{3,2},{4,5},{5,4},{6,7},{7,6},{8,9},{9,8},{10,11... | collective-permute-start | bytes 786440 | tf_op jit(solution)/shard_map/ppermute | solution.py:30
  80.2 1.9 collective-permute-start.19
  80.2 1.9 collective-permute-start.23
  92.0 16.5 %all-to-all-start.1 = ((f32[16,24,128]{2,1,0:T(8,128)}), f32[16,24,128]{2,1,0:T(8,128)S(1)}, u32[]{:S(2)}, u32[]{:S(2)}) async-start(f32[16,24,128]{2,1,0:T(8,128)} %get-tuple-element.22), calls=%async_computation.1 | async-start | bytes 393216 | tf_op jit(solution)/shard_map/all_to_all | solution.py:396
  96.0 3.7 %collective-permute-start.24 = (f32[8,128]{1,0:T(8,128)S(1)}, f32[8,128]{1,0:T(8,128)S(1)}, u32[]{:S(2)}, u32[]{:S(2)}) collective-permute-start(f32[8,128]{1,0:T(8,128)S(1)} %get-tuple-element.21), channel_id=1, source_target_pairs={{0,16},{16,0},{1,17},{17,1},{2,18},{18,2},{3,19},{19,3},{4,20},{20... | collective-permute-start | bytes 12296 | tf_op jit(solution)/shard_map/ppermute | solution.py:397
  99.7 5.1 %collective-permute-start.27 = (f32[8,128]{1,0:T(8,128)S(1)}, f32[8,128]{1,0:T(8,128)S(1)}, u32[]{:S(2)}, u32[]{:S(2)}) collective-permute-start(f32[8,128]{1,0:T(8,128)S(1)} %add.28.r0), channel_id=1, source_target_pairs={{0,64},{32,96},{64,0},{96,32},{1,65},{33,97},{65,1},{97,33},{2,66}... | collective-permute-start | bytes 12296 | tf_op jit(solution)/shard_map/ppermute | solution.py:398
  102.4 3.6 %collective-permute-start.26 = (f32[8,128]{1,0:T(8,128)S(1)}, f32[8,128]{1,0:T(8,128)S(1)}, u32[]{:S(2)}, u32[]{:S(2)}) collective-permute-start(f32[8,128]{1,0:T(8,128)S(1)} %add.28.r0), channel_id=1, source_target_pairs={{0,96},{32,0},{64,32},{96,64},{1,97},{33,1},{65,33},{97,65},{2,98}... | collective-permute-start | bytes 12296 | tf_op jit(solution)/shard_map/ppermute | solution.py:398
  103.7 4.8 %collective-permute-start.25 = (f32[8,128]{1,0:T(8,128)S(1)}, f32[8,128]{1,0:T(8,128)S(1)}, u32[]{:S(2)}, u32[]{:S(2)}) collective-permute-start(f32[8,128]{1,0:T(8,128)S(1)} %add.28.r0), channel_id=1, source_target_pairs={{0,32},{32,64},{64,96},{96,0},{1,33},{33,65},{65,97},{97,1},{2,34}... | collective-permute-start | bytes 12296 | tf_op jit(solution)/shard_map/ppermute | solution.py:398
  145.3 29.0 %copy-start = (bf16[2048,320]{0,1:T(8,128)(2,1)S(1)}, bf16[2048,320]{0,1:T(8,128)(2,1)}, u32[]{:S(2)}) copy-start(bf16[2048,320]{0,1:T(8,128)(2,1)} %param.3) | copy-start | bytes 3932164
  146.1 8.0 %collective-permute-start.28 = (bf16[128,1024]{1,0:T(8,128)(2,1)S(1)}, bf16[128,1024]{1,0:T(8,128)(2,1)S(1)}, u32[]{:S(2)}, u32[]{:S(2)}) collective-permute-start(bf16[128,1024]{1,0:T(8,128)(2,1)S(1)} %multiply_convert_fusion.refs_0_), channel_id=1, source_target_pairs={{0,2},{2,0},{1,3},{3,1},{4,6},{6,4},{5,7},{7,5},{8,10},{10,8},{9,1... | collective-permute-start | bytes 786440 | tf_op jit(solution)/shard_map/ppermute | solution.py:42
  149.7 7.6 %collective-permute-start.31 = (bf16[128,1024]{1,0:T(8,128)(2,1)S(1)}, bf16[128,1024]{1,0:T(8,128)(2,1)S(1)}, u32[]{:S(2)}, u32[]{:S(2)}) collective-permute-start(bf16[128,1024]{1,0:T(8,128)(2,1)S(1)} %multiply_convert_fusion.refs_0_), channel_id=1, source_target_pairs={{0,4},{4,8},{8,12},{12,0},{1,5},{5,9},{9,13},{13,1},{2,6},{6,10},{... | collective-permute-start | bytes 786440 | tf_op jit(solution)/shard_map/ppermute | solution.py:44
  151.2 6.4 %collective-permute-start.29 = (bf16[128,1024]{1,0:T(8,128)(2,1)S(1)}, bf16[128,1024]{1,0:T(8,128)(2,1)S(1)}, u32[]{:S(2)}, u32[]{:S(2)}) collective-permute-start(bf16[128,1024]{1,0:T(8,128)(2,1)S(1)} %multiply_convert_fusion.refs_0_), channel_id=1, source_target_pairs={{0,12},{4,0},{8,4},{12,8},{1,13},{5,1},{9,5},{13,9},{2,14},{6,2},{... | collective-permute-start | bytes 786440 | tf_op jit(solution)/shard_map/ppermute | solution.py:43
  153.0 7.8 %collective-permute-start.35 = (bf16[128,1024]{1,0:T(8,128)(2,1)S(1)}, bf16[128,1024]{1,0:T(8,128)(2,1)S(1)}, u32[]{:S(2)}, u32[]{:S(2)}) collective-permute-start(bf16[128,1024]{1,0:T(8,128)(2,1)S(1)} %multiply_convert_fusion.refs_0_), channel_id=1, source_target_pairs={{0,1},{1,0},{2,3},{3,2},{4,5},{5,4},{6,7},{7,6},{8,9},{9,8},{10,11... | collective-permute-start | bytes 786440 | tf_op jit(solution)/shard_map/ppermute | solution.py:30
  154.1 8.8 %collective-permute-start.32 = (bf16[128,1024]{1,0:T(8,128)(2,1)S(1)}, bf16[128,1024]{1,0:T(8,128)(2,1)S(1)}, u32[]{:S(2)}, u32[]{:S(2)}) collective-permute-start(bf16[128,1024]{1,0:T(8,128)(2,1)S(1)} %collective-permute-done.28.refs_1_), channel_id=1, source_target_pairs={{0,4},{4,8},{8,12},{12,0},{1,5},{5,9},{9,13},{13,1},{2,6},{6,10},{... | collective-permute-start | bytes 786440 | tf_op jit(solution)/shard_map/ppermute | solution.py:47
  157.3 5.9 %collective-permute-start.39 = (bf16[128,1024]{1,0:T(8,128)(2,1)S(1)}, bf16[128,1024]{1,0:T(8,128)(2,1)S(1)}, u32[]{:S(2)}, u32[]{:S(2)}) collective-permute-start(bf16[128,1024]{1,0:T(8,128)(2,1)S(1)} %collective-permute-done.31.refs_4_), channel_id=1, source_target_pairs={{0,1},{1,0},{2,3},{3,2},{4,5},{5,4},{6,7},{7,6},{8,9},{9,8},{10,11... | collective-permute-start | bytes 786440 | tf_op jit(solution)/shard_map/ppermute | solution.py:30
  157.6 5.6 %collective-permute-start.37 = (bf16[128,1024]{1,0:T(8,128)(2,1)S(1)}, bf16[128,1024]{1,0:T(8,128)(2,1)S(1)}, u32[]{:S(2)}, u32[]{:S(2)}) collective-permute-start(bf16[128,1024]{1,0:T(8,128)(2,1)S(1)} %collective-permute-done.29.refs_2_), channel_id=1, source_target_pairs={{0,1},{1,0},{2,3},{3,2},{4,5},{5,4},{6,7},{7,6},{8,9},{9,8},{10,11... | collective-permute-start | bytes 786440 | tf_op jit(solution)/shard_map/ppermute | solution.py:30
  157.8 9.6 %collective-permute-start.33 = (bf16[128,1024]{1,0:T(8,128)(2,1)S(1)}, bf16[128,1024]{1,0:T(8,128)(2,1)S(1)}, u32[]{:S(2)}, u32[]{:S(2)}) collective-permute-start(bf16[128,1024]{1,0:T(8,128)(2,1)S(1)} %collective-permute-done.29.refs_2_), channel_id=1, source_target_pairs={{0,12},{4,0},{8,4},{12,8},{1,13},{5,1},{9,5},{13,9},{2,14},{6,2},{... | collective-permute-start | bytes 786440 | tf_op jit(solution)/shard_map/ppermute | solution.py:45
  160.8 11.6 %collective-permute-start.30 = (bf16[128,1024]{1,0:T(8,128)(2,1)S(1)}, bf16[128,1024]{1,0:T(8,128)(2,1)S(1)}, u32[]{:S(2)}, u32[]{:S(2)}) collective-permute-start(bf16[128,1024]{1,0:T(8,128)(2,1)S(1)} %collective-permute-done.28.refs_1_), channel_id=1, source_target_pairs={{0,12},{4,0},{8,4},{12,8},{1,13},{5,1},{9,5},{13,9},{2,14},{6,2},{... | collective-permute-start | bytes 786440 | tf_op jit(solution)/shard_map/ppermute | solution.py:46
  162.9 9.5 %collective-permute-start.34 = (bf16[128,1024]{1,0:T(8,128)(2,1)S(1)}, bf16[128,1024]{1,0:T(8,128)(2,1)S(1)}, u32[]{:S(2)}, u32[]{:S(2)}) collective-permute-start(bf16[128,1024]{1,0:T(8,128)(2,1)S(1)} %collective-permute-done.32.refs_5_), channel_id=1, source_target_pairs={{0,4},{4,8},{8,12},{12,0},{1,5},{5,9},{9,13},{13,1},{2,6},{6,10},{... | collective-permute-start | bytes 786440 | tf_op jit(solution)/shard_map/ppermute | solution.py:51
  163.2 9.7 %collective-permute-start.36 = (bf16[128,1024]{1,0:T(8,128)(2,1)S(1)}, bf16[128,1024]{1,0:T(8,128)(2,1)S(1)}, u32[]{:S(2)}, u32[]{:S(2)}) collective-permute-start(bf16[128,1024]{1,0:T(8,128)(2,1)S(1)} %collective-permute-done.28.refs_1_), channel_id=1, source_target_pairs={{0,1},{1,0},{2,3},{3,2},{4,5},{5,4},{6,7},{7,6},{8,9},{9,8},{10,11... | collective-permute-start | bytes 786440 | tf_op jit(solution)/shard_map/ppermute | solution.py:30
  163.2 9.7 %collective-permute-start.40 = (bf16[128,1024]{1,0:T(8,128)(2,1)S(1)}, bf16[128,1024]{1,0:T(8,128)(2,1)S(1)}, u32[]{:S(2)}, u32[]{:S(2)}) collective-permute-start(bf16[128,1024]{1,0:T(8,128)(2,1)S(1)} %collective-permute-done.32.refs_5_), channel_id=1, source_target_pairs={{0,1},{1,0},{2,3},{3,2},{4,5},{5,4},{6,7},{7,6},{8,9},{9,8},{10,11... | collective-permute-start | bytes 786440 | tf_op jit(solution)/shard_map/ppermute | solution.py:30
  167.4 5.5 %collective-permute-start.41 = (bf16[128,1024]{1,0:T(8,128)(2,1)S(1)}, bf16[128,1024]{1,0:T(8,128)(2,1)S(1)}, u32[]{:S(2)}, u32[]{:S(2)}) collective-permute-start(bf16[128,1024]{1,0:T(8,128)(2,1)S(1)} %collective-permute-done.33.refs_6_), channel_id=1, source_target_pairs={{0,1},{1,0},{2,3},{3,2},{4,5},{5,4},{6,7},{7,6},{8,9},{9,8},{10,11... | collective-permute-start | bytes 786440 | tf_op jit(solution)/shard_map/ppermute | solution.py:30
  172.4 1.5 collective-permute-start.38
  172.4 1.9 collective-permute-start.42
  177.5 19.4 %copy-start.2 = (bf16[320,1024]{1,0:T(8,128)(2,1)S(1)}, bf16[320,1024]{1,0:T(8,128)(2,1)}, u32[]{:S(2)}) copy-start(bf16[320,1024]{1,0:T(8,128)(2,1)} %param.4) | copy-start | bytes 1966084
  193.3 13.6 %all-to-all-start.4 = ((bf16[8,320,128]{2,1,0:T(8,128)(2,1)}), bf16[8,320,128]{2,1,0:T(8,128)(2,1)S(1)}, u32[]{:S(2)}, u32[]{:S(2)}) async-start(bf16[8,320,128]{2,1,0:T(8,128)(2,1)} %broadcast_in_dim.2), calls=%async_computation.4 | async-start | bytes 1310720 | tf_op jit(solution)/shard_map/all_to_all | solution.py:34

commit v11 on v10

--- a/solution.py
+++ b/solution.py
@@ -240,9 +240,9 @@
 
 
 def head_kernel(place, summaries, rider, *refs):
-    piece_refs, (head_ref, all_ref, rows, copy_sem, out_sem) = refs[:16], refs[16:]
+    piece_refs, (head_ref, all_ref, rows, held, held_sem, copy_sem, out_sem) = refs[:16], refs[16:]
     features = summaries.shape[0]
-    copies, outs = [], []
+    copies, outs = [pltpu.make_async_copy(summaries, held, held_sem)], []
     for n in range(8):
         for i, chunk in enumerate(query_chunks(place, n)):
             to = pl.ds(pl.multiple_of(chunk * ROWS, ROWS), ROWS)
@@ -257,7 +257,7 @@
         head_ref[j, features:] = rider[...]
     for copy in copies:
         copy.wait()
-    total = jnp.dot(summaries[...], rows[...], preferred_element_type=F32).astype(BF16)
+    total = jnp.dot(held[...], rows[...], preferred_element_type=F32).astype(BF16)
     for j in range(8):
         head_ref[j, :features] = total[:, j * ROWS : (j + 1) * ROWS]
     for out in outs:
@@ -348,11 +348,13 @@
         grid_spec=pltpu.PrefetchScalarGridSpec(
             num_scalar_prefetch=1,
             grid=(1,),
-            in_specs=[whole((features, GROUP)), whole((16, ROWS))]
+            in_specs=[pl.BlockSpec(memory_space=pl.ANY), whole((16, ROWS))]
             + [pl.BlockSpec(memory_space=pl.ANY)] * 16,
             out_specs=[whole((8, features + 16, ROWS)), pl.BlockSpec(memory_space=pltpu.HBM)],
             scratch_shapes=[
                 pltpu.VMEM((GROUP, WIDTH), BF16),
+                pltpu.VMEM((features, GROUP), BF16),
+                pltpu.SemaphoreType.DMA,
                 pltpu.SemaphoreType.DMA((16,)),
                 pltpu.SemaphoreType.DMA((16,)),
             ],

time: 210 us -> 210 us (level)
  no operation moved by 1% of the time
where the time goes in v11:
time: 210 us; the launch traced here: 209 us
  blocking collectives  78.5 us (37%)
  starting transfers between devices  48.8 us (23%)
  waiting for transfers between devices  43.1 us (21%)
  Pallas kernels  22.1 us (11%)
  matrix products  8.72 us (4%)
  other arithmetic  3.22 us (2%)
  between operations  2.62 us (1%)
  local copies, waits for them, and re-layouts  2.17 us (1%)
    all_to_all x2, blocking collectives, sum_exchange(): return jnp.sum(lax.all_to_all(parts, axes, 0, 0).astype(F32), axis=0)  63.8 us
    all_to_all x1, blocking collectives, shards(): pieces = lax.all_to_all(head_part, XZ, 0, 0)  14.8 us
    pallas_call x1, Pallas kernels, score_call(): pl.pallas_call(score_kernel, grid_spec=pltpu.PrefetchScalarGridSpec(num_s...  9.8 us
    pallas_call x1, Pallas kernels, grad_call(): pl.pallas_call(grad_kernel, grid_spec=pltpu.PrefetchScalarGridSpec(num_sc...  9.1 us
    ppermute x3, waiting for transfers between devices, gather_ring(): far_own = lax.ppermute(after_own, long_axis, RING[3])  8.02 us
    ppermute x3, waiting for transfers between devices, gather_ring(): after_other = lax.ppermute(other, long_axis, RING[3])  7.67 us
    ppermute x3, waiting for transfers between devices, gather_ring(): other = lax.ppermute(own, short_axis, SWAP)  7.02 us
    ppermute x3, starting transfers between devices, gather_ring(): after_other = lax.ppermute(other, long_axis, RING[3])  6.91 us
  transfers between devices with their start and end apart: 45, of which 23 were waited for; matrix products, arithmetic and copies ran while one was open for 4% of the time, Pallas kernels for 0%

profile of v11, /device:TPU:0, one launch (start us, length us, event | category | flops | bytes accessed | tf_op | source)
XLA Modules:
  0.0 209.3 jit_solution(4122347652521064416)
XLA Ops:
  0.6 1.1 dynamic-slice_bitcast_fusion
  2.4 2.6 %fusion = f32[1024,1024]{1,0:T(8,128)S(1)} fusion(bf16[320,1024]{1,0:T(8,128)(2,1)} %param.4, bf16[2048,320]{0,1:T(8,128)(2,1)} %param.3, s32[]{:T(128)S(6)} %select_n.6), kind=kOutput, calls=%fused_computation.8 | convolution fusion | flops 671088640 | bytes 5505028 | tf_op jit(solution)/shard_map/dot_general | solution.py:384
  5.1 1.3 add_convert_fusion
  6.5 36.1 %all_to_all.25 = bf16[8,128,1024]{2,1,0:T(8,128)(2,1)S(1)} all-to-all(bf16[8,128,1024]{2,1,0:T(8,128)(2,1)S(1)} %bitcast.26), channel_id=1, replica_groups=mesh['x'=4,'zl'=2,'y'=4,'zh'=2,'c'=2] {'y','zh'}, dimensions={0} | all-to-all | bytes 4194304 | tf_op jit(solution)/shard_map/all_to_all | solution.py:38
  43.5 3.0 %collective-permute-start.10 = (bf16[128,1024]{1,0:T(8,128)(2,1)S(1)}, bf16[128,1024]{1,0:T(8,128)(2,1)S(1)}, u32[]{:S(2)}, u32[]{:S(2)}) collective-permute-start(bf16[128,1024]{1,0:T(8,128)(2,1)S(1)} %multiply_convert_fusion.1.refs_0_.refs_8_), channel_id=1, source_target_pairs={{0,12},{4,0},{8,4},{12,8},{1,13},{5,1},{9,5},{13,9},{2,14},{6,2},{... | collective-permute-start | bytes 786440 | tf_op jit(solution)/shard_map/ppermute | solution.py:43
  46.5 1.2 collective-permute-start.9
  47.7 1.5 collective-permute-start.5
  49.2 1.7 collective-permute-start.3
  50.9 2.2 %collective-permute-done.12.refs_12_ = bf16[128,1024]{1,0:T(8,128)(2,1)S(1)} collective-permute-done((bf16[128,1024]{1,0:T(8,128)(2,1)S(1)}, bf16[128,1024]{1,0:T(8,128)(2,1)S(1)}, u32[]{:S(2)}, u32[]{:S(2)}) %collective-permute-start.12) | collective-permute-done | bytes 262176 | tf_op jit(solution)/shard_map/ppermute | solution.py:44
  53.1 1.0 collective-permute-start.2
  54.1 1.9 collective-permute-done.9.refs_9_
  57.0 4.0 %collective-permute-done.2.refs_1_ = bf16[128,1024]{1,0:T(8,128)(2,1)S(1)} collective-permute-done((bf16[128,1024]{1,0:T(8,128)(2,1)S(1)}, bf16[128,1024]{1,0:T(8,128)(2,1)S(1)}, u32[]{:S(2)}, u32[]{:S(2)}) %collective-permute-start.2) | collective-permute-done | bytes 262176 | tf_op jit(solution)/shard_map/ppermute | solution.py:42
  61.0 3.2 %collective-permute-start.11 = (bf16[128,1024]{1,0:T(8,128)(2,1)S(1)}, bf16[128,1024]{1,0:T(8,128)(2,1)S(1)}, u32[]{:S(2)}, u32[]{:S(2)}) collective-permute-start(bf16[128,1024]{1,0:T(8,128)(2,1)S(1)} %collective-permute-done.9.refs_9_), channel_id=1, source_target_pairs={{0,12},{4,0},{8,4},{12,8},{1,13},{5,1},{9,5},{13,9},{2,14},{6,2},{... | collective-permute-start | bytes 786440 | tf_op jit(solution)/shard_map/ppermute | solution.py:46
  64.2 2.8 %collective-permute-start.7 = (bf16[128,1024]{1,0:T(8,128)(2,1)S(1)}, bf16[128,1024]{1,0:T(8,128)(2,1)S(1)}, u32[]{:S(2)}, u32[]{:S(2)}) collective-permute-start(bf16[128,1024]{1,0:T(8,128)(2,1)S(1)} %collective-permute-done.3.refs_2_), channel_id=1, source_target_pairs={{0,96},{32,0},{64,32},{96,64},{1,97},{33,1},{65,33},{97,65},{2,98}... | collective-permute-start | bytes 786440 | tf_op jit(solution)/shard_map/ppermute | solution.py:45
  67.0 1.2 collective-permute-start.8
  69.2 1.3 collective-permute-done.11.refs_11_
  70.4 2.8 %collective-permute-start.4 = (bf16[128,1024]{1,0:T(8,128)(2,1)S(1)}, bf16[128,1024]{1,0:T(8,128)(2,1)S(1)}, u32[]{:S(2)}, u32[]{:S(2)}) collective-permute-start(bf16[128,1024]{1,0:T(8,128)(2,1)S(1)} %collective-permute-done.2.refs_1_), channel_id=1, source_target_pairs={{0,96},{32,0},{64,32},{96,64},{1,97},{33,1},{65,33},{97,65},{2,98}... | collective-permute-start | bytes 786440 | tf_op jit(solution)/shard_map/ppermute | solution.py:46
  73.2 4.4 %collective-permute-done.7.refs_6_ = bf16[128,1024]{1,0:T(8,128)(2,1)S(1)} collective-permute-done((bf16[128,1024]{1,0:T(8,128)(2,1)S(1)}, bf16[128,1024]{1,0:T(8,128)(2,1)S(1)}, u32[]{:S(2)}, u32[]{:S(2)}) %collective-permute-start.7) | collective-permute-done | bytes 262176 | tf_op jit(solution)/shard_map/ppermute | solution.py:45
  78.1 2.2 %collective-permute-done.6.refs_5_ = bf16[128,1024]{1,0:T(8,128)(2,1)S(1)} collective-permute-done((bf16[128,1024]{1,0:T(8,128)(2,1)S(1)}, bf16[128,1024]{1,0:T(8,128)(2,1)S(1)}, u32[]{:S(2)}, u32[]{:S(2)}) %collective-permute-start.6) | collective-permute-done | bytes 262176 | tf_op jit(solution)/shard_map/ppermute | solution.py:47
  80.7 1.4 collective-permute-done.4.refs_3_
  82.2 9.8 %scores.1 = (bf16[1024,2048]{1,0:T(8,128)(2,1)}, f32[8,128]{1,0:T(8,128)S(1)}, f32[8,128]{1,0:T(8,128)S(1)}, f32[16,24,128]{2,1,0:T(8,128)}, bf16[2048,1024]{1,0:T(8,128)(2,1)}) custom-call(s32[5]{0:T(128)S(1)} %stack.23.place, bf16[128,1024]{1,0:T(8,128)(2,1)S(1)} %multiply_convert_fusion.1.refs_0_.refs_8_, ...), custom_call_target="tpu_custom_call" | custom-call | flops 4294967296 | bytes 14680064 | tf_op jit(solution)/shard_map/scores/pallas_call | solution.py:272
  92.0 4.0 %all-to-all-start.1 = ((f32[16,24,128]{2,1,0:T(8,128)}), f32[16,24,128]{2,1,0:T(8,128)S(1)}, u32[]{:S(2)}, u32[]{:S(2)}) async-start(f32[16,24,128]{2,1,0:T(8,128)} %get-tuple-element.22), calls=%async_computation.1 | async-start | bytes 393216 | tf_op jit(solution)/shard_map/all_to_all | solution.py:398
  96.0 1.3 collective-permute-start.24
  97.3 2.4 %collective-permute-done.24 = f32[8,128]{1,0:T(8,128)S(1)} collective-permute-done((f32[8,128]{1,0:T(8,128)S(1)}, f32[8,128]{1,0:T(8,128)S(1)}, u32[]{:S(2)}, u32[]{:S(2)}) %collective-permute-start.24) | collective-permute-done | bytes 4128 | tf_op jit(solution)/shard_map/ppermute | solution.py:399
  99.7 2.7 %collective-permute-start.27 = (f32[8,128]{1,0:T(8,128)S(1)}, f32[8,128]{1,0:T(8,128)S(1)}, u32[]{:S(2)}, u32[]{:S(2)}) collective-permute-start(f32[8,128]{1,0:T(8,128)S(1)} %add.28.r0), channel_id=1, source_target_pairs={{0,64},{32,96},{64,0},{96,32},{1,65},{33,97},{65,1},{97,33},{2,66}... | collective-permute-start | bytes 12296 | tf_op jit(solution)/shard_map/ppermute | solution.py:400
  102.4 1.2 collective-permute-start.26
  104.8 1.2 collective-permute-done.26.r2
  106.0 2.5 %collective-permute-done.25.r1 = f32[8,128]{1,0:T(8,128)S(1)} collective-permute-done((f32[8,128]{1,0:T(8,128)S(1)}, f32[8,128]{1,0:T(8,128)S(1)}, u32[]{:S(2)}, u32[]{:S(2)}) %collective-permute-start.25) | collective-permute-done | bytes 4128 | tf_op jit(solution)/shard_map/ppermute | solution.py:400
  108.5 9.1 %grads.1 = (bf16[4,2,128,1024]{3,2,1,0:T(8,128)(2,1)S(1)}, bf16[16,128]{1,0:T(8,128)(2,1)S(1)}) custom-call(s32[5]{0:T(128)S(1)} %stack.23.place, bf16[1024,2048]{1,0:T(8,128)(2,1)} %get-tuple-element.18.w_ref, bf16[2048,1024]{1,0:T(8,128)(2,1)} %get-tuple-element.19.query_ref, f32[8,128]{1,0:T(8,128)S(1)} %get-tuple-element.20.hit_ref, ...), custom_call_target="tpu_custom_call" | custom-call | flops 4294967296 | bytes 14680064 | tf_op jit(solution)/shard_map/grads/pallas_call | solution.py:314
  117.6 27.7 %all_to_all.26 = bf16[8,128,1024]{2,1,0:T(8,128)(2,1)S(1)} all-to-all(bf16[8,128,1024]{2,1,0:T(8,128)(2,1)S(1)} %bitcast.23), channel_id=1, replica_groups=mesh['x'=4,'zl'=2,'y'=4,'zh'=2,'c'=2] {'x','zl'}, dimensions={0} | all-to-all | bytes 4194304 | tf_op jit(solution)/shard_map/all_to_all | solution.py:38
  146.1 3.6 %collective-permute-start.28 = (bf16[128,1024]{1,0:T(8,128)(2,1)S(1)}, bf16[128,1024]{1,0:T(8,128)(2,1)S(1)}, u32[]{:S(2)}, u32[]{:S(2)}) collective-permute-start(bf16[128,1024]{1,0:T(8,128)(2,1)S(1)} %multiply_convert_fusion.refs_0_), channel_id=1, source_target_pairs={{0,2},{2,0},{1,3},{3,1},{4,6},{6,4},{5,7},{7,5},{8,10},{10,8},{9,1... | collective-permute-start | bytes 786440 | tf_op jit(solution)/shard_map/ppermute | solution.py:42
  149.7 1.5 collective-permute-start.31
  151.2 1.7 collective-permute-start.29
  153.0 1.1 collective-permute-done.28.refs_1_
  154.1 1.5 collective-permute-start.32
  155.6 1.7 collective-permute-done.31.refs_4_
  157.8 2.9 %collective-permute-start.33 = (bf16[128,1024]{1,0:T(8,128)(2,1)S(1)}, bf16[128,1024]{1,0:T(8,128)(2,1)S(1)}, u32[]{:S(2)}, u32[]{:S(2)}) collective-permute-start(bf16[128,1024]{1,0:T(8,128)(2,1)S(1)} %collective-permute-done.29.refs_2_), channel_id=1, source_target_pairs={{0,12},{4,0},{8,4},{12,8},{1,13},{5,1},{9,5},{13,9},{2,14},{6,2},{... | collective-permute-start | bytes 786440 | tf_op jit(solution)/shard_map/ppermute | solution.py:45
  160.8 0.9 collective-permute-start.30
  161.7 1.2 collective-permute-done.32.refs_5_
  163.7 3.7 %collective-permute-done.33.refs_6_ = bf16[128,1024]{1,0:T(8,128)(2,1)S(1)} collective-permute-done((bf16[128,1024]{1,0:T(8,128)(2,1)S(1)}, bf16[128,1024]{1,0:T(8,128)(2,1)S(1)}, u32[]{:S(2)}, u32[]{:S(2)}) %collective-permute-start.33) | collective-permute-done | bytes 262176 | tf_op jit(solution)/shard_map/ppermute | solution.py:45
  167.4 5.0 %collective-permute-done.30.refs_3_ = bf16[128,1024]{1,0:T(8,128)(2,1)S(1)} collective-permute-done((bf16[128,1024]{1,0:T(8,128)(2,1)S(1)}, bf16[128,1024]{1,0:T(8,128)(2,1)S(1)}, u32[]{:S(2)}, u32[]{:S(2)}) %collective-permute-start.30) | collective-permute-done | bytes 262176 | tf_op jit(solution)/shard_map/ppermute | solution.py:46
  172.9 1.0 collective-permute-done.38.refs_11_
  174.3 3.2 %head_parts.1 = (bf16[8,336,128]{2,1,0:T(8,128)(2,1)S(1)}, bf16[2048,1024]{1,0:T(8,128)(2,1)}) custom-call(s32[5]{0:T(128)S(1)} %stack.23.place, bf16[320,2048]{1,0:T(8,128)(2,1)S(1)} %bitcast.22, bf16[16,128]{1,0:T(8,128)(2,1)S(1)} %get-tuple-element.23.rider, bf16[128,1024]{1,0:T(8,128)(2,1)S(1)} %multiply_convert_fusion.refs_0_, ...), custom_call_target="tpu_custom_call" | custom-call | flops 1342177280 | bytes 10485760 | tf_op jit(solution)/shard_map/head_parts/pallas_call | solution.py:346
  177.6 14.8 %all_to_all.27 = bf16[8,336,128]{2,1,0:T(8,128)(2,1)S(1)} all-to-all(bf16[8,336,128]{2,1,0:T(8,128)(2,1)S(1)} %get-tuple-element.25), channel_id=1, replica_groups=mesh['x'=4,'zl'=2,'y'=4,'zh'=2,'c'=2] {'x','zl'}, dimensions={0} | all-to-all | bytes 1376256 | tf_op jit(solution)/shard_map/all_to_all | solution.py:408
  193.4 3.5 %all-to-all-start.4 = ((bf16[8,320,128]{2,1,0:T(8,128)(2,1)}), bf16[8,320,128]{2,1,0:T(8,128)(2,1)S(1)}, u32[]{:S(2)}, u32[]{:S(2)}) async-start(bf16[8,320,128]{2,1,0:T(8,128)(2,1)} %broadcast_in_dim.2), calls=%async_computation.4 | async-start | bytes 1310720 | tf_op jit(solution)/shard_map/all_to_all | solution.py:34
  196.9 4.8 %convolution_convert_fusion = bf16[2048,320]{0,1:T(8,128)(2,1)} fusion(bf16[2048,1024]{1,0:T(8,128)(2,1)} %get-tuple-element.26, bf16[320,1024]{1,0:T(8,128)(2,1)S(1)} %copy-done.2), kind=kOutput, calls=%fused_computation.3 | convolution fusion | flops 1342832640 | bytes 6160384 | tf_op jit(solution)/shard_map/dot_general | solution.py:416
  203.0 4.0 %all-to-all-done.4 = bf16[8,320,128]{2,1,0:T(8,128)(2,1)S(1)} async-done(((bf16[8,320,128]{2,1,0:T(8,128)(2,1)}), bf16[8,320,128]{2,1,0:T(8,128)(2,1)S(1)}, u32[]{:S(2)}, u32[]{:S(2)}) %all-to-all-start.4) | async-done | bytes 655392 | tf_op jit(solution)/shard_map/all_to_all | solution.py:34
  206.9 1.2 copy_bitcast_fusion
  (72 shorter events, 10.3 us)
Async XLA Ops:
  1.8 3.3 %collective-permute-start = (bf16[320,1024]{1,0:T(8,128)(2,1)S(1)}, bf16[320,1024]{1,0:T(8,128)(2,1)S(1)}, u32[]{:S(2)}, u32[]{:S(2)}) collective-permute-start(bf16[320,1024]{1,0:T(8,128)(2,1)S(1)} %dynamic-slice_bitcast_fusion), channel_id=1, source_target_pairs={{0,1},{1,0},{2,3},{3,2},{4,5},{5,4},{6,7},{7,6},{8,9},{9,8},{10,11... | collective-permute-start | bytes 1966088 | tf_op jit(solution)/shard_map/ppermute | solution.py:30
  1.9 3.2 %collective-permute-start.1 = (bf16[320,1024]{1,0:T(8,128)(2,1)}, bf16[320,1024]{1,0:T(8,128)(2,1)S(1)}, u32[]{:S(2)}, u32[]{:S(2)}) collective-permute-start(bf16[320,1024]{1,0:T(8,128)(2,1)} %param.4), channel_id=1, source_target_pairs={{0,1},{1,0},{2,3},{3,2},{4,5},{5,4},{6,7},{7,6},{8,9},{9,8},{10,11... | collective-permute-start | bytes 1966088 | tf_op jit(solution)/shard_map/ppermute | solution.py:30
  42.5 39.7 %copy-start.1 = (s32[2048]{0:T(1024)S(1)}, s32[2048]{0:T(1024)}, u32[]{:S(2)}) copy-start(s32[2048]{0:T(1024)} %param.5) | copy-start | bytes 24580
  43.1 6.1 %collective-permute-start.16 = (bf16[128,1024]{1,0:T(8,128)(2,1)S(1)}, bf16[128,1024]{1,0:T(8,128)(2,1)S(1)}, u32[]{:S(2)}, u32[]{:S(2)}) collective-permute-start(bf16[128,1024]{1,0:T(8,128)(2,1)S(1)} %multiply_convert_fusion.1.refs_0_.refs_8_), channel_id=1, source_target_pairs={{0,1},{1,0},{2,3},{3,2},{4,5},{5,4},{6,7},{7,6},{8,9},{9,8},{10,11... | collective-permute-start | bytes 786440 | tf_op jit(solution)/shard_map/ppermute | solution.py:30
  43.2 9.9 %collective-permute-start.12 = (bf16[128,1024]{1,0:T(8,128)(2,1)S(1)}, bf16[128,1024]{1,0:T(8,128)(2,1)S(1)}, u32[]{:S(2)}, u32[]{:S(2)}) collective-permute-start(bf16[128,1024]{1,0:T(8,128)(2,1)S(1)} %multiply_convert_fusion.1.refs_0_.refs_8_), channel_id=1, source_target_pairs={{0,4},{4,8},{8,12},{12,0},{1,5},{5,9},{9,13},{13,1},{2,6},{6,10},{... | collective-permute-start | bytes 786440 | tf_op jit(solution)/shard_map/ppermute | solution.py:44
  43.5 10.6 %collective-permute-start.10 = (bf16[128,1024]{1,0:T(8,128)(2,1)S(1)}, bf16[128,1024]{1,0:T(8,128)(2,1)S(1)}, u32[]{:S(2)}, u32[]{:S(2)}) collective-permute-start(bf16[128,1024]{1,0:T(8,128)(2,1)S(1)} %multiply_convert_fusion.1.refs_0_.refs_8_), channel_id=1, source_target_pairs={{0,12},{4,0},{8,4},{12,8},{1,13},{5,1},{9,5},{13,9},{2,14},{6,2},{... | collective-permute-start | bytes 786440 | tf_op jit(solution)/shard_map/ppermute | solution.py:43
  46.5 9.6 %collective-permute-start.9 = (bf16[128,1024]{1,0:T(8,128)(2,1)S(1)}, bf16[128,1024]{1,0:T(8,128)(2,1)S(1)}, u32[]{:S(2)}, u32[]{:S(2)}) collective-permute-start(bf16[128,1024]{1,0:T(8,128)(2,1)S(1)} %multiply_convert_fusion.1.refs_0_.refs_8_), channel_id=1, source_target_pairs={{0,2},{2,0},{1,3},{3,1},{4,6},{6,4},{5,7},{7,5},{8,10},{10,8},{9,1... | collective-permute-start | bytes 786440 | tf_op jit(solution)/shard_map/ppermute | solution.py:42
  47.7 9.0 %collective-permute-start.5 = (bf16[128,1024]{1,0:T(8,128)(2,1)S(1)}, bf16[128,1024]{1,0:T(8,128)(2,1)S(1)}, u32[]{:S(2)}, u32[]{:S(2)}) collective-permute-start(bf16[128,1024]{1,0:T(8,128)(2,1)S(1)} %multiply_convert_fusion.1.refs_0_.refs_8_), channel_id=1, source_target_pairs={{0,32},{32,64},{64,96},{96,0},{1,33},{33,65},{65,97},{97,1},{2,34}... | collective-permute-start | bytes 786440 | tf_op jit(solution)/shard_map/ppermute | solution.py:44
  49.2 7.8 %collective-permute-start.3 = (bf16[128,1024]{1,0:T(8,128)(2,1)S(1)}, bf16[128,1024]{1,0:T(8,128)(2,1)S(1)}, u32[]{:S(2)}, u32[]{:S(2)}) collective-permute-start(bf16[128,1024]{1,0:T(8,128)(2,1)S(1)} %multiply_convert_fusion.1.refs_0_.refs_8_), channel_id=1, source_target_pairs={{0,96},{32,0},{64,32},{96,64},{1,97},{33,1},{65,33},{97,65},{2,98}... | collective-permute-start | bytes 786440 | tf_op jit(solution)/shard_map/ppermute | solution.py:43
  53.1 7.9 %collective-permute-start.2 = (bf16[128,1024]{1,0:T(8,128)(2,1)S(1)}, bf16[128,1024]{1,0:T(8,128)(2,1)S(1)}, u32[]{:S(2)}, u32[]{:S(2)}) collective-permute-start(bf16[128,1024]{1,0:T(8,128)(2,1)S(1)} %multiply_convert_fusion.1.refs_0_.refs_8_), channel_id=1, source_target_pairs={{0,16},{16,0},{1,17},{17,1},{2,18},{18,2},{3,19},{19,3},{4,20},{20... | collective-permute-start | bytes 786440 | tf_op jit(solution)/shard_map/ppermute | solution.py:42
  54.1 6.8 %collective-permute-start.20 = (bf16[128,1024]{1,0:T(8,128)(2,1)S(1)}, bf16[128,1024]{1,0:T(8,128)(2,1)S(1)}, u32[]{:S(2)}, u32[]{:S(2)}) collective-permute-start(bf16[128,1024]{1,0:T(8,128)(2,1)S(1)} %collective-permute-done.12.refs_12_), channel_id=1, source_target_pairs={{0,1},{1,0},{2,3},{3,2},{4,5},{5,4},{6,7},{7,6},{8,9},{9,8},{10,11... | collective-permute-start | bytes 786440 | tf_op jit(solution)/shard_map/ppermute | solution.py:30
  56.1 8.1 %collective-permute-start.18 = (bf16[128,1024]{1,0:T(8,128)(2,1)S(1)}, bf16[128,1024]{1,0:T(8,128)(2,1)S(1)}, u32[]{:S(2)}, u32[]{:S(2)}) collective-permute-start(bf16[128,1024]{1,0:T(8,128)(2,1)S(1)} %collective-permute-done.10.refs_10_), channel_id=1, source_target_pairs={{0,1},{1,0},{2,3},{3,2},{4,5},{5,4},{6,7},{7,6},{8,9},{9,8},{10,11... | collective-permute-start | bytes 786440 | tf_op jit(solution)/shard_map/ppermute | solution.py:30
  56.7 10.3 %collective-permute-start.14 = (bf16[128,1024]{1,0:T(8,128)(2,1)S(1)}, bf16[128,1024]{1,0:T(8,128)(2,1)S(1)}, u32[]{:S(2)}, u32[]{:S(2)}) collective-permute-start(bf16[128,1024]{1,0:T(8,128)(2,1)S(1)} %collective-permute-done.10.refs_10_), channel_id=1, source_target_pairs={{0,12},{4,0},{8,4},{12,8},{1,13},{5,1},{9,5},{13,9},{2,14},{6,2},{... | collective-permute-start | bytes 786440 | tf_op jit(solution)/shard_map/ppermute | solution.py:45
  57.0 11.2 %collective-permute-start.17 = (bf16[128,1024]{1,0:T(8,128)(2,1)S(1)}, bf16[128,1024]{1,0:T(8,128)(2,1)S(1)}, u32[]{:S(2)}, u32[]{:S(2)}) collective-permute-start(bf16[128,1024]{1,0:T(8,128)(2,1)S(1)} %collective-permute-done.9.refs_9_), channel_id=1, source_target_pairs={{0,1},{1,0},{2,3},{3,2},{4,5},{5,4},{6,7},{7,6},{8,9},{9,8},{10,11... | collective-permute-start | bytes 786440 | tf_op jit(solution)/shard_map/ppermute | solution.py:30
  61.0 8.2 %collective-permute-start.13 = (bf16[128,1024]{1,0:T(8,128)(2,1)S(1)}, bf16[128,1024]{1,0:T(8,128)(2,1)S(1)}, u32[]{:S(2)}, u32[]{:S(2)}) collective-permute-start(bf16[128,1024]{1,0:T(8,128)(2,1)S(1)} %collective-permute-done.9.refs_9_), channel_id=1, source_target_pairs={{0,4},{4,8},{8,12},{12,0},{1,5},{5,9},{9,13},{13,1},{2,6},{6,10},{... | collective-permute-start | bytes 786440 | tf_op jit(solution)/shard_map/ppermute | solution.py:47
  61.0 9.4 %collective-permute-start.11 = (bf16[128,1024]{1,0:T(8,128)(2,1)S(1)}, bf16[128,1024]{1,0:T(8,128)(2,1)S(1)}, u32[]{:S(2)}, u32[]{:S(2)}) collective-permute-start(bf16[128,1024]{1,0:T(8,128)(2,1)S(1)} %collective-permute-done.9.refs_9_), channel_id=1, source_target_pairs={{0,12},{4,0},{8,4},{12,8},{1,13},{5,1},{9,5},{13,9},{2,14},{6,2},{... | collective-permute-start | bytes 786440 | tf_op jit(solution)/shard_map/ppermute | solution.py:46
  64.2 13.3 %collective-permute-start.7 = (bf16[128,1024]{1,0:T(8,128)(2,1)S(1)}, bf16[128,1024]{1,0:T(8,128)(2,1)S(1)}, u32[]{:S(2)}, u32[]{:S(2)}) collective-permute-start(bf16[128,1024]{1,0:T(8,128)(2,1)S(1)} %collective-permute-done.3.refs_2_), channel_id=1, source_target_pairs={{0,96},{32,0},{64,32},{96,64},{1,97},{33,1},{65,33},{97,65},{2,98}... | collective-permute-start | bytes 786440 | tf_op jit(solution)/shard_map/ppermute | solution.py:45
  67.0 10.6 %collective-permute-start.8 = (bf16[128,1024]{1,0:T(8,128)(2,1)S(1)}, bf16[128,1024]{1,0:T(8,128)(2,1)S(1)}, u32[]{:S(2)}, u32[]{:S(2)}) collective-permute-start(bf16[128,1024]{1,0:T(8,128)(2,1)S(1)} %collective-permute-done.2.refs_1_), channel_id=1, source_target_pairs={{0,64},{32,96},{64,0},{96,32},{1,65},{33,97},{65,1},{97,33},{2,66}... | collective-permute-start | bytes 786440 | tf_op jit(solution)/shard_map/ppermute | solution.py:49
  68.2 12.0 %collective-permute-start.6 = (bf16[128,1024]{1,0:T(8,128)(2,1)S(1)}, bf16[128,1024]{1,0:T(8,128)(2,1)S(1)}, u32[]{:S(2)}, u32[]{:S(2)}) collective-permute-start(bf16[128,1024]{1,0:T(8,128)(2,1)S(1)} %collective-permute-done.2.refs_1_), channel_id=1, source_target_pairs={{0,32},{32,64},{64,96},{96,0},{1,33},{33,65},{65,97},{97,1},{2,34}... | collective-permute-start | bytes 786440 | tf_op jit(solution)/shard_map/ppermute | solution.py:47
  69.2 11.1 %collective-permute-start.15 = (bf16[128,1024]{1,0:T(8,128)(2,1)S(1)}, bf16[128,1024]{1,0:T(8,128)(2,1)S(1)}, u32[]{:S(2)}, u32[]{:S(2)}) collective-permute-start(bf16[128,1024]{1,0:T(8,128)(2,1)S(1)} %collective-permute-done.13.refs_13_), channel_id=1, source_target_pairs={{0,4},{4,8},{8,12},{12,0},{1,5},{5,9},{9,13},{13,1},{2,6},{6,10},{... | collective-permute-start | bytes 786440 | tf_op jit(solution)/shard_map/ppermute | solution.py:51
  70.4 11.7 %collective-permute-start.4 = (bf16[128,1024]{1,0:T(8,128)(2,1)S(1)}, bf16[128,1024]{1,0:T(8,128)(2,1)S(1)}, u32[]{:S(2)}, u32[]{:S(2)}) collective-permute-start(bf16[128,1024]{1,0:T(8,128)(2,1)S(1)} %collective-permute-done.2.refs_1_), channel_id=1, source_target_pairs={{0,96},{32,0},{64,32},{96,64},{1,97},{33,1},{65,33},{97,65},{2,98}... | collective-permute-start | bytes 786440 | tf_op jit(solution)/shard_map/ppermute | solution.py:46
  77.6 4.6 %collective-permute-start.21 = (bf16[128,1024]{1,0:T(8,128)(2,1)S(1)}, bf16[128,1024]{1,0:T(8,128)(2,1)S(1)}, u32[]{:S(2)}, u32[]{:S(2)}) collective-permute-start(bf16[128,1024]{1,0:T(8,128)(2,1)S(1)} %collective-permute-done.13.refs_13_), channel_id=1, source_target_pairs={{0,1},{1,0},{2,3},{3,2},{4,5},{5,4},{6,7},{7,6},{8,9},{9,8},{10,11... | collective-permute-start | bytes 786440 | tf_op jit(solution)/shard_map/ppermute | solution.py:30
  77.6 4.6 %collective-permute-start.22 = (bf16[128,1024]{1,0:T(8,128)(2,1)S(1)}, bf16[128,1024]{1,0:T(8,128)(2,1)S(1)}, u32[]{:S(2)}, u32[]{:S(2)}) collective-permute-start(bf16[128,1024]{1,0:T(8,128)(2,1)S(1)} %collective-permute-done.14.refs_14_), channel_id=1, source_target_pairs={{0,1},{1,0},{2,3},{3,2},{4,5},{5,4},{6,7},{7,6},{8,9},{9,8},{10,11... | collective-permute-start | bytes 786440 | tf_op jit(solution)/shard_map/ppermute | solution.py:30
  80.2 1.9 collective-permute-start.19
  80.2 1.9 collective-permute-start.23
  92.0 16.5 %all-to-all-start.1 = ((f32[16,24,128]{2,1,0:T(8,128)}), f32[16,24,128]{2,1,0:T(8,128)S(1)}, u32[]{:S(2)}, u32[]{:S(2)}) async-start(f32[16,24,128]{2,1,0:T(8,128)} %get-tuple-element.22), calls=%async_computation.1 | async-start | bytes 393216 | tf_op jit(solution)/shard_map/all_to_all | solution.py:398
  96.0 3.7 %collective-permute-start.24 = (f32[8,128]{1,0:T(8,128)S(1)}, f32[8,128]{1,0:T(8,128)S(1)}, u32[]{:S(2)}, u32[]{:S(2)}) collective-permute-start(f32[8,128]{1,0:T(8,128)S(1)} %get-tuple-element.21), channel_id=1, source_target_pairs={{0,16},{16,0},{1,17},{17,1},{2,18},{18,2},{3,19},{19,3},{4,20},{20... | collective-permute-start | bytes 12296 | tf_op jit(solution)/shard_map/ppermute | solution.py:399
  99.7 5.1 %collective-permute-start.27 = (f32[8,128]{1,0:T(8,128)S(1)}, f32[8,128]{1,0:T(8,128)S(1)}, u32[]{:S(2)}, u32[]{:S(2)}) collective-permute-start(f32[8,128]{1,0:T(8,128)S(1)} %add.28.r0), channel_id=1, source_target_pairs={{0,64},{32,96},{64,0},{96,32},{1,65},{33,97},{65,1},{97,33},{2,66}... | collective-permute-start | bytes 12296 | tf_op jit(solution)/shard_map/ppermute | solution.py:400
  102.4 3.6 %collective-permute-start.26 = (f32[8,128]{1,0:T(8,128)S(1)}, f32[8,128]{1,0:T(8,128)S(1)}, u32[]{:S(2)}, u32[]{:S(2)}) collective-permute-start(f32[8,128]{1,0:T(8,128)S(1)} %add.28.r0), channel_id=1, source_target_pairs={{0,96},{32,0},{64,32},{96,64},{1,97},{33,1},{65,33},{97,65},{2,98}... | collective-permute-start | bytes 12296 | tf_op jit(solution)/shard_map/ppermute | solution.py:400
  103.7 4.8 %collective-permute-start.25 = (f32[8,128]{1,0:T(8,128)S(1)}, f32[8,128]{1,0:T(8,128)S(1)}, u32[]{:S(2)}, u32[]{:S(2)}) collective-permute-start(f32[8,128]{1,0:T(8,128)S(1)} %add.28.r0), channel_id=1, source_target_pairs={{0,32},{32,64},{64,96},{96,0},{1,33},{33,65},{65,97},{97,1},{2,34}... | collective-permute-start | bytes 12296 | tf_op jit(solution)/shard_map/ppermute | solution.py:400
  145.3 29.0 %copy-start = (bf16[2048,320]{0,1:T(8,128)(2,1)S(1)}, bf16[2048,320]{0,1:T(8,128)(2,1)}, u32[]{:S(2)}) copy-start(bf16[2048,320]{0,1:T(8,128)(2,1)} %param.3) | copy-start | bytes 3932164
  146.1 8.0 %collective-permute-start.28 = (bf16[128,1024]{1,0:T(8,128)(2,1)S(1)}, bf16[128,1024]{1,0:T(8,128)(2,1)S(1)}, u32[]{:S(2)}, u32[]{:S(2)}) collective-permute-start(bf16[128,1024]{1,0:T(8,128)(2,1)S(1)} %multiply_convert_fusion.refs_0_), channel_id=1, source_target_pairs={{0,2},{2,0},{1,3},{3,1},{4,6},{6,4},{5,7},{7,5},{8,10},{10,8},{9,1... | collective-permute-start | bytes 786440 | tf_op jit(solution)/shard_map/ppermute | solution.py:42
  149.7 7.6 %collective-permute-start.31 = (bf16[128,1024]{1,0:T(8,128)(2,1)S(1)}, bf16[128,1024]{1,0:T(8,128)(2,1)S(1)}, u32[]{:S(2)}, u32[]{:S(2)}) collective-permute-start(bf16[128,1024]{1,0:T(8,128)(2,1)S(1)} %multiply_convert_fusion.refs_0_), channel_id=1, source_target_pairs={{0,4},{4,8},{8,12},{12,0},{1,5},{5,9},{9,13},{13,1},{2,6},{6,10},{... | collective-permute-start | bytes 786440 | tf_op jit(solution)/shard_map/ppermute | solution.py:44
  151.2 6.4 %collective-permute-start.29 = (bf16[128,1024]{1,0:T(8,128)(2,1)S(1)}, bf16[128,1024]{1,0:T(8,128)(2,1)S(1)}, u32[]{:S(2)}, u32[]{:S(2)}) collective-permute-start(bf16[128,1024]{1,0:T(8,128)(2,1)S(1)} %multiply_convert_fusion.refs_0_), channel_id=1, source_target_pairs={{0,12},{4,0},{8,4},{12,8},{1,13},{5,1},{9,5},{13,9},{2,14},{6,2},{... | collective-permute-start | bytes 786440 | tf_op jit(solution)/shard_map/ppermute | solution.py:43
  153.0 7.8 %collective-permute-start.35 = (bf16[128,1024]{1,0:T(8,128)(2,1)S(1)}, bf16[128,1024]{1,0:T(8,128)(2,1)S(1)}, u32[]{:S(2)}, u32[]{:S(2)}) collective-permute-start(bf16[128,1024]{1,0:T(8,128)(2,1)S(1)} %multiply_convert_fusion.refs_0_), channel_id=1, source_target_pairs={{0,1},{1,0},{2,3},{3,2},{4,5},{5,4},{6,7},{7,6},{8,9},{9,8},{10,11... | collective-permute-start | bytes 786440 | tf_op jit(solution)/shard_map/ppermute | solution.py:30
  154.1 8.8 %collective-permute-start.32 = (bf16[128,1024]{1,0:T(8,128)(2,1)S(1)}, bf16[128,1024]{1,0:T(8,128)(2,1)S(1)}, u32[]{:S(2)}, u32[]{:S(2)}) collective-permute-start(bf16[128,1024]{1,0:T(8,128)(2,1)S(1)} %collective-permute-done.28.refs_1_), channel_id=1, source_target_pairs={{0,4},{4,8},{8,12},{12,0},{1,5},{5,9},{9,13},{13,1},{2,6},{6,10},{... | collective-permute-start | bytes 786440 | tf_op jit(solution)/shard_map/ppermute | solution.py:47
  157.3 5.9 %collective-permute-start.39 = (bf16[128,1024]{1,0:T(8,128)(2,1)S(1)}, bf16[128,1024]{1,0:T(8,128)(2,1)S(1)}, u32[]{:S(2)}, u32[]{:S(2)}) collective-permute-start(bf16[128,1024]{1,0:T(8,128)(2,1)S(1)} %collective-permute-done.31.refs_4_), channel_id=1, source_target_pairs={{0,1},{1,0},{2,3},{3,2},{4,5},{5,4},{6,7},{7,6},{8,9},{9,8},{10,11... | collective-permute-start | bytes 786440 | tf_op jit(solution)/shard_map/ppermute | solution.py:30
  157.6 5.6 %collective-permute-start.37 = (bf16[128,1024]{1,0:T(8,128)(2,1)S(1)}, bf16[128,1024]{1,0:T(8,128)(2,1)S(1)}, u32[]{:S(2)}, u32[]{:S(2)}) collective-permute-start(bf16[128,1024]{1,0:T(8,128)(2,1)S(1)} %collective-permute-done.29.refs_2_), channel_id=1, source_target_pairs={{0,1},{1,0},{2,3},{3,2},{4,5},{5,4},{6,7},{7,6},{8,9},{9,8},{10,11... | collective-permute-start | bytes 786440 | tf_op jit(solution)/shard_map/ppermute | solution.py:30
  157.8 9.6 %collective-permute-start.33 = (bf16[128,1024]{1,0:T(8,128)(2,1)S(1)}, bf16[128,1024]{1,0:T(8,128)(2,1)S(1)}, u32[]{:S(2)}, u32[]{:S(2)}) collective-permute-start(bf16[128,1024]{1,0:T(8,128)(2,1)S(1)} %collective-permute-done.29.refs_2_), channel_id=1, source_target_pairs={{0,12},{4,0},{8,4},{12,8},{1,13},{5,1},{9,5},{13,9},{2,14},{6,2},{... | collective-permute-start | bytes 786440 | tf_op jit(solution)/shard_map/ppermute | solution.py:45
  160.8 11.6 %collective-permute-start.30 = (bf16[128,1024]{1,0:T(8,128)(2,1)S(1)}, bf16[128,1024]{1,0:T(8,128)(2,1)S(1)}, u32[]{:S(2)}, u32[]{:S(2)}) collective-permute-start(bf16[128,1024]{1,0:T(8,128)(2,1)S(1)} %collective-permute-done.28.refs_1_), channel_id=1, source_target_pairs={{0,12},{4,0},{8,4},{12,8},{1,13},{5,1},{9,5},{13,9},{2,14},{6,2},{... | collective-permute-start | bytes 786440 | tf_op jit(solution)/shard_map/ppermute | solution.py:46
  162.9 9.5 %collective-permute-start.34 = (bf16[128,1024]{1,0:T(8,128)(2,1)S(1)}, bf16[128,1024]{1,0:T(8,128)(2,1)S(1)}, u32[]{:S(2)}, u32[]{:S(2)}) collective-permute-start(bf16[128,1024]{1,0:T(8,128)(2,1)S(1)} %collective-permute-done.32.refs_5_), channel_id=1, source_target_pairs={{0,4},{4,8},{8,12},{12,0},{1,5},{5,9},{9,13},{13,1},{2,6},{6,10},{... | collective-permute-start | bytes 786440 | tf_op jit(solution)/shard_map/ppermute | solution.py:51
  163.2 9.7 %collective-permute-start.36 = (bf16[128,1024]{1,0:T(8,128)(2,1)S(1)}, bf16[128,1024]{1,0:T(8,128)(2,1)S(1)}, u32[]{:S(2)}, u32[]{:S(2)}) collective-permute-start(bf16[128,1024]{1,0:T(8,128)(2,1)S(1)} %collective-permute-done.28.refs_1_), channel_id=1, source_target_pairs={{0,1},{1,0},{2,3},{3,2},{4,5},{5,4},{6,7},{7,6},{8,9},{9,8},{10,11... | collective-permute-start | bytes 786440 | tf_op jit(solution)/shard_map/ppermute | solution.py:30
  163.2 9.7 %collective-permute-start.40 = (bf16[128,1024]{1,0:T(8,128)(2,1)S(1)}, bf16[128,1024]{1,0:T(8,128)(2,1)S(1)}, u32[]{:S(2)}, u32[]{:S(2)}) collective-permute-start(bf16[128,1024]{1,0:T(8,128)(2,1)S(1)} %collective-permute-done.32.refs_5_), channel_id=1, source_target_pairs={{0,1},{1,0},{2,3},{3,2},{4,5},{5,4},{6,7},{7,6},{8,9},{9,8},{10,11... | collective-permute-start | bytes 786440 | tf_op jit(solution)/shard_map/ppermute | solution.py:30
  167.4 5.5 %collective-permute-start.41 = (bf16[128,1024]{1,0:T(8,128)(2,1)S(1)}, bf16[128,1024]{1,0:T(8,128)(2,1)S(1)}, u32[]{:S(2)}, u32[]{:S(2)}) collective-permute-start(bf16[128,1024]{1,0:T(8,128)(2,1)S(1)} %collective-permute-done.33.refs_6_), channel_id=1, source_target_pairs={{0,1},{1,0},{2,3},{3,2},{4,5},{5,4},{6,7},{7,6},{8,9},{9,8},{10,11... | collective-permute-start | bytes 786440 | tf_op jit(solution)/shard_map/ppermute | solution.py:30
  172.4 1.5 collective-permute-start.38
  172.4 1.9 collective-permute-start.42
  177.6 19.4 %copy-start.2 = (bf16[320,1024]{1,0:T(8,128)(2,1)S(1)}, bf16[320,1024]{1,0:T(8,128)(2,1)}, u32[]{:S(2)}) copy-start(bf16[320,1024]{1,0:T(8,128)(2,1)} %param.4) | copy-start | bytes 1966084
  193.4 13.6 %all-to-all-start.4 = ((bf16[8,320,128]{2,1,0:T(8,128)(2,1)}), bf16[8,320,128]{2,1,0:T(8,128)(2,1)S(1)}, u32[]{:S(2)}, u32[]{:S(2)}) async-start(bf16[8,320,128]{2,1,0:T(8,128)(2,1)} %broadcast_in_dim.2), calls=%async_computation.4 | async-start | bytes 1310720 | tf_op jit(solution)/shard_map/all_to_all | solution.py:34
